TPU v7x, 32 devices: a whole 2x2x4 slice. The times are simulated.
32 devices in a mesh: grp: 2 (over y), ka: 4 (over z), pb: 2 (over x), wa: 2 (over core).
Axes of the slice: x: 2, y: 2, z: 4, core: 2. Of those that a mesh axis runs over, the one named last changes fastest.
Arguments:
- green: bfloat16 [2, 8, 2, 8, 208], P('wa', ('grp', 'ka'), 'pb'), parts along dimension 1, may hold values from -14 to 14
- fields: float32 [2, 2, 8, 256], P('wa', 'pb', 'grp'), parts along dimension 2, may hold values from -5 to 5
- orbitals: float32 [2, 8, 8, 208], P('wa', 'ka', 'grp'), parts along dimension 2, may hold values from -6 to 6
- chol_half: bfloat16 [2, 8, 2, 104, 256], P('pb', 'ka'), may hold values from -0.21875 to 0.21875
- chol_full: bfloat16 [2, 8, 2, 676, 256], P('pb', 'ka'), may hold values from -0.0546875 to 0.0546875
- chol_count: int32 [2], replicated, may hold values from 128 to 256, as said below
- kq_map: int32 [2, 8], replicated, may hold values from 0 to 7, each once within a row
Outputs:
- propagated: float32 [2, 8, 8, 208], P('wa', 'ka', 'grp'), parts along dimension 2
- energy: float32 [2, 8], P('wa', ('grp', 'ka')), parts along dimension 1
There are 2 independent parts, one for each index of `grp`. A program takes and returns all parts, laid end to end along the dimension named above; an argument that names none is the same for every part. Nothing has to cross between parts.
Inputs may be any that keep to these rules, and one draw needn't show every extreme that they name: `chol_count`: one momentum transfer keeps all 256 vectors.
All inputs are finite; a program needn't handle non-finite values.
Results may differ from a plain program's by a relative error of at most 0.0037.
Values may be sent and summed in bfloat16 or wider, within the bound.
No kernel may reach another device: no remote copies, remote signals or barrier semaphores. Data moves between devices by JAX's collectives and lax.ppermute only.
A program may use at most 64 MiB of HBM per device.

v0:
```python
import jax
import jax.numpy as jnp
from jax import lax
from jax.sharding import PartitionSpec as P

M = 26
NOCC = 4
TAYLOR = 3


BIAS_STEP = 0.5
PROP_STEP = 0.5


def complex_dot(pattern, left_re, left_im, right_re, right_im):
    real_part = jnp.einsum(
        pattern, left_re, right_re, preferred_element_type=jnp.float32
    ) - jnp.einsum(pattern, left_im, right_im, preferred_element_type=jnp.float32)
    imag_part = jnp.einsum(
        pattern, left_re, right_im, preferred_element_type=jnp.float32
    ) + jnp.einsum(pattern, left_im, right_re, preferred_element_type=jnp.float32)
    return (real_part, imag_part)


def make_picker(wanted):

    def picker(running, shard_rows, first_row):
        row_count = shard_rows.shape[0]
        select = (wanted[:, None] == jnp.arange(row_count, dtype=jnp.int32)[None, :]).astype(
            jnp.bfloat16
        )
        return jnp.dot(select, shard_rows, preferred_element_type=jnp.float32)

    return picker


def on_device(green, fields, orbitals, chol_half, chol_full, chol_count, kq_map):
    q_local = chol_half.shape[0]
    k_local = chol_half.shape[1]
    pair_width = chol_half.shape[3]
    chol_cols = chol_half.shape[4]
    ka_count = lax.axis_size("ka")
    pb_count = lax.axis_size("pb")
    ka_pos = lax.axis_index("ka")
    pb_pos = lax.axis_index("pb")
    local_green = lax.all_to_all(green, "ka", split_axis=3, concat_axis=1, tiled=True)
    walkers = local_green.shape[1]
    per_device = walkers // ka_count
    greens = local_green[0].reshape(walkers, q_local, k_local, 2, pair_width)
    counts = lax.dynamic_slice_in_dim(chol_count, pb_pos * q_local, q_local)
    vec_mask = (jnp.arange(chol_cols, dtype=jnp.int32)[None, :] < counts[:, None]).astype(
        jnp.float32
    )
    transfer = 0
    part_re, part_im = complex_dot(
        "wkx,kxn->wn",
        greens[:, transfer, :, 0],
        greens[:, transfer, :, 1],
        chol_half[transfer, :, 0],
        chol_half[transfer, :, 1],
    )
    bias_list_re = [part_re]
    bias_list_im = [part_im]
    bias_re = jnp.stack(bias_list_re)
    bias_im = jnp.stack(bias_list_im)
    field_now = fields[0]
    own_rows = (jnp.arange(walkers, dtype=jnp.int32) // per_device == ka_pos).astype(jnp.float32)
    bias_re, bias_im = lax.psum((bias_re, bias_im), "ka")
    bias_re = bias_re * vec_mask[:, None, :]
    bias_im = bias_im * vec_mask[:, None, :]
    hartree = 0.5 * jnp.sum(bias_re * bias_re + bias_im * bias_im, axis=(0, 2)) * own_rows
    shift_re = ((field_now - BIAS_STEP * bias_re) * vec_mask[:, None, :]).astype(jnp.bfloat16)
    shift_im = (-BIAS_STEP * bias_im * vec_mask[:, None, :]).astype(jnp.bfloat16)
    exchange = jnp.zeros((walkers,), jnp.float32)
    transfer = 0
    for kpoint in range(k_local):
        chol_row = chol_half[transfer, kpoint].reshape(2, NOCC, M, chol_cols)
        green_row = greens[:, transfer, kpoint].reshape(walkers, 2, NOCC, M)
        cross_re, cross_im = complex_dot(
            "ipn,wjp->wijn", chol_row[0], chol_row[1], green_row[:, 0], green_row[:, 1]
        )
        exchange = exchange + 0.5 * jnp.sum(
            (cross_re * cross_re + cross_im * cross_im) * vec_mask[transfer], axis=(1, 2, 3)
        )
    prop_re, prop_im = complex_dot(
        "wn,kyn->wky",
        shift_re[transfer],
        shift_im[transfer],
        chol_full[transfer, :, 0],
        chol_full[transfer, :, 1],
    )
    operators = (
        (PROP_STEP * prop_re).astype(jnp.bfloat16).reshape(walkers, k_local, M, M),
        (PROP_STEP * prop_im).astype(jnp.bfloat16).reshape(walkers, k_local, M, M),
    )
    normalizer = q_local * pb_count * chol_cols
    total_energy = lax.psum(hartree - exchange, ("ka", "pb")) / normalizer
    energy = lax.dynamic_slice_in_dim(total_energy, ka_pos * per_device, per_device).reshape(
        1, per_device
    )
    initial = orbitals[0].reshape(k_local, walkers, 2, NOCC, M)
    row_width = 2 * pair_width
    my_rows = lax.dynamic_slice_in_dim(kq_map, pb_pos * q_local, q_local, 0)
    wanted = lax.dynamic_slice_in_dim(my_rows, ka_pos * k_local, k_local, 1).reshape(
        q_local * k_local
    )
    picker = make_picker(wanted)
    current = initial
    summed_terms = initial
    for degree in range(1, TAYLOR + 1):
        rounded = current.astype(jnp.bfloat16).reshape(k_local, walkers * row_width)
        empty = jnp.zeros((q_local * k_local, walkers * row_width), jnp.float32)
        fetched = picker(empty, lax.all_gather(rounded, "ka", axis=0, tiled=True), jnp.int32(0))
        shifted_rows = fetched.astype(jnp.bfloat16).reshape(q_local, k_local, walkers, 2, NOCC, M)
        out_re, out_im = complex_dot(
            "wkpq,kwiq->kwip",
            operators[0],
            operators[1],
            shifted_rows[0, :, :, 0],
            shifted_rows[0, :, :, 1],
        )
        applied = jnp.stack([out_re, out_im], axis=2)
        applied = lax.psum(applied, "pb")
        current = applied / degree
        summed_terms = summed_terms + current
    propagated = summed_terms.reshape(1, k_local, walkers, row_width)
    return (propagated, energy)


def solution(mesh):
    placed = (
        P("wa", ("grp", "ka"), "pb", None, None),
        P("wa", "pb", "grp", None),
        P("wa", "ka", "grp", None),
        P("pb", "ka", None, None, None),
        P("pb", "ka", None, None, None),
        P(),
        P(),
    )
    return jax.shard_map(
        on_device,
        mesh=mesh,
        in_specs=placed,
        out_specs=(P("wa", "ka", "grp", None), P("wa", ("grp", "ka"))),
        check_vma=False,
    )
```

profile of v0, /device:TPU:0, one launch (start us, length us, event | category | flops | bytes accessed | tf_op | source)
XLA Modules:
  0.0 120.1 jit_solution(11401734015179807088)
XLA Ops:
  0.6 0.7 copy.120
  1.3 0.5 broadcast.57
  1.9 0.7 reduce.4
  2.5 0.6 reshape.104
  3.1 6.3 %all-to-all-start = ((bf16[4,2,208]{2,1,0:T(2,128)(2,1)}), bf16[4,2,208]{2,1,0:T(2,128)(2,1)S(1)}, u32[]{:S(2)}, u32[]{:S(2)}) async-start(bf16[4,2,208]{2,1,0:T(2,128)(2,1)} %reshape.104), calls=%async_computation | async-start | bytes 8192 | tf_op jit(solution)/shard_map/all_to_all | solution.py:46
  9.5 1.2 %dynamic_slice.11 = s32[1]{0:T(128)} dynamic-slice(s32[2]{0:T(128)} %param.12, s32[]{:T(128)S(6)} %select_n.17), dynamic_slice_sizes={1} | dynamic-slice | bytes 12 | tf_op jit(solution)/shard_map/dynamic_slice | solution.py:50
  10.7 0.6 fusion.51
  11.4 0.7 convert_element_type.51
  12.1 13.7 %all-gather = bf16[4,2,832]{2,1,0:T(2,128)(2,1)S(1)} all-gather(bf16[1,2,832]{2,1,0:T(2,128)(2,1)S(1)} %reshape.74), channel_id=1, replica_groups=mesh['grp'=2,'ka'=4,'pb'=2,'wa'=2] {'ka'}, dimensions={0}, use_global_device_ids=true | all-gather | bytes 16640 | tf_op jit(solution)/shard_map/all_gather | solution.py:113
  25.9 0.9 fusion.59
  26.8 4.2 %fusion.58 = (bf16[1,2,1,676,256]{4,2,3,1,0:T(2,128)(2,1)S(1)}, bf16[1,2,1,676,256]{4,2,3,1,0:T(2,128)(2,1)S(1)}) fusion(bf16[1,2,2,676,256]{4,2,3,1,0:T(2,128)(2,1)} %param.11), kind=kLoop, calls=%fused_computation.102 | loop fusion | bytes 2768896 | tf_op jit(solution)/shard_map/slice | solution.py:90
  31.1 0.2 convolution_convert_fusion.2
  31.3 0.6 fusion.50
  33.8 11.7 %all-reduce = (f32[1,4,256]{2,1,0:T(4,128)S(1)}, f32[1,4,256]{2,1,0:T(4,128)S(1)}) all-reduce(f32[1,4,256]{2,1,0:T(4,128)S(1)} %fusion.23, f32[1,4,256]{2,1,0:T(4,128)S(1)} %fusion.21), channel_id=1, replica_groups=mesh['grp'=2,'ka'=4,'pb'=2,'wa'=2] {'ka'}, use_global_device_ids=true, to_apply=%region_0.1 | all-reduce | flops 2048 | bytes 16384 | tf_op jit(solution)/shard_map/psum | solution.py:68
  45.6 0.3 fusion.25
  45.9 0.3 fusion.24
  46.2 0.3 fusion.12
  46.5 0.2 reshape.101
  46.9 0.3 fusion.13
  47.2 0.2 reshape.102
  47.7 8.3 %psum.44 = f32[2,4,2,4,26]{4,3,1,0,2:T(4,128)S(1)} all-reduce(f32[2,4,2,4,26]{4,3,1,0,2:T(4,128)S(1)} %pad_maximum_fusion), channel_id=1, replica_groups=mesh['grp'=2,'ka'=4,'pb'=2,'wa'=2] {'pb'}, use_global_device_ids=true, to_apply=%region_2.3 | all-reduce | flops 1664 | bytes 13312 | tf_op jit(solution)/shard_map/psum | solution.py:123
  56.2 13.1 %all-gather.1 = bf16[4,2,832]{2,1,0:T(2,128)(2,1)S(1)} all-gather(bf16[1,2,832]{2,1,0:T(2,128)(2,1)S(1)} %reshape.76), channel_id=1, replica_groups=mesh['grp'=2,'ka'=4,'pb'=2,'wa'=2] {'ka'}, dimensions={0}, use_global_device_ids=true | all-gather | bytes 16640 | tf_op jit(solution)/shard_map/all_gather | solution.py:113
  69.4 0.2 convolution_convert_fusion.1
  70.3 7.4 %psum.45 = f32[2,4,2,4,26]{4,3,1,0,2:T(4,128)S(1)} all-reduce(f32[2,4,2,4,26]{4,3,1,0,2:T(4,128)S(1)} %pad_maximum_fusion.1), channel_id=1, replica_groups=mesh['grp'=2,'ka'=4,'pb'=2,'wa'=2] {'pb'}, use_global_device_ids=true, to_apply=%region_3.4 | all-reduce | flops 1664 | bytes 13312 | tf_op jit(solution)/shard_map/psum | solution.py:123
  77.9 13.1 %all-gather.2 = bf16[4,2,832]{2,1,0:T(2,128)(2,1)S(1)} all-gather(bf16[1,2,832]{2,1,0:T(2,128)(2,1)S(1)} %reshape.78), channel_id=1, replica_groups=mesh['grp'=2,'ka'=4,'pb'=2,'wa'=2] {'ka'}, dimensions={0}, use_global_device_ids=true | all-gather | bytes 16640 | tf_op jit(solution)/shard_map/all_gather | solution.py:113
  91.0 0.2 convolution_convert_fusion
  91.6 0.3 fusion.9
  92.0 0.3 fusion.8
  92.4 18.6 %psum.47 = f32[4]{0:T(128)S(1)} all-reduce(f32[4]{0:T(128)S(1)} %fusion.52), channel_id=1, replica_groups=mesh['grp'=2,'ka'=4,'pb'=2,'wa'=2] {'ka','pb'}, use_global_device_ids=true, to_apply=%region_8.9 | all-reduce | flops 4 | bytes 32 | tf_op jit(solution)/shard_map/psum | solution.py:97
  111.4 7.4 %psum.46 = f32[2,4,2,4,26]{4,3,1,0,2:T(4,128)S(1)} all-reduce(f32[2,4,2,4,26]{4,3,1,0,2:T(4,128)S(1)} %pad_maximum_fusion.2), channel_id=1, replica_groups=mesh['grp'=2,'ka'=4,'pb'=2,'wa'=2] {'pb'}, use_global_device_ids=true, to_apply=%region_4.5 | all-reduce | flops 1664 | bytes 13312 | tf_op jit(solution)/shard_map/psum | solution.py:123
  118.8 0.7 reshape.72
  119.5 0.6 dynamic_slice.12
  (67 shorter events, 4.7 us)
Async XLA Ops:
  0.6 30.4 %copy-start = (s32[2,8]{1,0:T(2,128)S(1)}, s32[2,8]{1,0:T(2,128)}, u32[]{:S(2)}) copy-start(s32[2,8]{1,0:T(2,128)} %param.13) | copy-start | bytes 196
  3.1 29.2 %all-to-all-start = ((bf16[4,2,208]{2,1,0:T(2,128)(2,1)}), bf16[4,2,208]{2,1,0:T(2,128)(2,1)S(1)}, u32[]{:S(2)}, u32[]{:S(2)}) async-start(bf16[4,2,208]{2,1,0:T(2,128)(2,1)} %reshape.104), calls=%async_computation | async-start | bytes 8192 | tf_op jit(solution)/shard_map/all_to_all | solution.py:46
  26.8 5.2 %copy-start.2 = (f32[1,2,4,208]{3,2,1,0:T(4,128)S(1)}, f32[1,2,4,208]{3,2,1,0:T(4,128)}, u32[]{:S(2)}) copy-start(f32[1,2,4,208]{3,2,1,0:T(4,128)} %param.9) | copy-start | bytes 19972
  26.8 5.7 %copy-start.1 = (bf16[1,2,2,104,256]{4,3,2,1,0:T(8,128)(2,1)S(1)}, bf16[1,2,2,104,256]{4,3,2,1,0:T(8,128)(2,1)}, u32[]{:S(2)}) copy-start(bf16[1,2,2,104,256]{4,3,2,1,0:T(8,128)(2,1)} %param.10) | copy-start | bytes 638980
  31.0 14.4 %copy-start.3 = (f32[1,1,4,256]{3,2,1,0:T(4,128)S(1)}, f32[1,1,4,256]{3,2,1,0:T(4,128)}, u32[]{:S(2)}) copy-start(f32[1,1,4,256]{3,2,1,0:T(4,128)} %param.8) | copy-start | bytes 12292
where the time goes:
time: 121 us; the launch traced here: 120 us
  blocking collectives  93.4 us (77%)
  local copies, waits for them, and re-layouts  11.2 us (9%)
  starting transfers between devices  6.32 us (5%)
  matrix products  5.33 us (4%)
  other arithmetic  2.94 us (2%)
    all_gather x3, blocking collectives, on_device(): lax.all_gather(rounded, 'ka', axis=0, tiled=True)  39.9 us
    psum x3, blocking collectives, on_device(): applied = lax.psum(applied, 'pb')  23.1 us
    psum x1, blocking collectives, on_device(): total_energy = lax.psum(hartree - exchange, ('ka', 'pb')) / normalizer  18.6 us
    psum x1, blocking collectives, on_device(): bias_re, bias_im = lax.psum((bias_re, bias_im), 'ka')  11.7 us
    all_to_all x1, starting transfers between devices, on_device(): lax.all_to_all(green, 'ka', split_axis=3, concat_axis=1, tiled=True)  6.32 us
    slice x1, local copies, waits for them, and re-layouts, on_device(): chol_full[transfer, :, 1]  4.21 us
  transfers between devices with their start and end apart: 1, of which 0 were waited for; matrix products, arithmetic and copies ran while one was open for 8% of the time, Pallas kernels for 0%

commit v1 on v0

v1 whole, which is shorter than its diff:
```python
import functools

import jax
import jax.numpy as jnp
from jax import lax
from jax.experimental import pallas as pl
from jax.experimental.pallas import tpu as pltpu
from jax.sharding import PartitionSpec as P

M = 26
NOCC = 4
TAYLOR = 3
LANES = 128


BIAS_STEP = 0.5
PROP_STEP = 0.5

F32 = jnp.float32
BF16 = jnp.bfloat16


def complex_dot(pattern, left_re, left_im, right_re, right_im):
    real_part = jnp.einsum(
        pattern, left_re, right_re, preferred_element_type=jnp.float32
    ) - jnp.einsum(pattern, left_im, right_im, preferred_element_type=jnp.float32)
    imag_part = jnp.einsum(
        pattern, left_re, right_im, preferred_element_type=jnp.float32
    ) + jnp.einsum(pattern, left_im, right_re, preferred_element_type=jnp.float32)
    return (real_part, imag_part)


def make_picker(wanted):

    def picker(shard_rows):
        row_count = shard_rows.shape[0]
        select = (wanted[:, None] == jnp.arange(row_count, dtype=jnp.int32)[None, :]).astype(
            jnp.bfloat16
        )
        return jnp.dot(select, shard_rows, preferred_element_type=jnp.float32)

    return picker


def with_collectives(green, fields, orbitals, chol_half, chol_full, chol_count, kq_map):
    q_local = chol_half.shape[0]
    k_local = chol_half.shape[1]
    pair_width = chol_half.shape[3]
    chol_cols = chol_half.shape[4]
    ka_count = lax.axis_size("ka")
    pb_count = lax.axis_size("pb")
    ka_pos = lax.axis_index("ka")
    pb_pos = lax.axis_index("pb")
    local_green = lax.all_to_all(green, "ka", split_axis=3, concat_axis=1, tiled=True)
    walkers = local_green.shape[1]
    per_device = walkers // ka_count
    greens = local_green[0].reshape(walkers, q_local, k_local, 2, pair_width)
    counts = lax.dynamic_slice_in_dim(chol_count, pb_pos * q_local, q_local)
    vec_mask = (jnp.arange(chol_cols, dtype=jnp.int32)[None, :] < counts[:, None]).astype(
        jnp.float32
    )
    bias_re, bias_im = complex_dot(
        "wqkx,qkxn->qwn",
        greens[:, :, :, 0],
        greens[:, :, :, 1],
        chol_half[:, :, 0],
        chol_half[:, :, 1],
    )
    own_rows = (jnp.arange(walkers, dtype=jnp.int32) // per_device == ka_pos).astype(jnp.float32)
    bias_re, bias_im = lax.psum((bias_re, bias_im), "ka")
    bias_re = bias_re * vec_mask[:, None, :]
    bias_im = bias_im * vec_mask[:, None, :]
    hartree = 0.5 * jnp.sum(bias_re * bias_re + bias_im * bias_im, axis=(0, 2)) * own_rows
    field_now = jnp.transpose(fields, (1, 0, 2, 3)).reshape(q_local, walkers, chol_cols)
    shift_re = ((field_now - BIAS_STEP * bias_re) * vec_mask[:, None, :]).astype(jnp.bfloat16)
    shift_im = (-BIAS_STEP * bias_im * vec_mask[:, None, :]).astype(jnp.bfloat16)
    exchange = jnp.zeros((walkers,), jnp.float32)
    for transfer in range(q_local):
        for kpoint in range(k_local):
            chol_row = chol_half[transfer, kpoint].reshape(2, NOCC, M, chol_cols)
            green_row = greens[:, transfer, kpoint].reshape(walkers, 2, NOCC, M)
            cross_re, cross_im = complex_dot(
                "ipn,wjp->wijn", chol_row[0], chol_row[1], green_row[:, 0], green_row[:, 1]
            )
            exchange = exchange + 0.5 * jnp.sum(
                (cross_re * cross_re + cross_im * cross_im) * vec_mask[transfer], axis=(1, 2, 3)
            )
    prop_re, prop_im = complex_dot(
        "qwn,qkyn->qwky", shift_re, shift_im, chol_full[:, :, 0], chol_full[:, :, 1]
    )
    shape = (q_local, walkers, k_local, M, M)
    oper_re = (PROP_STEP * prop_re).astype(jnp.bfloat16).reshape(shape)
    oper_im = (PROP_STEP * prop_im).astype(jnp.bfloat16).reshape(shape)
    normalizer = q_local * pb_count * chol_cols
    total_energy = lax.psum(hartree - exchange, ("ka", "pb")) / normalizer
    energy = lax.dynamic_slice_in_dim(total_energy, ka_pos * per_device, per_device).reshape(
        1, per_device
    )
    initial = orbitals[0].reshape(k_local, walkers, 2, NOCC, M)
    row_width = 2 * pair_width
    my_rows = lax.dynamic_slice_in_dim(kq_map, pb_pos * q_local, q_local, 0)
    wanted = lax.dynamic_slice_in_dim(my_rows, ka_pos * k_local, k_local, 1).reshape(
        q_local * k_local
    )
    picker = make_picker(wanted)
    current = initial
    summed_terms = initial
    for degree in range(1, TAYLOR + 1):
        rounded = current.astype(jnp.bfloat16).reshape(k_local, walkers * row_width)
        fetched = picker(lax.all_gather(rounded, "ka", axis=0, tiled=True))
        shifted_rows = fetched.astype(jnp.bfloat16).reshape(q_local, k_local, walkers, 2, NOCC, M)
        out_re, out_im = complex_dot(
            "xwkpq,xkwiq->kwip",
            oper_re,
            oper_im,
            shifted_rows[:, :, :, 0],
            shifted_rows[:, :, :, 1],
        )
        applied = jnp.stack([out_re, out_im], axis=2)
        applied = lax.psum(applied, "pb")
        current = applied / degree
        summed_terms = summed_terms + current
    propagated = summed_terms.reshape(1, k_local, walkers, row_width)
    return (propagated, energy)


def ring(array, axis, shift):
    size = lax.axis_size(axis)
    return lax.ppermute(array, axis, [(at, (at + shift) % size) for at in range(size)])


def pair_ring(array, ka_shift, pb_shift):
    ka_count, pb_count = lax.axis_size("ka"), lax.axis_size("pb")
    pairs = []
    for ka_at in range(ka_count):
        for pb_at in range(pb_count):
            to_ka, to_pb = (ka_at + ka_shift) % ka_count, (pb_at + pb_shift) % pb_count
            pairs.append((ka_at * pb_count + pb_at, to_ka * pb_count + to_pb))
    return lax.ppermute(array, ("ka", "pb"), pairs)


def origin(axis, shift):
    size = lax.axis_size(axis)
    return lax.rem(lax.axis_index(axis) + (size - shift), size)


def column_mask(count_ref, rows, columns):
    kept = count_ref[lax.axis_index("pb")]
    return lax.broadcasted_iota(jnp.int32, (rows, columns), 1) < kept


def bias_kernel(ka_count, k_local, *refs):
    greens, (chol_ref, bias_ref, own_ref, table) = refs[:ka_count], refs[ka_count:]
    for shift, green_ref in enumerate(greens):
        table[origin("ka", shift)] = green_ref[...].astype(F32)
    first = lax.axis_index("ka") * k_local
    width = chol_ref.shape[2]
    total = jnp.zeros(bias_ref.shape, F32)
    for k in range(k_local):
        rows = jnp.concatenate(
            [table[w, pl.ds(first + k, 1), :] for w in range(ka_count)], axis=0
        )
        real, imag = rows[:, :width], rows[:, width:]
        both = jnp.concatenate([real, imag], axis=0)
        turned = jnp.concatenate([-imag, real], axis=0)
        own_ref[k] = both
        total += jnp.dot(both.astype(BF16), chol_ref[k, 0], preferred_element_type=F32)
        total += jnp.dot(turned.astype(BF16), chol_ref[k, 1], preferred_element_type=F32)
    bias_ref[...] = total


def exchange_kernel(k_local, count_ref, own_ref, chol_ref, out_ref):
    walkers, width, columns = own_ref.shape[1] // 2, own_ref.shape[2], chol_ref.shape[3]
    rows = 2 * walkers
    lane = lax.broadcasted_iota(jnp.int32, (rows, LANES), 1)
    total = jnp.zeros((rows, columns), F32)
    for k in range(k_local):
        both = jnp.concatenate([own_ref[k], jnp.zeros((rows, LANES - width), F32)], axis=1)
        turned = jnp.concatenate([-both[walkers:], both[:walkers]], axis=0)
        sides = []
        for side in (both, turned):
            rolled = {
                step: side if step == 0 else pltpu.roll(side, (step * M) % LANES, 1)
                for step in range(1 - NOCC, NOCC)
            }
            blocks = []
            for i in range(NOCC):
                inside = (lane >= i * M) & (lane < (i + 1) * M)
                for j in range(NOCC):
                    blocks.append(jnp.where(inside, rolled[i - j], 0.0))
            sides.append(jnp.concatenate(blocks, axis=0)[:, :width].astype(BF16))
        cross = jnp.dot(sides[0], chol_ref[k, 0], preferred_element_type=F32)
        cross += jnp.dot(sides[1], chol_ref[k, 1], preferred_element_type=F32)
        cross = cross * cross
        for block in range(NOCC * NOCC):
            total += cross[block * rows : (block + 1) * rows]
    total = jnp.where(column_mask(count_ref, rows, columns), total, 0.0)
    total = total[:walkers] + total[walkers:]
    summed = 0.5 * jnp.sum(total, axis=1, keepdims=True)
    out_ref[...] = jnp.broadcast_to(summed, out_ref.shape)


def operator_kernel(ka_count, k_local, count_ref, *refs):
    parts = refs[:ka_count]
    fields_ref, exchange_ref, chol_ref, out_ref, straight, crossed, turned_ref = refs[ka_count:]
    bias = parts[0][...]
    for part in parts[1:]:
        bias = bias + part[...]
    walkers, columns = fields_ref.shape
    pairs = M * M
    bias = jnp.where(column_mask(count_ref, 2 * walkers, columns), bias, 0.0)
    bias_re, bias_im = bias[:walkers], bias[walkers:]
    hartree = 0.5 * jnp.sum(bias_re * bias_re + bias_im * bias_im, axis=1, keepdims=True)
    own = lax.broadcasted_iota(jnp.int32, (walkers, 1), 0) == lax.axis_index("ka")
    energy = jnp.where(own, hartree, 0.0) - exchange_ref[:, :1]
    kept = column_mask(count_ref, walkers, columns)
    shift_re = jnp.where(kept, fields_ref[...] - BIAS_STEP * bias_re, 0.0)
    shift_im = jnp.where(kept, -BIAS_STEP * bias_im, 0.0)
    for k in range(k_local):
        before, after = k * walkers, (k_local - 1 - k) * walkers

        def placed(first, second):
            gap = jnp.zeros((before, columns), F32), jnp.zeros((after, columns), F32)
            rest = jnp.zeros((LANES - 2 * k_local * walkers, columns), F32)
            pieces = [gap[0], first, gap[1], gap[0], second, gap[1], rest]
            return jnp.concatenate([p for p in pieces if p.shape[0]], axis=0)

        sides = jnp.concatenate(
            [placed(shift_re, shift_im), placed(-shift_im, shift_re)], axis=0
        ).astype(BF16)
        product = lax.dot_general(
            chol_ref[k], sides, (((1,), (1,)), ((), ())), preferred_element_type=F32
        )
        if k == 0:
            straight[...] = product[:, :LANES]
            crossed[...] = product[:, LANES:]
        else:
            straight[...] += product[:, :LANES]
            crossed[...] += product[:, LANES:]
    turned_ref[:pairs] = PROP_STEP * (
        straight[pl.ds(0, pairs, stride=2), :] + crossed[pl.ds(1, pairs, stride=2), :]
    )
    rows = out_ref.shape[0]
    width = out_ref.shape[1]
    lane = lax.broadcasted_iota(jnp.int32, (rows, LANES), 1)
    for at in range(0, width, LANES):
        block = turned_ref[at : at + LANES].T[:rows]
        if at + LANES > pairs:
            share = jnp.concatenate([energy, jnp.zeros((rows - walkers, 1), F32)], axis=0)
            block = jnp.where(lane + at < pairs, block, 0.0)
            for piece in range(3):
                head = share.astype(BF16).astype(F32)
                block = jnp.where(lane + at == pairs + piece, head, block)
                share = share - head
        out_ref[:, at : at + LANES] = block.astype(BF16)


def start_kernel(ka_count, pb_count, walkers, map_ref, *refs):
    orbitals, (picks_ref, first_ref, table) = refs[:ka_count], refs[ka_count:]
    k_local, _, width = orbitals[0].shape
    kpoints = k_local * ka_count
    half = LANES // 2
    lane = lax.broadcasted_iota(jnp.int32, (1, LANES), 1)
    lane_q = lax.rem(lane, half) // (kpoints * walkers)
    lane_k = lax.rem(lane, kpoints * walkers) // walkers
    source = jnp.zeros((1, LANES), jnp.int32)
    for q in range(pb_count):
        for k in range(kpoints):
            source = jnp.where((lane_q == q) & (lane_k == k), map_ref[q, k], source)
    wanted = source * walkers + lax.rem(lane, walkers)
    row = lax.broadcasted_iota(jnp.int32, (LANES, LANES), 0)
    real = jnp.where(row == wanted, 1.0, 0.0)
    sign = jnp.where(lane < half, 1.0, -1.0)
    imag = jnp.where(row == wanted + half, sign, 0.0)
    picks = jnp.concatenate([real, imag], axis=1).astype(BF16)
    picks_ref[...] = picks
    pair = width // 2
    table[...] = jnp.zeros_like(table)
    for shift, rows_ref in enumerate(orbitals):
        count = k_local * walkers
        start = pl.multiple_of(origin("ka", shift) * count, count)
        rows = jnp.concatenate([rows_ref[k] for k in range(k_local)], axis=0)
        table[pl.ds(start, count), :pair] = rows[:, :pair]
        table[pl.ds(start + half, count), :pair] = rows[:, pair:]
    turned = table[...].T[:pair].astype(BF16)
    first_ref[...] = jnp.dot(turned, picks, preferred_element_type=F32)


def taylor_kernel(ka_count, pb_count, normalizer, *refs):
    blocks = refs[: ka_count * pb_count]
    picks_ref, first_ref, orbitals_ref, out_ref, energy_ref, table, turned, picked, term = refs[
        ka_count * pb_count :
    ]
    half = LANES // 2
    pairs = M * M
    rows = blocks[0].shape[0] // 2
    for at, block_ref in enumerate(blocks):
        ka_from, pb_from = origin("ka", at // pb_count), origin("pb", at % pb_count)
        start = pl.multiple_of((pb_from * ka_count + ka_from) * rows, rows)
        block = block_ref[...].astype(F32)
        table[pl.ds(start, rows), :] = block[:rows]
        table[pl.ds(start + half, rows), :] = block[rows:]
    for at in range(0, table.shape[1], LANES):
        turned[at : at + LANES] = table[:, at : at + LANES].T
    ka_pos = lax.axis_index("ka")
    last = pairs // LANES * LANES
    shares = table[:half, last : last + LANES]
    lane = lax.broadcasted_iota(jnp.int32, shares.shape, 1) + last
    row = lax.broadcasted_iota(jnp.int32, shares.shape, 0)
    shares = jnp.where(
        (lane >= pairs) & (lane < pairs + 3) & (lax.rem(row, rows) == ka_pos), shares, 0.0
    )
    shares = jnp.sum(jnp.sum(shares, axis=0, keepdims=True), axis=1, keepdims=True)
    energy_ref[...] = shares / normalizer
    sums = [jnp.zeros((M, LANES), F32) for _ in range(NOCC)]
    for degree in range(1, TAYLOR + 1):
        source = first_ref if degree == 1 else picked
        straight = [jnp.zeros((M, LANES), F32) for _ in range(NOCC)]
        crossed = [jnp.zeros((M, LANES), F32) for _ in range(NOCC)]
        for c in range(M):
            column = turned[pl.ds(c, M, stride=M), :]
            for i in range(NOCC):
                at = i * M + c
                straight[i] += column * source[at : at + 1, :LANES]
                crossed[i] += column * source[at : at + 1, LANES:]
        for i in range(NOCC):
            applied = straight[i] + pltpu.roll(crossed[i], half, 1)
            applied = applied + pltpu.roll(applied, LANES - half // pb_count, 1)
            current = applied / degree
            sums[i] = sums[i] + current
            term[i * M : (i + 1) * M] = current if degree < TAYLOR else sums[i]
        if degree < TAYLOR:
            picked[...] = jnp.dot(
                term[: NOCC * M].astype(BF16), picks_ref[...], preferred_element_type=F32
            )
    term[NOCC * M :] = jnp.zeros((LANES - NOCC * M, LANES), F32)
    table[:, :LANES] = term[...].T
    k_local, walkers, _ = out_ref.shape
    pair = NOCC * M
    start = pl.multiple_of(ka_pos * rows, rows)
    real = table[pl.ds(start, rows), :pair]
    imag = table[pl.ds(start + half, rows), :pair]
    both = jnp.concatenate([real, imag], axis=1)
    for k in range(k_local):
        out_ref[k] = orbitals_ref[k] + both[k * walkers : (k + 1) * walkers]


def call(kernel, out, scratch=(), scalars=0, operands=0):
    smem = [pl.BlockSpec(memory_space=pltpu.SMEM)] * scalars
    vmem = [pl.BlockSpec(memory_space=pltpu.VMEM)] * operands
    return pl.pallas_call(
        kernel,
        out_shape=out,
        in_specs=smem + vmem,
        out_specs=jax.tree.map(lambda _: pl.BlockSpec(memory_space=pltpu.VMEM), out),
        scratch_shapes=list(scratch),
        compiler_params=pltpu.CompilerParams(vmem_limit_bytes=24 * 2**20),
    )


def direct(green, fields, orbitals, chol_half, chol_full, chol_count, kq_map):
    k_local, pair_width, chol_cols = chol_half.shape[1], chol_half.shape[3], chol_half.shape[4]
    ka_count, pb_count = lax.axis_size("ka"), lax.axis_size("pb")
    walkers = ka_count
    kpoints = green.shape[3]
    shape = jax.ShapeDtypeStruct
    own_green = green.reshape(kpoints, 2 * pair_width)
    own_orbitals = orbitals.reshape(k_local, walkers, 2 * pair_width)
    greens = [own_green] + [ring(own_green, "ka", s) for s in range(1, ka_count)]
    windows = [own_orbitals] + [ring(own_orbitals, "ka", s) for s in range(1, ka_count)]
    half = chol_half.reshape(k_local, 2, pair_width, chol_cols)
    full = jnp.transpose(chol_full[0], (0, 2, 1, 3)).reshape(k_local, 2 * M * M, chol_cols)
    bias, own = call(
        functools.partial(bias_kernel, ka_count, k_local),
        (shape((2 * walkers, chol_cols), F32), shape((k_local, 2 * walkers, pair_width), F32)),
        [pltpu.VMEM((walkers, kpoints, 2 * pair_width), F32)],
        operands=ka_count + 1,
    )(*greens, half)
    parts = [bias] + [ring(bias, "ka", s) for s in range(1, ka_count)]
    exchange = call(
        functools.partial(exchange_kernel, k_local),
        shape((walkers, LANES), F32),
        scalars=1,
        operands=2,
    )(chol_count, own, half)
    rows = 2 * k_local * walkers
    width = -(-(M * M + 3) // LANES) * LANES
    block = call(
        functools.partial(operator_kernel, ka_count, k_local),
        shape((rows, width), BF16),
        [pltpu.VMEM((2 * M * M, LANES), F32)] * 2 + [pltpu.VMEM((width, LANES), F32)],
        scalars=1,
        operands=ka_count + 3,
    )(chol_count, *parts, fields.reshape(walkers, chol_cols), exchange, full)
    blocks = [
        pair_ring(block, a, b) if a or b else block
        for a in range(ka_count)
        for b in range(pb_count)
    ]
    picks, first = call(
        functools.partial(start_kernel, ka_count, pb_count, walkers),
        (shape((LANES, 2 * LANES), BF16), shape((pair_width, 2 * LANES), F32)),
        [pltpu.VMEM((LANES, LANES), F32)],
        scalars=1,
        operands=ka_count,
    )(kq_map, *windows)
    propagated, energy = call(
        functools.partial(taylor_kernel, ka_count, pb_count, float(pb_count * chol_cols)),
        (shape((k_local, walkers, 2 * pair_width), F32), shape((1, 1), F32)),
        [
            pltpu.VMEM((LANES, width), F32),
            pltpu.VMEM((width, LANES), F32),
            pltpu.VMEM((pair_width, 2 * LANES), F32),
            pltpu.VMEM((LANES, LANES), F32),
        ],
        operands=ka_count * pb_count + 3,
    )(*blocks, picks, first, own_orbitals)
    return (propagated[None], energy)


def on_device(green, fields, orbitals, chol_half, chol_full, chol_count, kq_map):
    ka_count, pb_count = lax.axis_size("ka"), lax.axis_size("pb")
    walkers = orbitals.shape[2]
    fits = 2 * pb_count * kq_map.shape[1] * walkers == LANES
    if fits and chol_half.shape[0] == 1 and walkers == ka_count:
        return direct(green, fields, orbitals, chol_half, chol_full, chol_count, kq_map)
    return with_collectives(green, fields, orbitals, chol_half, chol_full, chol_count, kq_map)


def solution(mesh):
    placed = (
        P("wa", ("grp", "ka"), "pb", None, None),
        P("wa", "pb", "grp", None),
        P("wa", "ka", "grp", None),
        P("pb", "ka", None, None, None),
        P("pb", "ka", None, None, None),
        P(),
        P(),
    )
    return jax.shard_map(
        on_device,
        mesh=mesh,
        in_specs=placed,
        out_specs=(P("wa", "ka", "grp", None), P("wa", ("grp", "ka"))),
        check_vma=False,
    )
```

time: 121 us -> 44.5 us (0.37)
  blocking collectives: 93.4 us -> 0 us
  starting transfers between devices: 6.32 us -> 25.8 us
  waiting for transfers between devices: 0.01 us -> 7.42 us
  local copies, waits for them, and re-layouts: 11.2 us -> 5.01 us
  matrix products: 5.33 us -> 0 us
  Pallas kernels: 0 us -> 5.33 us
  other arithmetic: 2.94 us -> 0 us
    psum x5 -> x0, blocking collectives: 53.4 us -> none  [the longest x3 23.1 us: on_device(): applied = lax.psum(applied, 'pb')]
    all_gather x3 -> x0, blocking collectives: 39.9 us -> none  [on_device(): lax.all_gather(rounded, 'ka', axis=0, tiled=True)]
    ppermute x0 -> x16, starting transfers between devices: none -> 25.8 us  [the longest x9 14.7 us: ring(): lax.ppermute(array, axis, [(at, (at + shift) % size) for at in range(size)])]
    ppermute x0 -> x16, waiting for transfers between devices: none -> 7.42 us  [the longest x9 4.1 us: ring(): lax.ppermute(array, axis, [(at, (at + shift) % size) for at in range(size)])]
    all_to_all x1 -> x0, starting transfers between devices: 6.32 us -> none  [on_device(): lax.all_to_all(green, 'ka', split_axis=3, concat_axis=1, tiled=True)]
    pallas_call x0 -> x5, Pallas kernels: none -> 5.33 us  [the longest x1 2.03 us: direct(): call(functools.partial(taylor_kernel, ka_count, pb_count, float(pb_count...]
    dot_general x31 -> x0, matrix products: 5.33 us -> none  [the longest x7 1.4 us: complex_dot(): jnp.einsum(pattern, left_im, right_re, preferred_element_type=jnp.float32)]
    slice x6 -> x0, local copies, waits for them, and re-layouts: 5.15 us -> none  [the longest x1 4.21 us: on_device(): chol_full[transfer, :, 1]]
  transfers between devices with their start and end apart: 1 -> 16, of which waited for: 0 -> 5; matrix products, arithmetic and copies ran while one was open for 8% -> 8% of each run, Pallas kernels for 0% -> 4%
where the time goes in v1:
time: 44.5 us; the launch traced here: 44.3 us
  starting transfers between devices  25.8 us (58%)
  waiting for transfers between devices  7.42 us (17%)
  Pallas kernels  5.33 us (12%)
  local copies, waits for them, and re-layouts  5.01 us (11%)
  between operations  0.73 us (2%)
    ppermute x9, starting transfers between devices, ring(): lax.ppermute(array, axis, [(at, (at + shift) % size) for at in range(size)])  14.7 us
    ppermute x7, starting transfers between devices, pair_ring(): return lax.ppermute(array, ('ka', 'pb'), pairs)  11.1 us
    ppermute x9, waiting for transfers between devices, ring(): lax.ppermute(array, axis, [(at, (at + shift) % size) for at in range(size)])  4.1 us
    reshape x1, local copies, waits for them, and re-layouts, direct(): jnp.transpose(chol_full[0], (0, 2, 1, 3))  3.37 us
    ppermute x7, waiting for transfers between devices, pair_ring(): return lax.ppermute(array, ('ka', 'pb'), pairs)  3.31 us
    pallas_call x1, Pallas kernels, direct(): call(functools.partial(taylor_kernel, ka_count, pb_count, float(pb_count...  2.03 us
    unnamed x14, local copies, waits for them, and re-layouts  1.64 us
    pallas_call x1, Pallas kernels, direct(): call(functools.partial(operator_kernel, ka_count, k_local), shape((rows,...  1.31 us
  transfers between devices with their start and end apart: 16, of which 5 were waited for; matrix products, arithmetic and copies ran while one was open for 8% of the time, Pallas kernels for 4%

profile of v1, /device:TPU:0, one launch (start us, length us, event | category | flops | bytes accessed | tf_op | source)
XLA Modules:
  0.0 44.3 jit_solution(13666760529447890658)
XLA Ops:
  0.6 3.1 %collective-permute-start = (bf16[8,208]{1,0:T(8,128)(2,1)}, bf16[8,208]{1,0:T(8,128)(2,1)S(1)}, u32[]{:S(2)}, u32[]{:S(2)}) collective-permute-start(bf16[8,208]{1,0:T(8,128)(2,1)} %bitcast.15), channel_id=1, source_target_pairs={{0,4},{4,8},{8,12},{12,0},{1,5},{5,9},{9,13},{13,1},{2,6},{6,10},{... | collective-permute-start | bytes 9992 | tf_op jit(solution)/shard_map/ppermute | solution.py:129
  3.7 2.6 %collective-permute-start.1 = (bf16[8,208]{1,0:T(8,128)(2,1)}, bf16[8,208]{1,0:T(8,128)(2,1)S(1)}, u32[]{:S(2)}, u32[]{:S(2)}) collective-permute-start(bf16[8,208]{1,0:T(8,128)(2,1)} %bitcast.16), channel_id=1, source_target_pairs={{0,8},{4,12},{8,0},{12,4},{1,9},{5,13},{9,1},{13,5},{2,10},{6,14},... | collective-permute-start | bytes 9992 | tf_op jit(solution)/shard_map/ppermute | solution.py:129
  6.3 1.3 %collective-permute-start.2 = (bf16[8,208]{1,0:T(8,128)(2,1)}, bf16[8,208]{1,0:T(8,128)(2,1)S(1)}, u32[]{:S(2)}, u32[]{:S(2)}) collective-permute-start(bf16[8,208]{1,0:T(8,128)(2,1)} %bitcast.17), channel_id=1, source_target_pairs={{0,12},{4,0},{8,4},{12,8},{1,13},{5,1},{9,5},{13,9},{2,14},{6,2},{... | collective-permute-start | bytes 9992 | tf_op jit(solution)/shard_map/ppermute | solution.py:129
  7.6 0.0 collective-permute-done.refs_1_
  7.6 0.8 %collective-permute-done.1.refs_2_ = bf16[8,208]{1,0:T(8,128)(2,1)S(1)} collective-permute-done((bf16[8,208]{1,0:T(8,128)(2,1)}, bf16[8,208]{1,0:T(8,128)(2,1)S(1)}, u32[]{:S(2)}, u32[]{:S(2)}) %collective-permute-start.1) | collective-permute-done | bytes 3360 | tf_op jit(solution)/shard_map/ppermute | solution.py:129
  8.5 1.7 %collective-permute-done.2.refs_3_ = bf16[8,208]{1,0:T(8,128)(2,1)S(1)} collective-permute-done((bf16[8,208]{1,0:T(8,128)(2,1)}, bf16[8,208]{1,0:T(8,128)(2,1)S(1)}, u32[]{:S(2)}, u32[]{:S(2)}) %collective-permute-start.2) | collective-permute-done | bytes 3360 | tf_op jit(solution)/shard_map/ppermute | solution.py:129
  10.1 0.9 %copy-done = bf16[1,2,2,104,256]{4,3,2,1,0:T(8,128)(2,1)S(1)} copy-done((bf16[1,2,2,104,256]{4,3,2,1,0:T(8,128)(2,1)S(1)}, bf16[1,2,2,104,256]{4,3,2,1,0:T(8,128)(2,1)}, u32[]{:S(2)}) %copy-start) | copy-done | bytes 213016
  11.0 0.7 %copy-done.3 = bf16[1,1,1,8,208]{4,3,2,1,0:T(8,128)(2,1)S(1)} copy-done((bf16[1,1,1,8,208]{4,3,2,1,0:T(8,128)(2,1)S(1)}, bf16[1,1,1,8,208]{4,3,2,1,0:T(8,128)(2,1)}, u32[]{:S(2)}) %copy-start.3) | copy-done | bytes 3352
  11.7 0.3 shard_map.86
  12.0 0.1 collective-permute-start.3
  12.1 3.6 %collective-permute-start.4 = (f32[8,256]{1,0:T(8,128)S(1)}, f32[8,256]{1,0:T(8,128)S(1)}, u32[]{:S(2)}, u32[]{:S(2)}) collective-permute-start(f32[8,256]{1,0:T(8,128)S(1)} %get-tuple-element.8.refs_0_), channel_id=1, source_target_pairs={{0,8},{4,12},{8,0},{12,4},{1,9},{5,13},{9,1},{13,5},{2,10},{6,14},... | collective-permute-start | bytes 24584 | tf_op jit(solution)/shard_map/ppermute | solution.py:129
  15.7 0.1 collective-permute-start.5
  15.9 3.4 %reshape.22.refs_6_ = bf16[2,1352,256]{2,1,0:T(8,128)(2,1)S(1)} reshape(bf16[2,676,2,256]{3,2,1,0:T(2,128)(2,1)} %bitcast.20) | data formatting | bytes 2768896 | tf_op jit(solution)/shard_map/reshape | solution.py:372
  19.2 0.0 copy-start.2
  19.3 0.0 copy-start.6
  19.3 0.9 %shard_map.87.refs_5_ = f32[4,128]{1,0:T(4,128)S(1)} custom-call(s32[2]{0:T(128)S(1)} %copy-done.5, f32[2,8,104]{2,1,0:T(8,128)S(1)} %get-tuple-element.9.own_ref, bf16[2,2,104,256]{3,2,1,0:T(8,128)(2,1)S(1)} %bitcast.9), custom_call_target="tpu_custom_call" | custom-call | tf_op jit(solution)/shard_map/pallas_call | solution.py:380
  20.2 0.0 collective-permute-done.3.refs_1_
  20.2 1.3 %shard_map.88.refs_0_ = bf16[16,768]{1,0:T(8,128)(2,1)S(1)} custom-call(s32[2]{0:T(128)S(1)} %copy-done.5, f32[8,256]{1,0:T(8,128)S(1)} %get-tuple-element.8.refs_0_, f32[8,256]{1,0:T(8,128)S(1)} %collective-permute-done.3.refs_1_, f32[8,256]{1,0:T(8,128)S(1)} %collective-permute-done.4.refs_2_, f32[8,256]{1,0:T(8,128)S(1)} %collective-permute-done.5.refs_3_, ...), custom_call_target="tpu_custom_call" | custom-call | tf_op jit(solution)/shard_map/pallas_call | solution.py:388
  21.5 3.0 %collective-permute-start.10 = (bf16[16,768]{1,0:T(8,128)(2,1)S(1)}, bf16[16,768]{1,0:T(8,128)(2,1)S(1)}, u32[]{:S(2)}, u32[]{:S(2)}) collective-permute-start(bf16[16,768]{1,0:T(8,128)(2,1)S(1)} %shard_map.88.refs_0_), channel_id=1, source_target_pairs={{0,10},{2,8},{4,14},{6,12},{8,2},{10,0},{12,6},{14,4},{1,11},{3,9}... | collective-permute-start | bytes 73736 | tf_op jit(solution)/shard_map/ppermute | solution.py:139
  24.5 2.2 %collective-permute-start.11 = (bf16[16,768]{1,0:T(8,128)(2,1)S(1)}, bf16[16,768]{1,0:T(8,128)(2,1)S(1)}, u32[]{:S(2)}, u32[]{:S(2)}) collective-permute-start(bf16[16,768]{1,0:T(8,128)(2,1)S(1)} %shard_map.88.refs_0_), channel_id=1, source_target_pairs={{0,12},{2,14},{4,0},{6,2},{8,4},{10,6},{12,8},{14,10},{1,13},{3,15... | collective-permute-start | bytes 73736 | tf_op jit(solution)/shard_map/ppermute | solution.py:139
  26.8 0.0 collective-permute-start.13
  26.8 0.7 %collective-permute-start.14 = (f32[2,4,208]{2,1,0:T(4,128)S(1)}, f32[2,4,208]{2,1,0:T(4,128)S(1)}, u32[]{:S(2)}, u32[]{:S(2)}) collective-permute-start(f32[2,4,208]{2,1,0:T(4,128)S(1)} %bitcast.11), channel_id=1, source_target_pairs={{0,8},{4,12},{8,0},{12,4},{1,9},{5,13},{9,1},{13,5},{2,10},{6,14},... | collective-permute-start | bytes 19976 | tf_op jit(solution)/shard_map/ppermute | solution.py:129
  27.4 3.1 %collective-permute-start.15 = (f32[2,4,208]{2,1,0:T(4,128)S(1)}, f32[2,4,208]{2,1,0:T(4,128)S(1)}, u32[]{:S(2)}, u32[]{:S(2)}) collective-permute-start(f32[2,4,208]{2,1,0:T(4,128)S(1)} %bitcast.12), channel_id=1, source_target_pairs={{0,12},{4,0},{8,4},{12,8},{1,13},{5,1},{9,5},{13,9},{2,14},{6,2},{... | collective-permute-start | bytes 19976 | tf_op jit(solution)/shard_map/ppermute | solution.py:129
  30.6 1.6 %collective-permute-done.13.refs_1_ = f32[2,4,208]{2,1,0:T(4,128)S(1)} collective-permute-done((f32[2,4,208]{2,1,0:T(4,128)S(1)}, f32[2,4,208]{2,1,0:T(4,128)S(1)}, u32[]{:S(2)}, u32[]{:S(2)}) %collective-permute-start.13) | collective-permute-done | bytes 6688 | tf_op jit(solution)/shard_map/ppermute | solution.py:129
  32.2 1.2 %collective-permute-start.6 = (bf16[16,768]{1,0:T(8,128)(2,1)S(1)}, bf16[16,768]{1,0:T(8,128)(2,1)S(1)}, u32[]{:S(2)}, u32[]{:S(2)}) collective-permute-start(bf16[16,768]{1,0:T(8,128)(2,1)S(1)} %shard_map.88.refs_0_), channel_id=1, source_target_pairs={{0,2},{2,0},{4,6},{6,4},{8,10},{10,8},{12,14},{14,12},{1,3},{3,1},... | collective-permute-start | bytes 73736 | tf_op jit(solution)/shard_map/ppermute | solution.py:139
  33.4 2.3 %collective-permute-start.7 = (bf16[16,768]{1,0:T(8,128)(2,1)S(1)}, bf16[16,768]{1,0:T(8,128)(2,1)S(1)}, u32[]{:S(2)}, u32[]{:S(2)}) collective-permute-start(bf16[16,768]{1,0:T(8,128)(2,1)S(1)} %shard_map.88.refs_0_), channel_id=1, source_target_pairs={{0,4},{2,6},{4,8},{6,10},{8,12},{10,14},{12,0},{14,2},{1,5},{3,7},... | collective-permute-start | bytes 73736 | tf_op jit(solution)/shard_map/ppermute | solution.py:139
  35.7 0.0 collective-permute-start.8
  35.8 2.3 %collective-permute-start.9 = (bf16[16,768]{1,0:T(8,128)(2,1)S(1)}, bf16[16,768]{1,0:T(8,128)(2,1)S(1)}, u32[]{:S(2)}, u32[]{:S(2)}) collective-permute-start(bf16[16,768]{1,0:T(8,128)(2,1)S(1)} %shard_map.88.refs_0_), channel_id=1, source_target_pairs={{0,8},{2,10},{4,12},{6,14},{8,0},{10,2},{12,4},{14,6},{1,9},{3,11}... | collective-permute-start | bytes 73736 | tf_op jit(solution)/shard_map/ppermute | solution.py:139
  38.1 0.8 %shard_map.89 = (bf16[128,256]{1,0:T(8,128)(2,1)S(1)}, f32[104,256]{1,0:T(8,128)S(1)}) custom-call(s32[2,8]{1,0:T(2,128)S(1)} %copy-done.6, f32[2,4,208]{2,1,0:T(4,128)S(1)} %bitcast.13, f32[2,4,208]{2,1,0:T(4,128)S(1)} %collective-permute-done.13.refs_1_, f32[2,4,208]{2,1,0:T(4,128)S(1)} %collective-permute-done.14.refs_2_, ...), custom_call_target="tpu_custom_call" | custom-call | tf_op jit(solution)/shard_map/pallas_call | solution.py:400
  38.9 0.1 collective-permute-done.7.refs_2_
  39.1 3.2 %collective-permute-done.8.refs_3_ = bf16[16,768]{1,0:T(8,128)(2,1)S(1)} collective-permute-done((bf16[16,768]{1,0:T(8,128)(2,1)S(1)}, bf16[16,768]{1,0:T(8,128)(2,1)S(1)}, u32[]{:S(2)}, u32[]{:S(2)}) %collective-permute-start.8) | collective-permute-done | bytes 24608 | tf_op jit(solution)/shard_map/ppermute | solution.py:139
  42.2 2.0 %shard_map.90 = (f32[2,4,208]{2,1,0:T(4,128)}, f32[1,1]{1,0:T(1,128)}) custom-call(bf16[16,768]{1,0:T(8,128)(2,1)S(1)} %shard_map.88.refs_0_, bf16[16,768]{1,0:T(8,128)(2,1)S(1)} %collective-permute-done.6.refs_1_, bf16[16,768]{1,0:T(8,128)(2,1)S(1)} %collective-permute-done.7.refs_2_, bf16[16,768]{1,0:T(8,128)(2,1)S(1)} %collective-permute-done.8.refs_3_, ...), custom_call_target="tpu_custom_call" | custom-call | tf_op jit(solution)/shard_map/pallas_call | solution.py:407
  (20 shorter events, 0.0 us)
Async XLA Ops:
  0.6 7.0 %collective-permute-start = (bf16[8,208]{1,0:T(8,128)(2,1)}, bf16[8,208]{1,0:T(8,128)(2,1)S(1)}, u32[]{:S(2)}, u32[]{:S(2)}) collective-permute-start(bf16[8,208]{1,0:T(8,128)(2,1)} %bitcast.15), channel_id=1, source_target_pairs={{0,4},{4,8},{8,12},{12,0},{1,5},{5,9},{9,13},{13,1},{2,6},{6,10},{... | collective-permute-start | bytes 9992 | tf_op jit(solution)/shard_map/ppermute | solution.py:129
  3.7 4.8 %collective-permute-start.1 = (bf16[8,208]{1,0:T(8,128)(2,1)}, bf16[8,208]{1,0:T(8,128)(2,1)S(1)}, u32[]{:S(2)}, u32[]{:S(2)}) collective-permute-start(bf16[8,208]{1,0:T(8,128)(2,1)} %bitcast.16), channel_id=1, source_target_pairs={{0,8},{4,12},{8,0},{12,4},{1,9},{5,13},{9,1},{13,5},{2,10},{6,14},... | collective-permute-start | bytes 9992 | tf_op jit(solution)/shard_map/ppermute | solution.py:129
  6.3 3.8 %collective-permute-start.2 = (bf16[8,208]{1,0:T(8,128)(2,1)}, bf16[8,208]{1,0:T(8,128)(2,1)S(1)}, u32[]{:S(2)}, u32[]{:S(2)}) collective-permute-start(bf16[8,208]{1,0:T(8,128)(2,1)} %bitcast.17), channel_id=1, source_target_pairs={{0,12},{4,0},{8,4},{12,8},{1,13},{5,1},{9,5},{13,9},{2,14},{6,2},{... | collective-permute-start | bytes 9992 | tf_op jit(solution)/shard_map/ppermute | solution.py:129
  10.1 0.9 %copy-start = (bf16[1,2,2,104,256]{4,3,2,1,0:T(8,128)(2,1)S(1)}, bf16[1,2,2,104,256]{4,3,2,1,0:T(8,128)(2,1)}, u32[]{:S(2)}) copy-start(bf16[1,2,2,104,256]{4,3,2,1,0:T(8,128)(2,1)} %param.10) | copy-start | bytes 638980
  11.0 0.7 %copy-start.3 = (bf16[1,1,1,8,208]{4,3,2,1,0:T(8,128)(2,1)S(1)}, bf16[1,1,1,8,208]{4,3,2,1,0:T(8,128)(2,1)}, u32[]{:S(2)}) copy-start(bf16[1,1,1,8,208]{4,3,2,1,0:T(8,128)(2,1)} %param.7) | copy-start | bytes 9988
  12.0 8.2 %collective-permute-start.3 = (f32[8,256]{1,0:T(8,128)S(1)}, f32[8,256]{1,0:T(8,128)S(1)}, u32[]{:S(2)}, u32[]{:S(2)}) collective-permute-start(f32[8,256]{1,0:T(8,128)S(1)} %get-tuple-element.8.refs_0_), channel_id=1, source_target_pairs={{0,4},{4,8},{8,12},{12,0},{1,5},{5,9},{9,13},{13,1},{2,6},{6,10},{... | collective-permute-start | bytes 24584 | tf_op jit(solution)/shard_map/ppermute | solution.py:129
  12.1 8.1 %collective-permute-start.4 = (f32[8,256]{1,0:T(8,128)S(1)}, f32[8,256]{1,0:T(8,128)S(1)}, u32[]{:S(2)}, u32[]{:S(2)}) collective-permute-start(f32[8,256]{1,0:T(8,128)S(1)} %get-tuple-element.8.refs_0_), channel_id=1, source_target_pairs={{0,8},{4,12},{8,0},{12,4},{1,9},{5,13},{9,1},{13,5},{2,10},{6,14},... | collective-permute-start | bytes 24584 | tf_op jit(solution)/shard_map/ppermute | solution.py:129
  15.7 4.5 %collective-permute-start.5 = (f32[8,256]{1,0:T(8,128)S(1)}, f32[8,256]{1,0:T(8,128)S(1)}, u32[]{:S(2)}, u32[]{:S(2)}) collective-permute-start(f32[8,256]{1,0:T(8,128)S(1)} %get-tuple-element.8.refs_0_), channel_id=1, source_target_pairs={{0,12},{4,0},{8,4},{12,8},{1,13},{5,1},{9,5},{13,9},{2,14},{6,2},{... | collective-permute-start | bytes 24584 | tf_op jit(solution)/shard_map/ppermute | solution.py:129
  15.9 3.4 %copy-start.1 = (bf16[1,2,2,104,256]{4,3,2,1,0:T(8,128)(2,1)S(1)}, bf16[1,2,2,104,256]{4,3,2,1,0:T(8,128)(2,1)}, u32[]{:S(2)}) copy-start(bf16[1,2,2,104,256]{4,3,2,1,0:T(8,128)(2,1)} %param.10) | copy-start | bytes 638980
  15.9 3.4 %copy-start.5 = (s32[2]{0:T(128)S(1)}, s32[2]{0:T(128)}, u32[]{:S(2)}) copy-start(s32[2]{0:T(128)} %count_ref.3) | copy-start | bytes 28
  15.9 4.3 %copy-start.4 = (f32[1,1,4,256]{3,2,1,0:T(4,128)S(1)}, f32[1,1,4,256]{3,2,1,0:T(4,128)}, u32[]{:S(2)}) copy-start(f32[1,1,4,256]{3,2,1,0:T(4,128)} %param.8) | copy-start | bytes 12292
  19.2 7.5 %copy-start.2 = (f32[1,2,4,208]{3,2,1,0:T(4,128)S(1)}, f32[1,2,4,208]{3,2,1,0:T(4,128)}, u32[]{:S(2)}) copy-start(f32[1,2,4,208]{3,2,1,0:T(4,128)} %param.9) | copy-start | bytes 19972
  19.3 18.8 %copy-start.6 = (s32[2,8]{1,0:T(2,128)S(1)}, s32[2,8]{1,0:T(2,128)}, u32[]{:S(2)}) copy-start(s32[2,8]{1,0:T(2,128)} %map_ref.1) | copy-start | bytes 196
  21.5 14.2 %collective-permute-start.10 = (bf16[16,768]{1,0:T(8,128)(2,1)S(1)}, bf16[16,768]{1,0:T(8,128)(2,1)S(1)}, u32[]{:S(2)}, u32[]{:S(2)}) collective-permute-start(bf16[16,768]{1,0:T(8,128)(2,1)S(1)} %shard_map.88.refs_0_), channel_id=1, source_target_pairs={{0,10},{2,8},{4,14},{6,12},{8,2},{10,0},{12,6},{14,4},{1,11},{3,9}... | collective-permute-start | bytes 73736 | tf_op jit(solution)/shard_map/ppermute | solution.py:139
  24.5 11.2 %collective-permute-start.11 = (bf16[16,768]{1,0:T(8,128)(2,1)S(1)}, bf16[16,768]{1,0:T(8,128)(2,1)S(1)}, u32[]{:S(2)}, u32[]{:S(2)}) collective-permute-start(bf16[16,768]{1,0:T(8,128)(2,1)S(1)} %shard_map.88.refs_0_), channel_id=1, source_target_pairs={{0,12},{2,14},{4,0},{6,2},{8,4},{10,6},{12,8},{14,10},{1,13},{3,15... | collective-permute-start | bytes 73736 | tf_op jit(solution)/shard_map/ppermute | solution.py:139
  26.8 5.4 %collective-permute-start.13 = (f32[2,4,208]{2,1,0:T(4,128)S(1)}, f32[2,4,208]{2,1,0:T(4,128)S(1)}, u32[]{:S(2)}, u32[]{:S(2)}) collective-permute-start(f32[2,4,208]{2,1,0:T(4,128)S(1)} %bitcast.10), channel_id=1, source_target_pairs={{0,4},{4,8},{8,12},{12,0},{1,5},{5,9},{9,13},{13,1},{2,6},{6,10},{... | collective-permute-start | bytes 19976 | tf_op jit(solution)/shard_map/ppermute | solution.py:129
  26.8 5.5 %collective-permute-start.14 = (f32[2,4,208]{2,1,0:T(4,128)S(1)}, f32[2,4,208]{2,1,0:T(4,128)S(1)}, u32[]{:S(2)}, u32[]{:S(2)}) collective-permute-start(f32[2,4,208]{2,1,0:T(4,128)S(1)} %bitcast.11), channel_id=1, source_target_pairs={{0,8},{4,12},{8,0},{12,4},{1,9},{5,13},{9,1},{13,5},{2,10},{6,14},... | collective-permute-start | bytes 19976 | tf_op jit(solution)/shard_map/ppermute | solution.py:129
  27.4 6.0 %collective-permute-start.15 = (f32[2,4,208]{2,1,0:T(4,128)S(1)}, f32[2,4,208]{2,1,0:T(4,128)S(1)}, u32[]{:S(2)}, u32[]{:S(2)}) collective-permute-start(f32[2,4,208]{2,1,0:T(4,128)S(1)} %bitcast.12), channel_id=1, source_target_pairs={{0,12},{4,0},{8,4},{12,8},{1,13},{5,1},{9,5},{13,9},{2,14},{6,2},{... | collective-permute-start | bytes 19976 | tf_op jit(solution)/shard_map/ppermute | solution.py:129
  32.2 6.7 %collective-permute-start.12 = (bf16[16,768]{1,0:T(8,128)(2,1)S(1)}, bf16[16,768]{1,0:T(8,128)(2,1)S(1)}, u32[]{:S(2)}, u32[]{:S(2)}) collective-permute-start(bf16[16,768]{1,0:T(8,128)(2,1)S(1)} %shard_map.88.refs_0_), channel_id=1, source_target_pairs={{0,14},{2,12},{4,2},{6,0},{8,6},{10,4},{12,10},{14,8},{1,15},{3,13... | collective-permute-start | bytes 73736 | tf_op jit(solution)/shard_map/ppermute | solution.py:139
  32.2 6.7 %collective-permute-start.6 = (bf16[16,768]{1,0:T(8,128)(2,1)S(1)}, bf16[16,768]{1,0:T(8,128)(2,1)S(1)}, u32[]{:S(2)}, u32[]{:S(2)}) collective-permute-start(bf16[16,768]{1,0:T(8,128)(2,1)S(1)} %shard_map.88.refs_0_), channel_id=1, source_target_pairs={{0,2},{2,0},{4,6},{6,4},{8,10},{10,8},{12,14},{14,12},{1,3},{3,1},... | collective-permute-start | bytes 73736 | tf_op jit(solution)/shard_map/ppermute | solution.py:139
  33.4 5.6 %collective-permute-start.7 = (bf16[16,768]{1,0:T(8,128)(2,1)S(1)}, bf16[16,768]{1,0:T(8,128)(2,1)S(1)}, u32[]{:S(2)}, u32[]{:S(2)}) collective-permute-start(bf16[16,768]{1,0:T(8,128)(2,1)S(1)} %shard_map.88.refs_0_), channel_id=1, source_target_pairs={{0,4},{2,6},{4,8},{6,10},{8,12},{10,14},{12,0},{14,2},{1,5},{3,7},... | collective-permute-start | bytes 73736 | tf_op jit(solution)/shard_map/ppermute | solution.py:139
  35.7 6.5 %collective-permute-start.8 = (bf16[16,768]{1,0:T(8,128)(2,1)S(1)}, bf16[16,768]{1,0:T(8,128)(2,1)S(1)}, u32[]{:S(2)}, u32[]{:S(2)}) collective-permute-start(bf16[16,768]{1,0:T(8,128)(2,1)S(1)} %shard_map.88.refs_0_), channel_id=1, source_target_pairs={{0,6},{2,4},{4,10},{6,8},{8,14},{10,12},{12,2},{14,0},{1,7},{3,5},... | collective-permute-start | bytes 73736 | tf_op jit(solution)/shard_map/ppermute | solution.py:139
  35.8 6.5 %collective-permute-start.9 = (bf16[16,768]{1,0:T(8,128)(2,1)S(1)}, bf16[16,768]{1,0:T(8,128)(2,1)S(1)}, u32[]{:S(2)}, u32[]{:S(2)}) collective-permute-start(bf16[16,768]{1,0:T(8,128)(2,1)S(1)} %shard_map.88.refs_0_), channel_id=1, source_target_pairs={{0,8},{2,10},{4,12},{6,14},{8,0},{10,2},{12,4},{14,6},{1,9},{3,11}... | collective-permute-start | bytes 73736 | tf_op jit(solution)/shard_map/ppermute | solution.py:139

commit v2 on v1

--- a/solution.py
+++ b/solution.py
@@ -124,49 +124,39 @@
     return (propagated, energy)
 
 
-def ring(array, axis, shift):
-    size = lax.axis_size(axis)
-    return lax.ppermute(array, axis, [(at, (at + shift) % size) for at in range(size)])
-
-
-def pair_ring(array, ka_shift, pb_shift):
-    ka_count, pb_count = lax.axis_size("ka"), lax.axis_size("pb")
-    pairs = []
-    for ka_at in range(ka_count):
-        for pb_at in range(pb_count):
-            to_ka, to_pb = (ka_at + ka_shift) % ka_count, (pb_at + pb_shift) % pb_count
-            pairs.append((ka_at * pb_count + pb_at, to_ka * pb_count + to_pb))
-    return lax.ppermute(array, ("ka", "pb"), pairs)
-
-
-def origin(axis, shift):
-    size = lax.axis_size(axis)
-    return lax.rem(lax.axis_index(axis) + (size - shift), size)
-
-
 def column_mask(count_ref, rows, columns):
     kept = count_ref[lax.axis_index("pb")]
     return lax.broadcasted_iota(jnp.int32, (rows, columns), 1) < kept
 
 
-def bias_kernel(ka_count, k_local, *refs):
-    greens, (chol_ref, bias_ref, own_ref, table) = refs[:ka_count], refs[ka_count:]
-    for shift, green_ref in enumerate(greens):
-        table[origin("ka", shift)] = green_ref[...].astype(F32)
-    first = lax.axis_index("ka") * k_local
+def pack_kernel(green_ref, orbitals_ref, out_ref):
+    peers, rows, _ = out_ref.shape
+    kpoints, width = green_ref.shape
+    k_local = kpoints // peers
+    green = green_ref[...].astype(F32)
+    window = jnp.concatenate([orbitals_ref[k] for k in range(k_local)], axis=0)
+    gap = jnp.zeros((rows - window.shape[0] - k_local, width), F32)
+    for peer in range(peers):
+        block = jnp.concatenate([green[peer * k_local : (peer + 1) * k_local], gap, window], axis=0)
+        out_ref[peer, :, :width] = block.astype(BF16)
+        out_ref[peer, :, width:] = jnp.zeros((rows, out_ref.shape[2] - width), BF16)
+
+
+def bias_kernel(k_local, packed_ref, chol_ref, bias_ref, own_ref):
+    copies, rows, columns = bias_ref.shape
     width = chol_ref.shape[2]
-    total = jnp.zeros(bias_ref.shape, F32)
+    blocks = [packed_ref[w].astype(F32) for w in range(packed_ref.shape[0])]
+    total = jnp.zeros((rows, columns), F32)
     for k in range(k_local):
-        rows = jnp.concatenate(
-            [table[w, pl.ds(first + k, 1), :] for w in range(ka_count)], axis=0
-        )
-        real, imag = rows[:, :width], rows[:, width:]
+        green = jnp.concatenate([block[k : k + 1] for block in blocks], axis=0)
+        real, imag = green[:, :width], green[:, width : 2 * width]
         both = jnp.concatenate([real, imag], axis=0)
         turned = jnp.concatenate([-imag, real], axis=0)
         own_ref[k] = both
         total += jnp.dot(both.astype(BF16), chol_ref[k, 0], preferred_element_type=F32)
         total += jnp.dot(turned.astype(BF16), chol_ref[k, 1], preferred_element_type=F32)
-    bias_ref[...] = total
+    for copy in range(copies):
+        bias_ref[copy] = total
 
 
 def exchange_kernel(k_local, count_ref, own_ref, chol_ref, out_ref):
@@ -200,14 +190,14 @@
     out_ref[...] = jnp.broadcast_to(summed, out_ref.shape)
 
 
-def operator_kernel(ka_count, k_local, count_ref, *refs):
-    parts = refs[:ka_count]
-    fields_ref, exchange_ref, chol_ref, out_ref, straight, crossed, turned_ref = refs[ka_count:]
-    bias = parts[0][...]
-    for part in parts[1:]:
-        bias = bias + part[...]
+def operator_kernel(k_local, count_ref, parts_ref, fields_ref, exchange_ref, chol_ref, out_ref, products, turned_ref):
+    bias = parts_ref[0]
+    for part in range(1, parts_ref.shape[0]):
+        bias = bias + parts_ref[part]
     walkers, columns = fields_ref.shape
     pairs = M * M
+    tiles = columns // LANES
+    group = LANES // (2 * tiles)
     bias = jnp.where(column_mask(count_ref, 2 * walkers, columns), bias, 0.0)
     bias_re, bias_im = bias[:walkers], bias[walkers:]
     hartree = 0.5 * jnp.sum(bias_re * bias_re + bias_im * bias_im, axis=1, keepdims=True)
@@ -216,35 +206,37 @@
     kept = column_mask(count_ref, walkers, columns)
     shift_re = jnp.where(kept, fields_ref[...] - BIAS_STEP * bias_re, 0.0)
     shift_im = jnp.where(kept, -BIAS_STEP * bias_im, 0.0)
+    span = k_local * walkers
     for k in range(k_local):
-        before, after = k * walkers, (k_local - 1 - k) * walkers
-
-        def placed(first, second):
-            gap = jnp.zeros((before, columns), F32), jnp.zeros((after, columns), F32)
-            rest = jnp.zeros((LANES - 2 * k_local * walkers, columns), F32)
-            pieces = [gap[0], first, gap[1], gap[0], second, gap[1], rest]
-            return jnp.concatenate([p for p in pieces if p.shape[0]], axis=0)
-
+        before, after = k * walkers, span - (k + 1) * walkers
+        pieces = []
+        for tile in range(tiles):
+            at = slice(tile * LANES, (tile + 1) * LANES)
+            for first, second in ((shift_re, shift_im), (-shift_im, shift_re)):
+                for side in (first, second):
+                    pieces += [(before, None), (walkers, side[:, at]), (after, None)]
+                pieces.append((group - 2 * span, None))
         sides = jnp.concatenate(
-            [placed(shift_re, shift_im), placed(-shift_im, shift_re)], axis=0
+            [jnp.zeros((n, LANES), F32) if p is None else p for n, p in pieces if n], axis=0
         ).astype(BF16)
         product = lax.dot_general(
             chol_ref[k], sides, (((1,), (1,)), ((), ())), preferred_element_type=F32
         )
         if k == 0:
-            straight[...] = product[:, :LANES]
-            crossed[...] = product[:, LANES:]
+            products[...] = product
         else:
-            straight[...] += product[:, :LANES]
-            crossed[...] += product[:, LANES:]
-    turned_ref[:pairs] = PROP_STEP * (
-        straight[pl.ds(0, pairs, stride=2), :] + crossed[pl.ds(1, pairs, stride=2), :]
-    )
-    rows = out_ref.shape[0]
-    width = out_ref.shape[1]
+            products[...] += product
+    lane = lax.broadcasted_iota(jnp.int32, (pairs, LANES), 1)
+    merged = products[pl.ds(0, pairs, stride=2 * tiles), :]
+    for at in range(1, 2 * tiles):
+        row = products[pl.ds(at, pairs, stride=2 * tiles), :]
+        merged = jnp.where(lane >= at * group, row, merged)
+    turned_ref[:pairs] = merged
+    copies, rows, width = out_ref.shape
     lane = lax.broadcasted_iota(jnp.int32, (rows, LANES), 1)
     for at in range(0, width, LANES):
-        block = turned_ref[at : at + LANES].T[:rows]
+        block = turned_ref[at : at + LANES].T
+        block = PROP_STEP * sum(block[n * group : n * group + rows] for n in range(2 * tiles))
         if at + LANES > pairs:
             share = jnp.concatenate([energy, jnp.zeros((rows - walkers, 1), F32)], axis=0)
             block = jnp.where(lane + at < pairs, block, 0.0)
@@ -252,13 +244,16 @@
                 head = share.astype(BF16).astype(F32)
                 block = jnp.where(lane + at == pairs + piece, head, block)
                 share = share - head
-        out_ref[:, at : at + LANES] = block.astype(BF16)
-
-
-def start_kernel(ka_count, pb_count, walkers, map_ref, *refs):
-    orbitals, (picks_ref, first_ref, table) = refs[:ka_count], refs[ka_count:]
-    k_local, _, width = orbitals[0].shape
-    kpoints = k_local * ka_count
+        for copy in range(copies):
+            out_ref[copy, :, at : at + LANES] = block.astype(BF16)
+
+
+def start_kernel(pb_count, map_ref, packed_ref, picks_ref, first_ref, table):
+    ka_count, packed_rows, _ = packed_ref.shape
+    kpoints = map_ref.shape[1]
+    pair = first_ref.shape[0]
+    walkers = ka_count
+    count = kpoints // ka_count * walkers
     half = LANES // 2
     lane = lax.broadcasted_iota(jnp.int32, (1, LANES), 1)
     lane_q = lax.rem(lane, half) // (kpoints * walkers)
@@ -274,32 +269,29 @@
     imag = jnp.where(row == wanted + half, sign, 0.0)
     picks = jnp.concatenate([real, imag], axis=1).astype(BF16)
     picks_ref[...] = picks
-    pair = width // 2
     table[...] = jnp.zeros_like(table)
-    for shift, rows_ref in enumerate(orbitals):
-        count = k_local * walkers
-        start = pl.multiple_of(origin("ka", shift) * count, count)
-        rows = jnp.concatenate([rows_ref[k] for k in range(k_local)], axis=0)
-        table[pl.ds(start, count), :pair] = rows[:, :pair]
-        table[pl.ds(start + half, count), :pair] = rows[:, pair:]
+    for peer in range(ka_count):
+        rows = packed_ref[peer].astype(F32)[packed_rows - count :]
+        table[peer * count : (peer + 1) * count, :pair] = rows[:, :pair]
+        table[peer * count + half : (peer + 1) * count + half, :pair] = rows[:, pair : 2 * pair]
     turned = table[...].T[:pair].astype(BF16)
     first_ref[...] = jnp.dot(turned, picks, preferred_element_type=F32)
 
 
-def taylor_kernel(ka_count, pb_count, normalizer, *refs):
-    blocks = refs[: ka_count * pb_count]
-    picks_ref, first_ref, orbitals_ref, out_ref, energy_ref, table, turned, picked, term = refs[
-        ka_count * pb_count :
-    ]
+def taylor_kernel(
+    pb_count, normalizer, blocks_ref, picks_ref, first_ref, orbitals_ref, out_ref, energy_ref,
+    table, turned, picked, term,
+):
     half = LANES // 2
     pairs = M * M
-    rows = blocks[0].shape[0] // 2
-    for at, block_ref in enumerate(blocks):
-        ka_from, pb_from = origin("ka", at // pb_count), origin("pb", at % pb_count)
-        start = pl.multiple_of((pb_from * ka_count + ka_from) * rows, rows)
-        block = block_ref[...].astype(F32)
-        table[pl.ds(start, rows), :] = block[:rows]
-        table[pl.ds(start + half, rows), :] = block[rows:]
+    ka_count = blocks_ref.shape[0] // pb_count
+    rows = blocks_ref.shape[1] // 2
+    for at in range(ka_count * pb_count):
+        ka_from, pb_from = at // pb_count, at % pb_count
+        start = (pb_from * ka_count + ka_from) * rows
+        block = blocks_ref[at].astype(F32)
+        table[start : start + rows, :] = block[:rows]
+        table[start + half : start + half + rows, :] = block[rows:]
     for at in range(0, table.shape[1], LANES):
         turned[at : at + LANES] = table[:, at : at + LANES].T
     ka_pos = lax.axis_index("ka")
@@ -363,49 +355,53 @@
     ka_count, pb_count = lax.axis_size("ka"), lax.axis_size("pb")
     walkers = ka_count
     kpoints = green.shape[3]
+    span = k_local * walkers
     shape = jax.ShapeDtypeStruct
-    own_green = green.reshape(kpoints, 2 * pair_width)
     own_orbitals = orbitals.reshape(k_local, walkers, 2 * pair_width)
-    greens = [own_green] + [ring(own_green, "ka", s) for s in range(1, ka_count)]
-    windows = [own_orbitals] + [ring(own_orbitals, "ka", s) for s in range(1, ka_count)]
     half = chol_half.reshape(k_local, 2, pair_width, chol_cols)
-    full = jnp.transpose(chol_full[0], (0, 2, 1, 3)).reshape(k_local, 2 * M * M, chol_cols)
+    tiles = chol_cols // LANES
+    full = jnp.transpose(
+        chol_full.reshape(k_local, 2, M * M, tiles, LANES), (0, 2, 3, 1, 4)
+    ).reshape(k_local, M * M * tiles * 2, LANES)
+    packed = call(
+        pack_kernel,
+        shape((ka_count, 8 + span, 2 * LANES), BF16),
+        operands=2,
+    )(green.reshape(kpoints, 2 * pair_width), own_orbitals)
+    packed = lax.all_to_all(packed, "ka", 0, 0, tiled=True)
     bias, own = call(
-        functools.partial(bias_kernel, ka_count, k_local),
-        (shape((2 * walkers, chol_cols), F32), shape((k_local, 2 * walkers, pair_width), F32)),
-        [pltpu.VMEM((walkers, kpoints, 2 * pair_width), F32)],
-        operands=ka_count + 1,
-    )(*greens, half)
-    parts = [bias] + [ring(bias, "ka", s) for s in range(1, ka_count)]
+        functools.partial(bias_kernel, k_local),
+        (
+            shape((ka_count, 2 * walkers, chol_cols), F32),
+            shape((k_local, 2 * walkers, pair_width), F32),
+        ),
+        operands=2,
+    )(packed, half)
+    parts = lax.all_to_all(bias, "ka", 0, 0, tiled=True)
     exchange = call(
         functools.partial(exchange_kernel, k_local),
         shape((walkers, LANES), F32),
         scalars=1,
         operands=2,
     )(chol_count, own, half)
-    rows = 2 * k_local * walkers
     width = -(-(M * M + 3) // LANES) * LANES
-    block = call(
-        functools.partial(operator_kernel, ka_count, k_local),
-        shape((rows, width), BF16),
-        [pltpu.VMEM((2 * M * M, LANES), F32)] * 2 + [pltpu.VMEM((width, LANES), F32)],
+    blocks = call(
+        functools.partial(operator_kernel, k_local),
+        shape((ka_count * pb_count, 2 * span, width), BF16),
+        [pltpu.VMEM((2 * M * M * tiles, LANES), F32), pltpu.VMEM((width, LANES), F32)],
         scalars=1,
-        operands=ka_count + 3,
-    )(chol_count, *parts, fields.reshape(walkers, chol_cols), exchange, full)
-    blocks = [
-        pair_ring(block, a, b) if a or b else block
-        for a in range(ka_count)
-        for b in range(pb_count)
-    ]
+        operands=4,
+    )(chol_count, parts, fields.reshape(walkers, chol_cols), exchange, full)
+    blocks = lax.all_to_all(blocks, ("ka", "pb"), 0, 0, tiled=True)
     picks, first = call(
-        functools.partial(start_kernel, ka_count, pb_count, walkers),
+        functools.partial(start_kernel, pb_count),
         (shape((LANES, 2 * LANES), BF16), shape((pair_width, 2 * LANES), F32)),
         [pltpu.VMEM((LANES, LANES), F32)],
         scalars=1,
-        operands=ka_count,
-    )(kq_map, *windows)
+        operands=1,
+    )(kq_map, packed)
     propagated, energy = call(
-        functools.partial(taylor_kernel, ka_count, pb_count, float(pb_count * chol_cols)),
+        functools.partial(taylor_kernel, pb_count, float(pb_count * chol_cols)),
         (shape((k_local, walkers, 2 * pair_width), F32), shape((1, 1), F32)),
         [
             pltpu.VMEM((LANES, width), F32),
@@ -413,8 +409,8 @@
             pltpu.VMEM((pair_width, 2 * LANES), F32),
             pltpu.VMEM((LANES, LANES), F32),
         ],
-        operands=ka_count * pb_count + 3,
-    )(*blocks, picks, first, own_orbitals)
+        operands=4,
+    )(blocks, picks, first, own_orbitals)
     return (propagated[None], energy)
 
 
@@ -422,6 +418,7 @@
     ka_count, pb_count = lax.axis_size("ka"), lax.axis_size("pb")
     walkers = orbitals.shape[2]
     fits = 2 * pb_count * kq_map.shape[1] * walkers == LANES
+    fits = fits and chol_half.shape[1] * walkers == 8 and chol_half.shape[4] == 2 * LANES
     if fits and chol_half.shape[0] == 1 and walkers == ka_count:
         return direct(green, fields, orbitals, chol_half, chol_full, chol_count, kq_map)
     return with_collectives(green, fields, orbitals, chol_half, chol_full, chol_count, kq_map)

time: 44.5 us -> 42.5 us (0.955)
  starting transfers between devices: 25.8 us -> 6.65 us
  blocking collectives: 0 us -> 11.8 us
  waiting for transfers between devices: 7.42 us -> 10 us
  Pallas kernels: 5.33 us -> 6.91 us
  local copies, waits for them, and re-layouts: 5.01 us -> 5.93 us
    ppermute x16 -> x0, starting transfers between devices: 25.8 us -> none  [the longest x9 14.7 us: ring(): lax.ppermute(array, axis, [(at, (at + shift) % size) for at in range(size)])]
    all_to_all x0 -> x1, blocking collectives: none -> 11.8 us  [direct(): packed = lax.all_to_all(packed, 'ka', 0, 0, tiled=True)]
    all_to_all x0 -> x2, waiting for transfers between devices: none -> 10 us  [the longest x1 6.89 us: direct(): blocks = lax.all_to_all(blocks, ('ka', 'pb'), 0, 0, tiled=True)]
    ppermute x16 -> x0, waiting for transfers between devices: 7.42 us -> none  [the longest x9 4.1 us: ring(): lax.ppermute(array, axis, [(at, (at + shift) % size) for at in range(size)])]
    all_to_all x0 -> x2, starting transfers between devices: none -> 6.65 us  [the longest x1 3.39 us: direct(): blocks = lax.all_to_all(blocks, ('ka', 'pb'), 0, 0, tiled=True)]
    unnamed x14 -> x18, local copies, waits for them, and re-layouts: 1.64 us -> 5.93 us
    reshape x1 -> x0, local copies, waits for them, and re-layouts: 3.37 us -> none  [direct(): jnp.transpose(chol_full[0], (0, 2, 1, 3))]
    pallas_call x4 -> x5, Pallas kernels: 4.43 us -> 6 us  [the longest x1 2.34 us: direct(): call(functools.partial(operator_kernel, k_local), shape((ka_count * pb_co...]
  transfers between devices with their start and end apart: 16 -> 2, of which waited for: 5 -> 2; matrix products, arithmetic and copies ran while one was open for 8% -> 0% of each run, Pallas kernels for 4% -> 4%
where the time goes in v2:
time: 42.5 us; the launch traced here: 42 us
  blocking collectives  11.8 us (28%)
  waiting for transfers between devices  10 us (24%)
  Pallas kernels  6.91 us (16%)
  starting transfers between devices  6.65 us (16%)
  local copies, waits for them, and re-layouts  5.93 us (14%)
  between operations  0.7 us (2%)
    all_to_all x1, blocking collectives, direct(): packed = lax.all_to_all(packed, 'ka', 0, 0, tiled=True)  11.8 us
    all_to_all x1, waiting for transfers between devices, direct(): blocks = lax.all_to_all(blocks, ('ka', 'pb'), 0, 0, tiled=True)  6.89 us
    unnamed x18, local copies, waits for them, and re-layouts  5.93 us
    all_to_all x1, starting transfers between devices, direct(): blocks = lax.all_to_all(blocks, ('ka', 'pb'), 0, 0, tiled=True)  3.39 us
    all_to_all x1, starting transfers between devices, direct(): parts = lax.all_to_all(bias, 'ka', 0, 0, tiled=True)  3.26 us
    all_to_all x1, waiting for transfers between devices, direct(): parts = lax.all_to_all(bias, 'ka', 0, 0, tiled=True)  3.13 us
    pallas_call x1, Pallas kernels, direct(): call(functools.partial(operator_kernel, k_local), shape((ka_count * pb_co...  2.34 us
    pallas_call x1, Pallas kernels, direct(): call(functools.partial(taylor_kernel, pb_count, float(pb_count * chol_col...  1.96 us
  transfers between devices with their start and end apart: 2, of which 2 were waited for; matrix products, arithmetic and copies ran while one was open for 0% of the time, Pallas kernels for 4%

profile of v2, /device:TPU:0, one launch (start us, length us, event | category | flops | bytes accessed | tf_op | source)
XLA Modules:
  0.0 42.0 jit_solution(16935931845146054240)
XLA Ops:
  0.6 0.0 copy-start.8
  0.6 0.0 copy-start.3
  0.6 0.7 %copy-done.3 = f32[1,2,4,208]{3,2,1,0:T(4,128)S(1)} copy-done((f32[1,2,4,208]{3,2,1,0:T(4,128)S(1)}, f32[1,2,4,208]{3,2,1,0:T(4,128)}, u32[]{:S(2)}) %copy-start.3) | copy-done | bytes 6680
  1.3 0.0 copy-start.6
  1.3 0.7 %copy-done.6 = bf16[1,1,1,8,208]{4,3,2,1,0:T(8,128)(2,1)S(1)} copy-done((bf16[1,1,1,8,208]{4,3,2,1,0:T(8,128)(2,1)S(1)}, bf16[1,1,1,8,208]{4,3,2,1,0:T(8,128)(2,1)}, u32[]{:S(2)}) %copy-start.6) | copy-done | bytes 3352
  2.0 0.0 copy-start.4
  2.0 11.8 %all_to_all.15.packed_ref = bf16[4,16,256]{2,1,0:T(8,128)(2,1)S(1)} all-to-all(bf16[4,16,256]{2,1,0:T(8,128)(2,1)S(1)} %shard_map.86), channel_id=1, replica_groups=mesh['grp'=2,'ka'=4,'pb'=2,'wa'=2] {'ka'}, dimensions={0} | all-to-all | bytes 65536 | tf_op jit(solution)/shard_map/all_to_all | solution.py:371
  13.8 0.0 copy-start.1
  13.8 0.9 %copy-done.1 = bf16[1,2,2,104,256]{4,3,2,1,0:T(8,128)(2,1)S(1)} copy-done((bf16[1,2,2,104,256]{4,3,2,1,0:T(8,128)(2,1)S(1)}, bf16[1,2,2,104,256]{4,3,2,1,0:T(8,128)(2,1)}, u32[]{:S(2)}) %copy-start.1) | copy-done | bytes 213016
  14.8 0.9 %shard_map.87 = (f32[4,8,256]{2,1,0:T(8,128)}, f32[2,8,104]{2,1,0:T(8,128)S(1)}) custom-call(bf16[4,16,256]{2,1,0:T(8,128)(2,1)S(1)} %all_to_all.15.packed_ref, bf16[2,2,104,256]{3,2,1,0:T(8,128)(2,1)S(1)} %bitcast.11), custom_call_target="tpu_custom_call" | custom-call | tf_op jit(solution)/shard_map/pallas_call | solution.py:372
  15.6 3.3 %all-to-all-start.1 = ((f32[4,8,256]{2,1,0:T(8,128)}), f32[4,8,256]{2,1,0:T(8,128)S(1)}, u32[]{:S(2)}, u32[]{:S(2)}) async-start(f32[4,8,256]{2,1,0:T(8,128)} %get-tuple-element.8), calls=%async_computation.1 | async-start | bytes 65536 | tf_op jit(solution)/shard_map/all_to_all | solution.py:380
  18.9 0.0 copy-start.2
  18.9 0.9 %copy-done.2 = bf16[1,2,2,104,256]{4,3,2,1,0:T(8,128)(2,1)S(1)} copy-done((bf16[1,2,2,104,256]{4,3,2,1,0:T(8,128)(2,1)S(1)}, bf16[1,2,2,104,256]{4,3,2,1,0:T(8,128)(2,1)}, u32[]{:S(2)}) %copy-start.2) | copy-done | bytes 213016
  19.8 0.0 copy-start.7
  19.8 0.7 %copy-done.7 = s32[2]{0:T(128)S(1)} copy-done((s32[2]{0:T(128)S(1)}, s32[2]{0:T(128)}, u32[]{:S(2)}) %copy-start.7) | copy-done | bytes 32
  20.5 0.9 %shard_map.88.exchange_ref = f32[4,128]{1,0:T(4,128)S(1)} custom-call(s32[2]{0:T(128)S(1)} %copy-done.7, f32[2,8,104]{2,1,0:T(8,128)S(1)} %get-tuple-element.9.own_ref, bf16[2,2,104,256]{3,2,1,0:T(8,128)(2,1)S(1)} %bitcast.12), custom_call_target="tpu_custom_call" | custom-call | tf_op jit(solution)/shard_map/pallas_call | solution.py:381
  21.4 3.1 %all-to-all-done.1.parts_ref = f32[4,8,256]{2,1,0:T(8,128)S(1)} async-done(((f32[4,8,256]{2,1,0:T(8,128)}), f32[4,8,256]{2,1,0:T(8,128)S(1)}, u32[]{:S(2)}, u32[]{:S(2)}) %all-to-all-start.1) | async-done | bytes 32800 | tf_op jit(solution)/shard_map/all_to_all | solution.py:380
  24.5 0.0 copy-start
  24.5 1.3 %copy-done = bf16[1,2,2,676,256]{4,2,3,1,0:T(2,128)(2,1)S(1)} copy-done((bf16[1,2,2,676,256]{4,2,3,1,0:T(2,128)(2,1)S(1)}, bf16[1,2,2,676,256]{4,2,3,1,0:T(2,128)(2,1)}, u32[]{:S(2)}) %copy-start) | copy-done | bytes 1384472
  25.9 0.0 copy-start.5
  25.9 0.7 %copy-done.5 = f32[1,1,4,256]{3,2,1,0:T(4,128)S(1)} copy-done((f32[1,1,4,256]{3,2,1,0:T(4,128)S(1)}, f32[1,1,4,256]{3,2,1,0:T(4,128)}, u32[]{:S(2)}) %copy-start.5) | copy-done | bytes 4120
  26.6 2.3 %shard_map.89 = bf16[8,16,768]{2,1,0:T(8,128)(2,1)} custom-call(s32[2]{0:T(128)S(1)} %copy-done.7, f32[4,8,256]{2,1,0:T(8,128)S(1)} %all-to-all-done.1.parts_ref, f32[4,256]{1,0:T(4,128)S(1)} %bitcast.15, f32[4,128]{1,0:T(4,128)S(1)} %shard_map.88.exchange_ref, bf16[2,2704,128]{2,1,0:T(8,128)(2,1)S(1)} %bitcast.10), custom_call_target="tpu_custom_call" | custom-call | tf_op jit(solution)/shard_map/pallas_call | solution.py:388
  28.9 3.4 %all-to-all-start.2 = ((bf16[8,16,768]{2,1,0:T(8,128)(2,1)}), bf16[8,16,768]{2,1,0:T(8,128)(2,1)S(1)}, u32[]{:S(2)}, u32[]{:S(2)}) async-start(bf16[8,16,768]{2,1,0:T(8,128)(2,1)} %shard_map.89), calls=%async_computation.2 | async-start | bytes 393216 | tf_op jit(solution)/shard_map/all_to_all | solution.py:395
  32.3 0.0 copy-done.8
  32.3 0.8 %shard_map.90 = (bf16[128,256]{1,0:T(8,128)(2,1)S(1)}, f32[104,256]{1,0:T(8,128)S(1)}) custom-call(s32[2,8]{1,0:T(2,128)S(1)} %copy-done.8, bf16[4,16,256]{2,1,0:T(8,128)(2,1)S(1)} %all_to_all.15.packed_ref), custom_call_target="tpu_custom_call" | custom-call | tf_op jit(solution)/shard_map/pallas_call | solution.py:396
  33.1 6.9 %all-to-all-done.2.blocks_ref = bf16[8,16,768]{2,1,0:T(8,128)(2,1)S(1)} async-done(((bf16[8,16,768]{2,1,0:T(8,128)(2,1)}), bf16[8,16,768]{2,1,0:T(8,128)(2,1)S(1)}, u32[]{:S(2)}, u32[]{:S(2)}) %all-to-all-start.2) | async-done | bytes 196640 | tf_op jit(solution)/shard_map/all_to_all | solution.py:395
  40.0 0.0 copy-done.4
  40.0 2.0 %shard_map.91 = (f32[2,4,208]{2,1,0:T(4,128)}, f32[1,1]{1,0:T(1,128)}) custom-call(bf16[8,16,768]{2,1,0:T(8,128)(2,1)S(1)} %all-to-all-done.2.blocks_ref, bf16[128,256]{1,0:T(8,128)(2,1)S(1)} %get-tuple-element.10.picks_ref, f32[104,256]{1,0:T(8,128)S(1)} %get-tuple-element.11.first_ref, f32[2,4,208]{2,1,0:T(4,128)S(1)} %bitcast.14), custom_call_target="tpu_custom_call" | custom-call | tf_op jit(solution)/shard_map/pallas_call | solution.py:403
  (1 shorter events, 0.0 us)
Async XLA Ops:
  0.6 31.7 %copy-start.8 = (s32[2,8]{1,0:T(2,128)S(1)}, s32[2,8]{1,0:T(2,128)}, u32[]{:S(2)}) copy-start(s32[2,8]{1,0:T(2,128)} %map_ref.1) | copy-start | bytes 196
  0.6 0.7 %copy-start.3 = (f32[1,2,4,208]{3,2,1,0:T(4,128)S(1)}, f32[1,2,4,208]{3,2,1,0:T(4,128)}, u32[]{:S(2)}) copy-start(f32[1,2,4,208]{3,2,1,0:T(4,128)} %param.9) | copy-start | bytes 19972
  1.3 0.7 %copy-start.6 = (bf16[1,1,1,8,208]{4,3,2,1,0:T(8,128)(2,1)S(1)}, bf16[1,1,1,8,208]{4,3,2,1,0:T(8,128)(2,1)}, u32[]{:S(2)}) copy-start(bf16[1,1,1,8,208]{4,3,2,1,0:T(8,128)(2,1)} %param.7) | copy-start | bytes 9988
  2.0 38.0 %copy-start.4 = (f32[1,2,4,208]{3,2,1,0:T(4,128)S(1)}, f32[1,2,4,208]{3,2,1,0:T(4,128)}, u32[]{:S(2)}) copy-start(f32[1,2,4,208]{3,2,1,0:T(4,128)} %param.9) | copy-start | bytes 19972
  13.8 0.9 %copy-start.1 = (bf16[1,2,2,104,256]{4,3,2,1,0:T(8,128)(2,1)S(1)}, bf16[1,2,2,104,256]{4,3,2,1,0:T(8,128)(2,1)}, u32[]{:S(2)}) copy-start(bf16[1,2,2,104,256]{4,3,2,1,0:T(8,128)(2,1)} %param.10) | copy-start | bytes 638980
  15.6 8.9 %all-to-all-start.1 = ((f32[4,8,256]{2,1,0:T(8,128)}), f32[4,8,256]{2,1,0:T(8,128)S(1)}, u32[]{:S(2)}, u32[]{:S(2)}) async-start(f32[4,8,256]{2,1,0:T(8,128)} %get-tuple-element.8), calls=%async_computation.1 | async-start | bytes 65536 | tf_op jit(solution)/shard_map/all_to_all | solution.py:380
  18.9 0.9 %copy-start.2 = (bf16[1,2,2,104,256]{4,3,2,1,0:T(8,128)(2,1)S(1)}, bf16[1,2,2,104,256]{4,3,2,1,0:T(8,128)(2,1)}, u32[]{:S(2)}) copy-start(bf16[1,2,2,104,256]{4,3,2,1,0:T(8,128)(2,1)} %param.10) | copy-start | bytes 638980
  19.8 0.7 %copy-start.7 = (s32[2]{0:T(128)S(1)}, s32[2]{0:T(128)}, u32[]{:S(2)}) copy-start(s32[2]{0:T(128)} %count_ref.3) | copy-start | bytes 28
  24.5 1.3 %copy-start = (bf16[1,2,2,676,256]{4,2,3,1,0:T(2,128)(2,1)S(1)}, bf16[1,2,2,676,256]{4,2,3,1,0:T(2,128)(2,1)}, u32[]{:S(2)}) copy-start(bf16[1,2,2,676,256]{4,2,3,1,0:T(2,128)(2,1)} %param.11) | copy-start | bytes 4153348
  25.9 0.7 %copy-start.5 = (f32[1,1,4,256]{3,2,1,0:T(4,128)S(1)}, f32[1,1,4,256]{3,2,1,0:T(4,128)}, u32[]{:S(2)}) copy-start(f32[1,1,4,256]{3,2,1,0:T(4,128)} %param.8) | copy-start | bytes 12292
  28.9 11.1 %all-to-all-start.2 = ((bf16[8,16,768]{2,1,0:T(8,128)(2,1)}), bf16[8,16,768]{2,1,0:T(8,128)(2,1)S(1)}, u32[]{:S(2)}, u32[]{:S(2)}) async-start(bf16[8,16,768]{2,1,0:T(8,128)(2,1)} %shard_map.89), calls=%async_computation.2 | async-start | bytes 393216 | tf_op jit(solution)/shard_map/all_to_all | solution.py:395

commit v3 on v2

--- a/solution.py
+++ b/solution.py
@@ -124,42 +124,73 @@
     return (propagated, energy)
 
 
-def column_mask(count_ref, rows, columns):
+def ring(array, axis, shift):
+    size = lax.axis_size(axis)
+    return lax.ppermute(array, axis, [(at, (at + shift) % size) for at in range(size)])
+
+
+def origin(axis, shift):
+    size = lax.axis_size(axis)
+    return lax.rem(lax.axis_index(axis) + (size - shift), size)
+
+
+def prepare_kernel(pb_count, walkers, loads, map_ref, count_ref, *refs):
+    sources, (mask_ref, picks_ref) = refs[:loads], refs[loads : loads + 2]
+    targets, sems = refs[loads + 2 : 2 * loads + 2], refs[-1]
+    copies = [
+        pltpu.make_async_copy(source, target, sems.at[at])
+        for at, (source, target) in enumerate(zip(sources, targets))
+    ]
+    for copy in copies:
+        copy.start()
     kept = count_ref[lax.axis_index("pb")]
-    return lax.broadcasted_iota(jnp.int32, (rows, columns), 1) < kept
-
-
-def pack_kernel(green_ref, orbitals_ref, out_ref):
-    peers, rows, _ = out_ref.shape
-    kpoints, width = green_ref.shape
-    k_local = kpoints // peers
-    green = green_ref[...].astype(F32)
-    window = jnp.concatenate([orbitals_ref[k] for k in range(k_local)], axis=0)
-    gap = jnp.zeros((rows - window.shape[0] - k_local, width), F32)
-    for peer in range(peers):
-        block = jnp.concatenate([green[peer * k_local : (peer + 1) * k_local], gap, window], axis=0)
-        out_ref[peer, :, :width] = block.astype(BF16)
-        out_ref[peer, :, width:] = jnp.zeros((rows, out_ref.shape[2] - width), BF16)
-
-
-def bias_kernel(k_local, packed_ref, chol_ref, bias_ref, own_ref):
-    copies, rows, columns = bias_ref.shape
+    column = lax.broadcasted_iota(jnp.int32, mask_ref.shape, 1)
+    mask_ref[...] = jnp.where(column < kept, 1.0, 0.0)
+    kpoints = map_ref.shape[1]
+    half = LANES // 2
+    lane = lax.broadcasted_iota(jnp.int32, (1, LANES), 1)
+    lane_q = lax.rem(lane, half) // (kpoints * walkers)
+    lane_k = lax.rem(lane, kpoints * walkers) // walkers
+    source = jnp.zeros((1, LANES), jnp.int32)
+    for q in range(pb_count):
+        for k in range(kpoints):
+            source = jnp.where((lane_q == q) & (lane_k == k), map_ref[q, k], source)
+    wanted = source * walkers + lax.rem(lane, walkers)
+    row = lax.broadcasted_iota(jnp.int32, (LANES, LANES), 0)
+    real = jnp.where(row == wanted, 1.0, 0.0)
+    sign = jnp.where(lane < half, 1.0, -1.0)
+    imag = jnp.where(row == wanted + half, sign, 0.0)
+    picks_ref[...] = jnp.concatenate([real, imag], axis=1).astype(BF16)
+    for copy in copies:
+        copy.wait()
+
+
+def bias_kernel(ka_count, k_local, *refs):
+    greens, (chol_ref, orbitals_ref, bias_ref, own_ref, table) = refs[:ka_count], refs[ka_count:]
+    for shift, green_ref in enumerate(greens):
+        table[origin("ka", shift)] = green_ref[...].astype(F32)
+    first = lax.axis_index("ka") * k_local
     width = chol_ref.shape[2]
-    blocks = [packed_ref[w].astype(F32) for w in range(packed_ref.shape[0])]
-    total = jnp.zeros((rows, columns), F32)
+    rows = 2 * ka_count
+    total = jnp.zeros((rows, bias_ref.shape[1]), F32)
     for k in range(k_local):
-        green = jnp.concatenate([block[k : k + 1] for block in blocks], axis=0)
-        real, imag = green[:, :width], green[:, width : 2 * width]
+        green = jnp.concatenate(
+            [table[w, pl.ds(first + k, 1), :] for w in range(ka_count)], axis=0
+        )
+        real, imag = green[:, :width], green[:, width:]
         both = jnp.concatenate([real, imag], axis=0)
         turned = jnp.concatenate([-imag, real], axis=0)
         own_ref[k] = both
         total += jnp.dot(both.astype(BF16), chol_ref[k, 0], preferred_element_type=F32)
         total += jnp.dot(turned.astype(BF16), chol_ref[k, 1], preferred_element_type=F32)
-    for copy in range(copies):
-        bias_ref[copy] = total
-
-
-def exchange_kernel(k_local, count_ref, own_ref, chol_ref, out_ref):
+    bias_ref[:rows] = total
+    window = jnp.concatenate([orbitals_ref[k] for k in range(k_local)], axis=0)
+    count, width = window.shape
+    bias_ref[rows : rows + count, :width] = window
+    bias_ref[rows : rows + count, width:] = jnp.zeros((count, bias_ref.shape[1] - width), F32)
+
+
+def exchange_kernel(k_local, own_ref, chol_ref, mask_ref, out_ref):
     walkers, width, columns = own_ref.shape[1] // 2, own_ref.shape[2], chol_ref.shape[3]
     rows = 2 * walkers
     lane = lax.broadcasted_iota(jnp.int32, (rows, LANES), 1)
@@ -184,29 +215,32 @@
         cross = cross * cross
         for block in range(NOCC * NOCC):
             total += cross[block * rows : (block + 1) * rows]
-    total = jnp.where(column_mask(count_ref, rows, columns), total, 0.0)
+    total = total * mask_ref[:rows]
     total = total[:walkers] + total[walkers:]
     summed = 0.5 * jnp.sum(total, axis=1, keepdims=True)
     out_ref[...] = jnp.broadcast_to(summed, out_ref.shape)
 
 
-def operator_kernel(k_local, count_ref, parts_ref, fields_ref, exchange_ref, chol_ref, out_ref, products, turned_ref):
-    bias = parts_ref[0]
-    for part in range(1, parts_ref.shape[0]):
-        bias = bias + parts_ref[part]
+def operator_kernel(ka_count, k_local, *refs):
+    parts = refs[:ka_count]
+    fields_ref, mask_ref, exchange_ref, chol_ref, out_ref, products, turned_ref = refs[ka_count:]
     walkers, columns = fields_ref.shape
+    bias = parts[0][: 2 * walkers]
+    for part in parts[1:]:
+        bias = bias + part[: 2 * walkers]
     pairs = M * M
     tiles = columns // LANES
     group = LANES // (2 * tiles)
-    bias = jnp.where(column_mask(count_ref, 2 * walkers, columns), bias, 0.0)
+    bias = bias * mask_ref[: 2 * walkers]
     bias_re, bias_im = bias[:walkers], bias[walkers:]
     hartree = 0.5 * jnp.sum(bias_re * bias_re + bias_im * bias_im, axis=1, keepdims=True)
     own = lax.broadcasted_iota(jnp.int32, (walkers, 1), 0) == lax.axis_index("ka")
     energy = jnp.where(own, hartree, 0.0) - exchange_ref[:, :1]
-    kept = column_mask(count_ref, walkers, columns)
-    shift_re = jnp.where(kept, fields_ref[...] - BIAS_STEP * bias_re, 0.0)
-    shift_im = jnp.where(kept, -BIAS_STEP * bias_im, 0.0)
+    kept = mask_ref[:walkers]
+    shift_re = (fields_ref[...] - BIAS_STEP * bias_re) * kept
+    shift_im = -BIAS_STEP * bias_im * kept
     span = k_local * walkers
+    weights = []
     for k in range(k_local):
         before, after = k * walkers, span - (k + 1) * walkers
         pieces = []
@@ -216,16 +250,17 @@
                 for side in (first, second):
                     pieces += [(before, None), (walkers, side[:, at]), (after, None)]
                 pieces.append((group - 2 * span, None))
-        sides = jnp.concatenate(
-            [jnp.zeros((n, LANES), F32) if p is None else p for n, p in pieces if n], axis=0
-        ).astype(BF16)
-        product = lax.dot_general(
-            chol_ref[k], sides, (((1,), (1,)), ((), ())), preferred_element_type=F32
+        weights.append(
+            jnp.concatenate(
+                [jnp.zeros((n, LANES), F32) if p is None else p for n, p in pieces if n], axis=0
+            ).astype(BF16)
         )
-        if k == 0:
-            products[...] = product
-        else:
-            products[...] += product
+    products[...] = lax.dot_general(
+        jnp.concatenate([chol_ref[k] for k in range(k_local)], axis=1),
+        jnp.concatenate(weights, axis=1),
+        (((1,), (1,)), ((), ())),
+        preferred_element_type=F32,
+    )
     lane = lax.broadcasted_iota(jnp.int32, (pairs, LANES), 1)
     merged = products[pl.ds(0, pairs, stride=2 * tiles), :]
     for at in range(1, 2 * tiles):
@@ -248,43 +283,12 @@
             out_ref[copy, :, at : at + LANES] = block.astype(BF16)
 
 
-def start_kernel(pb_count, map_ref, packed_ref, picks_ref, first_ref, table):
-    ka_count, packed_rows, _ = packed_ref.shape
-    kpoints = map_ref.shape[1]
-    pair = first_ref.shape[0]
-    walkers = ka_count
-    count = kpoints // ka_count * walkers
-    half = LANES // 2
-    lane = lax.broadcasted_iota(jnp.int32, (1, LANES), 1)
-    lane_q = lax.rem(lane, half) // (kpoints * walkers)
-    lane_k = lax.rem(lane, kpoints * walkers) // walkers
-    source = jnp.zeros((1, LANES), jnp.int32)
-    for q in range(pb_count):
-        for k in range(kpoints):
-            source = jnp.where((lane_q == q) & (lane_k == k), map_ref[q, k], source)
-    wanted = source * walkers + lax.rem(lane, walkers)
-    row = lax.broadcasted_iota(jnp.int32, (LANES, LANES), 0)
-    real = jnp.where(row == wanted, 1.0, 0.0)
-    sign = jnp.where(lane < half, 1.0, -1.0)
-    imag = jnp.where(row == wanted + half, sign, 0.0)
-    picks = jnp.concatenate([real, imag], axis=1).astype(BF16)
-    picks_ref[...] = picks
-    table[...] = jnp.zeros_like(table)
-    for peer in range(ka_count):
-        rows = packed_ref[peer].astype(F32)[packed_rows - count :]
-        table[peer * count : (peer + 1) * count, :pair] = rows[:, :pair]
-        table[peer * count + half : (peer + 1) * count + half, :pair] = rows[:, pair : 2 * pair]
-    turned = table[...].T[:pair].astype(BF16)
-    first_ref[...] = jnp.dot(turned, picks, preferred_element_type=F32)
-
-
-def taylor_kernel(
-    pb_count, normalizer, blocks_ref, picks_ref, first_ref, orbitals_ref, out_ref, energy_ref,
-    table, turned, picked, term,
-):
+def taylor_kernel(ka_count, pb_count, normalizer, blocks_ref, *refs):
+    windows = refs[:ka_count]
+    picks_ref, orbitals_ref, out_ref, energy_ref, table, turned, picked, term = refs[ka_count:]
     half = LANES // 2
     pairs = M * M
-    ka_count = blocks_ref.shape[0] // pb_count
+    pair = NOCC * M
     rows = blocks_ref.shape[1] // 2
     for at in range(ka_count * pb_count):
         ka_from, pb_from = at // pb_count, at % pb_count
@@ -304,9 +308,18 @@
     )
     shares = jnp.sum(jnp.sum(shares, axis=0, keepdims=True), axis=1, keepdims=True)
     energy_ref[...] = shares / normalizer
+    term[...] = jnp.zeros_like(term)
+    for shift, window_ref in enumerate(windows):
+        start = pl.multiple_of(origin("ka", shift) * rows, rows)
+        window = window_ref[window_ref.shape[0] - rows :]
+        term[pl.ds(start, rows), :pair] = window[:, :pair]
+        term[pl.ds(start + half, rows), :pair] = window[:, pair : 2 * pair]
+    picked[...] = jnp.dot(
+        term[...].T[:pair].astype(BF16), picks_ref[...], preferred_element_type=F32
+    )
     sums = [jnp.zeros((M, LANES), F32) for _ in range(NOCC)]
     for degree in range(1, TAYLOR + 1):
-        source = first_ref if degree == 1 else picked
+        source = picked
         straight = [jnp.zeros((M, LANES), F32) for _ in range(NOCC)]
         crossed = [jnp.zeros((M, LANES), F32) for _ in range(NOCC)]
         for c in range(M):
@@ -328,7 +341,6 @@
     term[NOCC * M :] = jnp.zeros((LANES - NOCC * M, LANES), F32)
     table[:, :LANES] = term[...].T
     k_local, walkers, _ = out_ref.shape
-    pair = NOCC * M
     start = pl.multiple_of(ka_pos * rows, rows)
     real = table[pl.ds(start, rows), :pair]
     imag = table[pl.ds(start + half, rows), :pair]
@@ -337,13 +349,12 @@
         out_ref[k] = orbitals_ref[k] + both[k * walkers : (k + 1) * walkers]
 
 
-def call(kernel, out, scratch=(), scalars=0, operands=0):
-    smem = [pl.BlockSpec(memory_space=pltpu.SMEM)] * scalars
-    vmem = [pl.BlockSpec(memory_space=pltpu.VMEM)] * operands
+def call(kernel, out, scratch=(), scalars=0, operands=0, arrays=0):
+    spaces = [pltpu.SMEM] * scalars + [pl.ANY] * arrays + [pltpu.VMEM] * operands
     return pl.pallas_call(
         kernel,
         out_shape=out,
-        in_specs=smem + vmem,
+        in_specs=[pl.BlockSpec(memory_space=space) for space in spaces],
         out_specs=jax.tree.map(lambda _: pl.BlockSpec(memory_space=pltpu.VMEM), out),
         scratch_shapes=list(scratch),
         compiler_params=pltpu.CompilerParams(vmem_limit_bytes=24 * 2**20),
@@ -357,51 +368,53 @@
     kpoints = green.shape[3]
     span = k_local * walkers
     shape = jax.ShapeDtypeStruct
-    own_orbitals = orbitals.reshape(k_local, walkers, 2 * pair_width)
-    half = chol_half.reshape(k_local, 2, pair_width, chol_cols)
     tiles = chol_cols // LANES
-    full = jnp.transpose(
-        chol_full.reshape(k_local, 2, M * M, tiles, LANES), (0, 2, 3, 1, 4)
-    ).reshape(k_local, M * M * tiles * 2, LANES)
-    packed = call(
-        pack_kernel,
-        shape((ka_count, 8 + span, 2 * LANES), BF16),
-        operands=2,
-    )(green.reshape(kpoints, 2 * pair_width), own_orbitals)
-    packed = lax.all_to_all(packed, "ka", 0, 0, tiled=True)
+    own_green = green.reshape(kpoints, 2 * pair_width)
+    greens = [own_green] + [ring(own_green, "ka", s) for s in range(1, ka_count)]
+    loaded = (
+        chol_half.reshape(k_local, 2, pair_width, chol_cols),
+        jnp.transpose(
+            chol_full.reshape(k_local, 2, M * M, tiles, LANES), (0, 2, 3, 1, 4)
+        ).reshape(k_local, M * M * tiles * 2, LANES),
+        fields.reshape(walkers, chol_cols),
+        orbitals.reshape(k_local, walkers, 2 * pair_width),
+    )
+    mask, picks, half, full, own_fields, own_orbitals = call(
+        functools.partial(prepare_kernel, pb_count, walkers, len(loaded)),
+        (
+            shape((2 * walkers, chol_cols), F32),
+            shape((LANES, 2 * LANES), BF16),
+            *(shape(x.shape, x.dtype) for x in loaded),
+        ),
+        [pltpu.SemaphoreType.DMA((len(loaded),))],
+        scalars=2,
+        arrays=len(loaded),
+    )(kq_map, chol_count, *loaded)
     bias, own = call(
-        functools.partial(bias_kernel, k_local),
+        functools.partial(bias_kernel, ka_count, k_local),
         (
-            shape((ka_count, 2 * walkers, chol_cols), F32),
+            shape((2 * walkers + span, chol_cols), F32),
             shape((k_local, 2 * walkers, pair_width), F32),
         ),
-        operands=2,
-    )(packed, half)
-    parts = lax.all_to_all(bias, "ka", 0, 0, tiled=True)
+        [pltpu.VMEM((walkers, kpoints, 2 * pair_width), F32)],
+        operands=ka_count + 2,
+    )(*greens, half, own_orbitals)
+    parts = [bias] + [ring(bias, "ka", s) for s in range(1, ka_count)]
     exchange = call(
         functools.partial(exchange_kernel, k_local),
         shape((walkers, LANES), F32),
-        scalars=1,
-        operands=2,
-    )(chol_count, own, half)
+        operands=3,
+    )(own, half, mask)
     width = -(-(M * M + 3) // LANES) * LANES
     blocks = call(
-        functools.partial(operator_kernel, k_local),
+        functools.partial(operator_kernel, ka_count, k_local),
         shape((ka_count * pb_count, 2 * span, width), BF16),
         [pltpu.VMEM((2 * M * M * tiles, LANES), F32), pltpu.VMEM((width, LANES), F32)],
-        scalars=1,
-        operands=4,
-    )(chol_count, parts, fields.reshape(walkers, chol_cols), exchange, full)
+        operands=ka_count + 4,
+    )(*parts, own_fields, mask, exchange, full)
     blocks = lax.all_to_all(blocks, ("ka", "pb"), 0, 0, tiled=True)
-    picks, first = call(
-        functools.partial(start_kernel, pb_count),
-        (shape((LANES, 2 * LANES), BF16), shape((pair_width, 2 * LANES), F32)),
-        [pltpu.VMEM((LANES, LANES), F32)],
-        scalars=1,
-        operands=1,
-    )(kq_map, packed)
     propagated, energy = call(
-        functools.partial(taylor_kernel, pb_count, float(pb_count * chol_cols)),
+        functools.partial(taylor_kernel, ka_count, pb_count, float(pb_count * chol_cols)),
         (shape((k_local, walkers, 2 * pair_width), F32), shape((1, 1), F32)),
         [
             pltpu.VMEM((LANES, width), F32),
@@ -409,8 +422,8 @@
             pltpu.VMEM((pair_width, 2 * LANES), F32),
             pltpu.VMEM((LANES, LANES), F32),
         ],
-        operands=4,
-    )(blocks, picks, first, own_orbitals)
+        operands=ka_count + 3,
+    )(blocks, *parts, picks, own_orbitals)
     return (propagated[None], energy)
 
 

time: 42.5 us -> 36.2 us (0.85)
  waiting for transfers between devices: 10 us -> 5.18 us
  starting transfers between devices: 6.65 us -> 10.1 us
  Pallas kernels: 6.91 us -> 4.59 us
  blocking collectives: 11.8 us -> 10.3 us
  local copies, waits for them, and re-layouts: 5.93 us -> 4.99 us
    ppermute x0 -> x6, starting transfers between devices: none -> 10.1 us  [ring(): lax.ppermute(array, axis, [(at, (at + shift) % size) for at in range(size)])]
    all_to_all x2 -> x0, waiting for transfers between devices: 10 us -> none  [the longest x1 6.89 us: direct(): blocks = lax.all_to_all(blocks, ('ka', 'pb'), 0, 0, tiled=True)]
    all_to_all x2 -> x0, starting transfers between devices: 6.65 us -> none  [the longest x1 3.39 us: direct(): blocks = lax.all_to_all(blocks, ('ka', 'pb'), 0, 0, tiled=True)]
    ppermute x0 -> x6, waiting for transfers between devices: none -> 5.18 us  [ring(): lax.ppermute(array, axis, [(at, (at + shift) % size) for at in range(size)])]
    pallas_call x5 -> x4, Pallas kernels: 6 us -> 4.23 us  [the longest x1 2.08 us: direct(): call(functools.partial(taylor_kernel, ka_count, pb_count, float(pb_count...]
    all_to_all x1, blocking collectives: 11.8 us -> 10.3 us  [direct(): blocks = lax.all_to_all(blocks, ('ka', 'pb'), 0, 0, tiled=True)]
    unnamed x18 -> x14, local copies, waits for them, and re-layouts: 5.93 us -> 4.99 us
    pallas_call x1, Pallas kernels: 0.9 us -> 0.36 us  [direct(): call(functools.partial(exchange_kernel, k_local), shape((walkers, LANES),...]
  transfers between devices with their start and end apart: 2 -> 6, of which waited for: 2 -> 2; matrix products, arithmetic and copies ran while one was open for 0% -> 0% of each run, Pallas kernels for 4% -> 4%
where the time goes in v3:
time: 36.2 us; the launch traced here: 35.9 us
  blocking collectives  10.3 us (28%)
  starting transfers between devices  10.1 us (28%)
  waiting for transfers between devices  5.18 us (14%)
  local copies, waits for them, and re-layouts  4.99 us (14%)
  Pallas kernels  4.59 us (13%)
  between operations  0.7 us (2%)
    all_to_all x1, blocking collectives, direct(): blocks = lax.all_to_all(blocks, ('ka', 'pb'), 0, 0, tiled=True)  10.3 us
    ppermute x6, starting transfers between devices, ring(): lax.ppermute(array, axis, [(at, (at + shift) % size) for at in range(size)])  10.1 us
    ppermute x6, waiting for transfers between devices, ring(): lax.ppermute(array, axis, [(at, (at + shift) % size) for at in range(size)])  5.18 us
    unnamed x14, local copies, waits for them, and re-layouts  4.99 us
    pallas_call x1, Pallas kernels, direct(): call(functools.partial(taylor_kernel, ka_count, pb_count, float(pb_count...  2.08 us
    pallas_call x1, Pallas kernels, direct(): call(functools.partial(prepare_kernel, pb_count, walkers, len(loaded)), (...  1.1 us
    pallas_call x1, Pallas kernels, direct(): call(functools.partial(operator_kernel, ka_count, k_local), shape((ka_cou...  0.77 us
  transfers between devices with their start and end apart: 6, of which 2 were waited for; matrix products, arithmetic and copies ran while one was open for 0% of the time, Pallas kernels for 4%

profile of v3, /device:TPU:0, one launch (start us, length us, event | category | flops | bytes accessed | tf_op | source)
XLA Modules:
  0.0 35.9 jit_solution(18437245981724859831)
XLA Ops:
  0.6 0.0 copy-start.3
  0.6 5.1 %collective-permute-start.2 = (bf16[8,208]{1,0:T(8,128)(2,1)}, bf16[8,208]{1,0:T(8,128)(2,1)S(1)}, u32[]{:S(2)}, u32[]{:S(2)}) collective-permute-start(bf16[8,208]{1,0:T(8,128)(2,1)} %bitcast.13), channel_id=1, source_target_pairs={{0,12},{4,0},{8,4},{12,8},{1,13},{5,1},{9,5},{13,9},{2,14},{6,2},{... | collective-permute-start | bytes 9992 | tf_op jit(solution)/shard_map/ppermute | solution.py:129
  5.7 0.0 collective-permute-start.1
  5.7 1.0 %collective-permute-start = (bf16[8,208]{1,0:T(8,128)(2,1)}, bf16[8,208]{1,0:T(8,128)(2,1)S(1)}, u32[]{:S(2)}, u32[]{:S(2)}) collective-permute-start(bf16[8,208]{1,0:T(8,128)(2,1)} %bitcast.15), channel_id=1, source_target_pairs={{0,4},{4,8},{8,12},{12,0},{1,5},{5,9},{9,13},{13,1},{2,6},{6,10},{... | collective-permute-start | bytes 9992 | tf_op jit(solution)/shard_map/ppermute | solution.py:129
  6.8 0.0 copy-start
  6.8 1.3 %copy-done = bf16[1,2,2,676,256]{4,2,3,1,0:T(2,128)(2,1)S(1)} copy-done((bf16[1,2,2,676,256]{4,2,3,1,0:T(2,128)(2,1)S(1)}, bf16[1,2,2,676,256]{4,2,3,1,0:T(2,128)(2,1)}, u32[]{:S(2)}) %copy-start) | copy-done | bytes 1384472
  8.1 0.0 copy-start.1
  8.1 0.9 %copy-done.1 = bf16[1,2,2,104,256]{4,3,2,1,0:T(8,128)(2,1)S(1)} copy-done((bf16[1,2,2,104,256]{4,3,2,1,0:T(8,128)(2,1)S(1)}, bf16[1,2,2,104,256]{4,3,2,1,0:T(8,128)(2,1)}, u32[]{:S(2)}) %copy-start.1) | copy-done | bytes 213016
  9.0 0.0 copy-start.2
  9.0 0.7 %copy-done.2 = f32[1,2,4,208]{3,2,1,0:T(4,128)S(1)} copy-done((f32[1,2,4,208]{3,2,1,0:T(4,128)S(1)}, f32[1,2,4,208]{3,2,1,0:T(4,128)}, u32[]{:S(2)}) %copy-start.2) | copy-done | bytes 6680
  9.7 0.0 copy-start.4
  9.7 0.7 %copy-done.4 = f32[1,1,4,256]{3,2,1,0:T(4,128)S(1)} copy-done((f32[1,1,4,256]{3,2,1,0:T(4,128)S(1)}, f32[1,1,4,256]{3,2,1,0:T(4,128)}, u32[]{:S(2)}) %copy-start.4) | copy-done | bytes 4120
  10.4 0.0 copy-start.5
  10.4 0.7 %copy-done.5 = s32[2,8]{1,0:T(2,128)S(1)} copy-done((s32[2,8]{1,0:T(2,128)S(1)}, s32[2,8]{1,0:T(2,128)}, u32[]{:S(2)}) %copy-start.5) | copy-done | bytes 88
  11.1 0.0 copy-start.6
  11.1 0.7 %copy-done.6 = s32[2]{0:T(128)S(1)} copy-done((s32[2]{0:T(128)S(1)}, s32[2]{0:T(128)}, u32[]{:S(2)}) %copy-start.6) | copy-done | bytes 32
  11.8 1.1 %shard_map.86 = (f32[8,256]{1,0:T(8,128)S(1)}, bf16[128,256]{1,0:T(8,128)(2,1)S(1)}, bf16[2,2,104,256]{3,2,1,0:T(8,128)(2,1)S(1)}, bf16[2,2704,128]{2,1,0:T(8,12...) custom-call(s32[2,8]{1,0:T(2,128)S(1)} %copy-done.5, s32[2]{0:T(128)S(1)} %copy-done.6, ...), custom_call_target="tpu_custom_call" | custom-call | tf_op jit(solution)/shard_map/pallas_call | solution.py:382
  12.9 0.0 collective-permute-done.2.refs_3_
  12.9 0.0 collective-permute-done.1.refs_2_
  12.9 0.0 collective-permute-done.refs_1_
  12.9 0.0 copy-done.3
  12.9 0.3 shard_map.87
  13.2 2.8 %collective-permute-start.5 = (f32[16,256]{1,0:T(8,128)S(1)}, f32[16,256]{1,0:T(8,128)S(1)}, u32[]{:S(2)}, u32[]{:S(2)}) collective-permute-start(f32[16,256]{1,0:T(8,128)S(1)} %get-tuple-element.14.refs_0_), channel_id=1, source_target_pairs={{0,12},{4,0},{8,4},{12,8},{1,13},{5,1},{9,5},{13,9},{2,14},{6,2},{... | collective-permute-start | bytes 49160 | tf_op jit(solution)/shard_map/ppermute | solution.py:129
  16.0 1.1 %collective-permute-start.4 = (f32[16,256]{1,0:T(8,128)S(1)}, f32[16,256]{1,0:T(8,128)S(1)}, u32[]{:S(2)}, u32[]{:S(2)}) collective-permute-start(f32[16,256]{1,0:T(8,128)S(1)} %get-tuple-element.14.refs_0_), channel_id=1, source_target_pairs={{0,8},{4,12},{8,0},{12,4},{1,9},{5,13},{9,1},{13,5},{2,10},{6,14},... | collective-permute-start | bytes 49160 | tf_op jit(solution)/shard_map/ppermute | solution.py:129
  17.1 0.0 collective-permute-start.3
  17.1 0.4 %shard_map.88.refs_6_ = f32[4,128]{1,0:T(4,128)S(1)} custom-call(f32[2,8,104]{2,1,0:T(8,128)S(1)} %get-tuple-element.17.own_ref, bf16[2,2,104,256]{3,2,1,0:T(8,128)(2,1)S(1)} %get-tuple-element.12.refs_4_.chol_ref, f32[8,256]{1,0:T(8,128)S(1)} %get-tuple-element.16.mask_ref.refs_5_), custom_call_target="tpu_custom_call" | custom-call | tf_op jit(solution)/shard_map/pallas_call | solution.py:403
  17.5 0.0 collective-permute-done.5.refs_3_
  17.5 3.1 %collective-permute-done.4.refs_2_ = f32[16,256]{1,0:T(8,128)S(1)} collective-permute-done((f32[16,256]{1,0:T(8,128)S(1)}, f32[16,256]{1,0:T(8,128)S(1)}, u32[]{:S(2)}, u32[]{:S(2)}) %collective-permute-start.4) | collective-permute-done | bytes 16416 | tf_op jit(solution)/shard_map/ppermute | solution.py:129
  20.7 2.0 %collective-permute-done.3.refs_1_ = f32[16,256]{1,0:T(8,128)S(1)} collective-permute-done((f32[16,256]{1,0:T(8,128)S(1)}, f32[16,256]{1,0:T(8,128)S(1)}, u32[]{:S(2)}, u32[]{:S(2)}) %collective-permute-start.3) | collective-permute-done | bytes 16416 | tf_op jit(solution)/shard_map/ppermute | solution.py:129
  22.7 0.8 %shard_map.89 = bf16[8,16,768]{2,1,0:T(8,128)(2,1)S(1)} custom-call(f32[16,256]{1,0:T(8,128)S(1)} %get-tuple-element.14.refs_0_, f32[16,256]{1,0:T(8,128)S(1)} %collective-permute-done.3.refs_1_, f32[16,256]{1,0:T(8,128)S(1)} %collective-permute-done.4.refs_2_, f32[16,256]{1,0:T(8,128)S(1)} %collective-permute-done.5.refs_3_, ...), custom_call_target="tpu_custom_call" | custom-call | tf_op jit(solution)/shard_map/pallas_call | solution.py:409
  23.5 10.3 %all_to_all.5.blocks_ref = bf16[8,16,768]{2,1,0:T(8,128)(2,1)S(1)} all-to-all(bf16[8,16,768]{2,1,0:T(8,128)(2,1)S(1)} %shard_map.89), channel_id=1, replica_groups=mesh['grp'=2,'ka'=4,'pb'=2,'wa'=2] {'ka','pb'}, dimensions={0} | all-to-all | bytes 393216 | tf_op jit(solution)/shard_map/all_to_all | solution.py:415
  33.8 2.1 %shard_map.90 = (f32[2,4,208]{2,1,0:T(4,128)}, f32[1,1]{1,0:T(1,128)}) custom-call(bf16[8,16,768]{2,1,0:T(8,128)(2,1)S(1)} %all_to_all.5.blocks_ref, f32[16,256]{1,0:T(8,128)S(1)} %get-tuple-element.14.refs_0_, f32[16,256]{1,0:T(8,128)S(1)} %collective-permute-done.3.refs_1_, f32[16,256]{1,0:T(8,128)S(1)} %collective-permute-done.4.refs_2_, ...), custom_call_target="tpu_custom_call" | custom-call | tf_op jit(solution)/shard_map/pallas_call | solution.py:416
Async XLA Ops:
  0.6 12.3 %copy-start.3 = (bf16[1,1,1,8,208]{4,3,2,1,0:T(8,128)(2,1)S(1)}, bf16[1,1,1,8,208]{4,3,2,1,0:T(8,128)(2,1)}, u32[]{:S(2)}) copy-start(bf16[1,1,1,8,208]{4,3,2,1,0:T(8,128)(2,1)} %param.7) | copy-start | bytes 9988
  0.6 12.2 %collective-permute-start.2 = (bf16[8,208]{1,0:T(8,128)(2,1)}, bf16[8,208]{1,0:T(8,128)(2,1)S(1)}, u32[]{:S(2)}, u32[]{:S(2)}) collective-permute-start(bf16[8,208]{1,0:T(8,128)(2,1)} %bitcast.13), channel_id=1, source_target_pairs={{0,12},{4,0},{8,4},{12,8},{1,13},{5,1},{9,5},{13,9},{2,14},{6,2},{... | collective-permute-start | bytes 9992 | tf_op jit(solution)/shard_map/ppermute | solution.py:129
  5.7 7.1 %collective-permute-start.1 = (bf16[8,208]{1,0:T(8,128)(2,1)}, bf16[8,208]{1,0:T(8,128)(2,1)S(1)}, u32[]{:S(2)}, u32[]{:S(2)}) collective-permute-start(bf16[8,208]{1,0:T(8,128)(2,1)} %bitcast.14), channel_id=1, source_target_pairs={{0,8},{4,12},{8,0},{12,4},{1,9},{5,13},{9,1},{13,5},{2,10},{6,14},... | collective-permute-start | bytes 9992 | tf_op jit(solution)/shard_map/ppermute | solution.py:129
  5.7 7.1 %collective-permute-start = (bf16[8,208]{1,0:T(8,128)(2,1)}, bf16[8,208]{1,0:T(8,128)(2,1)S(1)}, u32[]{:S(2)}, u32[]{:S(2)}) collective-permute-start(bf16[8,208]{1,0:T(8,128)(2,1)} %bitcast.15), channel_id=1, source_target_pairs={{0,4},{4,8},{8,12},{12,0},{1,5},{5,9},{9,13},{13,1},{2,6},{6,10},{... | collective-permute-start | bytes 9992 | tf_op jit(solution)/shard_map/ppermute | solution.py:129
  6.8 1.3 %copy-start = (bf16[1,2,2,676,256]{4,2,3,1,0:T(2,128)(2,1)S(1)}, bf16[1,2,2,676,256]{4,2,3,1,0:T(2,128)(2,1)}, u32[]{:S(2)}) copy-start(bf16[1,2,2,676,256]{4,2,3,1,0:T(2,128)(2,1)} %param.11) | copy-start | bytes 4153348
  8.1 0.9 %copy-start.1 = (bf16[1,2,2,104,256]{4,3,2,1,0:T(8,128)(2,1)S(1)}, bf16[1,2,2,104,256]{4,3,2,1,0:T(8,128)(2,1)}, u32[]{:S(2)}) copy-start(bf16[1,2,2,104,256]{4,3,2,1,0:T(8,128)(2,1)} %param.10) | copy-start | bytes 638980
  9.0 0.7 %copy-start.2 = (f32[1,2,4,208]{3,2,1,0:T(4,128)S(1)}, f32[1,2,4,208]{3,2,1,0:T(4,128)}, u32[]{:S(2)}) copy-start(f32[1,2,4,208]{3,2,1,0:T(4,128)} %param.9) | copy-start | bytes 19972
  9.7 0.7 %copy-start.4 = (f32[1,1,4,256]{3,2,1,0:T(4,128)S(1)}, f32[1,1,4,256]{3,2,1,0:T(4,128)}, u32[]{:S(2)}) copy-start(f32[1,1,4,256]{3,2,1,0:T(4,128)} %param.8) | copy-start | bytes 12292
  10.4 0.7 %copy-start.5 = (s32[2,8]{1,0:T(2,128)S(1)}, s32[2,8]{1,0:T(2,128)}, u32[]{:S(2)}) copy-start(s32[2,8]{1,0:T(2,128)} %map_ref.1) | copy-start | bytes 196
  11.1 0.7 %copy-start.6 = (s32[2]{0:T(128)S(1)}, s32[2]{0:T(128)}, u32[]{:S(2)}) copy-start(s32[2]{0:T(128)} %count_ref.1) | copy-start | bytes 28
  13.2 4.3 %collective-permute-start.5 = (f32[16,256]{1,0:T(8,128)S(1)}, f32[16,256]{1,0:T(8,128)S(1)}, u32[]{:S(2)}, u32[]{:S(2)}) collective-permute-start(f32[16,256]{1,0:T(8,128)S(1)} %get-tuple-element.14.refs_0_), channel_id=1, source_target_pairs={{0,12},{4,0},{8,4},{12,8},{1,13},{5,1},{9,5},{13,9},{2,14},{6,2},{... | collective-permute-start | bytes 49160 | tf_op jit(solution)/shard_map/ppermute | solution.py:129
  16.0 4.6 %collective-permute-start.4 = (f32[16,256]{1,0:T(8,128)S(1)}, f32[16,256]{1,0:T(8,128)S(1)}, u32[]{:S(2)}, u32[]{:S(2)}) collective-permute-start(f32[16,256]{1,0:T(8,128)S(1)} %get-tuple-element.14.refs_0_), channel_id=1, source_target_pairs={{0,8},{4,12},{8,0},{12,4},{1,9},{5,13},{9,1},{13,5},{2,10},{6,14},... | collective-permute-start | bytes 49160 | tf_op jit(solution)/shard_map/ppermute | solution.py:129
  17.1 5.5 %collective-permute-start.3 = (f32[16,256]{1,0:T(8,128)S(1)}, f32[16,256]{1,0:T(8,128)S(1)}, u32[]{:S(2)}, u32[]{:S(2)}) collective-permute-start(f32[16,256]{1,0:T(8,128)S(1)} %get-tuple-element.14.refs_0_), channel_id=1, source_target_pairs={{0,4},{4,8},{8,12},{12,0},{1,5},{5,9},{9,13},{13,1},{2,6},{6,10},{... | collective-permute-start | bytes 49160 | tf_op jit(solution)/shard_map/ppermute | solution.py:129

commit v4 on v3

--- a/solution.py
+++ b/solution.py
@@ -124,25 +124,16 @@
     return (propagated, energy)
 
 
-def ring(array, axis, shift):
+def swap(array, axis, step):
     size = lax.axis_size(axis)
-    return lax.ppermute(array, axis, [(at, (at + shift) % size) for at in range(size)])
-
-
-def origin(axis, shift):
-    size = lax.axis_size(axis)
-    return lax.rem(lax.axis_index(axis) + (size - shift), size)
-
-
-def prepare_kernel(pb_count, walkers, loads, map_ref, count_ref, *refs):
-    sources, (mask_ref, picks_ref) = refs[:loads], refs[loads : loads + 2]
-    targets, sems = refs[loads + 2 : 2 * loads + 2], refs[-1]
-    copies = [
-        pltpu.make_async_copy(source, target, sems.at[at])
-        for at, (source, target) in enumerate(zip(sources, targets))
-    ]
-    for copy in copies:
-        copy.start()
+    return lax.ppermute(array, axis, [(at, at ^ step) for at in range(size)])
+
+
+def origin(axis, step):
+    return lax.axis_index(axis) ^ step
+
+
+def prepare_kernel(pb_count, walkers, map_ref, count_ref, mask_ref, picks_ref):
     kept = count_ref[lax.axis_index("pb")]
     column = lax.broadcasted_iota(jnp.int32, mask_ref.shape, 1)
     mask_ref[...] = jnp.where(column < kept, 1.0, 0.0)
@@ -161,14 +152,13 @@
     sign = jnp.where(lane < half, 1.0, -1.0)
     imag = jnp.where(row == wanted + half, sign, 0.0)
     picks_ref[...] = jnp.concatenate([real, imag], axis=1).astype(BF16)
-    for copy in copies:
-        copy.wait()
 
 
 def bias_kernel(ka_count, k_local, *refs):
-    greens, (chol_ref, orbitals_ref, bias_ref, own_ref, table) = refs[:ka_count], refs[ka_count:]
-    for shift, green_ref in enumerate(greens):
-        table[origin("ka", shift)] = green_ref[...].astype(F32)
+    greens = refs[:ka_count]
+    chol_ref, orbitals_ref, mask_ref, bias_ref, own_ref, table = refs[ka_count:]
+    for step, green_ref in enumerate(greens):
+        table[origin("ka", step)] = green_ref[...].astype(F32)
     first = lax.axis_index("ka") * k_local
     width = chol_ref.shape[2]
     rows = 2 * ka_count
@@ -183,7 +173,7 @@
         own_ref[k] = both
         total += jnp.dot(both.astype(BF16), chol_ref[k, 0], preferred_element_type=F32)
         total += jnp.dot(turned.astype(BF16), chol_ref[k, 1], preferred_element_type=F32)
-    bias_ref[:rows] = total
+    bias_ref[:rows] = total * mask_ref[...]
     window = jnp.concatenate([orbitals_ref[k] for k in range(k_local)], axis=0)
     count, width = window.shape
     bias_ref[rows : rows + count, :width] = window
@@ -231,7 +221,6 @@
     pairs = M * M
     tiles = columns // LANES
     group = LANES // (2 * tiles)
-    bias = bias * mask_ref[: 2 * walkers]
     bias_re, bias_im = bias[:walkers], bias[walkers:]
     hartree = 0.5 * jnp.sum(bias_re * bias_re + bias_im * bias_im, axis=1, keepdims=True)
     own = lax.broadcasted_iota(jnp.int32, (walkers, 1), 0) == lax.axis_index("ka")
@@ -309,8 +298,8 @@
     shares = jnp.sum(jnp.sum(shares, axis=0, keepdims=True), axis=1, keepdims=True)
     energy_ref[...] = shares / normalizer
     term[...] = jnp.zeros_like(term)
-    for shift, window_ref in enumerate(windows):
-        start = pl.multiple_of(origin("ka", shift) * rows, rows)
+    for step, window_ref in enumerate(windows):
+        start = pl.multiple_of(origin("ka", step) * rows, rows)
         window = window_ref[window_ref.shape[0] - rows :]
         term[pl.ds(start, rows), :pair] = window[:, :pair]
         term[pl.ds(start + half, rows), :pair] = window[:, pair : 2 * pair]
@@ -349,14 +338,18 @@
         out_ref[k] = orbitals_ref[k] + both[k * walkers : (k + 1) * walkers]
 
 
-def call(kernel, out, scratch=(), scalars=0, operands=0, arrays=0):
-    spaces = [pltpu.SMEM] * scalars + [pl.ANY] * arrays + [pltpu.VMEM] * operands
+def call(kernel, out, scratch=(), scalars=0, operands=0, flops=None):
+    spaces = [pltpu.SMEM] * scalars + [pltpu.VMEM] * operands
+    cost = None
+    if flops is not None:
+        cost = pl.CostEstimate(flops=flops, bytes_accessed=0, transcendentals=0)
     return pl.pallas_call(
         kernel,
         out_shape=out,
         in_specs=[pl.BlockSpec(memory_space=space) for space in spaces],
         out_specs=jax.tree.map(lambda _: pl.BlockSpec(memory_space=pltpu.VMEM), out),
         scratch_shapes=list(scratch),
+        cost_estimate=cost,
         compiler_params=pltpu.CompilerParams(vmem_limit_bytes=24 * 2**20),
     )
 
@@ -370,26 +363,19 @@
     shape = jax.ShapeDtypeStruct
     tiles = chol_cols // LANES
     own_green = green.reshape(kpoints, 2 * pair_width)
-    greens = [own_green] + [ring(own_green, "ka", s) for s in range(1, ka_count)]
-    loaded = (
-        chol_half.reshape(k_local, 2, pair_width, chol_cols),
-        jnp.transpose(
-            chol_full.reshape(k_local, 2, M * M, tiles, LANES), (0, 2, 3, 1, 4)
-        ).reshape(k_local, M * M * tiles * 2, LANES),
-        fields.reshape(walkers, chol_cols),
-        orbitals.reshape(k_local, walkers, 2 * pair_width),
-    )
-    mask, picks, half, full, own_fields, own_orbitals = call(
-        functools.partial(prepare_kernel, pb_count, walkers, len(loaded)),
-        (
-            shape((2 * walkers, chol_cols), F32),
-            shape((LANES, 2 * LANES), BF16),
-            *(shape(x.shape, x.dtype) for x in loaded),
-        ),
-        [pltpu.SemaphoreType.DMA((len(loaded),))],
+    greens = [own_green] + [swap(own_green, "ka", s) for s in range(1, ka_count)]
+    half = chol_half.reshape(k_local, 2, pair_width, chol_cols)
+    full = jnp.transpose(
+        chol_full.reshape(k_local, 2, M * M, tiles, LANES), (0, 2, 3, 1, 4)
+    ).reshape(k_local, M * M * tiles * 2, LANES)
+    own_fields = fields.reshape(walkers, chol_cols)
+    own_orbitals = orbitals.reshape(k_local, walkers, 2 * pair_width)
+    mask, picks = call(
+        functools.partial(prepare_kernel, pb_count, walkers),
+        (shape((2 * walkers, chol_cols), F32), shape((LANES, 2 * LANES), BF16)),
         scalars=2,
-        arrays=len(loaded),
-    )(kq_map, chol_count, *loaded)
+        flops=10**9,
+    )(kq_map, chol_count)
     bias, own = call(
         functools.partial(bias_kernel, ka_count, k_local),
         (
@@ -397,9 +383,9 @@
             shape((k_local, 2 * walkers, pair_width), F32),
         ),
         [pltpu.VMEM((walkers, kpoints, 2 * pair_width), F32)],
-        operands=ka_count + 2,
-    )(*greens, half, own_orbitals)
-    parts = [bias] + [ring(bias, "ka", s) for s in range(1, ka_count)]
+        operands=ka_count + 3,
+    )(*greens, half, own_orbitals, mask)
+    parts = [bias] + [swap(bias, "ka", s) for s in range(1, ka_count)]
     exchange = call(
         functools.partial(exchange_kernel, k_local),
         shape((walkers, LANES), F32),
@@ -432,6 +418,7 @@
     walkers = orbitals.shape[2]
     fits = 2 * pb_count * kq_map.shape[1] * walkers == LANES
     fits = fits and chol_half.shape[1] * walkers == 8 and chol_half.shape[4] == 2 * LANES
+    fits = fits and ka_count & (ka_count - 1) == 0
     if fits and chol_half.shape[0] == 1 and walkers == ka_count:
         return direct(green, fields, orbitals, chol_half, chol_full, chol_count, kq_map)
     return with_collectives(green, fields, orbitals, chol_half, chol_full, chol_count, kq_map)

time: 36.2 us -> 32.4 us (0.90)
  local copies, waits for them, and re-layouts: 4.99 us -> 1.35 us
  blocking collectives: 10.3 us -> 12.2 us
  waiting for transfers between devices: 5.18 us -> 3.67 us
  Pallas kernels: 4.59 us -> 4.07 us
    unnamed x14, local copies, waits for them, and re-layouts: 4.99 us -> 1.35 us
    all_to_all x1, blocking collectives: 10.3 us -> 12.2 us  [direct(): blocks = lax.all_to_all(blocks, ('ka', 'pb'), 0, 0, tiled=True)]
    ppermute x6, waiting for transfers between devices: 5.18 us -> 3.67 us  [swap(): return lax.ppermute(array, axis, [(at, at ^ step) for at in range(size)])]
    pallas_call x1, Pallas kernels: 1.1 us -> 0.59 us  [direct(): call(functools.partial(prepare_kernel, pb_count, walkers), (shape((2 * wa...]
  transfers between devices with their start and end apart: 6 -> 6, of which waited for: 2 -> 3; matrix products, arithmetic and copies ran while one was open for 0% -> 0% of each run, Pallas kernels for 4% -> 3%
where the time goes in v4:
time: 32.4 us; the launch traced here: 32.2 us
  blocking collectives  12.2 us (38%)
  starting transfers between devices  10.2 us (31%)
  Pallas kernels  4.07 us (13%)
  waiting for transfers between devices  3.67 us (11%)
  local copies, waits for them, and re-layouts  1.35 us (4%)
  between operations  0.72 us (2%)
    all_to_all x1, blocking collectives, direct(): blocks = lax.all_to_all(blocks, ('ka', 'pb'), 0, 0, tiled=True)  12.2 us
    ppermute x6, starting transfers between devices, swap(): return lax.ppermute(array, axis, [(at, at ^ step) for at in range(size)])  10.2 us
    ppermute x6, waiting for transfers between devices, swap(): return lax.ppermute(array, axis, [(at, at ^ step) for at in range(size)])  3.67 us
    pallas_call x1, Pallas kernels, direct(): call(functools.partial(taylor_kernel, ka_count, pb_count, float(pb_count...  2.09 us
    unnamed x14, local copies, waits for them, and re-layouts  1.35 us
    pallas_call x1, Pallas kernels, direct(): call(functools.partial(operator_kernel, ka_count, k_local), shape((ka_cou...  0.76 us
  transfers between devices with their start and end apart: 6, of which 3 were waited for; matrix products, arithmetic and copies ran while one was open for 0% of the time, Pallas kernels for 3%

profile of v4, /device:TPU:0, one launch (start us, length us, event | category | flops | bytes accessed | tf_op | source)
XLA Modules:
  0.0 32.2 jit_solution(426824874438423823)
XLA Ops:
  0.6 0.0 copy-start.1
  0.6 0.0 copy-start.2
  0.7 0.0 copy-start.3
  0.7 0.0 copy-start
  0.7 0.0 copy-start.4
  0.7 5.1 %collective-permute-start.2 = (bf16[8,208]{1,0:T(8,128)(2,1)}, bf16[8,208]{1,0:T(8,128)(2,1)S(1)}, u32[]{:S(2)}, u32[]{:S(2)}) collective-permute-start(bf16[8,208]{1,0:T(8,128)(2,1)} %bitcast.15), channel_id=1, source_target_pairs={{0,12},{4,8},{8,4},{12,0},{1,13},{5,9},{9,5},{13,1},{2,14},{6,10},... | collective-permute-start | bytes 9992 | tf_op jit(solution)/shard_map/ppermute | solution.py:129
  5.8 0.0 collective-permute-start.1
  5.8 0.6 %collective-permute-start = (bf16[8,208]{1,0:T(8,128)(2,1)}, bf16[8,208]{1,0:T(8,128)(2,1)S(1)}, u32[]{:S(2)}, u32[]{:S(2)}) collective-permute-start(bf16[8,208]{1,0:T(8,128)(2,1)} %bitcast.17), channel_id=1, source_target_pairs={{0,4},{4,0},{8,12},{12,8},{1,5},{5,1},{9,13},{13,9},{2,6},{6,2},{1... | collective-permute-start | bytes 9992 | tf_op jit(solution)/shard_map/ppermute | solution.py:129
  6.4 0.0 copy-start.5
  6.4 0.7 %copy-done.5 = s32[2,8]{1,0:T(2,128)S(1)} copy-done((s32[2,8]{1,0:T(2,128)S(1)}, s32[2,8]{1,0:T(2,128)}, u32[]{:S(2)}) %copy-start.5) | copy-done | bytes 88
  7.1 0.0 copy-start.6
  7.1 0.7 %copy-done.6 = s32[2]{0:T(128)S(1)} copy-done((s32[2]{0:T(128)S(1)}, s32[2]{0:T(128)}, u32[]{:S(2)}) %copy-start.6) | copy-done | bytes 32
  7.8 0.6 %shard_map.86 = (f32[8,256]{1,0:T(8,128)S(1)}, bf16[128,256]{1,0:T(8,128)(2,1)S(1)}) custom-call(s32[2,8]{1,0:T(2,128)S(1)} %copy-done.5, s32[2]{0:T(128)S(1)} %copy-done.6), custom_call_target="tpu_custom_call" | custom-call | flops 1000000000 | tf_op jit(solution)/shard_map/pallas_call | solution.py:373
  8.4 0.0 collective-permute-done.2.refs_3_
  8.4 2.1 %collective-permute-done.1.refs_2_ = bf16[8,208]{1,0:T(8,128)(2,1)S(1)} collective-permute-done((bf16[8,208]{1,0:T(8,128)(2,1)}, bf16[8,208]{1,0:T(8,128)(2,1)S(1)}, u32[]{:S(2)}, u32[]{:S(2)}) %collective-permute-start.1) | collective-permute-done | bytes 3360 | tf_op jit(solution)/shard_map/ppermute | solution.py:129
  10.5 0.0 collective-permute-done.refs_1_
  10.5 0.0 copy-done.1
  10.5 0.0 copy-done.2
  10.5 0.0 copy-done.3
  10.5 0.3 shard_map.87
  10.8 1.7 %collective-permute-start.5 = (f32[16,256]{1,0:T(8,128)S(1)}, f32[16,256]{1,0:T(8,128)S(1)}, u32[]{:S(2)}, u32[]{:S(2)}) collective-permute-start(f32[16,256]{1,0:T(8,128)S(1)} %get-tuple-element.9.refs_0_), channel_id=1, source_target_pairs={{0,12},{4,8},{8,4},{12,0},{1,13},{5,9},{9,5},{13,1},{2,14},{6,10},... | collective-permute-start | bytes 49160 | tf_op jit(solution)/shard_map/ppermute | solution.py:129
  12.5 0.4 %collective-permute-start.4 = (f32[16,256]{1,0:T(8,128)S(1)}, f32[16,256]{1,0:T(8,128)S(1)}, u32[]{:S(2)}, u32[]{:S(2)}) collective-permute-start(f32[16,256]{1,0:T(8,128)S(1)} %get-tuple-element.9.refs_0_), channel_id=1, source_target_pairs={{0,8},{4,12},{8,0},{12,4},{1,9},{5,13},{9,1},{13,5},{2,10},{6,14},... | collective-permute-start | bytes 49160 | tf_op jit(solution)/shard_map/ppermute | solution.py:129
  12.9 2.3 %collective-permute-start.3 = (f32[16,256]{1,0:T(8,128)S(1)}, f32[16,256]{1,0:T(8,128)S(1)}, u32[]{:S(2)}, u32[]{:S(2)}) collective-permute-start(f32[16,256]{1,0:T(8,128)S(1)} %get-tuple-element.9.refs_0_), channel_id=1, source_target_pairs={{0,4},{4,0},{8,12},{12,8},{1,5},{5,1},{9,13},{13,9},{2,6},{6,2},{1... | collective-permute-start | bytes 49160 | tf_op jit(solution)/shard_map/ppermute | solution.py:129
  15.2 0.4 %shard_map.88.refs_6_ = f32[4,128]{1,0:T(4,128)S(1)} custom-call(f32[2,8,104]{2,1,0:T(8,128)S(1)} %get-tuple-element.10.own_ref, bf16[2,2,104,256]{3,2,1,0:T(8,128)(2,1)S(1)} %bitcast.12, f32[8,256]{1,0:T(8,128)S(1)} %get-tuple-element.8.refs_6_.mask_ref.refs_5_), custom_call_target="tpu_custom_call" | custom-call | tf_op jit(solution)/shard_map/pallas_call | solution.py:389
  15.6 0.8 %collective-permute-done.5.refs_3_ = f32[16,256]{1,0:T(8,128)S(1)} collective-permute-done((f32[16,256]{1,0:T(8,128)S(1)}, f32[16,256]{1,0:T(8,128)S(1)}, u32[]{:S(2)}, u32[]{:S(2)}) %collective-permute-start.5) | collective-permute-done | bytes 16416 | tf_op jit(solution)/shard_map/ppermute | solution.py:129
  16.4 0.7 %collective-permute-done.4.refs_2_ = f32[16,256]{1,0:T(8,128)S(1)} collective-permute-done((f32[16,256]{1,0:T(8,128)S(1)}, f32[16,256]{1,0:T(8,128)S(1)}, u32[]{:S(2)}, u32[]{:S(2)}) %collective-permute-start.4) | collective-permute-done | bytes 16416 | tf_op jit(solution)/shard_map/ppermute | solution.py:129
  17.1 0.0 collective-permute-done.3.refs_1_
  17.1 0.0 copy-done
  17.1 0.0 copy-done.4
  17.1 0.8 %shard_map.89 = bf16[8,16,768]{2,1,0:T(8,128)(2,1)S(1)} custom-call(f32[16,256]{1,0:T(8,128)S(1)} %get-tuple-element.9.refs_0_, f32[16,256]{1,0:T(8,128)S(1)} %collective-permute-done.3.refs_1_, f32[16,256]{1,0:T(8,128)S(1)} %collective-permute-done.4.refs_2_, f32[16,256]{1,0:T(8,128)S(1)} %collective-permute-done.5.refs_3_, f32[4,256]{1,0:T(4,128)S(1)} %bitcast.19, ...), custom_call_target="tpu_custom_call" | custom-call | tf_op jit(solution)/shard_map/pallas_call | solution.py:395
  17.9 12.2 %all_to_all.5.blocks_ref = bf16[8,16,768]{2,1,0:T(8,128)(2,1)S(1)} all-to-all(bf16[8,16,768]{2,1,0:T(8,128)(2,1)S(1)} %shard_map.89), channel_id=1, replica_groups=mesh['grp'=2,'ka'=4,'pb'=2,'wa'=2] {'ka','pb'}, dimensions={0} | all-to-all | bytes 393216 | tf_op jit(solution)/shard_map/all_to_all | solution.py:401
  30.1 2.1 %shard_map.90 = (f32[2,4,208]{2,1,0:T(4,128)}, f32[1,1]{1,0:T(1,128)}) custom-call(bf16[8,16,768]{2,1,0:T(8,128)(2,1)S(1)} %all_to_all.5.blocks_ref, f32[16,256]{1,0:T(8,128)S(1)} %get-tuple-element.9.refs_0_, f32[16,256]{1,0:T(8,128)S(1)} %collective-permute-done.3.refs_1_, f32[16,256]{1,0:T(8,128)S(1)} %collective-permute-done.4.refs_2_, ...), custom_call_target="tpu_custom_call" | custom-call | tf_op jit(solution)/shard_map/pallas_call | solution.py:402
Async XLA Ops:
  0.6 9.9 %copy-start.1 = (bf16[1,2,2,104,256]{4,3,2,1,0:T(8,128)(2,1)S(1)}, bf16[1,2,2,104,256]{4,3,2,1,0:T(8,128)(2,1)}, u32[]{:S(2)}) copy-start(bf16[1,2,2,104,256]{4,3,2,1,0:T(8,128)(2,1)} %param.10) | copy-start | bytes 638980
  0.6 9.9 %copy-start.2 = (f32[1,2,4,208]{3,2,1,0:T(4,128)S(1)}, f32[1,2,4,208]{3,2,1,0:T(4,128)}, u32[]{:S(2)}) copy-start(f32[1,2,4,208]{3,2,1,0:T(4,128)} %param.9) | copy-start | bytes 19972
  0.7 9.9 %copy-start.3 = (bf16[1,1,1,8,208]{4,3,2,1,0:T(8,128)(2,1)S(1)}, bf16[1,1,1,8,208]{4,3,2,1,0:T(8,128)(2,1)}, u32[]{:S(2)}) copy-start(bf16[1,1,1,8,208]{4,3,2,1,0:T(8,128)(2,1)} %param.7) | copy-start | bytes 9988
  0.7 16.5 %copy-start = (bf16[1,2,2,676,256]{4,2,3,1,0:T(2,128)(2,1)S(1)}, bf16[1,2,2,676,256]{4,2,3,1,0:T(2,128)(2,1)}, u32[]{:S(2)}) copy-start(bf16[1,2,2,676,256]{4,2,3,1,0:T(2,128)(2,1)} %param.11) | copy-start | bytes 4153348
  0.7 16.4 %copy-start.4 = (f32[1,1,4,256]{3,2,1,0:T(4,128)S(1)}, f32[1,1,4,256]{3,2,1,0:T(4,128)}, u32[]{:S(2)}) copy-start(f32[1,1,4,256]{3,2,1,0:T(4,128)} %param.8) | copy-start | bytes 12292
  0.7 7.7 %collective-permute-start.2 = (bf16[8,208]{1,0:T(8,128)(2,1)}, bf16[8,208]{1,0:T(8,128)(2,1)S(1)}, u32[]{:S(2)}, u32[]{:S(2)}) collective-permute-start(bf16[8,208]{1,0:T(8,128)(2,1)} %bitcast.15), channel_id=1, source_target_pairs={{0,12},{4,8},{8,4},{12,0},{1,13},{5,9},{9,5},{13,1},{2,14},{6,10},... | collective-permute-start | bytes 9992 | tf_op jit(solution)/shard_map/ppermute | solution.py:129
  5.8 4.7 %collective-permute-start.1 = (bf16[8,208]{1,0:T(8,128)(2,1)}, bf16[8,208]{1,0:T(8,128)(2,1)S(1)}, u32[]{:S(2)}, u32[]{:S(2)}) collective-permute-start(bf16[8,208]{1,0:T(8,128)(2,1)} %bitcast.16), channel_id=1, source_target_pairs={{0,8},{4,12},{8,0},{12,4},{1,9},{5,13},{9,1},{13,5},{2,10},{6,14},... | collective-permute-start | bytes 9992 | tf_op jit(solution)/shard_map/ppermute | solution.py:129
  5.8 4.7 %collective-permute-start = (bf16[8,208]{1,0:T(8,128)(2,1)}, bf16[8,208]{1,0:T(8,128)(2,1)S(1)}, u32[]{:S(2)}, u32[]{:S(2)}) collective-permute-start(bf16[8,208]{1,0:T(8,128)(2,1)} %bitcast.17), channel_id=1, source_target_pairs={{0,4},{4,0},{8,12},{12,8},{1,5},{5,1},{9,13},{13,9},{2,6},{6,2},{1... | collective-permute-start | bytes 9992 | tf_op jit(solution)/shard_map/ppermute | solution.py:129
  6.4 0.7 %copy-start.5 = (s32[2,8]{1,0:T(2,128)S(1)}, s32[2,8]{1,0:T(2,128)}, u32[]{:S(2)}) copy-start(s32[2,8]{1,0:T(2,128)} %map_ref.1) | copy-start | bytes 196
  7.1 0.7 %copy-start.6 = (s32[2]{0:T(128)S(1)}, s32[2]{0:T(128)}, u32[]{:S(2)}) copy-start(s32[2]{0:T(128)} %count_ref.1) | copy-start | bytes 28
  10.8 5.6 %collective-permute-start.5 = (f32[16,256]{1,0:T(8,128)S(1)}, f32[16,256]{1,0:T(8,128)S(1)}, u32[]{:S(2)}, u32[]{:S(2)}) collective-permute-start(f32[16,256]{1,0:T(8,128)S(1)} %get-tuple-element.9.refs_0_), channel_id=1, source_target_pairs={{0,12},{4,8},{8,4},{12,0},{1,13},{5,9},{9,5},{13,1},{2,14},{6,10},... | collective-permute-start | bytes 49160 | tf_op jit(solution)/shard_map/ppermute | solution.py:129
  12.5 4.6 %collective-permute-start.4 = (f32[16,256]{1,0:T(8,128)S(1)}, f32[16,256]{1,0:T(8,128)S(1)}, u32[]{:S(2)}, u32[]{:S(2)}) collective-permute-start(f32[16,256]{1,0:T(8,128)S(1)} %get-tuple-element.9.refs_0_), channel_id=1, source_target_pairs={{0,8},{4,12},{8,0},{12,4},{1,9},{5,13},{9,1},{13,5},{2,10},{6,14},... | collective-permute-start | bytes 49160 | tf_op jit(solution)/shard_map/ppermute | solution.py:129
  12.9 4.2 %collective-permute-start.3 = (f32[16,256]{1,0:T(8,128)S(1)}, f32[16,256]{1,0:T(8,128)S(1)}, u32[]{:S(2)}, u32[]{:S(2)}) collective-permute-start(f32[16,256]{1,0:T(8,128)S(1)} %get-tuple-element.9.refs_0_), channel_id=1, source_target_pairs={{0,4},{4,0},{8,12},{12,8},{1,5},{5,1},{9,13},{13,9},{2,6},{6,2},{1... | collective-permute-start | bytes 49160 | tf_op jit(solution)/shard_map/ppermute | solution.py:129

commit v5 on v4

--- a/solution.py
+++ b/solution.py
@@ -11,6 +11,7 @@
 NOCC = 4
 TAYLOR = 3
 LANES = 128
+ROWS = 32
 
 
 BIAS_STEP = 0.5
@@ -133,24 +134,28 @@
     return lax.axis_index(axis) ^ step
 
 
-def prepare_kernel(pb_count, walkers, map_ref, count_ref, mask_ref, picks_ref):
+def prepare_kernel(ka_count, pb_count, walkers, map_ref, count_ref, mask_ref, picks_ref):
     kept = count_ref[lax.axis_index("pb")]
     column = lax.broadcasted_iota(jnp.int32, mask_ref.shape, 1)
     mask_ref[...] = jnp.where(column < kept, 1.0, 0.0)
     kpoints = map_ref.shape[1]
-    half = LANES // 2
+    k_local = kpoints // ka_count
+    span = k_local * walkers
     lane = lax.broadcasted_iota(jnp.int32, (1, LANES), 1)
-    lane_q = lax.rem(lane, half) // (kpoints * walkers)
-    lane_k = lax.rem(lane, kpoints * walkers) // walkers
-    source = jnp.zeros((1, LANES), jnp.int32)
+    lane_q = lane // (LANES // pb_count)
+    lane_ka = lax.rem(lane, LANES // pb_count) // (2 * span)
+    lane_part = lax.rem(lane, 2 * span) // span
+    lane_k = lane_ka * k_local + lax.rem(lane, span) // walkers
+    wanted = jnp.zeros((1, LANES), jnp.int32)
     for q in range(pb_count):
         for k in range(kpoints):
-            source = jnp.where((lane_q == q) & (lane_k == k), map_ref[q, k], source)
-    wanted = source * walkers + lax.rem(lane, walkers)
+            source = map_ref[q, k]
+            source = source // k_local * (2 * span) + lax.rem(source, k_local) * walkers
+            wanted = jnp.where((lane_q == q) & (lane_k == k), source, wanted)
+    wanted = wanted + lax.rem(lane, walkers)
     row = lax.broadcasted_iota(jnp.int32, (LANES, LANES), 0)
     real = jnp.where(row == wanted, 1.0, 0.0)
-    sign = jnp.where(lane < half, 1.0, -1.0)
-    imag = jnp.where(row == wanted + half, sign, 0.0)
+    imag = jnp.where(row == wanted + span, jnp.where(lane_part == 0, 1.0, -1.0), 0.0)
     picks_ref[...] = jnp.concatenate([real, imag], axis=1).astype(BF16)
 
 
@@ -274,66 +279,58 @@
 
 def taylor_kernel(ka_count, pb_count, normalizer, blocks_ref, *refs):
     windows = refs[:ka_count]
-    picks_ref, orbitals_ref, out_ref, energy_ref, table, turned, picked, term = refs[ka_count:]
-    half = LANES // 2
+    picks_ref, orbitals_ref, out_ref, energy_ref, turned, picked, term = refs[ka_count:]
     pairs = M * M
     pair = NOCC * M
-    rows = blocks_ref.shape[1] // 2
-    for at in range(ka_count * pb_count):
-        ka_from, pb_from = at // pb_count, at % pb_count
-        start = (pb_from * ka_count + ka_from) * rows
-        block = blocks_ref[at].astype(F32)
-        table[start : start + rows, :] = block[:rows]
-        table[start + half : start + half + rows, :] = block[rows:]
-    for at in range(0, table.shape[1], LANES):
-        turned[at : at + LANES] = table[:, at : at + LANES].T
+    k_local, walkers, _ = out_ref.shape
+    span = k_local * walkers
     ka_pos = lax.axis_index("ka")
-    last = pairs // LANES * LANES
-    shares = table[:half, last : last + LANES]
-    lane = lax.broadcasted_iota(jnp.int32, shares.shape, 1) + last
-    row = lax.broadcasted_iota(jnp.int32, shares.shape, 0)
-    shares = jnp.where(
-        (lane >= pairs) & (lane < pairs + 3) & (lax.rem(row, rows) == ka_pos), shares, 0.0
-    )
+    term[...] = jnp.zeros_like(term)
+    for step, window_ref in enumerate(windows):
+        start = pl.multiple_of(origin("ka", step) * (2 * span), 2 * span)
+        window = window_ref[window_ref.shape[0] - span :]
+        term[pl.ds(start, span), :pair] = window[:, :pair]
+        term[pl.ds(start + span, span), :pair] = window[:, pair : 2 * pair]
+    picked[...] = jnp.dot(term[...].T.astype(BF16), picks_ref[...], preferred_element_type=F32)
+    count, rows, width = blocks_ref.shape
+    for at in range(0, width, LANES):
+        tile = jnp.concatenate([blocks_ref[n, :, at : at + LANES] for n in range(count)], axis=0)
+        turned[at : at + LANES] = tile.T.astype(F32)
+    shares = turned[pairs : pairs + 3]
+    lane = lax.broadcasted_iota(jnp.int32, shares.shape, 1)
+    shares = jnp.where(lax.rem(lane, 2 * span) == ka_pos, shares, 0.0)
     shares = jnp.sum(jnp.sum(shares, axis=0, keepdims=True), axis=1, keepdims=True)
     energy_ref[...] = shares / normalizer
-    term[...] = jnp.zeros_like(term)
-    for step, window_ref in enumerate(windows):
-        start = pl.multiple_of(origin("ka", step) * rows, rows)
-        window = window_ref[window_ref.shape[0] - rows :]
-        term[pl.ds(start, rows), :pair] = window[:, :pair]
-        term[pl.ds(start + half, rows), :pair] = window[:, pair : 2 * pair]
-    picked[...] = jnp.dot(
-        term[...].T[:pair].astype(BF16), picks_ref[...], preferred_element_type=F32
-    )
+    lane = lax.broadcasted_iota(jnp.int32, (M, LANES), 1)
+    imaginary = lax.rem(lane, 2 * span) >= span
     sums = [jnp.zeros((M, LANES), F32) for _ in range(NOCC)]
     for degree in range(1, TAYLOR + 1):
-        source = picked
+        stride = M if degree == 1 else ROWS
         straight = [jnp.zeros((M, LANES), F32) for _ in range(NOCC)]
         crossed = [jnp.zeros((M, LANES), F32) for _ in range(NOCC)]
         for c in range(M):
             column = turned[pl.ds(c, M, stride=M), :]
             for i in range(NOCC):
-                at = i * M + c
-                straight[i] += column * source[at : at + 1, :LANES]
-                crossed[i] += column * source[at : at + 1, LANES:]
+                at = i * stride + c
+                straight[i] += column * picked[at : at + 1, :LANES]
+                crossed[i] += column * picked[at : at + 1, LANES:]
         for i in range(NOCC):
-            applied = straight[i] + pltpu.roll(crossed[i], half, 1)
-            applied = applied + pltpu.roll(applied, LANES - half // pb_count, 1)
+            other = jnp.where(
+                imaginary, pltpu.roll(crossed[i], span, 1), pltpu.roll(crossed[i], LANES - span, 1)
+            )
+            applied = straight[i] + other
+            applied = applied + pltpu.roll(applied, LANES // pb_count, 1)
             current = applied / degree
             sums[i] = sums[i] + current
-            term[i * M : (i + 1) * M] = current if degree < TAYLOR else sums[i]
+            term[i * ROWS : i * ROWS + M] = current if degree < TAYLOR else sums[i]
         if degree < TAYLOR:
             picked[...] = jnp.dot(
-                term[: NOCC * M].astype(BF16), picks_ref[...], preferred_element_type=F32
+                term[...].astype(BF16), picks_ref[...], preferred_element_type=F32
             )
-    term[NOCC * M :] = jnp.zeros((LANES - NOCC * M, LANES), F32)
-    table[:, :LANES] = term[...].T
-    k_local, walkers, _ = out_ref.shape
-    start = pl.multiple_of(ka_pos * rows, rows)
-    real = table[pl.ds(start, rows), :pair]
-    imag = table[pl.ds(start + half, rows), :pair]
-    both = jnp.concatenate([real, imag], axis=1)
+    turned[:LANES] = term[...].T
+    both = turned[pl.ds(pl.multiple_of(ka_pos * (2 * span), 2 * span), 2 * span), :]
+    both = jnp.concatenate([both[:, i * ROWS : i * ROWS + M] for i in range(NOCC)], axis=1)
+    both = jnp.concatenate([both[:span], both[span:]], axis=1)
     for k in range(k_local):
         out_ref[k] = orbitals_ref[k] + both[k * walkers : (k + 1) * walkers]
 
@@ -371,7 +368,7 @@
     own_fields = fields.reshape(walkers, chol_cols)
     own_orbitals = orbitals.reshape(k_local, walkers, 2 * pair_width)
     mask, picks = call(
-        functools.partial(prepare_kernel, pb_count, walkers),
+        functools.partial(prepare_kernel, ka_count, pb_count, walkers),
         (shape((2 * walkers, chol_cols), F32), shape((LANES, 2 * LANES), BF16)),
         scalars=2,
         flops=10**9,
@@ -398,14 +395,13 @@
         [pltpu.VMEM((2 * M * M * tiles, LANES), F32), pltpu.VMEM((width, LANES), F32)],
         operands=ka_count + 4,
     )(*parts, own_fields, mask, exchange, full)
-    blocks = lax.all_to_all(blocks, ("ka", "pb"), 0, 0, tiled=True)
+    blocks = lax.all_to_all(blocks, ("pb", "ka"), 0, 0, tiled=True)
     propagated, energy = call(
         functools.partial(taylor_kernel, ka_count, pb_count, float(pb_count * chol_cols)),
         (shape((k_local, walkers, 2 * pair_width), F32), shape((1, 1), F32)),
         [
-            pltpu.VMEM((LANES, width), F32),
             pltpu.VMEM((width, LANES), F32),
-            pltpu.VMEM((pair_width, 2 * LANES), F32),
+            pltpu.VMEM((NOCC * ROWS, 2 * LANES), F32),
             pltpu.VMEM((LANES, LANES), F32),
         ],
         operands=ka_count + 3,

time: 32.4 us -> 32.7 us (level)
  no operation moved by 1% of the time
where the time goes in v5:
time: 32.7 us; the launch traced here: 32.5 us
  blocking collectives  12.4 us (38%)
  starting transfers between devices  10.2 us (31%)
  Pallas kernels  4.21 us (13%)
  waiting for transfers between devices  3.67 us (11%)
  local copies, waits for them, and re-layouts  1.35 us (4%)
  between operations  0.72 us (2%)
    all_to_all x1, blocking collectives, direct(): blocks = lax.all_to_all(blocks, ('pb', 'ka'), 0, 0, tiled=True)  12.4 us
    ppermute x6, starting transfers between devices, swap(): return lax.ppermute(array, axis, [(at, at ^ step) for at in range(size)])  10.2 us
    ppermute x6, waiting for transfers between devices, swap(): return lax.ppermute(array, axis, [(at, at ^ step) for at in range(size)])  3.67 us
    pallas_call x1, Pallas kernels, direct(): call(functools.partial(taylor_kernel, ka_count, pb_count, float(pb_count...  2.15 us
    unnamed x14, local copies, waits for them, and re-layouts  1.35 us
    pallas_call x1, Pallas kernels, direct(): call(functools.partial(operator_kernel, ka_count, k_local), shape((ka_cou...  0.77 us
    pallas_call x1, Pallas kernels, direct(): call(functools.partial(prepare_kernel, ka_count, pb_count, walkers), (sha...  0.66 us
  transfers between devices with their start and end apart: 6, of which 3 were waited for; matrix products, arithmetic and copies ran while one was open for 0% of the time, Pallas kernels for 3%

profile of v5, /device:TPU:0, one launch (start us, length us, event | category | flops | bytes accessed | tf_op | source)
XLA Modules:
  0.0 32.5 jit_solution(8511627913295301773)
XLA Ops:
  0.6 0.0 copy-start.1
  0.6 0.0 copy-start.2
  0.7 0.0 copy-start.3
  0.7 0.0 copy-start
  0.7 0.0 copy-start.4
  0.7 5.1 %collective-permute-start.2 = (bf16[8,208]{1,0:T(8,128)(2,1)}, bf16[8,208]{1,0:T(8,128)(2,1)S(1)}, u32[]{:S(2)}, u32[]{:S(2)}) collective-permute-start(bf16[8,208]{1,0:T(8,128)(2,1)} %bitcast.15), channel_id=1, source_target_pairs={{0,12},{4,8},{8,4},{12,0},{1,13},{5,9},{9,5},{13,1},{2,14},{6,10},... | collective-permute-start | bytes 9992 | tf_op jit(solution)/shard_map/ppermute | solution.py:130
  5.8 0.0 collective-permute-start.1
  5.8 0.6 %collective-permute-start = (bf16[8,208]{1,0:T(8,128)(2,1)}, bf16[8,208]{1,0:T(8,128)(2,1)S(1)}, u32[]{:S(2)}, u32[]{:S(2)}) collective-permute-start(bf16[8,208]{1,0:T(8,128)(2,1)} %bitcast.17), channel_id=1, source_target_pairs={{0,4},{4,0},{8,12},{12,8},{1,5},{5,1},{9,13},{13,9},{2,6},{6,2},{1... | collective-permute-start | bytes 9992 | tf_op jit(solution)/shard_map/ppermute | solution.py:130
  6.4 0.0 copy-start.5
  6.4 0.7 %copy-done.5 = s32[2,8]{1,0:T(2,128)S(1)} copy-done((s32[2,8]{1,0:T(2,128)S(1)}, s32[2,8]{1,0:T(2,128)}, u32[]{:S(2)}) %copy-start.5) | copy-done | bytes 88
  7.1 0.0 copy-start.6
  7.1 0.7 %copy-done.6 = s32[2]{0:T(128)S(1)} copy-done((s32[2]{0:T(128)S(1)}, s32[2]{0:T(128)}, u32[]{:S(2)}) %copy-start.6) | copy-done | bytes 32
  7.8 0.7 %shard_map.86 = (f32[8,256]{1,0:T(8,128)S(1)}, bf16[128,256]{1,0:T(8,128)(2,1)S(1)}) custom-call(s32[2,8]{1,0:T(2,128)S(1)} %copy-done.5, s32[2]{0:T(128)S(1)} %copy-done.6), custom_call_target="tpu_custom_call" | custom-call | flops 1000000000 | tf_op jit(solution)/shard_map/pallas_call | solution.py:370
  8.4 0.0 collective-permute-done.2.refs_3_
  8.4 2.1 %collective-permute-done.1.refs_2_ = bf16[8,208]{1,0:T(8,128)(2,1)S(1)} collective-permute-done((bf16[8,208]{1,0:T(8,128)(2,1)}, bf16[8,208]{1,0:T(8,128)(2,1)S(1)}, u32[]{:S(2)}, u32[]{:S(2)}) %collective-permute-start.1) | collective-permute-done | bytes 3360 | tf_op jit(solution)/shard_map/ppermute | solution.py:130
  10.5 0.0 collective-permute-done.refs_1_
  10.5 0.0 copy-done.1
  10.5 0.0 copy-done.2
  10.5 0.0 copy-done.3
  10.5 0.3 shard_map.87
  10.8 1.7 %collective-permute-start.5 = (f32[16,256]{1,0:T(8,128)S(1)}, f32[16,256]{1,0:T(8,128)S(1)}, u32[]{:S(2)}, u32[]{:S(2)}) collective-permute-start(f32[16,256]{1,0:T(8,128)S(1)} %get-tuple-element.9.refs_0_), channel_id=1, source_target_pairs={{0,12},{4,8},{8,4},{12,0},{1,13},{5,9},{9,5},{13,1},{2,14},{6,10},... | collective-permute-start | bytes 49160 | tf_op jit(solution)/shard_map/ppermute | solution.py:130
  12.5 0.4 %collective-permute-start.4 = (f32[16,256]{1,0:T(8,128)S(1)}, f32[16,256]{1,0:T(8,128)S(1)}, u32[]{:S(2)}, u32[]{:S(2)}) collective-permute-start(f32[16,256]{1,0:T(8,128)S(1)} %get-tuple-element.9.refs_0_), channel_id=1, source_target_pairs={{0,8},{4,12},{8,0},{12,4},{1,9},{5,13},{9,1},{13,5},{2,10},{6,14},... | collective-permute-start | bytes 49160 | tf_op jit(solution)/shard_map/ppermute | solution.py:130
  12.9 2.3 %collective-permute-start.3 = (f32[16,256]{1,0:T(8,128)S(1)}, f32[16,256]{1,0:T(8,128)S(1)}, u32[]{:S(2)}, u32[]{:S(2)}) collective-permute-start(f32[16,256]{1,0:T(8,128)S(1)} %get-tuple-element.9.refs_0_), channel_id=1, source_target_pairs={{0,4},{4,0},{8,12},{12,8},{1,5},{5,1},{9,13},{13,9},{2,6},{6,2},{1... | collective-permute-start | bytes 49160 | tf_op jit(solution)/shard_map/ppermute | solution.py:130
  15.2 0.4 %shard_map.88.refs_6_ = f32[4,128]{1,0:T(4,128)S(1)} custom-call(f32[2,8,104]{2,1,0:T(8,128)S(1)} %get-tuple-element.10.own_ref, bf16[2,2,104,256]{3,2,1,0:T(8,128)(2,1)S(1)} %bitcast.12, f32[8,256]{1,0:T(8,128)S(1)} %get-tuple-element.8.refs_6_.mask_ref.refs_5_), custom_call_target="tpu_custom_call" | custom-call | tf_op jit(solution)/shard_map/pallas_call | solution.py:386
  15.6 0.8 %collective-permute-done.5.refs_3_ = f32[16,256]{1,0:T(8,128)S(1)} collective-permute-done((f32[16,256]{1,0:T(8,128)S(1)}, f32[16,256]{1,0:T(8,128)S(1)}, u32[]{:S(2)}, u32[]{:S(2)}) %collective-permute-start.5) | collective-permute-done | bytes 16416 | tf_op jit(solution)/shard_map/ppermute | solution.py:130
  16.4 0.8 %collective-permute-done.4.refs_2_ = f32[16,256]{1,0:T(8,128)S(1)} collective-permute-done((f32[16,256]{1,0:T(8,128)S(1)}, f32[16,256]{1,0:T(8,128)S(1)}, u32[]{:S(2)}, u32[]{:S(2)}) %collective-permute-start.4) | collective-permute-done | bytes 16416 | tf_op jit(solution)/shard_map/ppermute | solution.py:130
  17.2 0.0 collective-permute-done.3.refs_1_
  17.2 0.0 copy-done
  17.2 0.0 copy-done.4
  17.2 0.8 %shard_map.89 = bf16[8,16,768]{2,1,0:T(8,128)(2,1)S(1)} custom-call(f32[16,256]{1,0:T(8,128)S(1)} %get-tuple-element.9.refs_0_, f32[16,256]{1,0:T(8,128)S(1)} %collective-permute-done.3.refs_1_, f32[16,256]{1,0:T(8,128)S(1)} %collective-permute-done.4.refs_2_, f32[16,256]{1,0:T(8,128)S(1)} %collective-permute-done.5.refs_3_, f32[4,256]{1,0:T(4,128)S(1)} %bitcast.19, ...), custom_call_target="tpu_custom_call" | custom-call | tf_op jit(solution)/shard_map/pallas_call | solution.py:392
  18.0 12.4 %all_to_all.5.blocks_ref = bf16[8,16,768]{2,1,0:T(8,128)(2,1)S(1)} all-to-all(bf16[8,16,768]{2,1,0:T(8,128)(2,1)S(1)} %shard_map.89), channel_id=1, replica_groups=mesh['grp'=2,'ka'=4,'pb'=2,'wa'=2] {'pb','ka'}, dimensions={0} | all-to-all | bytes 393216 | tf_op jit(solution)/shard_map/all_to_all | solution.py:398
  30.3 2.2 %shard_map.90 = (f32[2,4,208]{2,1,0:T(4,128)}, f32[1,1]{1,0:T(1,128)}) custom-call(bf16[8,16,768]{2,1,0:T(8,128)(2,1)S(1)} %all_to_all.5.blocks_ref, f32[16,256]{1,0:T(8,128)S(1)} %get-tuple-element.9.refs_0_, f32[16,256]{1,0:T(8,128)S(1)} %collective-permute-done.3.refs_1_, f32[16,256]{1,0:T(8,128)S(1)} %collective-permute-done.4.refs_2_, ...), custom_call_target="tpu_custom_call" | custom-call | tf_op jit(solution)/shard_map/pallas_call | solution.py:399
Async XLA Ops:
  0.6 9.9 %copy-start.1 = (bf16[1,2,2,104,256]{4,3,2,1,0:T(8,128)(2,1)S(1)}, bf16[1,2,2,104,256]{4,3,2,1,0:T(8,128)(2,1)}, u32[]{:S(2)}) copy-start(bf16[1,2,2,104,256]{4,3,2,1,0:T(8,128)(2,1)} %param.10) | copy-start | bytes 638980
  0.6 9.9 %copy-start.2 = (f32[1,2,4,208]{3,2,1,0:T(4,128)S(1)}, f32[1,2,4,208]{3,2,1,0:T(4,128)}, u32[]{:S(2)}) copy-start(f32[1,2,4,208]{3,2,1,0:T(4,128)} %param.9) | copy-start | bytes 19972
  0.7 9.9 %copy-start.3 = (bf16[1,1,1,8,208]{4,3,2,1,0:T(8,128)(2,1)S(1)}, bf16[1,1,1,8,208]{4,3,2,1,0:T(8,128)(2,1)}, u32[]{:S(2)}) copy-start(bf16[1,1,1,8,208]{4,3,2,1,0:T(8,128)(2,1)} %param.7) | copy-start | bytes 9988
  0.7 16.5 %copy-start = (bf16[1,2,2,676,256]{4,2,3,1,0:T(2,128)(2,1)S(1)}, bf16[1,2,2,676,256]{4,2,3,1,0:T(2,128)(2,1)}, u32[]{:S(2)}) copy-start(bf16[1,2,2,676,256]{4,2,3,1,0:T(2,128)(2,1)} %param.11) | copy-start | bytes 4153348
  0.7 16.5 %copy-start.4 = (f32[1,1,4,256]{3,2,1,0:T(4,128)S(1)}, f32[1,1,4,256]{3,2,1,0:T(4,128)}, u32[]{:S(2)}) copy-start(f32[1,1,4,256]{3,2,1,0:T(4,128)} %param.8) | copy-start | bytes 12292
  0.7 7.8 %collective-permute-start.2 = (bf16[8,208]{1,0:T(8,128)(2,1)}, bf16[8,208]{1,0:T(8,128)(2,1)S(1)}, u32[]{:S(2)}, u32[]{:S(2)}) collective-permute-start(bf16[8,208]{1,0:T(8,128)(2,1)} %bitcast.15), channel_id=1, source_target_pairs={{0,12},{4,8},{8,4},{12,0},{1,13},{5,9},{9,5},{13,1},{2,14},{6,10},... | collective-permute-start | bytes 9992 | tf_op jit(solution)/shard_map/ppermute | solution.py:130
  5.8 4.7 %collective-permute-start.1 = (bf16[8,208]{1,0:T(8,128)(2,1)}, bf16[8,208]{1,0:T(8,128)(2,1)S(1)}, u32[]{:S(2)}, u32[]{:S(2)}) collective-permute-start(bf16[8,208]{1,0:T(8,128)(2,1)} %bitcast.16), channel_id=1, source_target_pairs={{0,8},{4,12},{8,0},{12,4},{1,9},{5,13},{9,1},{13,5},{2,10},{6,14},... | collective-permute-start | bytes 9992 | tf_op jit(solution)/shard_map/ppermute | solution.py:130
  5.8 4.7 %collective-permute-start = (bf16[8,208]{1,0:T(8,128)(2,1)}, bf16[8,208]{1,0:T(8,128)(2,1)S(1)}, u32[]{:S(2)}, u32[]{:S(2)}) collective-permute-start(bf16[8,208]{1,0:T(8,128)(2,1)} %bitcast.17), channel_id=1, source_target_pairs={{0,4},{4,0},{8,12},{12,8},{1,5},{5,1},{9,13},{13,9},{2,6},{6,2},{1... | collective-permute-start | bytes 9992 | tf_op jit(solution)/shard_map/ppermute | solution.py:130
  6.4 0.7 %copy-start.5 = (s32[2,8]{1,0:T(2,128)S(1)}, s32[2,8]{1,0:T(2,128)}, u32[]{:S(2)}) copy-start(s32[2,8]{1,0:T(2,128)} %map_ref.1) | copy-start | bytes 196
  7.1 0.7 %copy-start.6 = (s32[2]{0:T(128)S(1)}, s32[2]{0:T(128)}, u32[]{:S(2)}) copy-start(s32[2]{0:T(128)} %count_ref.1) | copy-start | bytes 28
  10.8 5.6 %collective-permute-start.5 = (f32[16,256]{1,0:T(8,128)S(1)}, f32[16,256]{1,0:T(8,128)S(1)}, u32[]{:S(2)}, u32[]{:S(2)}) collective-permute-start(f32[16,256]{1,0:T(8,128)S(1)} %get-tuple-element.9.refs_0_), channel_id=1, source_target_pairs={{0,12},{4,8},{8,4},{12,0},{1,13},{5,9},{9,5},{13,1},{2,14},{6,10},... | collective-permute-start | bytes 49160 | tf_op jit(solution)/shard_map/ppermute | solution.py:130
  12.5 4.6 %collective-permute-start.4 = (f32[16,256]{1,0:T(8,128)S(1)}, f32[16,256]{1,0:T(8,128)S(1)}, u32[]{:S(2)}, u32[]{:S(2)}) collective-permute-start(f32[16,256]{1,0:T(8,128)S(1)} %get-tuple-element.9.refs_0_), channel_id=1, source_target_pairs={{0,8},{4,12},{8,0},{12,4},{1,9},{5,13},{9,1},{13,5},{2,10},{6,14},... | collective-permute-start | bytes 49160 | tf_op jit(solution)/shard_map/ppermute | solution.py:130
  12.9 4.3 %collective-permute-start.3 = (f32[16,256]{1,0:T(8,128)S(1)}, f32[16,256]{1,0:T(8,128)S(1)}, u32[]{:S(2)}, u32[]{:S(2)}) collective-permute-start(f32[16,256]{1,0:T(8,128)S(1)} %get-tuple-element.9.refs_0_), channel_id=1, source_target_pairs={{0,4},{4,0},{8,12},{12,8},{1,5},{5,1},{9,13},{13,9},{2,6},{6,2},{1... | collective-permute-start | bytes 49160 | tf_op jit(solution)/shard_map/ppermute | solution.py:130

commit v6 on v5

--- a/solution.py
+++ b/solution.py
@@ -12,6 +12,19 @@
 TAYLOR = 3
 LANES = 128
 ROWS = 32
+
+GREEN_ROUNDS = (
+    ((3, 0), (2, 1)),
+    ((0, 3), (2, 0), (3, 1), (1, 2)),
+    ((0, 1), (3, 2), (1, 3)),
+    ((0, 2), (2, 3), (1, 0)),
+)[::-1]
+BIAS_ROUNDS = (
+    ((0, 1), (3, 2), (2, 3)),
+    ((3, 1), (2, 0), (1, 3)),
+    ((1, 2), (3, 0), (0, 3)),
+    ((1, 0), (0, 2), (2, 1)),
+)[::-1]
 
 
 BIAS_STEP = 0.5
@@ -125,13 +138,19 @@
     return (propagated, energy)
 
 
-def swap(array, axis, step):
-    size = lax.axis_size(axis)
-    return lax.ppermute(array, axis, [(at, at ^ step) for at in range(size)])
-
-
-def origin(axis, step):
-    return lax.axis_index(axis) ^ step
+def exchange(array, axis, rounds):
+    return [array] + [lax.ppermute(array, axis, pairs) for pairs in rounds]
+
+
+def origins(axis, rounds):
+    at, size = lax.axis_index(axis), lax.axis_size(axis)
+    found = [at]
+    for pairs in rounds:
+        source = jnp.int32(size)
+        for sender, receiver in pairs:
+            source = jnp.where(at == receiver, sender, source)
+        found.append(source)
+    return found
 
 
 def prepare_kernel(ka_count, pb_count, walkers, map_ref, count_ref, mask_ref, picks_ref):
@@ -160,10 +179,9 @@
 
 
 def bias_kernel(ka_count, k_local, *refs):
-    greens = refs[:ka_count]
-    chol_ref, orbitals_ref, mask_ref, bias_ref, own_ref, table = refs[ka_count:]
-    for step, green_ref in enumerate(greens):
-        table[origin("ka", step)] = green_ref[...].astype(F32)
+    *greens, chol_ref, orbitals_ref, mask_ref, bias_ref, own_ref, table = refs
+    for source, green_ref in zip(origins("ka", GREEN_ROUNDS), greens):
+        table[source] = green_ref[...].astype(F32)
     first = lax.axis_index("ka") * k_local
     width = chol_ref.shape[2]
     rows = 2 * ka_count
@@ -216,9 +234,8 @@
     out_ref[...] = jnp.broadcast_to(summed, out_ref.shape)
 
 
-def operator_kernel(ka_count, k_local, *refs):
-    parts = refs[:ka_count]
-    fields_ref, mask_ref, exchange_ref, chol_ref, out_ref, products, turned_ref = refs[ka_count:]
+def operator_kernel(k_local, *refs):
+    *parts, fields_ref, mask_ref, exchange_ref, chol_ref, out_ref, products, turned_ref = refs
     walkers, columns = fields_ref.shape
     bias = parts[0][: 2 * walkers]
     for part in parts[1:]:
@@ -277,17 +294,16 @@
             out_ref[copy, :, at : at + LANES] = block.astype(BF16)
 
 
-def taylor_kernel(ka_count, pb_count, normalizer, blocks_ref, *refs):
-    windows = refs[:ka_count]
-    picks_ref, orbitals_ref, out_ref, energy_ref, turned, picked, term = refs[ka_count:]
+def taylor_kernel(pb_count, normalizer, blocks_ref, *refs):
+    *windows, picks_ref, orbitals_ref, out_ref, energy_ref, turned, picked, term = refs
     pairs = M * M
     pair = NOCC * M
     k_local, walkers, _ = out_ref.shape
     span = k_local * walkers
     ka_pos = lax.axis_index("ka")
     term[...] = jnp.zeros_like(term)
-    for step, window_ref in enumerate(windows):
-        start = pl.multiple_of(origin("ka", step) * (2 * span), 2 * span)
+    for source, window_ref in zip(origins("ka", BIAS_ROUNDS), windows):
+        start = pl.multiple_of(source * (2 * span), 2 * span)
         window = window_ref[window_ref.shape[0] - span :]
         term[pl.ds(start, span), :pair] = window[:, :pair]
         term[pl.ds(start + span, span), :pair] = window[:, pair : 2 * pair]
@@ -360,7 +376,7 @@
     shape = jax.ShapeDtypeStruct
     tiles = chol_cols // LANES
     own_green = green.reshape(kpoints, 2 * pair_width)
-    greens = [own_green] + [swap(own_green, "ka", s) for s in range(1, ka_count)]
+    greens = exchange(own_green, "ka", GREEN_ROUNDS)
     half = chol_half.reshape(k_local, 2, pair_width, chol_cols)
     full = jnp.transpose(
         chol_full.reshape(k_local, 2, M * M, tiles, LANES), (0, 2, 3, 1, 4)
@@ -379,32 +395,32 @@
             shape((2 * walkers + span, chol_cols), F32),
             shape((k_local, 2 * walkers, pair_width), F32),
         ),
-        [pltpu.VMEM((walkers, kpoints, 2 * pair_width), F32)],
-        operands=ka_count + 3,
+        [pltpu.VMEM((walkers + 1, kpoints, 2 * pair_width), F32)],
+        operands=len(greens) + 3,
     )(*greens, half, own_orbitals, mask)
-    parts = [bias] + [swap(bias, "ka", s) for s in range(1, ka_count)]
-    exchange = call(
+    parts = exchange(bias, "ka", BIAS_ROUNDS)
+    shares = call(
         functools.partial(exchange_kernel, k_local),
         shape((walkers, LANES), F32),
         operands=3,
     )(own, half, mask)
     width = -(-(M * M + 3) // LANES) * LANES
     blocks = call(
-        functools.partial(operator_kernel, ka_count, k_local),
+        functools.partial(operator_kernel, k_local),
         shape((ka_count * pb_count, 2 * span, width), BF16),
         [pltpu.VMEM((2 * M * M * tiles, LANES), F32), pltpu.VMEM((width, LANES), F32)],
-        operands=ka_count + 4,
-    )(*parts, own_fields, mask, exchange, full)
+        operands=len(parts) + 4,
+    )(*parts, own_fields, mask, shares, full)
     blocks = lax.all_to_all(blocks, ("pb", "ka"), 0, 0, tiled=True)
     propagated, energy = call(
-        functools.partial(taylor_kernel, ka_count, pb_count, float(pb_count * chol_cols)),
+        functools.partial(taylor_kernel, pb_count, float(pb_count * chol_cols)),
         (shape((k_local, walkers, 2 * pair_width), F32), shape((1, 1), F32)),
         [
             pltpu.VMEM((width, LANES), F32),
             pltpu.VMEM((NOCC * ROWS, 2 * LANES), F32),
             pltpu.VMEM((LANES, LANES), F32),
         ],
-        operands=ka_count + 3,
+        operands=len(parts) + 3,
     )(blocks, *parts, picks, own_orbitals)
     return (propagated[None], energy)
 
@@ -414,7 +430,7 @@
     walkers = orbitals.shape[2]
     fits = 2 * pb_count * kq_map.shape[1] * walkers == LANES
     fits = fits and chol_half.shape[1] * walkers == 8 and chol_half.shape[4] == 2 * LANES
-    fits = fits and ka_count & (ka_count - 1) == 0
+    fits = fits and ka_count == 4
     if fits and chol_half.shape[0] == 1 and walkers == ka_count:
         return direct(green, fields, orbitals, chol_half, chol_full, chol_count, kq_map)
     return with_collectives(green, fields, orbitals, chol_half, chol_full, chol_count, kq_map)

time: 32.7 us -> 44.2 us (1.35)
  starting transfers between devices: 10.2 us -> 21.2 us
  waiting for transfers between devices: 3.67 us -> 4.91 us
  blocking collectives: 12.4 us -> 11.4 us
    ppermute x6 -> x8, starting transfers between devices: 10.2 us -> 21.2 us  [exchange(): return [array] + [lax.ppermute(array, axis, pairs) for pairs in rounds]]
    ppermute x6 -> x8, waiting for transfers between devices: 3.67 us -> 4.91 us  [exchange(): return [array] + [lax.ppermute(array, axis, pairs) for pairs in rounds]]
    all_to_all x1, blocking collectives: 12.4 us -> 11.4 us  [direct(): blocks = lax.all_to_all(blocks, ('pb', 'ka'), 0, 0, tiled=True)]
  transfers between devices with their start and end apart: 6 -> 8, of which waited for: 3 -> 3; matrix products, arithmetic and copies ran while one was open for 0% -> 0% of each run, Pallas kernels for 3% -> 2%
where the time goes in v6:
time: 44.2 us; the launch traced here: 43.9 us
  starting transfers between devices  21.2 us (48%)
  blocking collectives  11.4 us (26%)
  waiting for transfers between devices  4.91 us (11%)
  Pallas kernels  4.22 us (10%)
  local copies, waits for them, and re-layouts  1.35 us (3%)
  between operations  0.78 us (2%)
    ppermute x8, starting transfers between devices, exchange(): return [array] + [lax.ppermute(array, axis, pairs) for pairs in rounds]  21.2 us
    all_to_all x1, blocking collectives, direct(): blocks = lax.all_to_all(blocks, ('pb', 'ka'), 0, 0, tiled=True)  11.4 us
    ppermute x8, waiting for transfers between devices, exchange(): return [array] + [lax.ppermute(array, axis, pairs) for pairs in rounds]  4.91 us
    pallas_call x1, Pallas kernels, direct(): call(functools.partial(taylor_kernel, pb_count, float(pb_count * chol_col...  2.16 us
    unnamed x14, local copies, waits for them, and re-layouts  1.35 us
  transfers between devices with their start and end apart: 8, of which 3 were waited for; matrix products, arithmetic and copies ran while one was open for 0% of the time, Pallas kernels for 2%

profile of v6, /device:TPU:0, one launch (start us, length us, event | category | flops | bytes accessed | tf_op | source)
XLA Modules:
  0.0 43.9 jit_solution(7039558173698614245)
XLA Ops:
  0.6 0.0 copy-start.1
  0.6 0.0 copy-start.2
  0.7 0.0 copy-start.3
  0.7 0.0 copy-start
  0.7 0.0 copy-start.4
  0.7 1.4 %collective-permute-start.3 = (bf16[8,208]{1,0:T(8,128)(2,1)}, bf16[8,208]{1,0:T(8,128)(2,1)S(1)}, u32[]{:S(2)}, u32[]{:S(2)}) collective-permute-start(bf16[8,208]{1,0:T(8,128)(2,1)} %bitcast.15), channel_id=1, source_target_pairs={{12,0},{8,4},{13,1},{9,5},{14,2},{10,6},{15,3},{11,7},{28,16},{24,... | collective-permute-start | bytes 9992 | tf_op jit(solution)/shard_map/ppermute | solution.py:142
  2.1 5.1 %collective-permute-start.2 = (bf16[8,208]{1,0:T(8,128)(2,1)}, bf16[8,208]{1,0:T(8,128)(2,1)S(1)}, u32[]{:S(2)}, u32[]{:S(2)}) collective-permute-start(bf16[8,208]{1,0:T(8,128)(2,1)} %bitcast.16), channel_id=1, source_target_pairs={{0,12},{8,0},{12,4},{4,8},{1,13},{9,1},{13,5},{5,9},{2,14},{10,2},... | collective-permute-start | bytes 9992 | tf_op jit(solution)/shard_map/ppermute | solution.py:142
  7.2 2.5 %collective-permute-start.1 = (bf16[8,208]{1,0:T(8,128)(2,1)}, bf16[8,208]{1,0:T(8,128)(2,1)S(1)}, u32[]{:S(2)}, u32[]{:S(2)}) collective-permute-start(bf16[8,208]{1,0:T(8,128)(2,1)} %bitcast.17), channel_id=1, source_target_pairs={{0,4},{12,8},{4,12},{1,5},{13,9},{5,13},{2,6},{14,10},{6,14},{3,7}... | collective-permute-start | bytes 9992 | tf_op jit(solution)/shard_map/ppermute | solution.py:142
  9.7 1.9 %collective-permute-start = (bf16[8,208]{1,0:T(8,128)(2,1)}, bf16[8,208]{1,0:T(8,128)(2,1)S(1)}, u32[]{:S(2)}, u32[]{:S(2)}) collective-permute-start(bf16[8,208]{1,0:T(8,128)(2,1)} %bitcast.18), channel_id=1, source_target_pairs={{0,8},{8,12},{4,0},{1,9},{9,13},{5,1},{2,10},{10,14},{6,2},{3,11},... | collective-permute-start | bytes 9992 | tf_op jit(solution)/shard_map/ppermute | solution.py:142
  11.7 0.7 %copy-done.5 = s32[2,8]{1,0:T(2,128)S(1)} copy-done((s32[2,8]{1,0:T(2,128)S(1)}, s32[2,8]{1,0:T(2,128)}, u32[]{:S(2)}) %copy-start.5) | copy-done | bytes 88
  12.3 0.7 %copy-done.6 = s32[2]{0:T(128)S(1)} copy-done((s32[2]{0:T(128)S(1)}, s32[2]{0:T(128)}, u32[]{:S(2)}) %copy-start.6) | copy-done | bytes 32
  13.0 0.7 %shard_map.86 = (f32[8,256]{1,0:T(8,128)S(1)}, bf16[128,256]{1,0:T(8,128)(2,1)S(1)}) custom-call(s32[2,8]{1,0:T(2,128)S(1)} %copy-done.5, s32[2]{0:T(128)S(1)} %copy-done.6), custom_call_target="tpu_custom_call" | custom-call | flops 1000000000 | tf_op jit(solution)/shard_map/pallas_call | solution.py:386
  13.7 0.0 collective-permute-done.3.refs_4_
  13.7 0.0 collective-permute-done.2.refs_3_
  13.7 0.0 collective-permute-done.1.refs_2_
  13.7 1.8 %collective-permute-done.refs_1_ = bf16[8,208]{1,0:T(8,128)(2,1)S(1)} collective-permute-done((bf16[8,208]{1,0:T(8,128)(2,1)}, bf16[8,208]{1,0:T(8,128)(2,1)S(1)}, u32[]{:S(2)}, u32[]{:S(2)}) %collective-permute-start) | collective-permute-done | bytes 3360 | tf_op jit(solution)/shard_map/ppermute | solution.py:142
  15.4 0.0 copy-done.1
  15.4 0.0 copy-done.3
  15.4 0.3 shard_map.87
  15.7 2.2 %collective-permute-start.7 = (f32[16,256]{1,0:T(8,128)S(1)}, f32[16,256]{1,0:T(8,128)S(1)}, u32[]{:S(2)}, u32[]{:S(2)}) collective-permute-start(f32[16,256]{1,0:T(8,128)S(1)} %get-tuple-element.9.refs_0_), channel_id=1, source_target_pairs={{0,4},{12,8},{8,12},{1,5},{13,9},{9,13},{2,6},{14,10},{10,14},{3,7... | collective-permute-start | bytes 49160 | tf_op jit(solution)/shard_map/ppermute | solution.py:142
  17.9 1.3 %collective-permute-start.6 = (f32[16,256]{1,0:T(8,128)S(1)}, f32[16,256]{1,0:T(8,128)S(1)}, u32[]{:S(2)}, u32[]{:S(2)}) collective-permute-start(f32[16,256]{1,0:T(8,128)S(1)} %get-tuple-element.9.refs_0_), channel_id=1, source_target_pairs={{12,4},{8,0},{4,12},{13,5},{9,1},{5,13},{14,6},{10,2},{6,14},{15,7... | collective-permute-start | bytes 49160 | tf_op jit(solution)/shard_map/ppermute | solution.py:142
  19.2 4.6 %collective-permute-start.5 = (f32[16,256]{1,0:T(8,128)S(1)}, f32[16,256]{1,0:T(8,128)S(1)}, u32[]{:S(2)}, u32[]{:S(2)}) collective-permute-start(f32[16,256]{1,0:T(8,128)S(1)} %get-tuple-element.9.refs_0_), channel_id=1, source_target_pairs={{4,8},{12,0},{0,12},{5,9},{13,1},{1,13},{6,10},{14,2},{2,14},{7,11... | collective-permute-start | bytes 49160 | tf_op jit(solution)/shard_map/ppermute | solution.py:142
  23.9 2.1 %collective-permute-start.4 = (f32[16,256]{1,0:T(8,128)S(1)}, f32[16,256]{1,0:T(8,128)S(1)}, u32[]{:S(2)}, u32[]{:S(2)}) collective-permute-start(f32[16,256]{1,0:T(8,128)S(1)} %get-tuple-element.9.refs_0_), channel_id=1, source_target_pairs={{4,0},{0,8},{8,4},{5,1},{1,9},{9,5},{6,2},{2,10},{10,6},{7,3},{3,1... | collective-permute-start | bytes 49160 | tf_op jit(solution)/shard_map/ppermute | solution.py:142
  26.0 0.4 shard_map.88.refs_7_
  26.4 0.0 collective-permute-done.7.refs_4_
  26.4 0.0 collective-permute-done.6.refs_3_
  26.4 0.3 collective-permute-done.5.refs_2_
  26.7 2.8 %collective-permute-done.4.refs_1_ = f32[16,256]{1,0:T(8,128)S(1)} collective-permute-done((f32[16,256]{1,0:T(8,128)S(1)}, f32[16,256]{1,0:T(8,128)S(1)}, u32[]{:S(2)}, u32[]{:S(2)}) %collective-permute-start.4) | collective-permute-done | bytes 16416 | tf_op jit(solution)/shard_map/ppermute | solution.py:142
  29.5 0.0 copy-done
  29.5 0.8 %shard_map.89 = bf16[8,16,768]{2,1,0:T(8,128)(2,1)S(1)} custom-call(f32[16,256]{1,0:T(8,128)S(1)} %get-tuple-element.9.refs_0_, f32[16,256]{1,0:T(8,128)S(1)} %collective-permute-done.4.refs_1_, f32[16,256]{1,0:T(8,128)S(1)} %collective-permute-done.5.refs_2_, f32[16,256]{1,0:T(8,128)S(1)} %collective-permute-done.6.refs_3_, ...), custom_call_target="tpu_custom_call" | custom-call | tf_op jit(solution)/shard_map/pallas_call | solution.py:408
  30.3 11.4 %all_to_all.5.blocks_ref = bf16[8,16,768]{2,1,0:T(8,128)(2,1)S(1)} all-to-all(bf16[8,16,768]{2,1,0:T(8,128)(2,1)S(1)} %shard_map.89), channel_id=1, replica_groups=mesh['grp'=2,'ka'=4,'pb'=2,'wa'=2] {'pb','ka'}, dimensions={0} | all-to-all | bytes 393216 | tf_op jit(solution)/shard_map/all_to_all | solution.py:414
  41.7 2.2 %shard_map.90 = (f32[2,4,208]{2,1,0:T(4,128)}, f32[1,1]{1,0:T(1,128)}) custom-call(bf16[8,16,768]{2,1,0:T(8,128)(2,1)S(1)} %all_to_all.5.blocks_ref, f32[16,256]{1,0:T(8,128)S(1)} %get-tuple-element.9.refs_0_, f32[16,256]{1,0:T(8,128)S(1)} %collective-permute-done.4.refs_1_, f32[16,256]{1,0:T(8,128)S(1)} %collective-permute-done.5.refs_2_, ...), custom_call_target="tpu_custom_call" | custom-call | tf_op jit(solution)/shard_map/pallas_call | solution.py:415
  (4 shorter events, 0.0 us)
Async XLA Ops:
  0.6 14.8 %copy-start.1 = (bf16[1,2,2,104,256]{4,3,2,1,0:T(8,128)(2,1)S(1)}, bf16[1,2,2,104,256]{4,3,2,1,0:T(8,128)(2,1)}, u32[]{:S(2)}) copy-start(bf16[1,2,2,104,256]{4,3,2,1,0:T(8,128)(2,1)} %param.10) | copy-start | bytes 638980
  0.6 14.8 %copy-start.2 = (f32[1,2,4,208]{3,2,1,0:T(4,128)S(1)}, f32[1,2,4,208]{3,2,1,0:T(4,128)}, u32[]{:S(2)}) copy-start(f32[1,2,4,208]{3,2,1,0:T(4,128)} %param.9) | copy-start | bytes 19972
  0.7 14.8 %copy-start.3 = (bf16[1,1,1,8,208]{4,3,2,1,0:T(8,128)(2,1)S(1)}, bf16[1,1,1,8,208]{4,3,2,1,0:T(8,128)(2,1)}, u32[]{:S(2)}) copy-start(bf16[1,1,1,8,208]{4,3,2,1,0:T(8,128)(2,1)} %param.7) | copy-start | bytes 9988
  0.7 28.8 %copy-start = (bf16[1,2,2,676,256]{4,2,3,1,0:T(2,128)(2,1)S(1)}, bf16[1,2,2,676,256]{4,2,3,1,0:T(2,128)(2,1)}, u32[]{:S(2)}) copy-start(bf16[1,2,2,676,256]{4,2,3,1,0:T(2,128)(2,1)} %param.11) | copy-start | bytes 4153348
  0.7 28.8 %copy-start.4 = (f32[1,1,4,256]{3,2,1,0:T(4,128)S(1)}, f32[1,1,4,256]{3,2,1,0:T(4,128)}, u32[]{:S(2)}) copy-start(f32[1,1,4,256]{3,2,1,0:T(4,128)} %param.8) | copy-start | bytes 12292
  0.7 13.0 %collective-permute-start.3 = (bf16[8,208]{1,0:T(8,128)(2,1)}, bf16[8,208]{1,0:T(8,128)(2,1)S(1)}, u32[]{:S(2)}, u32[]{:S(2)}) collective-permute-start(bf16[8,208]{1,0:T(8,128)(2,1)} %bitcast.15), channel_id=1, source_target_pairs={{12,0},{8,4},{13,1},{9,5},{14,2},{10,6},{15,3},{11,7},{28,16},{24,... | collective-permute-start | bytes 9992 | tf_op jit(solution)/shard_map/ppermute | solution.py:142
  2.1 11.6 %collective-permute-start.2 = (bf16[8,208]{1,0:T(8,128)(2,1)}, bf16[8,208]{1,0:T(8,128)(2,1)S(1)}, u32[]{:S(2)}, u32[]{:S(2)}) collective-permute-start(bf16[8,208]{1,0:T(8,128)(2,1)} %bitcast.16), channel_id=1, source_target_pairs={{0,12},{8,0},{12,4},{4,8},{1,13},{9,1},{13,5},{5,9},{2,14},{10,2},... | collective-permute-start | bytes 9992 | tf_op jit(solution)/shard_map/ppermute | solution.py:142
  7.2 6.5 %collective-permute-start.1 = (bf16[8,208]{1,0:T(8,128)(2,1)}, bf16[8,208]{1,0:T(8,128)(2,1)S(1)}, u32[]{:S(2)}, u32[]{:S(2)}) collective-permute-start(bf16[8,208]{1,0:T(8,128)(2,1)} %bitcast.17), channel_id=1, source_target_pairs={{0,4},{12,8},{4,12},{1,5},{13,9},{5,13},{2,6},{14,10},{6,14},{3,7}... | collective-permute-start | bytes 9992 | tf_op jit(solution)/shard_map/ppermute | solution.py:142
  9.7 5.7 %collective-permute-start = (bf16[8,208]{1,0:T(8,128)(2,1)}, bf16[8,208]{1,0:T(8,128)(2,1)S(1)}, u32[]{:S(2)}, u32[]{:S(2)}) collective-permute-start(bf16[8,208]{1,0:T(8,128)(2,1)} %bitcast.18), channel_id=1, source_target_pairs={{0,8},{8,12},{4,0},{1,9},{9,13},{5,1},{2,10},{10,14},{6,2},{3,11},... | collective-permute-start | bytes 9992 | tf_op jit(solution)/shard_map/ppermute | solution.py:142
  11.7 0.7 %copy-start.5 = (s32[2,8]{1,0:T(2,128)S(1)}, s32[2,8]{1,0:T(2,128)}, u32[]{:S(2)}) copy-start(s32[2,8]{1,0:T(2,128)} %map_ref.1) | copy-start | bytes 196
  12.3 0.7 %copy-start.6 = (s32[2]{0:T(128)S(1)}, s32[2]{0:T(128)}, u32[]{:S(2)}) copy-start(s32[2]{0:T(128)} %count_ref.1) | copy-start | bytes 28
  15.7 10.6 %collective-permute-start.7 = (f32[16,256]{1,0:T(8,128)S(1)}, f32[16,256]{1,0:T(8,128)S(1)}, u32[]{:S(2)}, u32[]{:S(2)}) collective-permute-start(f32[16,256]{1,0:T(8,128)S(1)} %get-tuple-element.9.refs_0_), channel_id=1, source_target_pairs={{0,4},{12,8},{8,12},{1,5},{13,9},{9,13},{2,6},{14,10},{10,14},{3,7... | collective-permute-start | bytes 49160 | tf_op jit(solution)/shard_map/ppermute | solution.py:142
  17.9 8.4 %collective-permute-start.6 = (f32[16,256]{1,0:T(8,128)S(1)}, f32[16,256]{1,0:T(8,128)S(1)}, u32[]{:S(2)}, u32[]{:S(2)}) collective-permute-start(f32[16,256]{1,0:T(8,128)S(1)} %get-tuple-element.9.refs_0_), channel_id=1, source_target_pairs={{12,4},{8,0},{4,12},{13,5},{9,1},{5,13},{14,6},{10,2},{6,14},{15,7... | collective-permute-start | bytes 49160 | tf_op jit(solution)/shard_map/ppermute | solution.py:142
  19.2 7.4 %collective-permute-start.5 = (f32[16,256]{1,0:T(8,128)S(1)}, f32[16,256]{1,0:T(8,128)S(1)}, u32[]{:S(2)}, u32[]{:S(2)}) collective-permute-start(f32[16,256]{1,0:T(8,128)S(1)} %get-tuple-element.9.refs_0_), channel_id=1, source_target_pairs={{4,8},{12,0},{0,12},{5,9},{13,1},{1,13},{6,10},{14,2},{2,14},{7,11... | collective-permute-start | bytes 49160 | tf_op jit(solution)/shard_map/ppermute | solution.py:142
  23.9 5.6 %collective-permute-start.4 = (f32[16,256]{1,0:T(8,128)S(1)}, f32[16,256]{1,0:T(8,128)S(1)}, u32[]{:S(2)}, u32[]{:S(2)}) collective-permute-start(f32[16,256]{1,0:T(8,128)S(1)} %get-tuple-element.9.refs_0_), channel_id=1, source_target_pairs={{4,0},{0,8},{8,4},{5,1},{1,9},{9,5},{6,2},{2,10},{10,6},{7,3},{3,1... | collective-permute-start | bytes 49160 | tf_op jit(solution)/shard_map/ppermute | solution.py:142

commit v7 on v6

--- a/solution.py
+++ b/solution.py
@@ -14,16 +14,14 @@
 ROWS = 32
 
 GREEN_ROUNDS = (
-    ((3, 0), (2, 1)),
-    ((0, 3), (2, 0), (3, 1), (1, 2)),
-    ((0, 1), (3, 2), (1, 3)),
-    ((0, 2), (2, 3), (1, 0)),
+    ((3, 0), (2, 1), (1, 3), (0, 2)),
+    ((3, 1), (2, 0), (0, 3), (1, 2)),
+    ((1, 0), (3, 2), (2, 3), (0, 1)),
 )[::-1]
 BIAS_ROUNDS = (
-    ((0, 1), (3, 2), (2, 3)),
-    ((3, 1), (2, 0), (1, 3)),
-    ((1, 2), (3, 0), (0, 3)),
-    ((1, 0), (0, 2), (2, 1)),
+    ((0, 3), (3, 0), (1, 2), (2, 1)),
+    ((1, 0), (0, 2), (2, 3), (3, 1)),
+    ((3, 2), (0, 1), (2, 0), (1, 3)),
 )[::-1]
 
 
@@ -143,10 +141,10 @@
 
 
 def origins(axis, rounds):
-    at, size = lax.axis_index(axis), lax.axis_size(axis)
+    at = lax.axis_index(axis)
     found = [at]
     for pairs in rounds:
-        source = jnp.int32(size)
+        source = jnp.int32(0)
         for sender, receiver in pairs:
             source = jnp.where(at == receiver, sender, source)
         found.append(source)
@@ -395,7 +393,7 @@
             shape((2 * walkers + span, chol_cols), F32),
             shape((k_local, 2 * walkers, pair_width), F32),
         ),
-        [pltpu.VMEM((walkers + 1, kpoints, 2 * pair_width), F32)],
+        [pltpu.VMEM((walkers, kpoints, 2 * pair_width), F32)],
         operands=len(greens) + 3,
     )(*greens, half, own_orbitals, mask)
     parts = exchange(bias, "ka", BIAS_ROUNDS)

time: 44.2 us -> 32.6 us (0.74)
  starting transfers between devices: 21.2 us -> 10.6 us
  waiting for transfers between devices: 4.91 us -> 3.56 us
  blocking collectives: 11.4 us -> 11.9 us
    ppermute x8 -> x6, starting transfers between devices: 21.2 us -> 10.6 us  [exchange(): return [array] + [lax.ppermute(array, axis, pairs) for pairs in rounds]]
    ppermute x8 -> x6, waiting for transfers between devices: 4.91 us -> 3.56 us  [exchange(): return [array] + [lax.ppermute(array, axis, pairs) for pairs in rounds]]
    all_to_all x1, blocking collectives: 11.4 us -> 11.9 us  [direct(): blocks = lax.all_to_all(blocks, ('pb', 'ka'), 0, 0, tiled=True)]
  transfers between devices with their start and end apart: 8 -> 6, of which waited for: 3 -> 5; matrix products, arithmetic and copies ran while one was open for 0% -> 0% of each run, Pallas kernels for 2% -> 3%
where the time goes in v7:
time: 32.6 us; the launch traced here: 32.4 us
  blocking collectives  11.9 us (37%)
  starting transfers between devices  10.6 us (33%)
  Pallas kernels  4.2 us (13%)
  waiting for transfers between devices  3.56 us (11%)
  local copies, waits for them, and re-layouts  1.35 us (4%)
  between operations  0.71 us (2%)
    all_to_all x1, blocking collectives, direct(): blocks = lax.all_to_all(blocks, ('pb', 'ka'), 0, 0, tiled=True)  11.9 us
    ppermute x6, starting transfers between devices, exchange(): return [array] + [lax.ppermute(array, axis, pairs) for pairs in rounds]  10.6 us
    ppermute x6, waiting for transfers between devices, exchange(): return [array] + [lax.ppermute(array, axis, pairs) for pairs in rounds]  3.56 us
    pallas_call x1, Pallas kernels, direct(): call(functools.partial(taylor_kernel, pb_count, float(pb_count * chol_col...  2.15 us
    unnamed x14, local copies, waits for them, and re-layouts  1.35 us
    pallas_call x1, Pallas kernels, direct(): call(functools.partial(operator_kernel, k_local), shape((ka_count * pb_co...  0.76 us
    pallas_call x1, Pallas kernels, direct(): call(functools.partial(prepare_kernel, ka_count, pb_count, walkers), (sha...  0.66 us
  transfers between devices with their start and end apart: 6, of which 5 were waited for; matrix products, arithmetic and copies ran while one was open for 0% of the time, Pallas kernels for 3%

profile of v7, /device:TPU:0, one launch (start us, length us, event | category | flops | bytes accessed | tf_op | source)
XLA Modules:
  0.0 32.4 jit_solution(12173996324674776090)
XLA Ops:
  0.6 0.0 copy-start.1
  0.6 0.0 copy-start.2
  0.7 0.0 copy-start.3
  0.7 0.0 copy-start
  0.7 0.0 copy-start.4
  0.7 4.1 %collective-permute-start.2 = (bf16[8,208]{1,0:T(8,128)(2,1)}, bf16[8,208]{1,0:T(8,128)(2,1)S(1)}, u32[]{:S(2)}, u32[]{:S(2)}) collective-permute-start(bf16[8,208]{1,0:T(8,128)(2,1)} %bitcast.15), channel_id=1, source_target_pairs={{12,0},{8,4},{4,12},{0,8},{13,1},{9,5},{5,13},{1,9},{14,2},{10,6},... | collective-permute-start | bytes 9992 | tf_op jit(solution)/shard_map/ppermute | solution.py:140
  4.8 1.1 %collective-permute-start.1 = (bf16[8,208]{1,0:T(8,128)(2,1)}, bf16[8,208]{1,0:T(8,128)(2,1)S(1)}, u32[]{:S(2)}, u32[]{:S(2)}) collective-permute-start(bf16[8,208]{1,0:T(8,128)(2,1)} %bitcast.16), channel_id=1, source_target_pairs={{12,4},{8,0},{0,12},{4,8},{13,5},{9,1},{1,13},{5,9},{14,6},{10,2},... | collective-permute-start | bytes 9992 | tf_op jit(solution)/shard_map/ppermute | solution.py:140
  5.8 0.5 %collective-permute-start = (bf16[8,208]{1,0:T(8,128)(2,1)}, bf16[8,208]{1,0:T(8,128)(2,1)S(1)}, u32[]{:S(2)}, u32[]{:S(2)}) collective-permute-start(bf16[8,208]{1,0:T(8,128)(2,1)} %bitcast.17), channel_id=1, source_target_pairs={{4,0},{12,8},{8,12},{0,4},{5,1},{13,9},{9,13},{1,5},{6,2},{14,10},... | collective-permute-start | bytes 9992 | tf_op jit(solution)/shard_map/ppermute | solution.py:140
  6.4 0.0 copy-start.5
  6.4 0.7 %copy-done.5 = s32[2,8]{1,0:T(2,128)S(1)} copy-done((s32[2,8]{1,0:T(2,128)S(1)}, s32[2,8]{1,0:T(2,128)}, u32[]{:S(2)}) %copy-start.5) | copy-done | bytes 88
  7.0 0.0 copy-start.6
  7.0 0.7 %copy-done.6 = s32[2]{0:T(128)S(1)} copy-done((s32[2]{0:T(128)S(1)}, s32[2]{0:T(128)}, u32[]{:S(2)}) %copy-start.6) | copy-done | bytes 32
  7.7 0.7 %shard_map.86 = (f32[8,256]{1,0:T(8,128)S(1)}, bf16[128,256]{1,0:T(8,128)(2,1)S(1)}) custom-call(s32[2,8]{1,0:T(2,128)S(1)} %copy-done.5, s32[2]{0:T(128)S(1)} %copy-done.6), custom_call_target="tpu_custom_call" | custom-call | flops 1000000000 | tf_op jit(solution)/shard_map/pallas_call | solution.py:384
  8.4 0.0 collective-permute-done.2.refs_3_
  8.4 1.1 %collective-permute-done.1.refs_2_ = bf16[8,208]{1,0:T(8,128)(2,1)S(1)} collective-permute-done((bf16[8,208]{1,0:T(8,128)(2,1)}, bf16[8,208]{1,0:T(8,128)(2,1)S(1)}, u32[]{:S(2)}, u32[]{:S(2)}) %collective-permute-start.1) | collective-permute-done | bytes 3360 | tf_op jit(solution)/shard_map/ppermute | solution.py:140
  9.5 0.2 collective-permute-done.refs_1_
  9.7 0.0 copy-done.1
  9.7 0.0 copy-done.2
  9.7 0.0 copy-done.3
  9.7 0.3 shard_map.87
  10.0 2.9 %collective-permute-start.5 = (f32[16,256]{1,0:T(8,128)S(1)}, f32[16,256]{1,0:T(8,128)S(1)}, u32[]{:S(2)}, u32[]{:S(2)}) collective-permute-start(f32[16,256]{1,0:T(8,128)S(1)} %get-tuple-element.9.refs_0_), channel_id=1, source_target_pairs={{0,12},{12,0},{4,8},{8,4},{1,13},{13,1},{5,9},{9,5},{2,14},{14,2},... | collective-permute-start | bytes 49160 | tf_op jit(solution)/shard_map/ppermute | solution.py:140
  12.8 0.0 collective-permute-start.4
  12.8 2.0 %collective-permute-start.3 = (f32[16,256]{1,0:T(8,128)S(1)}, f32[16,256]{1,0:T(8,128)S(1)}, u32[]{:S(2)}, u32[]{:S(2)}) collective-permute-start(f32[16,256]{1,0:T(8,128)S(1)} %get-tuple-element.9.refs_0_), channel_id=1, source_target_pairs={{12,8},{0,4},{8,0},{4,12},{13,9},{1,5},{9,1},{5,13},{14,10},{2,6},... | collective-permute-start | bytes 49160 | tf_op jit(solution)/shard_map/ppermute | solution.py:140
  14.9 0.4 %shard_map.88.refs_6_ = f32[4,128]{1,0:T(4,128)S(1)} custom-call(f32[2,8,104]{2,1,0:T(8,128)S(1)} %get-tuple-element.10.own_ref, bf16[2,2,104,256]{3,2,1,0:T(8,128)(2,1)S(1)} %bitcast.12, f32[8,256]{1,0:T(8,128)S(1)} %get-tuple-element.8.refs_6_.mask_ref.refs_5_), custom_call_target="tpu_custom_call" | custom-call | tf_op jit(solution)/shard_map/pallas_call | solution.py:400
  15.2 0.3 collective-permute-done.5.refs_3_
  15.5 1.1 %collective-permute-done.4.refs_2_ = f32[16,256]{1,0:T(8,128)S(1)} collective-permute-done((f32[16,256]{1,0:T(8,128)S(1)}, f32[16,256]{1,0:T(8,128)S(1)}, u32[]{:S(2)}, u32[]{:S(2)}) %collective-permute-start.4) | collective-permute-done | bytes 16416 | tf_op jit(solution)/shard_map/ppermute | solution.py:140
  16.6 0.9 %collective-permute-done.3.refs_1_ = f32[16,256]{1,0:T(8,128)S(1)} collective-permute-done((f32[16,256]{1,0:T(8,128)S(1)}, f32[16,256]{1,0:T(8,128)S(1)}, u32[]{:S(2)}, u32[]{:S(2)}) %collective-permute-start.3) | collective-permute-done | bytes 16416 | tf_op jit(solution)/shard_map/ppermute | solution.py:140
  17.5 0.0 copy-done
  17.5 0.0 copy-done.4
  17.5 0.8 %shard_map.89 = bf16[8,16,768]{2,1,0:T(8,128)(2,1)S(1)} custom-call(f32[16,256]{1,0:T(8,128)S(1)} %get-tuple-element.9.refs_0_, f32[16,256]{1,0:T(8,128)S(1)} %collective-permute-done.3.refs_1_, f32[16,256]{1,0:T(8,128)S(1)} %collective-permute-done.4.refs_2_, f32[16,256]{1,0:T(8,128)S(1)} %collective-permute-done.5.refs_3_, f32[4,256]{1,0:T(4,128)S(1)} %bitcast.19, ...), custom_call_target="tpu_custom_call" | custom-call | tf_op jit(solution)/shard_map/pallas_call | solution.py:406
  18.3 11.9 %all_to_all.5.blocks_ref = bf16[8,16,768]{2,1,0:T(8,128)(2,1)S(1)} all-to-all(bf16[8,16,768]{2,1,0:T(8,128)(2,1)S(1)} %shard_map.89), channel_id=1, replica_groups=mesh['grp'=2,'ka'=4,'pb'=2,'wa'=2] {'pb','ka'}, dimensions={0} | all-to-all | bytes 393216 | tf_op jit(solution)/shard_map/all_to_all | solution.py:412
  30.2 2.1 %shard_map.90 = (f32[2,4,208]{2,1,0:T(4,128)}, f32[1,1]{1,0:T(1,128)}) custom-call(bf16[8,16,768]{2,1,0:T(8,128)(2,1)S(1)} %all_to_all.5.blocks_ref, f32[16,256]{1,0:T(8,128)S(1)} %get-tuple-element.9.refs_0_, f32[16,256]{1,0:T(8,128)S(1)} %collective-permute-done.3.refs_1_, f32[16,256]{1,0:T(8,128)S(1)} %collective-permute-done.4.refs_2_, ...), custom_call_target="tpu_custom_call" | custom-call | tf_op jit(solution)/shard_map/pallas_call | solution.py:413
Async XLA Ops:
  0.6 9.0 %copy-start.1 = (bf16[1,2,2,104,256]{4,3,2,1,0:T(8,128)(2,1)S(1)}, bf16[1,2,2,104,256]{4,3,2,1,0:T(8,128)(2,1)}, u32[]{:S(2)}) copy-start(bf16[1,2,2,104,256]{4,3,2,1,0:T(8,128)(2,1)} %param.10) | copy-start | bytes 638980
  0.6 9.0 %copy-start.2 = (f32[1,2,4,208]{3,2,1,0:T(4,128)S(1)}, f32[1,2,4,208]{3,2,1,0:T(4,128)}, u32[]{:S(2)}) copy-start(f32[1,2,4,208]{3,2,1,0:T(4,128)} %param.9) | copy-start | bytes 19972
  0.7 9.0 %copy-start.3 = (bf16[1,1,1,8,208]{4,3,2,1,0:T(8,128)(2,1)S(1)}, bf16[1,1,1,8,208]{4,3,2,1,0:T(8,128)(2,1)}, u32[]{:S(2)}) copy-start(bf16[1,1,1,8,208]{4,3,2,1,0:T(8,128)(2,1)} %param.7) | copy-start | bytes 9988
  0.7 16.8 %copy-start = (bf16[1,2,2,676,256]{4,2,3,1,0:T(2,128)(2,1)S(1)}, bf16[1,2,2,676,256]{4,2,3,1,0:T(2,128)(2,1)}, u32[]{:S(2)}) copy-start(bf16[1,2,2,676,256]{4,2,3,1,0:T(2,128)(2,1)} %param.11) | copy-start | bytes 4153348
  0.7 16.8 %copy-start.4 = (f32[1,1,4,256]{3,2,1,0:T(4,128)S(1)}, f32[1,1,4,256]{3,2,1,0:T(4,128)}, u32[]{:S(2)}) copy-start(f32[1,1,4,256]{3,2,1,0:T(4,128)} %param.8) | copy-start | bytes 12292
  0.7 7.7 %collective-permute-start.2 = (bf16[8,208]{1,0:T(8,128)(2,1)}, bf16[8,208]{1,0:T(8,128)(2,1)S(1)}, u32[]{:S(2)}, u32[]{:S(2)}) collective-permute-start(bf16[8,208]{1,0:T(8,128)(2,1)} %bitcast.15), channel_id=1, source_target_pairs={{12,0},{8,4},{4,12},{0,8},{13,1},{9,5},{5,13},{1,9},{14,2},{10,6},... | collective-permute-start | bytes 9992 | tf_op jit(solution)/shard_map/ppermute | solution.py:140
  4.8 4.7 %collective-permute-start.1 = (bf16[8,208]{1,0:T(8,128)(2,1)}, bf16[8,208]{1,0:T(8,128)(2,1)S(1)}, u32[]{:S(2)}, u32[]{:S(2)}) collective-permute-start(bf16[8,208]{1,0:T(8,128)(2,1)} %bitcast.16), channel_id=1, source_target_pairs={{12,4},{8,0},{0,12},{4,8},{13,5},{9,1},{1,13},{5,9},{14,6},{10,2},... | collective-permute-start | bytes 9992 | tf_op jit(solution)/shard_map/ppermute | solution.py:140
  5.8 3.8 %collective-permute-start = (bf16[8,208]{1,0:T(8,128)(2,1)}, bf16[8,208]{1,0:T(8,128)(2,1)S(1)}, u32[]{:S(2)}, u32[]{:S(2)}) collective-permute-start(bf16[8,208]{1,0:T(8,128)(2,1)} %bitcast.17), channel_id=1, source_target_pairs={{4,0},{12,8},{8,12},{0,4},{5,1},{13,9},{9,13},{1,5},{6,2},{14,10},... | collective-permute-start | bytes 9992 | tf_op jit(solution)/shard_map/ppermute | solution.py:140
  6.4 0.7 %copy-start.5 = (s32[2,8]{1,0:T(2,128)S(1)}, s32[2,8]{1,0:T(2,128)}, u32[]{:S(2)}) copy-start(s32[2,8]{1,0:T(2,128)} %map_ref.1) | copy-start | bytes 196
  7.0 0.7 %copy-start.6 = (s32[2]{0:T(128)S(1)}, s32[2]{0:T(128)}, u32[]{:S(2)}) copy-start(s32[2]{0:T(128)} %count_ref.1) | copy-start | bytes 28
  10.0 5.6 %collective-permute-start.5 = (f32[16,256]{1,0:T(8,128)S(1)}, f32[16,256]{1,0:T(8,128)S(1)}, u32[]{:S(2)}, u32[]{:S(2)}) collective-permute-start(f32[16,256]{1,0:T(8,128)S(1)} %get-tuple-element.9.refs_0_), channel_id=1, source_target_pairs={{0,12},{12,0},{4,8},{8,4},{1,13},{13,1},{5,9},{9,5},{2,14},{14,2},... | collective-permute-start | bytes 49160 | tf_op jit(solution)/shard_map/ppermute | solution.py:140
  12.8 3.7 %collective-permute-start.4 = (f32[16,256]{1,0:T(8,128)S(1)}, f32[16,256]{1,0:T(8,128)S(1)}, u32[]{:S(2)}, u32[]{:S(2)}) collective-permute-start(f32[16,256]{1,0:T(8,128)S(1)} %get-tuple-element.9.refs_0_), channel_id=1, source_target_pairs={{4,0},{0,8},{8,12},{12,4},{5,1},{1,9},{9,13},{13,5},{6,2},{2,10},{... | collective-permute-start | bytes 49160 | tf_op jit(solution)/shard_map/ppermute | solution.py:140
  12.8 4.6 %collective-permute-start.3 = (f32[16,256]{1,0:T(8,128)S(1)}, f32[16,256]{1,0:T(8,128)S(1)}, u32[]{:S(2)}, u32[]{:S(2)}) collective-permute-start(f32[16,256]{1,0:T(8,128)S(1)} %get-tuple-element.9.refs_0_), channel_id=1, source_target_pairs={{12,8},{0,4},{8,0},{4,12},{13,9},{1,5},{9,1},{5,13},{14,10},{2,6},... | collective-permute-start | bytes 49160 | tf_op jit(solution)/shard_map/ppermute | solution.py:140

commit v8 on v7

--- a/solution.py
+++ b/solution.py
@@ -308,7 +308,7 @@
     picked[...] = jnp.dot(term[...].T.astype(BF16), picks_ref[...], preferred_element_type=F32)
     count, rows, width = blocks_ref.shape
     for at in range(0, width, LANES):
-        tile = jnp.concatenate([blocks_ref[n, :, at : at + LANES] for n in range(count)], axis=0)
+        tile = jnp.concatenate([blocks_ref[n, :, at : at + LANES] for n in reversed(range(count))], axis=0)
         turned[at : at + LANES] = tile.T.astype(F32)
     shares = turned[pairs : pairs + 3]
     lane = lax.broadcasted_iota(jnp.int32, shares.shape, 1)
@@ -409,7 +409,10 @@
         [pltpu.VMEM((2 * M * M * tiles, LANES), F32), pltpu.VMEM((width, LANES), F32)],
         operands=len(parts) + 4,
     )(*parts, own_fields, mask, shares, full)
-    blocks = lax.all_to_all(blocks, ("pb", "ka"), 0, 0, tiled=True)
+    group = list(range(ka_count * pb_count))[::-1]
+    blocks = lax.all_to_all(
+        blocks, ("pb", "ka"), 0, 0, axis_index_groups=[group], tiled=True
+    )
     propagated, energy = call(
         functools.partial(taylor_kernel, pb_count, float(pb_count * chol_cols)),
         (shape((k_local, walkers, 2 * pair_width), F32), shape((1, 1), F32)),

time: 32.6 us -> 30.3 us (0.929)
  blocking collectives: 11.9 us -> 9.71 us
    all_to_all x1, blocking collectives: 11.9 us -> 9.71 us  [direct(): lax.all_to_all(blocks, ('pb', 'ka'), 0, 0, axis_index_groups=[group], til...]
where the time goes in v8:
time: 30.3 us; the launch traced here: 30.1 us
  starting transfers between devices  10.6 us (35%)
  blocking collectives  9.71 us (32%)
  Pallas kernels  4.2 us (14%)
  waiting for transfers between devices  3.56 us (12%)
  local copies, waits for them, and re-layouts  1.35 us (4%)
  between operations  0.71 us (2%)
    ppermute x6, starting transfers between devices, exchange(): return [array] + [lax.ppermute(array, axis, pairs) for pairs in rounds]  10.6 us
    all_to_all x1, blocking collectives, direct(): lax.all_to_all(blocks, ('pb', 'ka'), 0, 0, axis_index_groups=[group], til...  9.71 us
    ppermute x6, waiting for transfers between devices, exchange(): return [array] + [lax.ppermute(array, axis, pairs) for pairs in rounds]  3.56 us
    pallas_call x1, Pallas kernels, direct(): call(functools.partial(taylor_kernel, pb_count, float(pb_count * chol_col...  2.15 us
    unnamed x14, local copies, waits for them, and re-layouts  1.35 us
    pallas_call x1, Pallas kernels, direct(): call(functools.partial(operator_kernel, k_local), shape((ka_count * pb_co...  0.76 us
    pallas_call x1, Pallas kernels, direct(): call(functools.partial(prepare_kernel, ka_count, pb_count, walkers), (sha...  0.66 us
  transfers between devices with their start and end apart: 6, of which 5 were waited for; matrix products, arithmetic and copies ran while one was open for 0% of the time, Pallas kernels for 3%

profile of v8, /device:TPU:0, one launch (start us, length us, event | category | flops | bytes accessed | tf_op | source)
XLA Modules:
  0.0 30.1 jit_solution(7126463383817634699)
XLA Ops:
  0.6 0.0 copy-start.1
  0.6 0.0 copy-start.2
  0.7 0.0 copy-start.3
  0.7 0.0 copy-start
  0.7 0.0 copy-start.4
  0.7 4.1 %collective-permute-start.2 = (bf16[8,208]{1,0:T(8,128)(2,1)}, bf16[8,208]{1,0:T(8,128)(2,1)S(1)}, u32[]{:S(2)}, u32[]{:S(2)}) collective-permute-start(bf16[8,208]{1,0:T(8,128)(2,1)} %bitcast.15), channel_id=1, source_target_pairs={{12,0},{8,4},{4,12},{0,8},{13,1},{9,5},{5,13},{1,9},{14,2},{10,6},... | collective-permute-start | bytes 9992 | tf_op jit(solution)/shard_map/ppermute | solution.py:140
  4.8 1.1 %collective-permute-start.1 = (bf16[8,208]{1,0:T(8,128)(2,1)}, bf16[8,208]{1,0:T(8,128)(2,1)S(1)}, u32[]{:S(2)}, u32[]{:S(2)}) collective-permute-start(bf16[8,208]{1,0:T(8,128)(2,1)} %bitcast.16), channel_id=1, source_target_pairs={{12,4},{8,0},{0,12},{4,8},{13,5},{9,1},{1,13},{5,9},{14,6},{10,2},... | collective-permute-start | bytes 9992 | tf_op jit(solution)/shard_map/ppermute | solution.py:140
  5.8 0.5 %collective-permute-start = (bf16[8,208]{1,0:T(8,128)(2,1)}, bf16[8,208]{1,0:T(8,128)(2,1)S(1)}, u32[]{:S(2)}, u32[]{:S(2)}) collective-permute-start(bf16[8,208]{1,0:T(8,128)(2,1)} %bitcast.17), channel_id=1, source_target_pairs={{4,0},{12,8},{8,12},{0,4},{5,1},{13,9},{9,13},{1,5},{6,2},{14,10},... | collective-permute-start | bytes 9992 | tf_op jit(solution)/shard_map/ppermute | solution.py:140
  6.4 0.0 copy-start.5
  6.4 0.7 %copy-done.5 = s32[2,8]{1,0:T(2,128)S(1)} copy-done((s32[2,8]{1,0:T(2,128)S(1)}, s32[2,8]{1,0:T(2,128)}, u32[]{:S(2)}) %copy-start.5) | copy-done | bytes 88
  7.0 0.0 copy-start.6
  7.0 0.7 %copy-done.6 = s32[2]{0:T(128)S(1)} copy-done((s32[2]{0:T(128)S(1)}, s32[2]{0:T(128)}, u32[]{:S(2)}) %copy-start.6) | copy-done | bytes 32
  7.7 0.7 %shard_map.86 = (f32[8,256]{1,0:T(8,128)S(1)}, bf16[128,256]{1,0:T(8,128)(2,1)S(1)}) custom-call(s32[2,8]{1,0:T(2,128)S(1)} %copy-done.5, s32[2]{0:T(128)S(1)} %copy-done.6), custom_call_target="tpu_custom_call" | custom-call | flops 1000000000 | tf_op jit(solution)/shard_map/pallas_call | solution.py:384
  8.4 0.0 collective-permute-done.2.refs_3_
  8.4 1.1 %collective-permute-done.1.refs_2_ = bf16[8,208]{1,0:T(8,128)(2,1)S(1)} collective-permute-done((bf16[8,208]{1,0:T(8,128)(2,1)}, bf16[8,208]{1,0:T(8,128)(2,1)S(1)}, u32[]{:S(2)}, u32[]{:S(2)}) %collective-permute-start.1) | collective-permute-done | bytes 3360 | tf_op jit(solution)/shard_map/ppermute | solution.py:140
  9.5 0.2 collective-permute-done.refs_1_
  9.7 0.0 copy-done.1
  9.7 0.0 copy-done.2
  9.7 0.0 copy-done.3
  9.7 0.3 shard_map.87
  10.0 2.9 %collective-permute-start.5 = (f32[16,256]{1,0:T(8,128)S(1)}, f32[16,256]{1,0:T(8,128)S(1)}, u32[]{:S(2)}, u32[]{:S(2)}) collective-permute-start(f32[16,256]{1,0:T(8,128)S(1)} %get-tuple-element.9.refs_0_), channel_id=1, source_target_pairs={{0,12},{12,0},{4,8},{8,4},{1,13},{13,1},{5,9},{9,5},{2,14},{14,2},... | collective-permute-start | bytes 49160 | tf_op jit(solution)/shard_map/ppermute | solution.py:140
  12.8 0.0 collective-permute-start.4
  12.8 2.0 %collective-permute-start.3 = (f32[16,256]{1,0:T(8,128)S(1)}, f32[16,256]{1,0:T(8,128)S(1)}, u32[]{:S(2)}, u32[]{:S(2)}) collective-permute-start(f32[16,256]{1,0:T(8,128)S(1)} %get-tuple-element.9.refs_0_), channel_id=1, source_target_pairs={{12,8},{0,4},{8,0},{4,12},{13,9},{1,5},{9,1},{5,13},{14,10},{2,6},... | collective-permute-start | bytes 49160 | tf_op jit(solution)/shard_map/ppermute | solution.py:140
  14.9 0.4 %shard_map.88.refs_6_ = f32[4,128]{1,0:T(4,128)S(1)} custom-call(f32[2,8,104]{2,1,0:T(8,128)S(1)} %get-tuple-element.10.own_ref, bf16[2,2,104,256]{3,2,1,0:T(8,128)(2,1)S(1)} %bitcast.12, f32[8,256]{1,0:T(8,128)S(1)} %get-tuple-element.8.refs_6_.mask_ref.refs_5_), custom_call_target="tpu_custom_call" | custom-call | tf_op jit(solution)/shard_map/pallas_call | solution.py:400
  15.2 0.3 collective-permute-done.5.refs_3_
  15.5 1.1 %collective-permute-done.4.refs_2_ = f32[16,256]{1,0:T(8,128)S(1)} collective-permute-done((f32[16,256]{1,0:T(8,128)S(1)}, f32[16,256]{1,0:T(8,128)S(1)}, u32[]{:S(2)}, u32[]{:S(2)}) %collective-permute-start.4) | collective-permute-done | bytes 16416 | tf_op jit(solution)/shard_map/ppermute | solution.py:140
  16.6 0.9 %collective-permute-done.3.refs_1_ = f32[16,256]{1,0:T(8,128)S(1)} collective-permute-done((f32[16,256]{1,0:T(8,128)S(1)}, f32[16,256]{1,0:T(8,128)S(1)}, u32[]{:S(2)}, u32[]{:S(2)}) %collective-permute-start.3) | collective-permute-done | bytes 16416 | tf_op jit(solution)/shard_map/ppermute | solution.py:140
  17.5 0.0 copy-done
  17.5 0.0 copy-done.4
  17.5 0.8 %shard_map.89 = bf16[8,16,768]{2,1,0:T(8,128)(2,1)S(1)} custom-call(f32[16,256]{1,0:T(8,128)S(1)} %get-tuple-element.9.refs_0_, f32[16,256]{1,0:T(8,128)S(1)} %collective-permute-done.3.refs_1_, f32[16,256]{1,0:T(8,128)S(1)} %collective-permute-done.4.refs_2_, f32[16,256]{1,0:T(8,128)S(1)} %collective-permute-done.5.refs_3_, f32[4,256]{1,0:T(4,128)S(1)} %bitcast.19, ...), custom_call_target="tpu_custom_call" | custom-call | tf_op jit(solution)/shard_map/pallas_call | solution.py:406
  18.3 9.7 %all_to_all.5.blocks_ref = bf16[8,16,768]{2,1,0:T(8,128)(2,1)S(1)} all-to-all(bf16[8,16,768]{2,1,0:T(8,128)(2,1)S(1)} %shard_map.89), channel_id=1, replica_groups={{14,10,6,2,12,8,4,0},{15,11,7,3,13,9,5,1},{30,26,22,18,28,24,20,16},{31..., dimensions={0} | all-to-all | bytes 393216 | tf_op jit(solution)/shard_map/all_to_all | solution.py:413
  28.0 2.1 %shard_map.90 = (f32[2,4,208]{2,1,0:T(4,128)}, f32[1,1]{1,0:T(1,128)}) custom-call(bf16[8,16,768]{2,1,0:T(8,128)(2,1)S(1)} %all_to_all.5.blocks_ref, f32[16,256]{1,0:T(8,128)S(1)} %get-tuple-element.9.refs_0_, f32[16,256]{1,0:T(8,128)S(1)} %collective-permute-done.3.refs_1_, f32[16,256]{1,0:T(8,128)S(1)} %collective-permute-done.4.refs_2_, ...), custom_call_target="tpu_custom_call" | custom-call | tf_op jit(solution)/shard_map/pallas_call | solution.py:416
Async XLA Ops:
  0.6 9.0 %copy-start.1 = (bf16[1,2,2,104,256]{4,3,2,1,0:T(8,128)(2,1)S(1)}, bf16[1,2,2,104,256]{4,3,2,1,0:T(8,128)(2,1)}, u32[]{:S(2)}) copy-start(bf16[1,2,2,104,256]{4,3,2,1,0:T(8,128)(2,1)} %param.10) | copy-start | bytes 638980
  0.6 9.0 %copy-start.2 = (f32[1,2,4,208]{3,2,1,0:T(4,128)S(1)}, f32[1,2,4,208]{3,2,1,0:T(4,128)}, u32[]{:S(2)}) copy-start(f32[1,2,4,208]{3,2,1,0:T(4,128)} %param.9) | copy-start | bytes 19972
  0.7 9.0 %copy-start.3 = (bf16[1,1,1,8,208]{4,3,2,1,0:T(8,128)(2,1)S(1)}, bf16[1,1,1,8,208]{4,3,2,1,0:T(8,128)(2,1)}, u32[]{:S(2)}) copy-start(bf16[1,1,1,8,208]{4,3,2,1,0:T(8,128)(2,1)} %param.7) | copy-start | bytes 9988
  0.7 16.8 %copy-start = (bf16[1,2,2,676,256]{4,2,3,1,0:T(2,128)(2,1)S(1)}, bf16[1,2,2,676,256]{4,2,3,1,0:T(2,128)(2,1)}, u32[]{:S(2)}) copy-start(bf16[1,2,2,676,256]{4,2,3,1,0:T(2,128)(2,1)} %param.11) | copy-start | bytes 4153348
  0.7 16.8 %copy-start.4 = (f32[1,1,4,256]{3,2,1,0:T(4,128)S(1)}, f32[1,1,4,256]{3,2,1,0:T(4,128)}, u32[]{:S(2)}) copy-start(f32[1,1,4,256]{3,2,1,0:T(4,128)} %param.8) | copy-start | bytes 12292
  0.7 7.7 %collective-permute-start.2 = (bf16[8,208]{1,0:T(8,128)(2,1)}, bf16[8,208]{1,0:T(8,128)(2,1)S(1)}, u32[]{:S(2)}, u32[]{:S(2)}) collective-permute-start(bf16[8,208]{1,0:T(8,128)(2,1)} %bitcast.15), channel_id=1, source_target_pairs={{12,0},{8,4},{4,12},{0,8},{13,1},{9,5},{5,13},{1,9},{14,2},{10,6},... | collective-permute-start | bytes 9992 | tf_op jit(solution)/shard_map/ppermute | solution.py:140
  4.8 4.7 %collective-permute-start.1 = (bf16[8,208]{1,0:T(8,128)(2,1)}, bf16[8,208]{1,0:T(8,128)(2,1)S(1)}, u32[]{:S(2)}, u32[]{:S(2)}) collective-permute-start(bf16[8,208]{1,0:T(8,128)(2,1)} %bitcast.16), channel_id=1, source_target_pairs={{12,4},{8,0},{0,12},{4,8},{13,5},{9,1},{1,13},{5,9},{14,6},{10,2},... | collective-permute-start | bytes 9992 | tf_op jit(solution)/shard_map/ppermute | solution.py:140
  5.8 3.8 %collective-permute-start = (bf16[8,208]{1,0:T(8,128)(2,1)}, bf16[8,208]{1,0:T(8,128)(2,1)S(1)}, u32[]{:S(2)}, u32[]{:S(2)}) collective-permute-start(bf16[8,208]{1,0:T(8,128)(2,1)} %bitcast.17), channel_id=1, source_target_pairs={{4,0},{12,8},{8,12},{0,4},{5,1},{13,9},{9,13},{1,5},{6,2},{14,10},... | collective-permute-start | bytes 9992 | tf_op jit(solution)/shard_map/ppermute | solution.py:140
  6.4 0.7 %copy-start.5 = (s32[2,8]{1,0:T(2,128)S(1)}, s32[2,8]{1,0:T(2,128)}, u32[]{:S(2)}) copy-start(s32[2,8]{1,0:T(2,128)} %map_ref.1) | copy-start | bytes 196
  7.0 0.7 %copy-start.6 = (s32[2]{0:T(128)S(1)}, s32[2]{0:T(128)}, u32[]{:S(2)}) copy-start(s32[2]{0:T(128)} %count_ref.1) | copy-start | bytes 28
  10.0 5.6 %collective-permute-start.5 = (f32[16,256]{1,0:T(8,128)S(1)}, f32[16,256]{1,0:T(8,128)S(1)}, u32[]{:S(2)}, u32[]{:S(2)}) collective-permute-start(f32[16,256]{1,0:T(8,128)S(1)} %get-tuple-element.9.refs_0_), channel_id=1, source_target_pairs={{0,12},{12,0},{4,8},{8,4},{1,13},{13,1},{5,9},{9,5},{2,14},{14,2},... | collective-permute-start | bytes 49160 | tf_op jit(solution)/shard_map/ppermute | solution.py:140
  12.8 3.7 %collective-permute-start.4 = (f32[16,256]{1,0:T(8,128)S(1)}, f32[16,256]{1,0:T(8,128)S(1)}, u32[]{:S(2)}, u32[]{:S(2)}) collective-permute-start(f32[16,256]{1,0:T(8,128)S(1)} %get-tuple-element.9.refs_0_), channel_id=1, source_target_pairs={{4,0},{0,8},{8,12},{12,4},{5,1},{1,9},{9,13},{13,5},{6,2},{2,10},{... | collective-permute-start | bytes 49160 | tf_op jit(solution)/shard_map/ppermute | solution.py:140
  12.8 4.6 %collective-permute-start.3 = (f32[16,256]{1,0:T(8,128)S(1)}, f32[16,256]{1,0:T(8,128)S(1)}, u32[]{:S(2)}, u32[]{:S(2)}) collective-permute-start(f32[16,256]{1,0:T(8,128)S(1)} %get-tuple-element.9.refs_0_), channel_id=1, source_target_pairs={{12,8},{0,4},{8,0},{4,12},{13,9},{1,5},{9,1},{5,13},{14,10},{2,6},... | collective-permute-start | bytes 49160 | tf_op jit(solution)/shard_map/ppermute | solution.py:140

commit v9 on v8

--- a/solution.py
+++ b/solution.py
@@ -19,9 +19,9 @@
     ((1, 0), (3, 2), (2, 3), (0, 1)),
 )[::-1]
 BIAS_ROUNDS = (
-    ((0, 3), (3, 0), (1, 2), (2, 1)),
-    ((1, 0), (0, 2), (2, 3), (3, 1)),
-    ((3, 2), (0, 1), (2, 0), (1, 3)),
+    ((0, 1), (1, 2), (2, 3), (3, 0)),
+    ((0, 2), (1, 3), (2, 0), (3, 1)),
+    ((0, 3), (1, 0), (2, 1), (3, 2)),
 )[::-1]
 
 

time: 30.3 us -> 30.6 us (level)
  blocking collectives: 9.71 us -> 10.4 us
    all_to_all x1, blocking collectives: 9.71 us -> 10.4 us  [direct(): lax.all_to_all(blocks, ('pb', 'ka'), 0, 0, axis_index_groups=[group], til...]
where the time goes in v9:
time: 30.6 us; the launch traced here: 30.4 us
  starting transfers between devices  10.5 us (34%)
  blocking collectives  10.4 us (34%)
  Pallas kernels  4.2 us (14%)
  waiting for transfers between devices  3.33 us (11%)
  local copies, waits for them, and re-layouts  1.35 us (4%)
  between operations  0.71 us (2%)
    ppermute x6, starting transfers between devices, exchange(): return [array] + [lax.ppermute(array, axis, pairs) for pairs in rounds]  10.5 us
    all_to_all x1, blocking collectives, direct(): lax.all_to_all(blocks, ('pb', 'ka'), 0, 0, axis_index_groups=[group], til...  10.4 us
    ppermute x6, waiting for transfers between devices, exchange(): return [array] + [lax.ppermute(array, axis, pairs) for pairs in rounds]  3.33 us
    pallas_call x1, Pallas kernels, direct(): call(functools.partial(taylor_kernel, pb_count, float(pb_count * chol_col...  2.15 us
    unnamed x14, local copies, waits for them, and re-layouts  1.35 us
    pallas_call x1, Pallas kernels, direct(): call(functools.partial(operator_kernel, k_local), shape((ka_count * pb_co...  0.76 us
    pallas_call x1, Pallas kernels, direct(): call(functools.partial(prepare_kernel, ka_count, pb_count, walkers), (sha...  0.66 us
  transfers between devices with their start and end apart: 6, of which 5 were waited for; matrix products, arithmetic and copies ran while one was open for 0% of the time, Pallas kernels for 3%

profile of v9, /device:TPU:0, one launch (start us, length us, event | category | flops | bytes accessed | tf_op | source)
XLA Modules:
  0.0 30.4 jit_solution(12906116749761464503)
XLA Ops:
  0.6 0.0 copy-start.1
  0.6 0.0 copy-start.2
  0.7 0.0 copy-start.3
  0.7 0.0 copy-start
  0.7 0.0 copy-start.4
  0.7 4.1 %collective-permute-start.2 = (bf16[8,208]{1,0:T(8,128)(2,1)}, bf16[8,208]{1,0:T(8,128)(2,1)S(1)}, u32[]{:S(2)}, u32[]{:S(2)}) collective-permute-start(bf16[8,208]{1,0:T(8,128)(2,1)} %bitcast.15), channel_id=1, source_target_pairs={{12,0},{8,4},{4,12},{0,8},{13,1},{9,5},{5,13},{1,9},{14,2},{10,6},... | collective-permute-start | bytes 9992 | tf_op jit(solution)/shard_map/ppermute | solution.py:140
  4.8 1.1 %collective-permute-start.1 = (bf16[8,208]{1,0:T(8,128)(2,1)}, bf16[8,208]{1,0:T(8,128)(2,1)S(1)}, u32[]{:S(2)}, u32[]{:S(2)}) collective-permute-start(bf16[8,208]{1,0:T(8,128)(2,1)} %bitcast.16), channel_id=1, source_target_pairs={{12,4},{8,0},{0,12},{4,8},{13,5},{9,1},{1,13},{5,9},{14,6},{10,2},... | collective-permute-start | bytes 9992 | tf_op jit(solution)/shard_map/ppermute | solution.py:140
  5.8 0.5 %collective-permute-start = (bf16[8,208]{1,0:T(8,128)(2,1)}, bf16[8,208]{1,0:T(8,128)(2,1)S(1)}, u32[]{:S(2)}, u32[]{:S(2)}) collective-permute-start(bf16[8,208]{1,0:T(8,128)(2,1)} %bitcast.17), channel_id=1, source_target_pairs={{4,0},{12,8},{8,12},{0,4},{5,1},{13,9},{9,13},{1,5},{6,2},{14,10},... | collective-permute-start | bytes 9992 | tf_op jit(solution)/shard_map/ppermute | solution.py:140
  6.4 0.0 copy-start.5
  6.4 0.7 %copy-done.5 = s32[2,8]{1,0:T(2,128)S(1)} copy-done((s32[2,8]{1,0:T(2,128)S(1)}, s32[2,8]{1,0:T(2,128)}, u32[]{:S(2)}) %copy-start.5) | copy-done | bytes 88
  7.0 0.0 copy-start.6
  7.0 0.7 %copy-done.6 = s32[2]{0:T(128)S(1)} copy-done((s32[2]{0:T(128)S(1)}, s32[2]{0:T(128)}, u32[]{:S(2)}) %copy-start.6) | copy-done | bytes 32
  7.7 0.7 %shard_map.86 = (f32[8,256]{1,0:T(8,128)S(1)}, bf16[128,256]{1,0:T(8,128)(2,1)S(1)}) custom-call(s32[2,8]{1,0:T(2,128)S(1)} %copy-done.5, s32[2]{0:T(128)S(1)} %copy-done.6), custom_call_target="tpu_custom_call" | custom-call | flops 1000000000 | tf_op jit(solution)/shard_map/pallas_call | solution.py:384
  8.4 0.0 collective-permute-done.2.refs_3_
  8.4 1.1 %collective-permute-done.1.refs_2_ = bf16[8,208]{1,0:T(8,128)(2,1)S(1)} collective-permute-done((bf16[8,208]{1,0:T(8,128)(2,1)}, bf16[8,208]{1,0:T(8,128)(2,1)S(1)}, u32[]{:S(2)}, u32[]{:S(2)}) %collective-permute-start.1) | collective-permute-done | bytes 3360 | tf_op jit(solution)/shard_map/ppermute | solution.py:140
  9.5 0.2 collective-permute-done.refs_1_
  9.7 0.0 copy-done.1
  9.7 0.0 copy-done.2
  9.7 0.0 copy-done.3
  9.7 0.3 shard_map.87
  10.0 1.4 %collective-permute-start.5 = (f32[16,256]{1,0:T(8,128)S(1)}, f32[16,256]{1,0:T(8,128)S(1)}, u32[]{:S(2)}, u32[]{:S(2)}) collective-permute-start(f32[16,256]{1,0:T(8,128)S(1)} %get-tuple-element.9.refs_0_), channel_id=1, source_target_pairs={{0,4},{4,8},{8,12},{12,0},{1,5},{5,9},{9,13},{13,1},{2,6},{6,10},{... | collective-permute-start | bytes 49160 | tf_op jit(solution)/shard_map/ppermute | solution.py:140
  11.4 2.0 %collective-permute-start.4 = (f32[16,256]{1,0:T(8,128)S(1)}, f32[16,256]{1,0:T(8,128)S(1)}, u32[]{:S(2)}, u32[]{:S(2)}) collective-permute-start(f32[16,256]{1,0:T(8,128)S(1)} %get-tuple-element.9.refs_0_), channel_id=1, source_target_pairs={{0,8},{4,12},{8,0},{12,4},{1,9},{5,13},{9,1},{13,5},{2,10},{6,14},... | collective-permute-start | bytes 49160 | tf_op jit(solution)/shard_map/ppermute | solution.py:140
  13.4 1.3 %collective-permute-start.3 = (f32[16,256]{1,0:T(8,128)S(1)}, f32[16,256]{1,0:T(8,128)S(1)}, u32[]{:S(2)}, u32[]{:S(2)}) collective-permute-start(f32[16,256]{1,0:T(8,128)S(1)} %get-tuple-element.9.refs_0_), channel_id=1, source_target_pairs={{0,12},{4,0},{8,4},{12,8},{1,13},{5,1},{9,5},{13,9},{2,14},{6,2},{... | collective-permute-start | bytes 49160 | tf_op jit(solution)/shard_map/ppermute | solution.py:140
  14.7 0.4 %shard_map.88.refs_6_ = f32[4,128]{1,0:T(4,128)S(1)} custom-call(f32[2,8,104]{2,1,0:T(8,128)S(1)} %get-tuple-element.10.own_ref, bf16[2,2,104,256]{3,2,1,0:T(8,128)(2,1)S(1)} %bitcast.12, f32[8,256]{1,0:T(8,128)S(1)} %get-tuple-element.8.refs_6_.mask_ref.refs_5_), custom_call_target="tpu_custom_call" | custom-call | tf_op jit(solution)/shard_map/pallas_call | solution.py:400
  15.1 0.4 %collective-permute-done.5.refs_3_ = f32[16,256]{1,0:T(8,128)S(1)} collective-permute-done((f32[16,256]{1,0:T(8,128)S(1)}, f32[16,256]{1,0:T(8,128)S(1)}, u32[]{:S(2)}, u32[]{:S(2)}) %collective-permute-start.5) | collective-permute-done | bytes 16416 | tf_op jit(solution)/shard_map/ppermute | solution.py:140
  15.5 0.5 %collective-permute-done.4.refs_2_ = f32[16,256]{1,0:T(8,128)S(1)} collective-permute-done((f32[16,256]{1,0:T(8,128)S(1)}, f32[16,256]{1,0:T(8,128)S(1)}, u32[]{:S(2)}, u32[]{:S(2)}) %collective-permute-start.4) | collective-permute-done | bytes 16416 | tf_op jit(solution)/shard_map/ppermute | solution.py:140
  16.0 1.1 %collective-permute-done.3.refs_1_ = f32[16,256]{1,0:T(8,128)S(1)} collective-permute-done((f32[16,256]{1,0:T(8,128)S(1)}, f32[16,256]{1,0:T(8,128)S(1)}, u32[]{:S(2)}, u32[]{:S(2)}) %collective-permute-start.3) | collective-permute-done | bytes 16416 | tf_op jit(solution)/shard_map/ppermute | solution.py:140
  17.1 0.0 copy-done
  17.1 0.0 copy-done.4
  17.1 0.8 %shard_map.89 = bf16[8,16,768]{2,1,0:T(8,128)(2,1)S(1)} custom-call(f32[16,256]{1,0:T(8,128)S(1)} %get-tuple-element.9.refs_0_, f32[16,256]{1,0:T(8,128)S(1)} %collective-permute-done.3.refs_1_, f32[16,256]{1,0:T(8,128)S(1)} %collective-permute-done.4.refs_2_, f32[16,256]{1,0:T(8,128)S(1)} %collective-permute-done.5.refs_3_, f32[4,256]{1,0:T(4,128)S(1)} %bitcast.19, ...), custom_call_target="tpu_custom_call" | custom-call | tf_op jit(solution)/shard_map/pallas_call | solution.py:406
  17.9 10.4 %all_to_all.5.blocks_ref = bf16[8,16,768]{2,1,0:T(8,128)(2,1)S(1)} all-to-all(bf16[8,16,768]{2,1,0:T(8,128)(2,1)S(1)} %shard_map.89), channel_id=1, replica_groups={{14,10,6,2,12,8,4,0},{15,11,7,3,13,9,5,1},{30,26,22,18,28,24,20,16},{31..., dimensions={0} | all-to-all | bytes 393216 | tf_op jit(solution)/shard_map/all_to_all | solution.py:413
  28.3 2.1 %shard_map.90 = (f32[2,4,208]{2,1,0:T(4,128)}, f32[1,1]{1,0:T(1,128)}) custom-call(bf16[8,16,768]{2,1,0:T(8,128)(2,1)S(1)} %all_to_all.5.blocks_ref, f32[16,256]{1,0:T(8,128)S(1)} %get-tuple-element.9.refs_0_, f32[16,256]{1,0:T(8,128)S(1)} %collective-permute-done.3.refs_1_, f32[16,256]{1,0:T(8,128)S(1)} %collective-permute-done.4.refs_2_, ...), custom_call_target="tpu_custom_call" | custom-call | tf_op jit(solution)/shard_map/pallas_call | solution.py:416
Async XLA Ops:
  0.6 9.0 %copy-start.1 = (bf16[1,2,2,104,256]{4,3,2,1,0:T(8,128)(2,1)S(1)}, bf16[1,2,2,104,256]{4,3,2,1,0:T(8,128)(2,1)}, u32[]{:S(2)}) copy-start(bf16[1,2,2,104,256]{4,3,2,1,0:T(8,128)(2,1)} %param.10) | copy-start | bytes 638980
  0.6 9.0 %copy-start.2 = (f32[1,2,4,208]{3,2,1,0:T(4,128)S(1)}, f32[1,2,4,208]{3,2,1,0:T(4,128)}, u32[]{:S(2)}) copy-start(f32[1,2,4,208]{3,2,1,0:T(4,128)} %param.9) | copy-start | bytes 19972
  0.7 9.0 %copy-start.3 = (bf16[1,1,1,8,208]{4,3,2,1,0:T(8,128)(2,1)S(1)}, bf16[1,1,1,8,208]{4,3,2,1,0:T(8,128)(2,1)}, u32[]{:S(2)}) copy-start(bf16[1,1,1,8,208]{4,3,2,1,0:T(8,128)(2,1)} %param.7) | copy-start | bytes 9988
  0.7 16.5 %copy-start = (bf16[1,2,2,676,256]{4,2,3,1,0:T(2,128)(2,1)S(1)}, bf16[1,2,2,676,256]{4,2,3,1,0:T(2,128)(2,1)}, u32[]{:S(2)}) copy-start(bf16[1,2,2,676,256]{4,2,3,1,0:T(2,128)(2,1)} %param.11) | copy-start | bytes 4153348
  0.7 16.5 %copy-start.4 = (f32[1,1,4,256]{3,2,1,0:T(4,128)S(1)}, f32[1,1,4,256]{3,2,1,0:T(4,128)}, u32[]{:S(2)}) copy-start(f32[1,1,4,256]{3,2,1,0:T(4,128)} %param.8) | copy-start | bytes 12292
  0.7 7.7 %collective-permute-start.2 = (bf16[8,208]{1,0:T(8,128)(2,1)}, bf16[8,208]{1,0:T(8,128)(2,1)S(1)}, u32[]{:S(2)}, u32[]{:S(2)}) collective-permute-start(bf16[8,208]{1,0:T(8,128)(2,1)} %bitcast.15), channel_id=1, source_target_pairs={{12,0},{8,4},{4,12},{0,8},{13,1},{9,5},{5,13},{1,9},{14,2},{10,6},... | collective-permute-start | bytes 9992 | tf_op jit(solution)/shard_map/ppermute | solution.py:140
  4.8 4.7 %collective-permute-start.1 = (bf16[8,208]{1,0:T(8,128)(2,1)}, bf16[8,208]{1,0:T(8,128)(2,1)S(1)}, u32[]{:S(2)}, u32[]{:S(2)}) collective-permute-start(bf16[8,208]{1,0:T(8,128)(2,1)} %bitcast.16), channel_id=1, source_target_pairs={{12,4},{8,0},{0,12},{4,8},{13,5},{9,1},{1,13},{5,9},{14,6},{10,2},... | collective-permute-start | bytes 9992 | tf_op jit(solution)/shard_map/ppermute | solution.py:140
  5.8 3.8 %collective-permute-start = (bf16[8,208]{1,0:T(8,128)(2,1)}, bf16[8,208]{1,0:T(8,128)(2,1)S(1)}, u32[]{:S(2)}, u32[]{:S(2)}) collective-permute-start(bf16[8,208]{1,0:T(8,128)(2,1)} %bitcast.17), channel_id=1, source_target_pairs={{4,0},{12,8},{8,12},{0,4},{5,1},{13,9},{9,13},{1,5},{6,2},{14,10},... | collective-permute-start | bytes 9992 | tf_op jit(solution)/shard_map/ppermute | solution.py:140
  6.4 0.7 %copy-start.5 = (s32[2,8]{1,0:T(2,128)S(1)}, s32[2,8]{1,0:T(2,128)}, u32[]{:S(2)}) copy-start(s32[2,8]{1,0:T(2,128)} %map_ref.1) | copy-start | bytes 196
  7.0 0.7 %copy-start.6 = (s32[2]{0:T(128)S(1)}, s32[2]{0:T(128)}, u32[]{:S(2)}) copy-start(s32[2]{0:T(128)} %count_ref.1) | copy-start | bytes 28
  10.0 5.6 %collective-permute-start.5 = (f32[16,256]{1,0:T(8,128)S(1)}, f32[16,256]{1,0:T(8,128)S(1)}, u32[]{:S(2)}, u32[]{:S(2)}) collective-permute-start(f32[16,256]{1,0:T(8,128)S(1)} %get-tuple-element.9.refs_0_), channel_id=1, source_target_pairs={{0,4},{4,8},{8,12},{12,0},{1,5},{5,9},{9,13},{13,1},{2,6},{6,10},{... | collective-permute-start | bytes 49160 | tf_op jit(solution)/shard_map/ppermute | solution.py:140
  11.4 4.6 %collective-permute-start.4 = (f32[16,256]{1,0:T(8,128)S(1)}, f32[16,256]{1,0:T(8,128)S(1)}, u32[]{:S(2)}, u32[]{:S(2)}) collective-permute-start(f32[16,256]{1,0:T(8,128)S(1)} %get-tuple-element.9.refs_0_), channel_id=1, source_target_pairs={{0,8},{4,12},{8,0},{12,4},{1,9},{5,13},{9,1},{13,5},{2,10},{6,14},... | collective-permute-start | bytes 49160 | tf_op jit(solution)/shard_map/ppermute | solution.py:140
  13.4 3.7 %collective-permute-start.3 = (f32[16,256]{1,0:T(8,128)S(1)}, f32[16,256]{1,0:T(8,128)S(1)}, u32[]{:S(2)}, u32[]{:S(2)}) collective-permute-start(f32[16,256]{1,0:T(8,128)S(1)} %get-tuple-element.9.refs_0_), channel_id=1, source_target_pairs={{0,12},{4,0},{8,4},{12,8},{1,13},{5,1},{9,5},{13,9},{2,14},{6,2},{... | collective-permute-start | bytes 49160 | tf_op jit(solution)/shard_map/ppermute | solution.py:140

commit v10 on v8

--- a/solution.py
+++ b/solution.py
@@ -19,9 +19,9 @@
     ((1, 0), (3, 2), (2, 3), (0, 1)),
 )[::-1]
 BIAS_ROUNDS = (
+    ((0, 1), (1, 3), (2, 0), (3, 2)),
     ((0, 3), (3, 0), (1, 2), (2, 1)),
-    ((1, 0), (0, 2), (2, 3), (3, 1)),
-    ((3, 2), (0, 1), (2, 0), (1, 3)),
+    ((0, 2), (1, 0), (2, 3), (3, 1)),
 )[::-1]
 
 
@@ -149,6 +149,12 @@
             source = jnp.where(at == receiver, sender, source)
         found.append(source)
     return found
+
+
+def operator_group(ka_count, pb_count):
+    first = (pb_count - 1) * ka_count + ka_count // 2
+    rest = [at for at in range(pb_count * ka_count) if at != first]
+    return [first] + rest[::-1]
 
 
 def prepare_kernel(ka_count, pb_count, walkers, map_ref, count_ref, mask_ref, picks_ref):
@@ -306,9 +312,11 @@
         term[pl.ds(start, span), :pair] = window[:, :pair]
         term[pl.ds(start + span, span), :pair] = window[:, pair : 2 * pair]
     picked[...] = jnp.dot(term[...].T.astype(BF16), picks_ref[...], preferred_element_type=F32)
-    count, rows, width = blocks_ref.shape
+    count, _, width = blocks_ref.shape
+    group = operator_group(count // pb_count, pb_count)
+    places = [group.index(n) for n in range(count)]
     for at in range(0, width, LANES):
-        tile = jnp.concatenate([blocks_ref[n, :, at : at + LANES] for n in reversed(range(count))], axis=0)
+        tile = jnp.concatenate([blocks_ref[n, :, at : at + LANES] for n in places], axis=0)
         turned[at : at + LANES] = tile.T.astype(F32)
     shares = turned[pairs : pairs + 3]
     lane = lax.broadcasted_iota(jnp.int32, shares.shape, 1)
@@ -409,7 +417,7 @@
         [pltpu.VMEM((2 * M * M * tiles, LANES), F32), pltpu.VMEM((width, LANES), F32)],
         operands=len(parts) + 4,
     )(*parts, own_fields, mask, shares, full)
-    group = list(range(ka_count * pb_count))[::-1]
+    group = operator_group(ka_count, pb_count)
     blocks = lax.all_to_all(
         blocks, ("pb", "ka"), 0, 0, axis_index_groups=[group], tiled=True
     )

time: 30.3 us -> 29.8 us (0.983)
  waiting for transfers between devices: 3.56 us -> 3.17 us
    ppermute x6, waiting for transfers between devices: 3.56 us -> 3.17 us  [exchange(): return [array] + [lax.ppermute(array, axis, pairs) for pairs in rounds]]
  transfers between devices with their start and end apart: 6 -> 6, of which waited for: 5 -> 4; matrix products, arithmetic and copies ran while one was open for 0% -> 0% of each run, Pallas kernels for 3% -> 3%
where the time goes in v10:
time: 29.8 us; the launch traced here: 29.6 us
  starting transfers between devices  10.6 us (36%)
  blocking collectives  9.62 us (32%)
  Pallas kernels  4.2 us (14%)
  waiting for transfers between devices  3.17 us (11%)
  local copies, waits for them, and re-layouts  1.35 us (5%)
  between operations  0.71 us (2%)
    ppermute x6, starting transfers between devices, exchange(): return [array] + [lax.ppermute(array, axis, pairs) for pairs in rounds]  10.6 us
    all_to_all x1, blocking collectives, direct(): lax.all_to_all(blocks, ('pb', 'ka'), 0, 0, axis_index_groups=[group], til...  9.62 us
    ppermute x6, waiting for transfers between devices, exchange(): return [array] + [lax.ppermute(array, axis, pairs) for pairs in rounds]  3.17 us
    pallas_call x1, Pallas kernels, direct(): call(functools.partial(taylor_kernel, pb_count, float(pb_count * chol_col...  2.15 us
    unnamed x14, local copies, waits for them, and re-layouts  1.35 us
    pallas_call x1, Pallas kernels, direct(): call(functools.partial(operator_kernel, k_local), shape((ka_count * pb_co...  0.76 us
    pallas_call x1, Pallas kernels, direct(): call(functools.partial(prepare_kernel, ka_count, pb_count, walkers), (sha...  0.66 us
  transfers between devices with their start and end apart: 6, of which 4 were waited for; matrix products, arithmetic and copies ran while one was open for 0% of the time, Pallas kernels for 3%

profile of v10, /device:TPU:0, one launch (start us, length us, event | category | flops | bytes accessed | tf_op | source)
XLA Modules:
  0.0 29.6 jit_solution(4590134577520266315)
XLA Ops:
  0.6 0.0 copy-start.1
  0.6 0.0 copy-start.2
  0.7 0.0 copy-start.3
  0.7 0.0 copy-start
  0.7 0.0 copy-start.4
  0.7 4.1 %collective-permute-start.2 = (bf16[8,208]{1,0:T(8,128)(2,1)}, bf16[8,208]{1,0:T(8,128)(2,1)S(1)}, u32[]{:S(2)}, u32[]{:S(2)}) collective-permute-start(bf16[8,208]{1,0:T(8,128)(2,1)} %bitcast.15), channel_id=1, source_target_pairs={{12,0},{8,4},{4,12},{0,8},{13,1},{9,5},{5,13},{1,9},{14,2},{10,6},... | collective-permute-start | bytes 9992 | tf_op jit(solution)/shard_map/ppermute | solution.py:140
  4.8 1.1 %collective-permute-start.1 = (bf16[8,208]{1,0:T(8,128)(2,1)}, bf16[8,208]{1,0:T(8,128)(2,1)S(1)}, u32[]{:S(2)}, u32[]{:S(2)}) collective-permute-start(bf16[8,208]{1,0:T(8,128)(2,1)} %bitcast.16), channel_id=1, source_target_pairs={{12,4},{8,0},{0,12},{4,8},{13,5},{9,1},{1,13},{5,9},{14,6},{10,2},... | collective-permute-start | bytes 9992 | tf_op jit(solution)/shard_map/ppermute | solution.py:140
  5.8 0.5 %collective-permute-start = (bf16[8,208]{1,0:T(8,128)(2,1)}, bf16[8,208]{1,0:T(8,128)(2,1)S(1)}, u32[]{:S(2)}, u32[]{:S(2)}) collective-permute-start(bf16[8,208]{1,0:T(8,128)(2,1)} %bitcast.17), channel_id=1, source_target_pairs={{4,0},{12,8},{8,12},{0,4},{5,1},{13,9},{9,13},{1,5},{6,2},{14,10},... | collective-permute-start | bytes 9992 | tf_op jit(solution)/shard_map/ppermute | solution.py:140
  6.4 0.0 copy-start.5
  6.4 0.7 %copy-done.5 = s32[2,8]{1,0:T(2,128)S(1)} copy-done((s32[2,8]{1,0:T(2,128)S(1)}, s32[2,8]{1,0:T(2,128)}, u32[]{:S(2)}) %copy-start.5) | copy-done | bytes 88
  7.0 0.0 copy-start.6
  7.0 0.7 %copy-done.6 = s32[2]{0:T(128)S(1)} copy-done((s32[2]{0:T(128)S(1)}, s32[2]{0:T(128)}, u32[]{:S(2)}) %copy-start.6) | copy-done | bytes 32
  7.7 0.7 %shard_map.86 = (f32[8,256]{1,0:T(8,128)S(1)}, bf16[128,256]{1,0:T(8,128)(2,1)S(1)}) custom-call(s32[2,8]{1,0:T(2,128)S(1)} %copy-done.5, s32[2]{0:T(128)S(1)} %copy-done.6), custom_call_target="tpu_custom_call" | custom-call | flops 1000000000 | tf_op jit(solution)/shard_map/pallas_call | solution.py:392
  8.4 0.0 collective-permute-done.2.refs_3_
  8.4 1.1 %collective-permute-done.1.refs_2_ = bf16[8,208]{1,0:T(8,128)(2,1)S(1)} collective-permute-done((bf16[8,208]{1,0:T(8,128)(2,1)}, bf16[8,208]{1,0:T(8,128)(2,1)S(1)}, u32[]{:S(2)}, u32[]{:S(2)}) %collective-permute-start.1) | collective-permute-done | bytes 3360 | tf_op jit(solution)/shard_map/ppermute | solution.py:140
  9.5 0.2 collective-permute-done.refs_1_
  9.7 0.0 copy-done.1
  9.7 0.0 copy-done.2
  9.7 0.0 copy-done.3
  9.7 0.3 shard_map.87
  10.0 1.4 %collective-permute-start.5 = (f32[16,256]{1,0:T(8,128)S(1)}, f32[16,256]{1,0:T(8,128)S(1)}, u32[]{:S(2)}, u32[]{:S(2)}) collective-permute-start(f32[16,256]{1,0:T(8,128)S(1)} %get-tuple-element.9.refs_0_), channel_id=1, source_target_pairs={{0,4},{4,12},{8,0},{12,8},{1,5},{5,13},{9,1},{13,9},{2,6},{6,14},{... | collective-permute-start | bytes 49160 | tf_op jit(solution)/shard_map/ppermute | solution.py:140
  11.4 1.9 %collective-permute-start.4 = (f32[16,256]{1,0:T(8,128)S(1)}, f32[16,256]{1,0:T(8,128)S(1)}, u32[]{:S(2)}, u32[]{:S(2)}) collective-permute-start(f32[16,256]{1,0:T(8,128)S(1)} %get-tuple-element.9.refs_0_), channel_id=1, source_target_pairs={{0,12},{12,0},{4,8},{8,4},{1,13},{13,1},{5,9},{9,5},{2,14},{14,2},... | collective-permute-start | bytes 49160 | tf_op jit(solution)/shard_map/ppermute | solution.py:140
  13.3 1.6 %collective-permute-start.3 = (f32[16,256]{1,0:T(8,128)S(1)}, f32[16,256]{1,0:T(8,128)S(1)}, u32[]{:S(2)}, u32[]{:S(2)}) collective-permute-start(f32[16,256]{1,0:T(8,128)S(1)} %get-tuple-element.9.refs_0_), channel_id=1, source_target_pairs={{0,8},{4,0},{8,12},{12,4},{1,9},{5,1},{9,13},{13,5},{2,10},{6,2},{... | collective-permute-start | bytes 49160 | tf_op jit(solution)/shard_map/ppermute | solution.py:140
  14.9 0.4 %shard_map.88.refs_6_ = f32[4,128]{1,0:T(4,128)S(1)} custom-call(f32[2,8,104]{2,1,0:T(8,128)S(1)} %get-tuple-element.10.own_ref, bf16[2,2,104,256]{3,2,1,0:T(8,128)(2,1)S(1)} %bitcast.12, f32[8,256]{1,0:T(8,128)S(1)} %get-tuple-element.8.refs_6_.mask_ref.refs_5_), custom_call_target="tpu_custom_call" | custom-call | tf_op jit(solution)/shard_map/pallas_call | solution.py:408
  15.2 0.0 collective-permute-done.5.refs_3_
  15.2 1.7 %collective-permute-done.4.refs_2_ = f32[16,256]{1,0:T(8,128)S(1)} collective-permute-done((f32[16,256]{1,0:T(8,128)S(1)}, f32[16,256]{1,0:T(8,128)S(1)}, u32[]{:S(2)}, u32[]{:S(2)}) %collective-permute-start.4) | collective-permute-done | bytes 16416 | tf_op jit(solution)/shard_map/ppermute | solution.py:140
  16.9 0.2 collective-permute-done.3.refs_1_
  17.1 0.0 copy-done
  17.1 0.0 copy-done.4
  17.1 0.8 %shard_map.89 = bf16[8,16,768]{2,1,0:T(8,128)(2,1)S(1)} custom-call(f32[16,256]{1,0:T(8,128)S(1)} %get-tuple-element.9.refs_0_, f32[16,256]{1,0:T(8,128)S(1)} %collective-permute-done.3.refs_1_, f32[16,256]{1,0:T(8,128)S(1)} %collective-permute-done.4.refs_2_, f32[16,256]{1,0:T(8,128)S(1)} %collective-permute-done.5.refs_3_, f32[4,256]{1,0:T(4,128)S(1)} %bitcast.19, ...), custom_call_target="tpu_custom_call" | custom-call | tf_op jit(solution)/shard_map/pallas_call | solution.py:414
  17.9 9.6 %all_to_all.5.blocks_ref = bf16[8,16,768]{2,1,0:T(8,128)(2,1)S(1)} all-to-all(bf16[8,16,768]{2,1,0:T(8,128)(2,1)S(1)} %shard_map.89), channel_id=1, replica_groups={{10,14,6,2,12,8,4,0},{11,15,7,3,13,9,5,1},{26,30,22,18,28,24,20,16},{27..., dimensions={0} | all-to-all | bytes 393216 | tf_op jit(solution)/shard_map/all_to_all | solution.py:421
  27.5 2.2 %shard_map.90 = (f32[2,4,208]{2,1,0:T(4,128)}, f32[1,1]{1,0:T(1,128)}) custom-call(bf16[8,16,768]{2,1,0:T(8,128)(2,1)S(1)} %all_to_all.5.blocks_ref, f32[16,256]{1,0:T(8,128)S(1)} %get-tuple-element.9.refs_0_, f32[16,256]{1,0:T(8,128)S(1)} %collective-permute-done.3.refs_1_, f32[16,256]{1,0:T(8,128)S(1)} %collective-permute-done.4.refs_2_, ...), custom_call_target="tpu_custom_call" | custom-call | tf_op jit(solution)/shard_map/pallas_call | solution.py:424
Async XLA Ops:
  0.6 9.0 %copy-start.1 = (bf16[1,2,2,104,256]{4,3,2,1,0:T(8,128)(2,1)S(1)}, bf16[1,2,2,104,256]{4,3,2,1,0:T(8,128)(2,1)}, u32[]{:S(2)}) copy-start(bf16[1,2,2,104,256]{4,3,2,1,0:T(8,128)(2,1)} %param.10) | copy-start | bytes 638980
  0.6 9.0 %copy-start.2 = (f32[1,2,4,208]{3,2,1,0:T(4,128)S(1)}, f32[1,2,4,208]{3,2,1,0:T(4,128)}, u32[]{:S(2)}) copy-start(f32[1,2,4,208]{3,2,1,0:T(4,128)} %param.9) | copy-start | bytes 19972
  0.7 9.0 %copy-start.3 = (bf16[1,1,1,8,208]{4,3,2,1,0:T(8,128)(2,1)S(1)}, bf16[1,1,1,8,208]{4,3,2,1,0:T(8,128)(2,1)}, u32[]{:S(2)}) copy-start(bf16[1,1,1,8,208]{4,3,2,1,0:T(8,128)(2,1)} %param.7) | copy-start | bytes 9988
  0.7 16.4 %copy-start = (bf16[1,2,2,676,256]{4,2,3,1,0:T(2,128)(2,1)S(1)}, bf16[1,2,2,676,256]{4,2,3,1,0:T(2,128)(2,1)}, u32[]{:S(2)}) copy-start(bf16[1,2,2,676,256]{4,2,3,1,0:T(2,128)(2,1)} %param.11) | copy-start | bytes 4153348
  0.7 16.4 %copy-start.4 = (f32[1,1,4,256]{3,2,1,0:T(4,128)S(1)}, f32[1,1,4,256]{3,2,1,0:T(4,128)}, u32[]{:S(2)}) copy-start(f32[1,1,4,256]{3,2,1,0:T(4,128)} %param.8) | copy-start | bytes 12292
  0.7 7.7 %collective-permute-start.2 = (bf16[8,208]{1,0:T(8,128)(2,1)}, bf16[8,208]{1,0:T(8,128)(2,1)S(1)}, u32[]{:S(2)}, u32[]{:S(2)}) collective-permute-start(bf16[8,208]{1,0:T(8,128)(2,1)} %bitcast.15), channel_id=1, source_target_pairs={{12,0},{8,4},{4,12},{0,8},{13,1},{9,5},{5,13},{1,9},{14,2},{10,6},... | collective-permute-start | bytes 9992 | tf_op jit(solution)/shard_map/ppermute | solution.py:140
  4.8 4.7 %collective-permute-start.1 = (bf16[8,208]{1,0:T(8,128)(2,1)}, bf16[8,208]{1,0:T(8,128)(2,1)S(1)}, u32[]{:S(2)}, u32[]{:S(2)}) collective-permute-start(bf16[8,208]{1,0:T(8,128)(2,1)} %bitcast.16), channel_id=1, source_target_pairs={{12,4},{8,0},{0,12},{4,8},{13,5},{9,1},{1,13},{5,9},{14,6},{10,2},... | collective-permute-start | bytes 9992 | tf_op jit(solution)/shard_map/ppermute | solution.py:140
  5.8 3.8 %collective-permute-start = (bf16[8,208]{1,0:T(8,128)(2,1)}, bf16[8,208]{1,0:T(8,128)(2,1)S(1)}, u32[]{:S(2)}, u32[]{:S(2)}) collective-permute-start(bf16[8,208]{1,0:T(8,128)(2,1)} %bitcast.17), channel_id=1, source_target_pairs={{4,0},{12,8},{8,12},{0,4},{5,1},{13,9},{9,13},{1,5},{6,2},{14,10},... | collective-permute-start | bytes 9992 | tf_op jit(solution)/shard_map/ppermute | solution.py:140
  6.4 0.7 %copy-start.5 = (s32[2,8]{1,0:T(2,128)S(1)}, s32[2,8]{1,0:T(2,128)}, u32[]{:S(2)}) copy-start(s32[2,8]{1,0:T(2,128)} %map_ref.1) | copy-start | bytes 196
  7.0 0.7 %copy-start.6 = (s32[2]{0:T(128)S(1)}, s32[2]{0:T(128)}, u32[]{:S(2)}) copy-start(s32[2]{0:T(128)} %count_ref.1) | copy-start | bytes 28
  10.0 5.3 %collective-permute-start.5 = (f32[16,256]{1,0:T(8,128)S(1)}, f32[16,256]{1,0:T(8,128)S(1)}, u32[]{:S(2)}, u32[]{:S(2)}) collective-permute-start(f32[16,256]{1,0:T(8,128)S(1)} %get-tuple-element.9.refs_0_), channel_id=1, source_target_pairs={{0,4},{4,12},{8,0},{12,8},{1,5},{5,13},{9,1},{13,9},{2,6},{6,14},{... | collective-permute-start | bytes 49160 | tf_op jit(solution)/shard_map/ppermute | solution.py:140
  11.4 5.5 %collective-permute-start.4 = (f32[16,256]{1,0:T(8,128)S(1)}, f32[16,256]{1,0:T(8,128)S(1)}, u32[]{:S(2)}, u32[]{:S(2)}) collective-permute-start(f32[16,256]{1,0:T(8,128)S(1)} %get-tuple-element.9.refs_0_), channel_id=1, source_target_pairs={{0,12},{12,0},{4,8},{8,4},{1,13},{13,1},{5,9},{9,5},{2,14},{14,2},... | collective-permute-start | bytes 49160 | tf_op jit(solution)/shard_map/ppermute | solution.py:140
  13.3 3.8 %collective-permute-start.3 = (f32[16,256]{1,0:T(8,128)S(1)}, f32[16,256]{1,0:T(8,128)S(1)}, u32[]{:S(2)}, u32[]{:S(2)}) collective-permute-start(f32[16,256]{1,0:T(8,128)S(1)} %get-tuple-element.9.refs_0_), channel_id=1, source_target_pairs={{0,8},{4,0},{8,12},{12,4},{1,9},{5,1},{9,13},{13,5},{2,10},{6,2},{... | collective-permute-start | bytes 49160 | tf_op jit(solution)/shard_map/ppermute | solution.py:140

commit v11 on v10

--- a/solution.py
+++ b/solution.py
@@ -299,19 +299,27 @@
 
 
 def taylor_kernel(pb_count, normalizer, blocks_ref, *refs):
-    *windows, picks_ref, orbitals_ref, out_ref, energy_ref, turned, picked, term = refs
+    *windows, picks_ref, orbitals_ref, out_ref, energy_ref, turned, straight, crossed, term = refs
     pairs = M * M
     pair = NOCC * M
     k_local, walkers, _ = out_ref.shape
     span = k_local * walkers
     ka_pos = lax.axis_index("ka")
+    picks = picks_ref[...]
+
+    def pick(rows):
+        both = jnp.dot(rows.astype(BF16), picks, preferred_element_type=F32)
+        return both[:, :LANES], both[:, LANES:]
+
     term[...] = jnp.zeros_like(term)
     for source, window_ref in zip(origins("ka", BIAS_ROUNDS), windows):
         start = pl.multiple_of(source * (2 * span), 2 * span)
         window = window_ref[window_ref.shape[0] - span :]
         term[pl.ds(start, span), :pair] = window[:, :pair]
         term[pl.ds(start + span, span), :pair] = window[:, pair : 2 * pair]
-    picked[...] = jnp.dot(term[...].T.astype(BF16), picks_ref[...], preferred_element_type=F32)
+    real, imag = pick(term[:LANES].T)
+    straight[:LANES] = real
+    crossed[:LANES] = imag
     count, _, width = blocks_ref.shape
     group = operator_group(count // pb_count, pb_count)
     places = [group.index(n) for n in range(count)]
@@ -323,33 +331,48 @@
     shares = jnp.where(lax.rem(lane, 2 * span) == ka_pos, shares, 0.0)
     shares = jnp.sum(jnp.sum(shares, axis=0, keepdims=True), axis=1, keepdims=True)
     energy_ref[...] = shares / normalizer
-    lane = lax.broadcasted_iota(jnp.int32, (M, LANES), 1)
+    tall = 2 * NOCC
+    lane = lax.broadcasted_iota(jnp.int32, (tall, LANES), 1)
     imaginary = lax.rem(lane, 2 * span) >= span
-    sums = [jnp.zeros((M, LANES), F32) for _ in range(NOCC)]
+    upper = lax.broadcasted_iota(jnp.int32, (tall, LANES), 0) < NOCC
+    columns = [
+        jnp.concatenate(
+            [straight[pl.ds(c, NOCC, stride=M), :], crossed[pl.ds(c, NOCC, stride=M), :]], axis=0
+        )
+        for c in range(M)
+    ]
     for degree in range(1, TAYLOR + 1):
-        stride = M if degree == 1 else ROWS
-        straight = [jnp.zeros((M, LANES), F32) for _ in range(NOCC)]
-        crossed = [jnp.zeros((M, LANES), F32) for _ in range(NOCC)]
-        for c in range(M):
-            column = turned[pl.ds(c, M, stride=M), :]
-            for i in range(NOCC):
-                at = i * stride + c
-                straight[i] += column * picked[at : at + 1, :LANES]
-                crossed[i] += column * picked[at : at + 1, LANES:]
-        for i in range(NOCC):
+        for p in range(M):
+            halves = [None, None]
+            for c in range(M):
+                row = turned[p * M + c : p * M + c + 1, :]
+                product = jnp.broadcast_to(row, (tall, LANES)) * columns[c]
+                half = halves[c % 2]
+                halves[c % 2] = product if half is None else half + product
+            applied = halves[0] + halves[1]
             other = jnp.where(
-                imaginary, pltpu.roll(crossed[i], span, 1), pltpu.roll(crossed[i], LANES - span, 1)
+                imaginary, pltpu.roll(applied, span, 1), pltpu.roll(applied, LANES - span, 1)
             )
-            applied = straight[i] + other
+            applied = jnp.where(upper, applied, other)
+            applied = applied + pltpu.roll(applied, NOCC, 0)
             applied = applied + pltpu.roll(applied, LANES // pb_count, 1)
             current = applied / degree
-            sums[i] = sums[i] + current
-            term[i * ROWS : i * ROWS + M] = current if degree < TAYLOR else sums[i]
+            at = slice(p * tall, (p + 1) * tall)
+            if degree == 1:
+                straight[at] = current
+            else:
+                straight[at] += current
+            if degree < TAYLOR:
+                term[at] = current
         if degree < TAYLOR:
-            picked[...] = jnp.dot(
-                term[...].astype(BF16), picks_ref[...], preferred_element_type=F32
-            )
-    turned[:LANES] = term[...].T
+            real, imag = pick(term[...])
+            columns = [
+                jnp.where(upper, real[c * tall : (c + 1) * tall], imag[c * tall : (c + 1) * tall])
+                for c in range(M)
+            ]
+    for i in range(NOCC):
+        term[i * ROWS : i * ROWS + M] = straight[pl.ds(i, M, stride=tall), :]
+    turned[:LANES] = term[:LANES].T
     both = turned[pl.ds(pl.multiple_of(ka_pos * (2 * span), 2 * span), 2 * span), :]
     both = jnp.concatenate([both[:, i * ROWS : i * ROWS + M] for i in range(NOCC)], axis=1)
     both = jnp.concatenate([both[:span], both[span:]], axis=1)
@@ -426,8 +449,7 @@
         (shape((k_local, walkers, 2 * pair_width), F32), shape((1, 1), F32)),
         [
             pltpu.VMEM((width, LANES), F32),
-            pltpu.VMEM((NOCC * ROWS, 2 * LANES), F32),
-            pltpu.VMEM((LANES, LANES), F32),
+            *[pltpu.VMEM((2 * NOCC * M, LANES), F32)] * 3,
         ],
         operands=len(parts) + 3,
     )(blocks, *parts, picks, own_orbitals)

time: 29.8 us -> 29.9 us (level)
  no operation moved by 1% of the time
where the time goes in v11:
time: 29.9 us; the launch traced here: 29.7 us
  starting transfers between devices  10.6 us (35%)
  blocking collectives  9.62 us (32%)
  Pallas kernels  4.28 us (14%)
  waiting for transfers between devices  3.17 us (11%)
  local copies, waits for them, and re-layouts  1.35 us (5%)
  between operations  0.71 us (2%)
    ppermute x6, starting transfers between devices, exchange(): return [array] + [lax.ppermute(array, axis, pairs) for pairs in rounds]  10.6 us
    all_to_all x1, blocking collectives, direct(): lax.all_to_all(blocks, ('pb', 'ka'), 0, 0, axis_index_groups=[group], til...  9.62 us
    ppermute x6, waiting for transfers between devices, exchange(): return [array] + [lax.ppermute(array, axis, pairs) for pairs in rounds]  3.17 us
    pallas_call x1, Pallas kernels, direct(): call(functools.partial(taylor_kernel, pb_count, float(pb_count * chol_col...  2.22 us
    unnamed x14, local copies, waits for them, and re-layouts  1.35 us
    pallas_call x1, Pallas kernels, direct(): call(functools.partial(operator_kernel, k_local), shape((ka_count * pb_co...  0.76 us
    pallas_call x1, Pallas kernels, direct(): call(functools.partial(prepare_kernel, ka_count, pb_count, walkers), (sha...  0.66 us
  transfers between devices with their start and end apart: 6, of which 4 were waited for; matrix products, arithmetic and copies ran while one was open for 0% of the time, Pallas kernels for 3%

profile of v11, /device:TPU:0, one launch (start us, length us, event | category | flops | bytes accessed | tf_op | source)
XLA Modules:
  0.0 29.7 jit_solution(17313852783971489762)
XLA Ops:
  0.6 0.0 copy-start.1
  0.6 0.0 copy-start.2
  0.7 0.0 copy-start.3
  0.7 0.0 copy-start
  0.7 0.0 copy-start.4
  0.7 4.1 %collective-permute-start.2 = (bf16[8,208]{1,0:T(8,128)(2,1)}, bf16[8,208]{1,0:T(8,128)(2,1)S(1)}, u32[]{:S(2)}, u32[]{:S(2)}) collective-permute-start(bf16[8,208]{1,0:T(8,128)(2,1)} %bitcast.15), channel_id=1, source_target_pairs={{12,0},{8,4},{4,12},{0,8},{13,1},{9,5},{5,13},{1,9},{14,2},{10,6},... | collective-permute-start | bytes 9992 | tf_op jit(solution)/shard_map/ppermute | solution.py:140
  4.8 1.1 %collective-permute-start.1 = (bf16[8,208]{1,0:T(8,128)(2,1)}, bf16[8,208]{1,0:T(8,128)(2,1)S(1)}, u32[]{:S(2)}, u32[]{:S(2)}) collective-permute-start(bf16[8,208]{1,0:T(8,128)(2,1)} %bitcast.16), channel_id=1, source_target_pairs={{12,4},{8,0},{0,12},{4,8},{13,5},{9,1},{1,13},{5,9},{14,6},{10,2},... | collective-permute-start | bytes 9992 | tf_op jit(solution)/shard_map/ppermute | solution.py:140
  5.8 0.5 %collective-permute-start = (bf16[8,208]{1,0:T(8,128)(2,1)}, bf16[8,208]{1,0:T(8,128)(2,1)S(1)}, u32[]{:S(2)}, u32[]{:S(2)}) collective-permute-start(bf16[8,208]{1,0:T(8,128)(2,1)} %bitcast.17), channel_id=1, source_target_pairs={{4,0},{12,8},{8,12},{0,4},{5,1},{13,9},{9,13},{1,5},{6,2},{14,10},... | collective-permute-start | bytes 9992 | tf_op jit(solution)/shard_map/ppermute | solution.py:140
  6.4 0.0 copy-start.5
  6.4 0.7 %copy-done.5 = s32[2,8]{1,0:T(2,128)S(1)} copy-done((s32[2,8]{1,0:T(2,128)S(1)}, s32[2,8]{1,0:T(2,128)}, u32[]{:S(2)}) %copy-start.5) | copy-done | bytes 88
  7.0 0.0 copy-start.6
  7.0 0.7 %copy-done.6 = s32[2]{0:T(128)S(1)} copy-done((s32[2]{0:T(128)S(1)}, s32[2]{0:T(128)}, u32[]{:S(2)}) %copy-start.6) | copy-done | bytes 32
  7.7 0.7 %shard_map.86 = (f32[8,256]{1,0:T(8,128)S(1)}, bf16[128,256]{1,0:T(8,128)(2,1)S(1)}) custom-call(s32[2,8]{1,0:T(2,128)S(1)} %copy-done.5, s32[2]{0:T(128)S(1)} %copy-done.6), custom_call_target="tpu_custom_call" | custom-call | flops 1000000000 | tf_op jit(solution)/shard_map/pallas_call | solution.py:415
  8.4 0.0 collective-permute-done.2.refs_3_
  8.4 1.1 %collective-permute-done.1.refs_2_ = bf16[8,208]{1,0:T(8,128)(2,1)S(1)} collective-permute-done((bf16[8,208]{1,0:T(8,128)(2,1)}, bf16[8,208]{1,0:T(8,128)(2,1)S(1)}, u32[]{:S(2)}, u32[]{:S(2)}) %collective-permute-start.1) | collective-permute-done | bytes 3360 | tf_op jit(solution)/shard_map/ppermute | solution.py:140
  9.5 0.2 collective-permute-done.refs_1_
  9.7 0.0 copy-done.1
  9.7 0.0 copy-done.2
  9.7 0.0 copy-done.3
  9.7 0.3 shard_map.87
  10.0 1.4 %collective-permute-start.5 = (f32[16,256]{1,0:T(8,128)S(1)}, f32[16,256]{1,0:T(8,128)S(1)}, u32[]{:S(2)}, u32[]{:S(2)}) collective-permute-start(f32[16,256]{1,0:T(8,128)S(1)} %get-tuple-element.9.refs_0_), channel_id=1, source_target_pairs={{0,4},{4,12},{8,0},{12,8},{1,5},{5,13},{9,1},{13,9},{2,6},{6,14},{... | collective-permute-start | bytes 49160 | tf_op jit(solution)/shard_map/ppermute | solution.py:140
  11.4 1.9 %collective-permute-start.4 = (f32[16,256]{1,0:T(8,128)S(1)}, f32[16,256]{1,0:T(8,128)S(1)}, u32[]{:S(2)}, u32[]{:S(2)}) collective-permute-start(f32[16,256]{1,0:T(8,128)S(1)} %get-tuple-element.9.refs_0_), channel_id=1, source_target_pairs={{0,12},{12,0},{4,8},{8,4},{1,13},{13,1},{5,9},{9,5},{2,14},{14,2},... | collective-permute-start | bytes 49160 | tf_op jit(solution)/shard_map/ppermute | solution.py:140
  13.3 1.6 %collective-permute-start.3 = (f32[16,256]{1,0:T(8,128)S(1)}, f32[16,256]{1,0:T(8,128)S(1)}, u32[]{:S(2)}, u32[]{:S(2)}) collective-permute-start(f32[16,256]{1,0:T(8,128)S(1)} %get-tuple-element.9.refs_0_), channel_id=1, source_target_pairs={{0,8},{4,0},{8,12},{12,4},{1,9},{5,1},{9,13},{13,5},{2,10},{6,2},{... | collective-permute-start | bytes 49160 | tf_op jit(solution)/shard_map/ppermute | solution.py:140
  14.9 0.4 %shard_map.88.refs_6_ = f32[4,128]{1,0:T(4,128)S(1)} custom-call(f32[2,8,104]{2,1,0:T(8,128)S(1)} %get-tuple-element.10.own_ref, bf16[2,2,104,256]{3,2,1,0:T(8,128)(2,1)S(1)} %bitcast.12, f32[8,256]{1,0:T(8,128)S(1)} %get-tuple-element.8.refs_6_.mask_ref.refs_5_), custom_call_target="tpu_custom_call" | custom-call | tf_op jit(solution)/shard_map/pallas_call | solution.py:431
  15.2 0.0 collective-permute-done.5.refs_3_
  15.2 1.7 %collective-permute-done.4.refs_2_ = f32[16,256]{1,0:T(8,128)S(1)} collective-permute-done((f32[16,256]{1,0:T(8,128)S(1)}, f32[16,256]{1,0:T(8,128)S(1)}, u32[]{:S(2)}, u32[]{:S(2)}) %collective-permute-start.4) | collective-permute-done | bytes 16416 | tf_op jit(solution)/shard_map/ppermute | solution.py:140
  16.9 0.2 collective-permute-done.3.refs_1_
  17.1 0.0 copy-done
  17.1 0.0 copy-done.4
  17.1 0.8 %shard_map.89 = bf16[8,16,768]{2,1,0:T(8,128)(2,1)S(1)} custom-call(f32[16,256]{1,0:T(8,128)S(1)} %get-tuple-element.9.refs_0_, f32[16,256]{1,0:T(8,128)S(1)} %collective-permute-done.3.refs_1_, f32[16,256]{1,0:T(8,128)S(1)} %collective-permute-done.4.refs_2_, f32[16,256]{1,0:T(8,128)S(1)} %collective-permute-done.5.refs_3_, f32[4,256]{1,0:T(4,128)S(1)} %bitcast.19, ...), custom_call_target="tpu_custom_call" | custom-call | tf_op jit(solution)/shard_map/pallas_call | solution.py:437
  17.9 9.6 %all_to_all.5.blocks_ref = bf16[8,16,768]{2,1,0:T(8,128)(2,1)S(1)} all-to-all(bf16[8,16,768]{2,1,0:T(8,128)(2,1)S(1)} %shard_map.89), channel_id=1, replica_groups={{10,14,6,2,12,8,4,0},{11,15,7,3,13,9,5,1},{26,30,22,18,28,24,20,16},{27..., dimensions={0} | all-to-all | bytes 393216 | tf_op jit(solution)/shard_map/all_to_all | solution.py:444
  27.5 2.2 %shard_map.90 = (f32[2,4,208]{2,1,0:T(4,128)}, f32[1,1]{1,0:T(1,128)}) custom-call(bf16[8,16,768]{2,1,0:T(8,128)(2,1)S(1)} %all_to_all.5.blocks_ref, f32[16,256]{1,0:T(8,128)S(1)} %get-tuple-element.9.refs_0_, f32[16,256]{1,0:T(8,128)S(1)} %collective-permute-done.3.refs_1_, f32[16,256]{1,0:T(8,128)S(1)} %collective-permute-done.4.refs_2_, ...), custom_call_target="tpu_custom_call" | custom-call | tf_op jit(solution)/shard_map/pallas_call | solution.py:447
Async XLA Ops:
  0.6 9.0 %copy-start.1 = (bf16[1,2,2,104,256]{4,3,2,1,0:T(8,128)(2,1)S(1)}, bf16[1,2,2,104,256]{4,3,2,1,0:T(8,128)(2,1)}, u32[]{:S(2)}) copy-start(bf16[1,2,2,104,256]{4,3,2,1,0:T(8,128)(2,1)} %param.10) | copy-start | bytes 638980
  0.6 9.0 %copy-start.2 = (f32[1,2,4,208]{3,2,1,0:T(4,128)S(1)}, f32[1,2,4,208]{3,2,1,0:T(4,128)}, u32[]{:S(2)}) copy-start(f32[1,2,4,208]{3,2,1,0:T(4,128)} %param.9) | copy-start | bytes 19972
  0.7 9.0 %copy-start.3 = (bf16[1,1,1,8,208]{4,3,2,1,0:T(8,128)(2,1)S(1)}, bf16[1,1,1,8,208]{4,3,2,1,0:T(8,128)(2,1)}, u32[]{:S(2)}) copy-start(bf16[1,1,1,8,208]{4,3,2,1,0:T(8,128)(2,1)} %param.7) | copy-start | bytes 9988
  0.7 16.4 %copy-start = (bf16[1,2,2,676,256]{4,2,3,1,0:T(2,128)(2,1)S(1)}, bf16[1,2,2,676,256]{4,2,3,1,0:T(2,128)(2,1)}, u32[]{:S(2)}) copy-start(bf16[1,2,2,676,256]{4,2,3,1,0:T(2,128)(2,1)} %param.11) | copy-start | bytes 4153348
  0.7 16.4 %copy-start.4 = (f32[1,1,4,256]{3,2,1,0:T(4,128)S(1)}, f32[1,1,4,256]{3,2,1,0:T(4,128)}, u32[]{:S(2)}) copy-start(f32[1,1,4,256]{3,2,1,0:T(4,128)} %param.8) | copy-start | bytes 12292
  0.7 7.7 %collective-permute-start.2 = (bf16[8,208]{1,0:T(8,128)(2,1)}, bf16[8,208]{1,0:T(8,128)(2,1)S(1)}, u32[]{:S(2)}, u32[]{:S(2)}) collective-permute-start(bf16[8,208]{1,0:T(8,128)(2,1)} %bitcast.15), channel_id=1, source_target_pairs={{12,0},{8,4},{4,12},{0,8},{13,1},{9,5},{5,13},{1,9},{14,2},{10,6},... | collective-permute-start | bytes 9992 | tf_op jit(solution)/shard_map/ppermute | solution.py:140
  4.8 4.7 %collective-permute-start.1 = (bf16[8,208]{1,0:T(8,128)(2,1)}, bf16[8,208]{1,0:T(8,128)(2,1)S(1)}, u32[]{:S(2)}, u32[]{:S(2)}) collective-permute-start(bf16[8,208]{1,0:T(8,128)(2,1)} %bitcast.16), channel_id=1, source_target_pairs={{12,4},{8,0},{0,12},{4,8},{13,5},{9,1},{1,13},{5,9},{14,6},{10,2},... | collective-permute-start | bytes 9992 | tf_op jit(solution)/shard_map/ppermute | solution.py:140
  5.8 3.8 %collective-permute-start = (bf16[8,208]{1,0:T(8,128)(2,1)}, bf16[8,208]{1,0:T(8,128)(2,1)S(1)}, u32[]{:S(2)}, u32[]{:S(2)}) collective-permute-start(bf16[8,208]{1,0:T(8,128)(2,1)} %bitcast.17), channel_id=1, source_target_pairs={{4,0},{12,8},{8,12},{0,4},{5,1},{13,9},{9,13},{1,5},{6,2},{14,10},... | collective-permute-start | bytes 9992 | tf_op jit(solution)/shard_map/ppermute | solution.py:140
  6.4 0.7 %copy-start.5 = (s32[2,8]{1,0:T(2,128)S(1)}, s32[2,8]{1,0:T(2,128)}, u32[]{:S(2)}) copy-start(s32[2,8]{1,0:T(2,128)} %map_ref.1) | copy-start | bytes 196
  7.0 0.7 %copy-start.6 = (s32[2]{0:T(128)S(1)}, s32[2]{0:T(128)}, u32[]{:S(2)}) copy-start(s32[2]{0:T(128)} %count_ref.1) | copy-start | bytes 28
  10.0 5.3 %collective-permute-start.5 = (f32[16,256]{1,0:T(8,128)S(1)}, f32[16,256]{1,0:T(8,128)S(1)}, u32[]{:S(2)}, u32[]{:S(2)}) collective-permute-start(f32[16,256]{1,0:T(8,128)S(1)} %get-tuple-element.9.refs_0_), channel_id=1, source_target_pairs={{0,4},{4,12},{8,0},{12,8},{1,5},{5,13},{9,1},{13,9},{2,6},{6,14},{... | collective-permute-start | bytes 49160 | tf_op jit(solution)/shard_map/ppermute | solution.py:140
  11.4 5.5 %collective-permute-start.4 = (f32[16,256]{1,0:T(8,128)S(1)}, f32[16,256]{1,0:T(8,128)S(1)}, u32[]{:S(2)}, u32[]{:S(2)}) collective-permute-start(f32[16,256]{1,0:T(8,128)S(1)} %get-tuple-element.9.refs_0_), channel_id=1, source_target_pairs={{0,12},{12,0},{4,8},{8,4},{1,13},{13,1},{5,9},{9,5},{2,14},{14,2},... | collective-permute-start | bytes 49160 | tf_op jit(solution)/shard_map/ppermute | solution.py:140
  13.3 3.8 %collective-permute-start.3 = (f32[16,256]{1,0:T(8,128)S(1)}, f32[16,256]{1,0:T(8,128)S(1)}, u32[]{:S(2)}, u32[]{:S(2)}) collective-permute-start(f32[16,256]{1,0:T(8,128)S(1)} %get-tuple-element.9.refs_0_), channel_id=1, source_target_pairs={{0,8},{4,0},{8,12},{12,4},{1,9},{5,1},{9,13},{13,5},{2,10},{6,2},{... | collective-permute-start | bytes 49160 | tf_op jit(solution)/shard_map/ppermute | solution.py:140

commit v12 on v10

--- a/solution.py
+++ b/solution.py
@@ -154,7 +154,7 @@
 def operator_group(ka_count, pb_count):
     first = (pb_count - 1) * ka_count + ka_count // 2
     rest = [at for at in range(pb_count * ka_count) if at != first]
-    return [first] + rest[::-1]
+    return [first] + rest
 
 
 def prepare_kernel(ka_count, pb_count, walkers, map_ref, count_ref, mask_ref, picks_ref):

time: 29.8 us -> 30.2 us (1.013)
  blocking collectives: 9.62 us -> 9.99 us
    all_to_all x1, blocking collectives: 9.62 us -> 9.99 us  [direct(): lax.all_to_all(blocks, ('pb', 'ka'), 0, 0, axis_index_groups=[group], til...]
where the time goes in v12:
time: 30.2 us; the launch traced here: 30 us
  starting transfers between devices  10.6 us (35%)
  blocking collectives  9.99 us (33%)
  Pallas kernels  4.2 us (14%)
  waiting for transfers between devices  3.17 us (10%)
  local copies, waits for them, and re-layouts  1.35 us (4%)
  between operations  0.71 us (2%)
    ppermute x6, starting transfers between devices, exchange(): return [array] + [lax.ppermute(array, axis, pairs) for pairs in rounds]  10.6 us
    all_to_all x1, blocking collectives, direct(): lax.all_to_all(blocks, ('pb', 'ka'), 0, 0, axis_index_groups=[group], til...  9.99 us
    ppermute x6, waiting for transfers between devices, exchange(): return [array] + [lax.ppermute(array, axis, pairs) for pairs in rounds]  3.17 us
    pallas_call x1, Pallas kernels, direct(): call(functools.partial(taylor_kernel, pb_count, float(pb_count * chol_col...  2.15 us
    unnamed x14, local copies, waits for them, and re-layouts  1.35 us
    pallas_call x1, Pallas kernels, direct(): call(functools.partial(operator_kernel, k_local), shape((ka_count * pb_co...  0.76 us
    pallas_call x1, Pallas kernels, direct(): call(functools.partial(prepare_kernel, ka_count, pb_count, walkers), (sha...  0.66 us
  transfers between devices with their start and end apart: 6, of which 4 were waited for; matrix products, arithmetic and copies ran while one was open for 0% of the time, Pallas kernels for 3%

profile of v12, /device:TPU:0, one launch (start us, length us, event | category | flops | bytes accessed | tf_op | source)
XLA Modules:
  0.0 30.0 jit_solution(4362796019165865844)
XLA Ops:
  0.6 0.0 copy-start.1
  0.6 0.0 copy-start.2
  0.7 0.0 copy-start.3
  0.7 0.0 copy-start
  0.7 0.0 copy-start.4
  0.7 4.1 %collective-permute-start.2 = (bf16[8,208]{1,0:T(8,128)(2,1)}, bf16[8,208]{1,0:T(8,128)(2,1)S(1)}, u32[]{:S(2)}, u32[]{:S(2)}) collective-permute-start(bf16[8,208]{1,0:T(8,128)(2,1)} %bitcast.15), channel_id=1, source_target_pairs={{12,0},{8,4},{4,12},{0,8},{13,1},{9,5},{5,13},{1,9},{14,2},{10,6},... | collective-permute-start | bytes 9992 | tf_op jit(solution)/shard_map/ppermute | solution.py:140
  4.8 1.1 %collective-permute-start.1 = (bf16[8,208]{1,0:T(8,128)(2,1)}, bf16[8,208]{1,0:T(8,128)(2,1)S(1)}, u32[]{:S(2)}, u32[]{:S(2)}) collective-permute-start(bf16[8,208]{1,0:T(8,128)(2,1)} %bitcast.16), channel_id=1, source_target_pairs={{12,4},{8,0},{0,12},{4,8},{13,5},{9,1},{1,13},{5,9},{14,6},{10,2},... | collective-permute-start | bytes 9992 | tf_op jit(solution)/shard_map/ppermute | solution.py:140
  5.8 0.5 %collective-permute-start = (bf16[8,208]{1,0:T(8,128)(2,1)}, bf16[8,208]{1,0:T(8,128)(2,1)S(1)}, u32[]{:S(2)}, u32[]{:S(2)}) collective-permute-start(bf16[8,208]{1,0:T(8,128)(2,1)} %bitcast.17), channel_id=1, source_target_pairs={{4,0},{12,8},{8,12},{0,4},{5,1},{13,9},{9,13},{1,5},{6,2},{14,10},... | collective-permute-start | bytes 9992 | tf_op jit(solution)/shard_map/ppermute | solution.py:140
  6.4 0.0 copy-start.5
  6.4 0.7 %copy-done.5 = s32[2,8]{1,0:T(2,128)S(1)} copy-done((s32[2,8]{1,0:T(2,128)S(1)}, s32[2,8]{1,0:T(2,128)}, u32[]{:S(2)}) %copy-start.5) | copy-done | bytes 88
  7.0 0.0 copy-start.6
  7.0 0.7 %copy-done.6 = s32[2]{0:T(128)S(1)} copy-done((s32[2]{0:T(128)S(1)}, s32[2]{0:T(128)}, u32[]{:S(2)}) %copy-start.6) | copy-done | bytes 32
  7.7 0.7 %shard_map.86 = (f32[8,256]{1,0:T(8,128)S(1)}, bf16[128,256]{1,0:T(8,128)(2,1)S(1)}) custom-call(s32[2,8]{1,0:T(2,128)S(1)} %copy-done.5, s32[2]{0:T(128)S(1)} %copy-done.6), custom_call_target="tpu_custom_call" | custom-call | flops 1000000000 | tf_op jit(solution)/shard_map/pallas_call | solution.py:392
  8.4 0.0 collective-permute-done.2.refs_3_
  8.4 1.1 %collective-permute-done.1.refs_2_ = bf16[8,208]{1,0:T(8,128)(2,1)S(1)} collective-permute-done((bf16[8,208]{1,0:T(8,128)(2,1)}, bf16[8,208]{1,0:T(8,128)(2,1)S(1)}, u32[]{:S(2)}, u32[]{:S(2)}) %collective-permute-start.1) | collective-permute-done | bytes 3360 | tf_op jit(solution)/shard_map/ppermute | solution.py:140
  9.5 0.2 collective-permute-done.refs_1_
  9.7 0.0 copy-done.1
  9.7 0.0 copy-done.2
  9.7 0.0 copy-done.3
  9.7 0.3 shard_map.87
  10.0 1.4 %collective-permute-start.5 = (f32[16,256]{1,0:T(8,128)S(1)}, f32[16,256]{1,0:T(8,128)S(1)}, u32[]{:S(2)}, u32[]{:S(2)}) collective-permute-start(f32[16,256]{1,0:T(8,128)S(1)} %get-tuple-element.9.refs_0_), channel_id=1, source_target_pairs={{0,4},{4,12},{8,0},{12,8},{1,5},{5,13},{9,1},{13,9},{2,6},{6,14},{... | collective-permute-start | bytes 49160 | tf_op jit(solution)/shard_map/ppermute | solution.py:140
  11.4 1.9 %collective-permute-start.4 = (f32[16,256]{1,0:T(8,128)S(1)}, f32[16,256]{1,0:T(8,128)S(1)}, u32[]{:S(2)}, u32[]{:S(2)}) collective-permute-start(f32[16,256]{1,0:T(8,128)S(1)} %get-tuple-element.9.refs_0_), channel_id=1, source_target_pairs={{0,12},{12,0},{4,8},{8,4},{1,13},{13,1},{5,9},{9,5},{2,14},{14,2},... | collective-permute-start | bytes 49160 | tf_op jit(solution)/shard_map/ppermute | solution.py:140
  13.3 1.6 %collective-permute-start.3 = (f32[16,256]{1,0:T(8,128)S(1)}, f32[16,256]{1,0:T(8,128)S(1)}, u32[]{:S(2)}, u32[]{:S(2)}) collective-permute-start(f32[16,256]{1,0:T(8,128)S(1)} %get-tuple-element.9.refs_0_), channel_id=1, source_target_pairs={{0,8},{4,0},{8,12},{12,4},{1,9},{5,1},{9,13},{13,5},{2,10},{6,2},{... | collective-permute-start | bytes 49160 | tf_op jit(solution)/shard_map/ppermute | solution.py:140
  14.9 0.4 %shard_map.88.refs_6_ = f32[4,128]{1,0:T(4,128)S(1)} custom-call(f32[2,8,104]{2,1,0:T(8,128)S(1)} %get-tuple-element.10.own_ref, bf16[2,2,104,256]{3,2,1,0:T(8,128)(2,1)S(1)} %bitcast.12, f32[8,256]{1,0:T(8,128)S(1)} %get-tuple-element.8.refs_6_.mask_ref.refs_5_), custom_call_target="tpu_custom_call" | custom-call | tf_op jit(solution)/shard_map/pallas_call | solution.py:408
  15.2 0.0 collective-permute-done.5.refs_3_
  15.2 1.7 %collective-permute-done.4.refs_2_ = f32[16,256]{1,0:T(8,128)S(1)} collective-permute-done((f32[16,256]{1,0:T(8,128)S(1)}, f32[16,256]{1,0:T(8,128)S(1)}, u32[]{:S(2)}, u32[]{:S(2)}) %collective-permute-start.4) | collective-permute-done | bytes 16416 | tf_op jit(solution)/shard_map/ppermute | solution.py:140
  16.9 0.2 collective-permute-done.3.refs_1_
  17.1 0.0 copy-done
  17.1 0.0 copy-done.4
  17.1 0.8 %shard_map.89 = bf16[8,16,768]{2,1,0:T(8,128)(2,1)S(1)} custom-call(f32[16,256]{1,0:T(8,128)S(1)} %get-tuple-element.9.refs_0_, f32[16,256]{1,0:T(8,128)S(1)} %collective-permute-done.3.refs_1_, f32[16,256]{1,0:T(8,128)S(1)} %collective-permute-done.4.refs_2_, f32[16,256]{1,0:T(8,128)S(1)} %collective-permute-done.5.refs_3_, f32[4,256]{1,0:T(4,128)S(1)} %bitcast.19, ...), custom_call_target="tpu_custom_call" | custom-call | tf_op jit(solution)/shard_map/pallas_call | solution.py:414
  17.9 10.0 %all_to_all.5.blocks_ref = bf16[8,16,768]{2,1,0:T(8,128)(2,1)S(1)} all-to-all(bf16[8,16,768]{2,1,0:T(8,128)(2,1)S(1)} %shard_map.89), channel_id=1, replica_groups={{10,0,4,8,12,2,6,14},{11,1,5,9,13,3,7,15},{26,16,20,24,28,18,22,30},{27..., dimensions={0} | all-to-all | bytes 393216 | tf_op jit(solution)/shard_map/all_to_all | solution.py:421
  27.9 2.1 %shard_map.90 = (f32[2,4,208]{2,1,0:T(4,128)}, f32[1,1]{1,0:T(1,128)}) custom-call(bf16[8,16,768]{2,1,0:T(8,128)(2,1)S(1)} %all_to_all.5.blocks_ref, f32[16,256]{1,0:T(8,128)S(1)} %get-tuple-element.9.refs_0_, f32[16,256]{1,0:T(8,128)S(1)} %collective-permute-done.3.refs_1_, f32[16,256]{1,0:T(8,128)S(1)} %collective-permute-done.4.refs_2_, ...), custom_call_target="tpu_custom_call" | custom-call | tf_op jit(solution)/shard_map/pallas_call | solution.py:424
Async XLA Ops:
  0.6 9.0 %copy-start.1 = (bf16[1,2,2,104,256]{4,3,2,1,0:T(8,128)(2,1)S(1)}, bf16[1,2,2,104,256]{4,3,2,1,0:T(8,128)(2,1)}, u32[]{:S(2)}) copy-start(bf16[1,2,2,104,256]{4,3,2,1,0:T(8,128)(2,1)} %param.10) | copy-start | bytes 638980
  0.6 9.0 %copy-start.2 = (f32[1,2,4,208]{3,2,1,0:T(4,128)S(1)}, f32[1,2,4,208]{3,2,1,0:T(4,128)}, u32[]{:S(2)}) copy-start(f32[1,2,4,208]{3,2,1,0:T(4,128)} %param.9) | copy-start | bytes 19972
  0.7 9.0 %copy-start.3 = (bf16[1,1,1,8,208]{4,3,2,1,0:T(8,128)(2,1)S(1)}, bf16[1,1,1,8,208]{4,3,2,1,0:T(8,128)(2,1)}, u32[]{:S(2)}) copy-start(bf16[1,1,1,8,208]{4,3,2,1,0:T(8,128)(2,1)} %param.7) | copy-start | bytes 9988
  0.7 16.4 %copy-start = (bf16[1,2,2,676,256]{4,2,3,1,0:T(2,128)(2,1)S(1)}, bf16[1,2,2,676,256]{4,2,3,1,0:T(2,128)(2,1)}, u32[]{:S(2)}) copy-start(bf16[1,2,2,676,256]{4,2,3,1,0:T(2,128)(2,1)} %param.11) | copy-start | bytes 4153348
  0.7 16.4 %copy-start.4 = (f32[1,1,4,256]{3,2,1,0:T(4,128)S(1)}, f32[1,1,4,256]{3,2,1,0:T(4,128)}, u32[]{:S(2)}) copy-start(f32[1,1,4,256]{3,2,1,0:T(4,128)} %param.8) | copy-start | bytes 12292
  0.7 7.7 %collective-permute-start.2 = (bf16[8,208]{1,0:T(8,128)(2,1)}, bf16[8,208]{1,0:T(8,128)(2,1)S(1)}, u32[]{:S(2)}, u32[]{:S(2)}) collective-permute-start(bf16[8,208]{1,0:T(8,128)(2,1)} %bitcast.15), channel_id=1, source_target_pairs={{12,0},{8,4},{4,12},{0,8},{13,1},{9,5},{5,13},{1,9},{14,2},{10,6},... | collective-permute-start | bytes 9992 | tf_op jit(solution)/shard_map/ppermute | solution.py:140
  4.8 4.7 %collective-permute-start.1 = (bf16[8,208]{1,0:T(8,128)(2,1)}, bf16[8,208]{1,0:T(8,128)(2,1)S(1)}, u32[]{:S(2)}, u32[]{:S(2)}) collective-permute-start(bf16[8,208]{1,0:T(8,128)(2,1)} %bitcast.16), channel_id=1, source_target_pairs={{12,4},{8,0},{0,12},{4,8},{13,5},{9,1},{1,13},{5,9},{14,6},{10,2},... | collective-permute-start | bytes 9992 | tf_op jit(solution)/shard_map/ppermute | solution.py:140
  5.8 3.8 %collective-permute-start = (bf16[8,208]{1,0:T(8,128)(2,1)}, bf16[8,208]{1,0:T(8,128)(2,1)S(1)}, u32[]{:S(2)}, u32[]{:S(2)}) collective-permute-start(bf16[8,208]{1,0:T(8,128)(2,1)} %bitcast.17), channel_id=1, source_target_pairs={{4,0},{12,8},{8,12},{0,4},{5,1},{13,9},{9,13},{1,5},{6,2},{14,10},... | collective-permute-start | bytes 9992 | tf_op jit(solution)/shard_map/ppermute | solution.py:140
  6.4 0.7 %copy-start.5 = (s32[2,8]{1,0:T(2,128)S(1)}, s32[2,8]{1,0:T(2,128)}, u32[]{:S(2)}) copy-start(s32[2,8]{1,0:T(2,128)} %map_ref.1) | copy-start | bytes 196
  7.0 0.7 %copy-start.6 = (s32[2]{0:T(128)S(1)}, s32[2]{0:T(128)}, u32[]{:S(2)}) copy-start(s32[2]{0:T(128)} %count_ref.1) | copy-start | bytes 28
  10.0 5.3 %collective-permute-start.5 = (f32[16,256]{1,0:T(8,128)S(1)}, f32[16,256]{1,0:T(8,128)S(1)}, u32[]{:S(2)}, u32[]{:S(2)}) collective-permute-start(f32[16,256]{1,0:T(8,128)S(1)} %get-tuple-element.9.refs_0_), channel_id=1, source_target_pairs={{0,4},{4,12},{8,0},{12,8},{1,5},{5,13},{9,1},{13,9},{2,6},{6,14},{... | collective-permute-start | bytes 49160 | tf_op jit(solution)/shard_map/ppermute | solution.py:140
  11.4 5.5 %collective-permute-start.4 = (f32[16,256]{1,0:T(8,128)S(1)}, f32[16,256]{1,0:T(8,128)S(1)}, u32[]{:S(2)}, u32[]{:S(2)}) collective-permute-start(f32[16,256]{1,0:T(8,128)S(1)} %get-tuple-element.9.refs_0_), channel_id=1, source_target_pairs={{0,12},{12,0},{4,8},{8,4},{1,13},{13,1},{5,9},{9,5},{2,14},{14,2},... | collective-permute-start | bytes 49160 | tf_op jit(solution)/shard_map/ppermute | solution.py:140
  13.3 3.8 %collective-permute-start.3 = (f32[16,256]{1,0:T(8,128)S(1)}, f32[16,256]{1,0:T(8,128)S(1)}, u32[]{:S(2)}, u32[]{:S(2)}) collective-permute-start(f32[16,256]{1,0:T(8,128)S(1)} %get-tuple-element.9.refs_0_), channel_id=1, source_target_pairs={{0,8},{4,0},{8,12},{12,4},{1,9},{5,1},{9,13},{13,5},{2,10},{6,2},{... | collective-permute-start | bytes 49160 | tf_op jit(solution)/shard_map/ppermute | solution.py:140

commit v13 on v12

--- a/solution.py
+++ b/solution.py
@@ -154,7 +154,7 @@
 def operator_group(ka_count, pb_count):
     first = (pb_count - 1) * ka_count + ka_count // 2
     rest = [at for at in range(pb_count * ka_count) if at != first]
-    return [first] + rest
+    return [first] + sorted(rest, key=lambda at: -(at // ka_count + at % ka_count))
 
 
 def prepare_kernel(ka_count, pb_count, walkers, map_ref, count_ref, mask_ref, picks_ref):

time: 30.2 us -> 30.2 us (level)
  no operation moved by 1% of the time
where the time goes in v13:
time: 30.2 us; the launch traced here: 30 us
  starting transfers between devices  10.6 us (35%)
  blocking collectives  9.98 us (33%)
  Pallas kernels  4.2 us (14%)
  waiting for transfers between devices  3.17 us (10%)
  local copies, waits for them, and re-layouts  1.35 us (4%)
  between operations  0.71 us (2%)
    ppermute x6, starting transfers between devices, exchange(): return [array] + [lax.ppermute(array, axis, pairs) for pairs in rounds]  10.6 us
    all_to_all x1, blocking collectives, direct(): lax.all_to_all(blocks, ('pb', 'ka'), 0, 0, axis_index_groups=[group], til...  9.98 us
    ppermute x6, waiting for transfers between devices, exchange(): return [array] + [lax.ppermute(array, axis, pairs) for pairs in rounds]  3.17 us
    pallas_call x1, Pallas kernels, direct(): call(functools.partial(taylor_kernel, pb_count, float(pb_count * chol_col...  2.15 us
    unnamed x14, local copies, waits for them, and re-layouts  1.35 us
    pallas_call x1, Pallas kernels, direct(): call(functools.partial(operator_kernel, k_local), shape((ka_count * pb_co...  0.76 us
    pallas_call x1, Pallas kernels, direct(): call(functools.partial(prepare_kernel, ka_count, pb_count, walkers), (sha...  0.66 us
  transfers between devices with their start and end apart: 6, of which 4 were waited for; matrix products, arithmetic and copies ran while one was open for 0% of the time, Pallas kernels for 3%

profile of v13, /device:TPU:0, one launch (start us, length us, event | category | flops | bytes accessed | tf_op | source)
XLA Modules:
  0.0 30.0 jit_solution(4945175986156404968)
XLA Ops:
  0.6 0.0 copy-start.1
  0.6 0.0 copy-start.2
  0.7 0.0 copy-start.3
  0.7 0.0 copy-start
  0.7 0.0 copy-start.4
  0.7 4.1 %collective-permute-start.2 = (bf16[8,208]{1,0:T(8,128)(2,1)}, bf16[8,208]{1,0:T(8,128)(2,1)S(1)}, u32[]{:S(2)}, u32[]{:S(2)}) collective-permute-start(bf16[8,208]{1,0:T(8,128)(2,1)} %bitcast.15), channel_id=1, source_target_pairs={{12,0},{8,4},{4,12},{0,8},{13,1},{9,5},{5,13},{1,9},{14,2},{10,6},... | collective-permute-start | bytes 9992 | tf_op jit(solution)/shard_map/ppermute | solution.py:140
  4.8 1.1 %collective-permute-start.1 = (bf16[8,208]{1,0:T(8,128)(2,1)}, bf16[8,208]{1,0:T(8,128)(2,1)S(1)}, u32[]{:S(2)}, u32[]{:S(2)}) collective-permute-start(bf16[8,208]{1,0:T(8,128)(2,1)} %bitcast.16), channel_id=1, source_target_pairs={{12,4},{8,0},{0,12},{4,8},{13,5},{9,1},{1,13},{5,9},{14,6},{10,2},... | collective-permute-start | bytes 9992 | tf_op jit(solution)/shard_map/ppermute | solution.py:140
  5.8 0.5 %collective-permute-start = (bf16[8,208]{1,0:T(8,128)(2,1)}, bf16[8,208]{1,0:T(8,128)(2,1)S(1)}, u32[]{:S(2)}, u32[]{:S(2)}) collective-permute-start(bf16[8,208]{1,0:T(8,128)(2,1)} %bitcast.17), channel_id=1, source_target_pairs={{4,0},{12,8},{8,12},{0,4},{5,1},{13,9},{9,13},{1,5},{6,2},{14,10},... | collective-permute-start | bytes 9992 | tf_op jit(solution)/shard_map/ppermute | solution.py:140
  6.4 0.0 copy-start.5
  6.4 0.7 %copy-done.5 = s32[2,8]{1,0:T(2,128)S(1)} copy-done((s32[2,8]{1,0:T(2,128)S(1)}, s32[2,8]{1,0:T(2,128)}, u32[]{:S(2)}) %copy-start.5) | copy-done | bytes 88
  7.0 0.0 copy-start.6
  7.0 0.7 %copy-done.6 = s32[2]{0:T(128)S(1)} copy-done((s32[2]{0:T(128)S(1)}, s32[2]{0:T(128)}, u32[]{:S(2)}) %copy-start.6) | copy-done | bytes 32
  7.7 0.7 %shard_map.86 = (f32[8,256]{1,0:T(8,128)S(1)}, bf16[128,256]{1,0:T(8,128)(2,1)S(1)}) custom-call(s32[2,8]{1,0:T(2,128)S(1)} %copy-done.5, s32[2]{0:T(128)S(1)} %copy-done.6), custom_call_target="tpu_custom_call" | custom-call | flops 1000000000 | tf_op jit(solution)/shard_map/pallas_call | solution.py:392
  8.4 0.0 collective-permute-done.2.refs_3_
  8.4 1.1 %collective-permute-done.1.refs_2_ = bf16[8,208]{1,0:T(8,128)(2,1)S(1)} collective-permute-done((bf16[8,208]{1,0:T(8,128)(2,1)}, bf16[8,208]{1,0:T(8,128)(2,1)S(1)}, u32[]{:S(2)}, u32[]{:S(2)}) %collective-permute-start.1) | collective-permute-done | bytes 3360 | tf_op jit(solution)/shard_map/ppermute | solution.py:140
  9.5 0.2 collective-permute-done.refs_1_
  9.7 0.0 copy-done.1
  9.7 0.0 copy-done.2
  9.7 0.0 copy-done.3
  9.7 0.3 shard_map.87
  10.0 1.4 %collective-permute-start.5 = (f32[16,256]{1,0:T(8,128)S(1)}, f32[16,256]{1,0:T(8,128)S(1)}, u32[]{:S(2)}, u32[]{:S(2)}) collective-permute-start(f32[16,256]{1,0:T(8,128)S(1)} %get-tuple-element.9.refs_0_), channel_id=1, source_target_pairs={{0,4},{4,12},{8,0},{12,8},{1,5},{5,13},{9,1},{13,9},{2,6},{6,14},{... | collective-permute-start | bytes 49160 | tf_op jit(solution)/shard_map/ppermute | solution.py:140
  11.4 1.9 %collective-permute-start.4 = (f32[16,256]{1,0:T(8,128)S(1)}, f32[16,256]{1,0:T(8,128)S(1)}, u32[]{:S(2)}, u32[]{:S(2)}) collective-permute-start(f32[16,256]{1,0:T(8,128)S(1)} %get-tuple-element.9.refs_0_), channel_id=1, source_target_pairs={{0,12},{12,0},{4,8},{8,4},{1,13},{13,1},{5,9},{9,5},{2,14},{14,2},... | collective-permute-start | bytes 49160 | tf_op jit(solution)/shard_map/ppermute | solution.py:140
  13.3 1.6 %collective-permute-start.3 = (f32[16,256]{1,0:T(8,128)S(1)}, f32[16,256]{1,0:T(8,128)S(1)}, u32[]{:S(2)}, u32[]{:S(2)}) collective-permute-start(f32[16,256]{1,0:T(8,128)S(1)} %get-tuple-element.9.refs_0_), channel_id=1, source_target_pairs={{0,8},{4,0},{8,12},{12,4},{1,9},{5,1},{9,13},{13,5},{2,10},{6,2},{... | collective-permute-start | bytes 49160 | tf_op jit(solution)/shard_map/ppermute | solution.py:140
  14.9 0.4 %shard_map.88.refs_6_ = f32[4,128]{1,0:T(4,128)S(1)} custom-call(f32[2,8,104]{2,1,0:T(8,128)S(1)} %get-tuple-element.10.own_ref, bf16[2,2,104,256]{3,2,1,0:T(8,128)(2,1)S(1)} %bitcast.12, f32[8,256]{1,0:T(8,128)S(1)} %get-tuple-element.8.refs_6_.mask_ref.refs_5_), custom_call_target="tpu_custom_call" | custom-call | tf_op jit(solution)/shard_map/pallas_call | solution.py:408
  15.2 0.0 collective-permute-done.5.refs_3_
  15.2 1.7 %collective-permute-done.4.refs_2_ = f32[16,256]{1,0:T(8,128)S(1)} collective-permute-done((f32[16,256]{1,0:T(8,128)S(1)}, f32[16,256]{1,0:T(8,128)S(1)}, u32[]{:S(2)}, u32[]{:S(2)}) %collective-permute-start.4) | collective-permute-done | bytes 16416 | tf_op jit(solution)/shard_map/ppermute | solution.py:140
  16.9 0.2 collective-permute-done.3.refs_1_
  17.1 0.0 copy-done
  17.1 0.0 copy-done.4
  17.1 0.8 %shard_map.89 = bf16[8,16,768]{2,1,0:T(8,128)(2,1)S(1)} custom-call(f32[16,256]{1,0:T(8,128)S(1)} %get-tuple-element.9.refs_0_, f32[16,256]{1,0:T(8,128)S(1)} %collective-permute-done.3.refs_1_, f32[16,256]{1,0:T(8,128)S(1)} %collective-permute-done.4.refs_2_, f32[16,256]{1,0:T(8,128)S(1)} %collective-permute-done.5.refs_3_, f32[4,256]{1,0:T(4,128)S(1)} %bitcast.19, ...), custom_call_target="tpu_custom_call" | custom-call | tf_op jit(solution)/shard_map/pallas_call | solution.py:414
  17.9 10.0 %all_to_all.5.blocks_ref = bf16[8,16,768]{2,1,0:T(8,128)(2,1)S(1)} all-to-all(bf16[8,16,768]{2,1,0:T(8,128)(2,1)S(1)} %shard_map.89), channel_id=1, replica_groups={{10,14,12,8,6,4,2,0},{11,15,13,9,7,5,3,1},{26,30,28,24,22,20,18,16},{27..., dimensions={0} | all-to-all | bytes 393216 | tf_op jit(solution)/shard_map/all_to_all | solution.py:421
  27.8 2.2 %shard_map.90 = (f32[2,4,208]{2,1,0:T(4,128)}, f32[1,1]{1,0:T(1,128)}) custom-call(bf16[8,16,768]{2,1,0:T(8,128)(2,1)S(1)} %all_to_all.5.blocks_ref, f32[16,256]{1,0:T(8,128)S(1)} %get-tuple-element.9.refs_0_, f32[16,256]{1,0:T(8,128)S(1)} %collective-permute-done.3.refs_1_, f32[16,256]{1,0:T(8,128)S(1)} %collective-permute-done.4.refs_2_, ...), custom_call_target="tpu_custom_call" | custom-call | tf_op jit(solution)/shard_map/pallas_call | solution.py:424
Async XLA Ops:
  0.6 9.0 %copy-start.1 = (bf16[1,2,2,104,256]{4,3,2,1,0:T(8,128)(2,1)S(1)}, bf16[1,2,2,104,256]{4,3,2,1,0:T(8,128)(2,1)}, u32[]{:S(2)}) copy-start(bf16[1,2,2,104,256]{4,3,2,1,0:T(8,128)(2,1)} %param.10) | copy-start | bytes 638980
  0.6 9.0 %copy-start.2 = (f32[1,2,4,208]{3,2,1,0:T(4,128)S(1)}, f32[1,2,4,208]{3,2,1,0:T(4,128)}, u32[]{:S(2)}) copy-start(f32[1,2,4,208]{3,2,1,0:T(4,128)} %param.9) | copy-start | bytes 19972
  0.7 9.0 %copy-start.3 = (bf16[1,1,1,8,208]{4,3,2,1,0:T(8,128)(2,1)S(1)}, bf16[1,1,1,8,208]{4,3,2,1,0:T(8,128)(2,1)}, u32[]{:S(2)}) copy-start(bf16[1,1,1,8,208]{4,3,2,1,0:T(8,128)(2,1)} %param.7) | copy-start | bytes 9988
  0.7 16.4 %copy-start = (bf16[1,2,2,676,256]{4,2,3,1,0:T(2,128)(2,1)S(1)}, bf16[1,2,2,676,256]{4,2,3,1,0:T(2,128)(2,1)}, u32[]{:S(2)}) copy-start(bf16[1,2,2,676,256]{4,2,3,1,0:T(2,128)(2,1)} %param.11) | copy-start | bytes 4153348
  0.7 16.4 %copy-start.4 = (f32[1,1,4,256]{3,2,1,0:T(4,128)S(1)}, f32[1,1,4,256]{3,2,1,0:T(4,128)}, u32[]{:S(2)}) copy-start(f32[1,1,4,256]{3,2,1,0:T(4,128)} %param.8) | copy-start | bytes 12292
  0.7 7.7 %collective-permute-start.2 = (bf16[8,208]{1,0:T(8,128)(2,1)}, bf16[8,208]{1,0:T(8,128)(2,1)S(1)}, u32[]{:S(2)}, u32[]{:S(2)}) collective-permute-start(bf16[8,208]{1,0:T(8,128)(2,1)} %bitcast.15), channel_id=1, source_target_pairs={{12,0},{8,4},{4,12},{0,8},{13,1},{9,5},{5,13},{1,9},{14,2},{10,6},... | collective-permute-start | bytes 9992 | tf_op jit(solution)/shard_map/ppermute | solution.py:140
  4.8 4.7 %collective-permute-start.1 = (bf16[8,208]{1,0:T(8,128)(2,1)}, bf16[8,208]{1,0:T(8,128)(2,1)S(1)}, u32[]{:S(2)}, u32[]{:S(2)}) collective-permute-start(bf16[8,208]{1,0:T(8,128)(2,1)} %bitcast.16), channel_id=1, source_target_pairs={{12,4},{8,0},{0,12},{4,8},{13,5},{9,1},{1,13},{5,9},{14,6},{10,2},... | collective-permute-start | bytes 9992 | tf_op jit(solution)/shard_map/ppermute | solution.py:140
  5.8 3.8 %collective-permute-start = (bf16[8,208]{1,0:T(8,128)(2,1)}, bf16[8,208]{1,0:T(8,128)(2,1)S(1)}, u32[]{:S(2)}, u32[]{:S(2)}) collective-permute-start(bf16[8,208]{1,0:T(8,128)(2,1)} %bitcast.17), channel_id=1, source_target_pairs={{4,0},{12,8},{8,12},{0,4},{5,1},{13,9},{9,13},{1,5},{6,2},{14,10},... | collective-permute-start | bytes 9992 | tf_op jit(solution)/shard_map/ppermute | solution.py:140
  6.4 0.7 %copy-start.5 = (s32[2,8]{1,0:T(2,128)S(1)}, s32[2,8]{1,0:T(2,128)}, u32[]{:S(2)}) copy-start(s32[2,8]{1,0:T(2,128)} %map_ref.1) | copy-start | bytes 196
  7.0 0.7 %copy-start.6 = (s32[2]{0:T(128)S(1)}, s32[2]{0:T(128)}, u32[]{:S(2)}) copy-start(s32[2]{0:T(128)} %count_ref.1) | copy-start | bytes 28
  10.0 5.3 %collective-permute-start.5 = (f32[16,256]{1,0:T(8,128)S(1)}, f32[16,256]{1,0:T(8,128)S(1)}, u32[]{:S(2)}, u32[]{:S(2)}) collective-permute-start(f32[16,256]{1,0:T(8,128)S(1)} %get-tuple-element.9.refs_0_), channel_id=1, source_target_pairs={{0,4},{4,12},{8,0},{12,8},{1,5},{5,13},{9,1},{13,9},{2,6},{6,14},{... | collective-permute-start | bytes 49160 | tf_op jit(solution)/shard_map/ppermute | solution.py:140
  11.4 5.5 %collective-permute-start.4 = (f32[16,256]{1,0:T(8,128)S(1)}, f32[16,256]{1,0:T(8,128)S(1)}, u32[]{:S(2)}, u32[]{:S(2)}) collective-permute-start(f32[16,256]{1,0:T(8,128)S(1)} %get-tuple-element.9.refs_0_), channel_id=1, source_target_pairs={{0,12},{12,0},{4,8},{8,4},{1,13},{13,1},{5,9},{9,5},{2,14},{14,2},... | collective-permute-start | bytes 49160 | tf_op jit(solution)/shard_map/ppermute | solution.py:140
  13.3 3.8 %collective-permute-start.3 = (f32[16,256]{1,0:T(8,128)S(1)}, f32[16,256]{1,0:T(8,128)S(1)}, u32[]{:S(2)}, u32[]{:S(2)}) collective-permute-start(f32[16,256]{1,0:T(8,128)S(1)} %get-tuple-element.9.refs_0_), channel_id=1, source_target_pairs={{0,8},{4,0},{8,12},{12,4},{1,9},{5,1},{9,13},{13,5},{2,10},{6,2},{... | collective-permute-start | bytes 49160 | tf_op jit(solution)/shard_map/ppermute | solution.py:140

commit v14 on v13

--- a/solution.py
+++ b/solution.py
@@ -152,9 +152,9 @@
 
 
 def operator_group(ka_count, pb_count):
+    size = pb_count * ka_count
     first = (pb_count - 1) * ka_count + ka_count // 2
-    rest = [at for at in range(pb_count * ka_count) if at != first]
-    return [first] + sorted(rest, key=lambda at: -(at // ka_count + at % ka_count))
+    return [(first - at) % size for at in range(size)]
 
 
 def prepare_kernel(ka_count, pb_count, walkers, map_ref, count_ref, mask_ref, picks_ref):

time: 30.2 us -> 29.8 us (0.987)
  blocking collectives: 9.98 us -> 9.61 us
    all_to_all x1, blocking collectives: 9.98 us -> 9.61 us  [direct(): lax.all_to_all(blocks, ('pb', 'ka'), 0, 0, axis_index_groups=[group], til...]
where the time goes in v14:
time: 29.8 us; the launch traced here: 29.6 us
  starting transfers between devices  10.6 us (36%)
  blocking collectives  9.61 us (32%)
  Pallas kernels  4.2 us (14%)
  waiting for transfers between devices  3.17 us (11%)
  local copies, waits for them, and re-layouts  1.35 us (5%)
  between operations  0.71 us (2%)
    ppermute x6, starting transfers between devices, exchange(): return [array] + [lax.ppermute(array, axis, pairs) for pairs in rounds]  10.6 us
    all_to_all x1, blocking collectives, direct(): lax.all_to_all(blocks, ('pb', 'ka'), 0, 0, axis_index_groups=[group], til...  9.61 us
    ppermute x6, waiting for transfers between devices, exchange(): return [array] + [lax.ppermute(array, axis, pairs) for pairs in rounds]  3.17 us
    pallas_call x1, Pallas kernels, direct(): call(functools.partial(taylor_kernel, pb_count, float(pb_count * chol_col...  2.15 us
    unnamed x14, local copies, waits for them, and re-layouts  1.35 us
    pallas_call x1, Pallas kernels, direct(): call(functools.partial(operator_kernel, k_local), shape((ka_count * pb_co...  0.76 us
    pallas_call x1, Pallas kernels, direct(): call(functools.partial(prepare_kernel, ka_count, pb_count, walkers), (sha...  0.66 us
  transfers between devices with their start and end apart: 6, of which 4 were waited for; matrix products, arithmetic and copies ran while one was open for 0% of the time, Pallas kernels for 3%

profile of v14, /device:TPU:0, one launch (start us, length us, event | category | flops | bytes accessed | tf_op | source)
XLA Modules:
  0.0 29.6 jit_solution(12424967131335581984)
XLA Ops:
  0.6 0.0 copy-start.1
  0.6 0.0 copy-start.2
  0.7 0.0 copy-start.3
  0.7 0.0 copy-start
  0.7 0.0 copy-start.4
  0.7 4.1 %collective-permute-start.2 = (bf16[8,208]{1,0:T(8,128)(2,1)}, bf16[8,208]{1,0:T(8,128)(2,1)S(1)}, u32[]{:S(2)}, u32[]{:S(2)}) collective-permute-start(bf16[8,208]{1,0:T(8,128)(2,1)} %bitcast.15), channel_id=1, source_target_pairs={{12,0},{8,4},{4,12},{0,8},{13,1},{9,5},{5,13},{1,9},{14,2},{10,6},... | collective-permute-start | bytes 9992 | tf_op jit(solution)/shard_map/ppermute | solution.py:140
  4.8 1.1 %collective-permute-start.1 = (bf16[8,208]{1,0:T(8,128)(2,1)}, bf16[8,208]{1,0:T(8,128)(2,1)S(1)}, u32[]{:S(2)}, u32[]{:S(2)}) collective-permute-start(bf16[8,208]{1,0:T(8,128)(2,1)} %bitcast.16), channel_id=1, source_target_pairs={{12,4},{8,0},{0,12},{4,8},{13,5},{9,1},{1,13},{5,9},{14,6},{10,2},... | collective-permute-start | bytes 9992 | tf_op jit(solution)/shard_map/ppermute | solution.py:140
  5.8 0.5 %collective-permute-start = (bf16[8,208]{1,0:T(8,128)(2,1)}, bf16[8,208]{1,0:T(8,128)(2,1)S(1)}, u32[]{:S(2)}, u32[]{:S(2)}) collective-permute-start(bf16[8,208]{1,0:T(8,128)(2,1)} %bitcast.17), channel_id=1, source_target_pairs={{4,0},{12,8},{8,12},{0,4},{5,1},{13,9},{9,13},{1,5},{6,2},{14,10},... | collective-permute-start | bytes 9992 | tf_op jit(solution)/shard_map/ppermute | solution.py:140
  6.4 0.0 copy-start.5
  6.4 0.7 %copy-done.5 = s32[2,8]{1,0:T(2,128)S(1)} copy-done((s32[2,8]{1,0:T(2,128)S(1)}, s32[2,8]{1,0:T(2,128)}, u32[]{:S(2)}) %copy-start.5) | copy-done | bytes 88
  7.0 0.0 copy-start.6
  7.0 0.7 %copy-done.6 = s32[2]{0:T(128)S(1)} copy-done((s32[2]{0:T(128)S(1)}, s32[2]{0:T(128)}, u32[]{:S(2)}) %copy-start.6) | copy-done | bytes 32
  7.7 0.7 %shard_map.86 = (f32[8,256]{1,0:T(8,128)S(1)}, bf16[128,256]{1,0:T(8,128)(2,1)S(1)}) custom-call(s32[2,8]{1,0:T(2,128)S(1)} %copy-done.5, s32[2]{0:T(128)S(1)} %copy-done.6), custom_call_target="tpu_custom_call" | custom-call | flops 1000000000 | tf_op jit(solution)/shard_map/pallas_call | solution.py:392
  8.4 0.0 collective-permute-done.2.refs_3_
  8.4 1.1 %collective-permute-done.1.refs_2_ = bf16[8,208]{1,0:T(8,128)(2,1)S(1)} collective-permute-done((bf16[8,208]{1,0:T(8,128)(2,1)}, bf16[8,208]{1,0:T(8,128)(2,1)S(1)}, u32[]{:S(2)}, u32[]{:S(2)}) %collective-permute-start.1) | collective-permute-done | bytes 3360 | tf_op jit(solution)/shard_map/ppermute | solution.py:140
  9.5 0.2 collective-permute-done.refs_1_
  9.7 0.0 copy-done.1
  9.7 0.0 copy-done.2
  9.7 0.0 copy-done.3
  9.7 0.3 shard_map.87
  10.0 1.4 %collective-permute-start.5 = (f32[16,256]{1,0:T(8,128)S(1)}, f32[16,256]{1,0:T(8,128)S(1)}, u32[]{:S(2)}, u32[]{:S(2)}) collective-permute-start(f32[16,256]{1,0:T(8,128)S(1)} %get-tuple-element.9.refs_0_), channel_id=1, source_target_pairs={{0,4},{4,12},{8,0},{12,8},{1,5},{5,13},{9,1},{13,9},{2,6},{6,14},{... | collective-permute-start | bytes 49160 | tf_op jit(solution)/shard_map/ppermute | solution.py:140
  11.4 1.9 %collective-permute-start.4 = (f32[16,256]{1,0:T(8,128)S(1)}, f32[16,256]{1,0:T(8,128)S(1)}, u32[]{:S(2)}, u32[]{:S(2)}) collective-permute-start(f32[16,256]{1,0:T(8,128)S(1)} %get-tuple-element.9.refs_0_), channel_id=1, source_target_pairs={{0,12},{12,0},{4,8},{8,4},{1,13},{13,1},{5,9},{9,5},{2,14},{14,2},... | collective-permute-start | bytes 49160 | tf_op jit(solution)/shard_map/ppermute | solution.py:140
  13.3 1.6 %collective-permute-start.3 = (f32[16,256]{1,0:T(8,128)S(1)}, f32[16,256]{1,0:T(8,128)S(1)}, u32[]{:S(2)}, u32[]{:S(2)}) collective-permute-start(f32[16,256]{1,0:T(8,128)S(1)} %get-tuple-element.9.refs_0_), channel_id=1, source_target_pairs={{0,8},{4,0},{8,12},{12,4},{1,9},{5,1},{9,13},{13,5},{2,10},{6,2},{... | collective-permute-start | bytes 49160 | tf_op jit(solution)/shard_map/ppermute | solution.py:140
  14.9 0.4 %shard_map.88.refs_6_ = f32[4,128]{1,0:T(4,128)S(1)} custom-call(f32[2,8,104]{2,1,0:T(8,128)S(1)} %get-tuple-element.10.own_ref, bf16[2,2,104,256]{3,2,1,0:T(8,128)(2,1)S(1)} %bitcast.12, f32[8,256]{1,0:T(8,128)S(1)} %get-tuple-element.8.refs_6_.mask_ref.refs_5_), custom_call_target="tpu_custom_call" | custom-call | tf_op jit(solution)/shard_map/pallas_call | solution.py:408
  15.2 0.0 collective-permute-done.5.refs_3_
  15.2 1.7 %collective-permute-done.4.refs_2_ = f32[16,256]{1,0:T(8,128)S(1)} collective-permute-done((f32[16,256]{1,0:T(8,128)S(1)}, f32[16,256]{1,0:T(8,128)S(1)}, u32[]{:S(2)}, u32[]{:S(2)}) %collective-permute-start.4) | collective-permute-done | bytes 16416 | tf_op jit(solution)/shard_map/ppermute | solution.py:140
  16.9 0.2 collective-permute-done.3.refs_1_
  17.1 0.0 copy-done
  17.1 0.0 copy-done.4
  17.1 0.8 %shard_map.89 = bf16[8,16,768]{2,1,0:T(8,128)(2,1)S(1)} custom-call(f32[16,256]{1,0:T(8,128)S(1)} %get-tuple-element.9.refs_0_, f32[16,256]{1,0:T(8,128)S(1)} %collective-permute-done.3.refs_1_, f32[16,256]{1,0:T(8,128)S(1)} %collective-permute-done.4.refs_2_, f32[16,256]{1,0:T(8,128)S(1)} %collective-permute-done.5.refs_3_, f32[4,256]{1,0:T(4,128)S(1)} %bitcast.19, ...), custom_call_target="tpu_custom_call" | custom-call | tf_op jit(solution)/shard_map/pallas_call | solution.py:414
  17.9 9.6 %all_to_all.5.blocks_ref = bf16[8,16,768]{2,1,0:T(8,128)(2,1)S(1)} all-to-all(bf16[8,16,768]{2,1,0:T(8,128)(2,1)S(1)} %shard_map.89), channel_id=1, replica_groups={{10,6,2,12,8,4,0,14},{11,7,3,13,9,5,1,15},{26,22,18,28,24,20,16,30},{27..., dimensions={0} | all-to-all | bytes 393216 | tf_op jit(solution)/shard_map/all_to_all | solution.py:421
  27.5 2.1 %shard_map.90 = (f32[2,4,208]{2,1,0:T(4,128)}, f32[1,1]{1,0:T(1,128)}) custom-call(bf16[8,16,768]{2,1,0:T(8,128)(2,1)S(1)} %all_to_all.5.blocks_ref, f32[16,256]{1,0:T(8,128)S(1)} %get-tuple-element.9.refs_0_, f32[16,256]{1,0:T(8,128)S(1)} %collective-permute-done.3.refs_1_, f32[16,256]{1,0:T(8,128)S(1)} %collective-permute-done.4.refs_2_, ...), custom_call_target="tpu_custom_call" | custom-call | tf_op jit(solution)/shard_map/pallas_call | solution.py:424
Async XLA Ops:
  0.6 9.0 %copy-start.1 = (bf16[1,2,2,104,256]{4,3,2,1,0:T(8,128)(2,1)S(1)}, bf16[1,2,2,104,256]{4,3,2,1,0:T(8,128)(2,1)}, u32[]{:S(2)}) copy-start(bf16[1,2,2,104,256]{4,3,2,1,0:T(8,128)(2,1)} %param.10) | copy-start | bytes 638980
  0.6 9.0 %copy-start.2 = (f32[1,2,4,208]{3,2,1,0:T(4,128)S(1)}, f32[1,2,4,208]{3,2,1,0:T(4,128)}, u32[]{:S(2)}) copy-start(f32[1,2,4,208]{3,2,1,0:T(4,128)} %param.9) | copy-start | bytes 19972
  0.7 9.0 %copy-start.3 = (bf16[1,1,1,8,208]{4,3,2,1,0:T(8,128)(2,1)S(1)}, bf16[1,1,1,8,208]{4,3,2,1,0:T(8,128)(2,1)}, u32[]{:S(2)}) copy-start(bf16[1,1,1,8,208]{4,3,2,1,0:T(8,128)(2,1)} %param.7) | copy-start | bytes 9988
  0.7 16.4 %copy-start = (bf16[1,2,2,676,256]{4,2,3,1,0:T(2,128)(2,1)S(1)}, bf16[1,2,2,676,256]{4,2,3,1,0:T(2,128)(2,1)}, u32[]{:S(2)}) copy-start(bf16[1,2,2,676,256]{4,2,3,1,0:T(2,128)(2,1)} %param.11) | copy-start | bytes 4153348
  0.7 16.4 %copy-start.4 = (f32[1,1,4,256]{3,2,1,0:T(4,128)S(1)}, f32[1,1,4,256]{3,2,1,0:T(4,128)}, u32[]{:S(2)}) copy-start(f32[1,1,4,256]{3,2,1,0:T(4,128)} %param.8) | copy-start | bytes 12292
  0.7 7.7 %collective-permute-start.2 = (bf16[8,208]{1,0:T(8,128)(2,1)}, bf16[8,208]{1,0:T(8,128)(2,1)S(1)}, u32[]{:S(2)}, u32[]{:S(2)}) collective-permute-start(bf16[8,208]{1,0:T(8,128)(2,1)} %bitcast.15), channel_id=1, source_target_pairs={{12,0},{8,4},{4,12},{0,8},{13,1},{9,5},{5,13},{1,9},{14,2},{10,6},... | collective-permute-start | bytes 9992 | tf_op jit(solution)/shard_map/ppermute | solution.py:140
  4.8 4.7 %collective-permute-start.1 = (bf16[8,208]{1,0:T(8,128)(2,1)}, bf16[8,208]{1,0:T(8,128)(2,1)S(1)}, u32[]{:S(2)}, u32[]{:S(2)}) collective-permute-start(bf16[8,208]{1,0:T(8,128)(2,1)} %bitcast.16), channel_id=1, source_target_pairs={{12,4},{8,0},{0,12},{4,8},{13,5},{9,1},{1,13},{5,9},{14,6},{10,2},... | collective-permute-start | bytes 9992 | tf_op jit(solution)/shard_map/ppermute | solution.py:140
  5.8 3.8 %collective-permute-start = (bf16[8,208]{1,0:T(8,128)(2,1)}, bf16[8,208]{1,0:T(8,128)(2,1)S(1)}, u32[]{:S(2)}, u32[]{:S(2)}) collective-permute-start(bf16[8,208]{1,0:T(8,128)(2,1)} %bitcast.17), channel_id=1, source_target_pairs={{4,0},{12,8},{8,12},{0,4},{5,1},{13,9},{9,13},{1,5},{6,2},{14,10},... | collective-permute-start | bytes 9992 | tf_op jit(solution)/shard_map/ppermute | solution.py:140
  6.4 0.7 %copy-start.5 = (s32[2,8]{1,0:T(2,128)S(1)}, s32[2,8]{1,0:T(2,128)}, u32[]{:S(2)}) copy-start(s32[2,8]{1,0:T(2,128)} %map_ref.1) | copy-start | bytes 196
  7.0 0.7 %copy-start.6 = (s32[2]{0:T(128)S(1)}, s32[2]{0:T(128)}, u32[]{:S(2)}) copy-start(s32[2]{0:T(128)} %count_ref.1) | copy-start | bytes 28
  10.0 5.3 %collective-permute-start.5 = (f32[16,256]{1,0:T(8,128)S(1)}, f32[16,256]{1,0:T(8,128)S(1)}, u32[]{:S(2)}, u32[]{:S(2)}) collective-permute-start(f32[16,256]{1,0:T(8,128)S(1)} %get-tuple-element.9.refs_0_), channel_id=1, source_target_pairs={{0,4},{4,12},{8,0},{12,8},{1,5},{5,13},{9,1},{13,9},{2,6},{6,14},{... | collective-permute-start | bytes 49160 | tf_op jit(solution)/shard_map/ppermute | solution.py:140
  11.4 5.5 %collective-permute-start.4 = (f32[16,256]{1,0:T(8,128)S(1)}, f32[16,256]{1,0:T(8,128)S(1)}, u32[]{:S(2)}, u32[]{:S(2)}) collective-permute-start(f32[16,256]{1,0:T(8,128)S(1)} %get-tuple-element.9.refs_0_), channel_id=1, source_target_pairs={{0,12},{12,0},{4,8},{8,4},{1,13},{13,1},{5,9},{9,5},{2,14},{14,2},... | collective-permute-start | bytes 49160 | tf_op jit(solution)/shard_map/ppermute | solution.py:140
  13.3 3.8 %collective-permute-start.3 = (f32[16,256]{1,0:T(8,128)S(1)}, f32[16,256]{1,0:T(8,128)S(1)}, u32[]{:S(2)}, u32[]{:S(2)}) collective-permute-start(f32[16,256]{1,0:T(8,128)S(1)} %get-tuple-element.9.refs_0_), channel_id=1, source_target_pairs={{0,8},{4,0},{8,12},{12,4},{1,9},{5,1},{9,13},{13,5},{2,10},{6,2},{... | collective-permute-start | bytes 49160 | tf_op jit(solution)/shard_map/ppermute | solution.py:140

commit v15 on v10

--- a/solution.py
+++ b/solution.py
@@ -157,13 +157,17 @@
     return [first] + rest[::-1]
 
 
-def prepare_kernel(ka_count, pb_count, walkers, map_ref, count_ref, mask_ref, picks_ref):
+def prepare_kernel(ka_count, pb_count, walkers, map_ref, count_ref, mask_ref, picks_ref, own_ref):
     kept = count_ref[lax.axis_index("pb")]
     column = lax.broadcasted_iota(jnp.int32, mask_ref.shape, 1)
     mask_ref[...] = jnp.where(column < kept, 1.0, 0.0)
     kpoints = map_ref.shape[1]
     k_local = kpoints // ka_count
     span = k_local * walkers
+
+    def place(k):
+        return k // k_local * (2 * span) + lax.rem(k, k_local) * walkers
+
     lane = lax.broadcasted_iota(jnp.int32, (1, LANES), 1)
     lane_q = lane // (LANES // pb_count)
     lane_ka = lax.rem(lane, LANES // pb_count) // (2 * span)
@@ -172,10 +176,17 @@
     wanted = jnp.zeros((1, LANES), jnp.int32)
     for q in range(pb_count):
         for k in range(kpoints):
-            source = map_ref[q, k]
-            source = source // k_local * (2 * span) + lax.rem(source, k_local) * walkers
-            wanted = jnp.where((lane_q == q) & (lane_k == k), source, wanted)
+            wanted = jnp.where((lane_q == q) & (lane_k == k), place(map_ref[q, k]), wanted)
     wanted = wanted + lax.rem(lane, walkers)
+    group = 2 * span
+    own_q = lax.rem(lane, pb_count * group) // group
+    own_k = lax.rem(lane, span) // walkers
+    own = jnp.zeros((1, LANES), jnp.int32)
+    first = lax.axis_index("ka") * k_local
+    for q in range(pb_count):
+        for k in range(k_local):
+            own = jnp.where((own_q == q) & (own_k == k), place(map_ref[q, first + k]), own)
+    own_ref[...] = jnp.broadcast_to(own + lax.rem(lane, walkers), own_ref.shape)
     row = lax.broadcasted_iota(jnp.int32, (LANES, LANES), 0)
     real = jnp.where(row == wanted, 1.0, 0.0)
     imag = jnp.where(row == wanted + span, jnp.where(lane_part == 0, 1.0, -1.0), 0.0)
@@ -207,7 +218,9 @@
     bias_ref[rows : rows + count, width:] = jnp.zeros((count, bias_ref.shape[1] - width), F32)
 
 
-def exchange_kernel(k_local, own_ref, chol_ref, mask_ref, out_ref):
+def exchange_kernel(
+    k_local, pb_count, own_ref, chol_ref, mask_ref, lanes_ref, out_ref, fold_ref, picks_ref
+):
     walkers, width, columns = own_ref.shape[1] // 2, own_ref.shape[2], chol_ref.shape[3]
     rows = 2 * walkers
     lane = lax.broadcasted_iota(jnp.int32, (rows, LANES), 1)
@@ -236,10 +249,26 @@
     total = total[:walkers] + total[walkers:]
     summed = 0.5 * jnp.sum(total, axis=1, keepdims=True)
     out_ref[...] = jnp.broadcast_to(summed, out_ref.shape)
+    span = k_local * walkers
+    group = 2 * span
+    lane = lax.broadcasted_iota(jnp.int32, (1, LANES), 1)
+    source = lax.rem(lane, pb_count * group) // group * (LANES // pb_count) + lax.rem(lane, group)
+    source = source + lax.axis_index("ka") * group
+    row = lax.broadcasted_iota(jnp.int32, (LANES, LANES), 0)
+    fold_ref[...] = jnp.where(row == source, 1.0, 0.0).astype(BF16)
+    wanted = lanes_ref[:1]
+    sign = jnp.where(lax.rem(lane, group) < span, 1.0, -1.0)
+    for i in range(NOCC):
+        inside = lane // (LANES // NOCC) == i
+        real = jnp.where(inside & (row == wanted), 1.0, 0.0)
+        imag = jnp.where(inside & (row == wanted + span), sign, 0.0)
+        both = jnp.concatenate([real, imag], axis=1)
+        picks_ref[i * LANES : (i + 1) * LANES] = both.astype(BF16)
 
 
 def operator_kernel(k_local, *refs):
-    *parts, fields_ref, mask_ref, exchange_ref, chol_ref, out_ref, products, turned_ref = refs
+    *parts, fields_ref, mask_ref, exchange_ref, chol_ref, picks_ref = refs[:-5]
+    out_ref, first_ref, products, turned_ref, term = refs[-5:]
     walkers, columns = fields_ref.shape
     bias = parts[0][: 2 * walkers]
     for part in parts[1:]:
@@ -255,6 +284,16 @@
     shift_re = (fields_ref[...] - BIAS_STEP * bias_re) * kept
     shift_im = -BIAS_STEP * bias_im * kept
     span = k_local * walkers
+    pair = NOCC * M
+    term[...] = jnp.zeros_like(term)
+    for source, part in zip(origins("ka", BIAS_ROUNDS), parts):
+        start = pl.multiple_of(source * (2 * span), 2 * span)
+        window = part[2 * walkers :]
+        term[pl.ds(start, span), :pair] = window[:, :pair]
+        term[pl.ds(start + span, span), :pair] = window[:, pair : 2 * pair]
+    first_ref[...] = jnp.dot(
+        term[...].T.astype(BF16), picks_ref[...], preferred_element_type=F32
+    )
     weights = []
     for k in range(k_local):
         before, after = k * walkers, span - (k + 1) * walkers
@@ -298,26 +337,21 @@
             out_ref[copy, :, at : at + LANES] = block.astype(BF16)
 
 
-def taylor_kernel(pb_count, normalizer, blocks_ref, *refs):
-    *windows, picks_ref, orbitals_ref, out_ref, energy_ref, turned, picked, term = refs
+def taylor_kernel(
+    pb_count, normalizer, blocks_ref, first_ref, picks_ref, fold_ref, own_picks_ref, orbitals_ref,
+    out_ref, energy_ref, turned, folded, picked, term, kept,
+):
     pairs = M * M
-    pair = NOCC * M
     k_local, walkers, _ = out_ref.shape
     span = k_local * walkers
     ka_pos = lax.axis_index("ka")
-    term[...] = jnp.zeros_like(term)
-    for source, window_ref in zip(origins("ka", BIAS_ROUNDS), windows):
-        start = pl.multiple_of(source * (2 * span), 2 * span)
-        window = window_ref[window_ref.shape[0] - span :]
-        term[pl.ds(start, span), :pair] = window[:, :pair]
-        term[pl.ds(start + span, span), :pair] = window[:, pair : 2 * pair]
-    picked[...] = jnp.dot(term[...].T.astype(BF16), picks_ref[...], preferred_element_type=F32)
     count, _, width = blocks_ref.shape
     group = operator_group(count // pb_count, pb_count)
     places = [group.index(n) for n in range(count)]
     for at in range(0, width, LANES):
-        tile = jnp.concatenate([blocks_ref[n, :, at : at + LANES] for n in places], axis=0)
-        turned[at : at + LANES] = tile.T.astype(F32)
+        tile = jnp.concatenate([blocks_ref[n, :, at : at + LANES] for n in places], axis=0).T
+        turned[at : at + LANES] = tile.astype(F32)
+        folded[at : at + LANES] = jnp.dot(tile, fold_ref[...], preferred_element_type=F32)
     shares = turned[pairs : pairs + 3]
     lane = lax.broadcasted_iota(jnp.int32, shares.shape, 1)
     shares = jnp.where(lax.rem(lane, 2 * span) == ka_pos, shares, 0.0)
@@ -325,32 +359,57 @@
     energy_ref[...] = shares / normalizer
     lane = lax.broadcasted_iota(jnp.int32, (M, LANES), 1)
     imaginary = lax.rem(lane, 2 * span) >= span
-    sums = [jnp.zeros((M, LANES), F32) for _ in range(NOCC)]
-    for degree in range(1, TAYLOR + 1):
-        stride = M if degree == 1 else ROWS
+
+    def joined(straight, crossed):
+        up, down = pltpu.roll(crossed, span, 1), pltpu.roll(crossed, LANES - span, 1)
+        return straight + jnp.where(imaginary, up, down)
+
+    sums = [None] * NOCC
+    for degree in range(1, TAYLOR):
+        source, stride = (first_ref, M) if degree == 1 else (picked, ROWS)
         straight = [jnp.zeros((M, LANES), F32) for _ in range(NOCC)]
         crossed = [jnp.zeros((M, LANES), F32) for _ in range(NOCC)]
         for c in range(M):
             column = turned[pl.ds(c, M, stride=M), :]
             for i in range(NOCC):
                 at = i * stride + c
-                straight[i] += column * picked[at : at + 1, :LANES]
-                crossed[i] += column * picked[at : at + 1, LANES:]
+                straight[i] += column * source[at : at + 1, :LANES]
+                crossed[i] += column * source[at : at + 1, LANES:]
         for i in range(NOCC):
-            other = jnp.where(
-                imaginary, pltpu.roll(crossed[i], span, 1), pltpu.roll(crossed[i], LANES - span, 1)
-            )
-            applied = straight[i] + other
+            applied = joined(straight[i], crossed[i])
             applied = applied + pltpu.roll(applied, LANES // pb_count, 1)
-            current = applied / degree
-            sums[i] = sums[i] + current
-            term[i * ROWS : i * ROWS + M] = current if degree < TAYLOR else sums[i]
-        if degree < TAYLOR:
+            current = applied * (1.0 / degree)
+            sums[i] = current if degree == 1 else sums[i] + current
+            at = i * ROWS
+            term[at : at + M] = current
+            if degree == 1:
+                term[at + M : at + ROWS] = jnp.zeros((ROWS - M, LANES), F32)
+        if degree < TAYLOR - 1:
             picked[...] = jnp.dot(
                 term[...].astype(BF16), picks_ref[...], preferred_element_type=F32
             )
-    turned[:LANES] = term[...].T
-    both = turned[pl.ds(pl.multiple_of(ka_pos * (2 * span), 2 * span), 2 * span), :]
+    wide = jnp.concatenate([term[i * ROWS : (i + 1) * ROWS] for i in range(NOCC)], axis=1)
+    picked[:ROWS] = jnp.dot(wide.astype(BF16), own_picks_ref[...], preferred_element_type=F32)
+    for i in range(NOCC):
+        kept[i * ROWS : i * ROWS + M] = sums[i]
+        kept[i * ROWS + M : (i + 1) * ROWS] = jnp.zeros((ROWS - M, LANES), F32)
+    turned[:LANES] = kept[...].T
+    sums = turned[pl.ds(pl.multiple_of(ka_pos * (2 * span), 2 * span), 2 * span), :]
+    straight = [jnp.zeros((M, LANES), F32) for _ in range(2)]
+    crossed = [jnp.zeros((M, LANES), F32) for _ in range(2)]
+    for c in range(M):
+        column = folded[pl.ds(c, M, stride=M), :]
+        straight[c % 2] += column * picked[c : c + 1, :LANES]
+        crossed[c % 2] += column * picked[c : c + 1, LANES:]
+    applied = joined(straight[0] + straight[1], crossed[0] + crossed[1])
+    applied = (applied + pltpu.roll(applied, LANES - 2 * span, 1)) * (1.0 / TAYLOR)
+    kept[:M] = applied
+    kept[M:ROWS] = jnp.zeros((ROWS - M, LANES), F32)
+    last = kept[:ROWS].T
+    last = jnp.concatenate(
+        [last[i * ROWS : i * ROWS + 2 * span] for i in range(NOCC)], axis=1
+    )
+    both = sums + last
     both = jnp.concatenate([both[:, i * ROWS : i * ROWS + M] for i in range(NOCC)], axis=1)
     both = jnp.concatenate([both[:span], both[span:]], axis=1)
     for k in range(k_local):
@@ -389,9 +448,13 @@
     ).reshape(k_local, M * M * tiles * 2, LANES)
     own_fields = fields.reshape(walkers, chol_cols)
     own_orbitals = orbitals.reshape(k_local, walkers, 2 * pair_width)
-    mask, picks = call(
+    mask, picks, own_lanes = call(
         functools.partial(prepare_kernel, ka_count, pb_count, walkers),
-        (shape((2 * walkers, chol_cols), F32), shape((LANES, 2 * LANES), BF16)),
+        (
+            shape((2 * walkers, chol_cols), F32),
+            shape((LANES, 2 * LANES), BF16),
+            shape((2 * walkers, LANES), jnp.int32),
+        ),
         scalars=2,
         flops=10**9,
     )(kq_map, chol_count)
@@ -405,18 +468,29 @@
         operands=len(greens) + 3,
     )(*greens, half, own_orbitals, mask)
     parts = exchange(bias, "ka", BIAS_ROUNDS)
-    shares = call(
-        functools.partial(exchange_kernel, k_local),
-        shape((walkers, LANES), F32),
-        operands=3,
-    )(own, half, mask)
+    shares, fold, own_picks = call(
+        functools.partial(exchange_kernel, k_local, pb_count),
+        (
+            shape((walkers, LANES), F32),
+            shape((LANES, LANES), BF16),
+            shape((NOCC * LANES, 2 * LANES), BF16),
+        ),
+        operands=4,
+    )(own, half, mask, own_lanes)
     width = -(-(M * M + 3) // LANES) * LANES
-    blocks = call(
+    blocks, first = call(
         functools.partial(operator_kernel, k_local),
-        shape((ka_count * pb_count, 2 * span, width), BF16),
-        [pltpu.VMEM((2 * M * M * tiles, LANES), F32), pltpu.VMEM((width, LANES), F32)],
-        operands=len(parts) + 4,
-    )(*parts, own_fields, mask, shares, full)
+        (
+            shape((ka_count * pb_count, 2 * span, width), BF16),
+            shape((LANES, 2 * LANES), F32),
+        ),
+        [
+            pltpu.VMEM((2 * M * M * tiles, LANES), F32),
+            pltpu.VMEM((width, LANES), F32),
+            pltpu.VMEM((LANES, LANES), F32),
+        ],
+        operands=len(parts) + 5,
+    )(*parts, own_fields, mask, shares, full, picks)
     group = operator_group(ka_count, pb_count)
     blocks = lax.all_to_all(
         blocks, ("pb", "ka"), 0, 0, axis_index_groups=[group], tiled=True
@@ -426,11 +500,13 @@
         (shape((k_local, walkers, 2 * pair_width), F32), shape((1, 1), F32)),
         [
             pltpu.VMEM((width, LANES), F32),
+            pltpu.VMEM((width, LANES), F32),
             pltpu.VMEM((NOCC * ROWS, 2 * LANES), F32),
-            pltpu.VMEM((LANES, LANES), F32),
+            pltpu.VMEM((NOCC * ROWS, LANES), F32),
+            pltpu.VMEM((NOCC * ROWS, LANES), F32),
         ],
-        operands=len(parts) + 3,
-    )(blocks, *parts, picks, own_orbitals)
+        operands=6,
+    )(blocks, first, picks, fold, own_picks, own_orbitals)
     return (propagated[None], energy)
 
 
@@ -439,7 +515,7 @@
     walkers = orbitals.shape[2]
     fits = 2 * pb_count * kq_map.shape[1] * walkers == LANES
     fits = fits and chol_half.shape[1] * walkers == 8 and chol_half.shape[4] == 2 * LANES
-    fits = fits and ka_count == 4
+    fits = fits and ka_count == 4 and pb_count == 2
     if fits and chol_half.shape[0] == 1 and walkers == ka_count:
         return direct(green, fields, orbitals, chol_half, chol_full, chol_count, kq_map)
     return with_collectives(green, fields, orbitals, chol_half, chol_full, chol_count, kq_map)

time: 29.8 us -> 29.9 us (level)
  no operation moved by 1% of the time
where the time goes in v15:
time: 29.9 us; the launch traced here: 29.7 us
  starting transfers between devices  10.6 us (35%)
  blocking collectives  9.61 us (32%)
  Pallas kernels  4.29 us (14%)
  waiting for transfers between devices  3.16 us (11%)
  local copies, waits for them, and re-layouts  1.35 us (5%)
  between operations  0.7 us (2%)
    ppermute x6, starting transfers between devices, exchange(): return [array] + [lax.ppermute(array, axis, pairs) for pairs in rounds]  10.6 us
    all_to_all x1, blocking collectives, direct(): lax.all_to_all(blocks, ('pb', 'ka'), 0, 0, axis_index_groups=[group], til...  9.61 us
    ppermute x6, waiting for transfers between devices, exchange(): return [array] + [lax.ppermute(array, axis, pairs) for pairs in rounds]  3.16 us
    pallas_call x1, Pallas kernels, direct(): call(functools.partial(taylor_kernel, pb_count, float(pb_count * chol_col...  2.12 us
    unnamed x14, local copies, waits for them, and re-layouts  1.35 us
    pallas_call x1, Pallas kernels, direct(): call(functools.partial(operator_kernel, k_local), (shape((ka_count * pb_c...  0.85 us
    pallas_call x1, Pallas kernels, direct(): call(functools.partial(prepare_kernel, ka_count, pb_count, walkers), (sha...  0.67 us
  transfers between devices with their start and end apart: 6, of which 4 were waited for; matrix products, arithmetic and copies ran while one was open for 0% of the time, Pallas kernels for 3%

profile of v15, /device:TPU:0, one launch (start us, length us, event | category | flops | bytes accessed | tf_op | source)
XLA Modules:
  0.0 29.7 jit_solution(16303460357559937244)
XLA Ops:
  0.6 0.0 copy-start.1
  0.6 0.0 copy-start.2
  0.7 0.0 copy-start.3
  0.7 0.0 copy-start
  0.7 0.0 copy-start.4
  0.7 4.1 %collective-permute-start.2 = (bf16[8,208]{1,0:T(8,128)(2,1)}, bf16[8,208]{1,0:T(8,128)(2,1)S(1)}, u32[]{:S(2)}, u32[]{:S(2)}) collective-permute-start(bf16[8,208]{1,0:T(8,128)(2,1)} %bitcast.15), channel_id=1, source_target_pairs={{12,0},{8,4},{4,12},{0,8},{13,1},{9,5},{5,13},{1,9},{14,2},{10,6},... | collective-permute-start | bytes 9992 | tf_op jit(solution)/shard_map/ppermute | solution.py:140
  4.8 1.1 %collective-permute-start.1 = (bf16[8,208]{1,0:T(8,128)(2,1)}, bf16[8,208]{1,0:T(8,128)(2,1)S(1)}, u32[]{:S(2)}, u32[]{:S(2)}) collective-permute-start(bf16[8,208]{1,0:T(8,128)(2,1)} %bitcast.16), channel_id=1, source_target_pairs={{12,4},{8,0},{0,12},{4,8},{13,5},{9,1},{1,13},{5,9},{14,6},{10,2},... | collective-permute-start | bytes 9992 | tf_op jit(solution)/shard_map/ppermute | solution.py:140
  5.8 0.5 %collective-permute-start = (bf16[8,208]{1,0:T(8,128)(2,1)}, bf16[8,208]{1,0:T(8,128)(2,1)S(1)}, u32[]{:S(2)}, u32[]{:S(2)}) collective-permute-start(bf16[8,208]{1,0:T(8,128)(2,1)} %bitcast.17), channel_id=1, source_target_pairs={{4,0},{12,8},{8,12},{0,4},{5,1},{13,9},{9,13},{1,5},{6,2},{14,10},... | collective-permute-start | bytes 9992 | tf_op jit(solution)/shard_map/ppermute | solution.py:140
  6.4 0.0 copy-start.5
  6.4 0.7 %copy-done.5 = s32[2,8]{1,0:T(2,128)S(1)} copy-done((s32[2,8]{1,0:T(2,128)S(1)}, s32[2,8]{1,0:T(2,128)}, u32[]{:S(2)}) %copy-start.5) | copy-done | bytes 88
  7.0 0.0 copy-start.6
  7.0 0.7 %copy-done.6 = s32[2]{0:T(128)S(1)} copy-done((s32[2]{0:T(128)S(1)}, s32[2]{0:T(128)}, u32[]{:S(2)}) %copy-start.6) | copy-done | bytes 32
  7.7 0.7 %shard_map.86 = (f32[8,256]{1,0:T(8,128)S(1)}, bf16[128,256]{1,0:T(8,128)(2,1)S(1)}, s32[8,128]{1,0:T(8,128)S(1)}) custom-call(s32[2,8]{1,0:T(2,128)S(1)} %copy-done.5, s32[2]{0:T(128)S(1)} %copy-done.6), custom_call_target="tpu_custom_call" | custom-call | flops 1000000000 | tf_op jit(solution)/shard_map/pallas_call | solution.py:451
  8.4 0.0 collective-permute-done.2.refs_3_
  8.4 1.1 %collective-permute-done.1.refs_2_ = bf16[8,208]{1,0:T(8,128)(2,1)S(1)} collective-permute-done((bf16[8,208]{1,0:T(8,128)(2,1)}, bf16[8,208]{1,0:T(8,128)(2,1)S(1)}, u32[]{:S(2)}, u32[]{:S(2)}) %collective-permute-start.1) | collective-permute-done | bytes 3360 | tf_op jit(solution)/shard_map/ppermute | solution.py:140
  9.5 0.2 collective-permute-done.refs_1_
  9.7 0.0 copy-done.1
  9.7 0.0 copy-done.2
  9.7 0.0 copy-done.3
  9.7 0.3 shard_map.87
  10.0 1.4 %collective-permute-start.5 = (f32[16,256]{1,0:T(8,128)S(1)}, f32[16,256]{1,0:T(8,128)S(1)}, u32[]{:S(2)}, u32[]{:S(2)}) collective-permute-start(f32[16,256]{1,0:T(8,128)S(1)} %get-tuple-element.15.refs_0_), channel_id=1, source_target_pairs={{0,4},{4,12},{8,0},{12,8},{1,5},{5,13},{9,1},{13,9},{2,6},{6,14},{... | collective-permute-start | bytes 49160 | tf_op jit(solution)/shard_map/ppermute | solution.py:140
  11.4 1.9 %collective-permute-start.4 = (f32[16,256]{1,0:T(8,128)S(1)}, f32[16,256]{1,0:T(8,128)S(1)}, u32[]{:S(2)}, u32[]{:S(2)}) collective-permute-start(f32[16,256]{1,0:T(8,128)S(1)} %get-tuple-element.15.refs_0_), channel_id=1, source_target_pairs={{0,12},{12,0},{4,8},{8,4},{1,13},{13,1},{5,9},{9,5},{2,14},{14,2},... | collective-permute-start | bytes 49160 | tf_op jit(solution)/shard_map/ppermute | solution.py:140
  13.3 1.6 %collective-permute-start.3 = (f32[16,256]{1,0:T(8,128)S(1)}, f32[16,256]{1,0:T(8,128)S(1)}, u32[]{:S(2)}, u32[]{:S(2)}) collective-permute-start(f32[16,256]{1,0:T(8,128)S(1)} %get-tuple-element.15.refs_0_), channel_id=1, source_target_pairs={{0,8},{4,0},{8,12},{12,4},{1,9},{5,1},{9,13},{13,5},{2,10},{6,2},{... | collective-permute-start | bytes 49160 | tf_op jit(solution)/shard_map/ppermute | solution.py:140
  14.9 0.4 %shard_map.88 = (f32[4,128]{1,0:T(4,128)S(1)}, bf16[128,128]{1,0:T(8,128)(2,1)S(1)}, bf16[512,256]{1,0:T(8,128)(2,1)S(1)}) custom-call(f32[2,8,104]{2,1,0:T(8,128)S(1)} %get-tuple-element.16.own_ref, bf16[2,2,104,256]{3,2,1,0:T(8,128)(2,1)S(1)} %bitcast.12, f32[8,256]{1,0:T(8,128)S(1)} %get-tuple-element.14.refs_6_.mask_ref.refs_5_, ...), custom_call_target="tpu_custom_call" | custom-call | tf_op jit(solution)/shard_map/pallas_call | solution.py:471
  15.2 0.0 collective-permute-done.5.refs_3_
  15.2 1.7 %collective-permute-done.4.refs_2_ = f32[16,256]{1,0:T(8,128)S(1)} collective-permute-done((f32[16,256]{1,0:T(8,128)S(1)}, f32[16,256]{1,0:T(8,128)S(1)}, u32[]{:S(2)}, u32[]{:S(2)}) %collective-permute-start.4) | collective-permute-done | bytes 16416 | tf_op jit(solution)/shard_map/ppermute | solution.py:140
  16.9 0.2 collective-permute-done.3.refs_1_
  17.1 0.0 copy-done
  17.1 0.0 copy-done.4
  17.1 0.9 %shard_map.89 = (bf16[8,16,768]{2,1,0:T(8,128)(2,1)S(1)}, f32[128,256]{1,0:T(8,128)S(1)}) custom-call(f32[16,256]{1,0:T(8,128)S(1)} %get-tuple-element.15.refs_0_, f32[16,256]{1,0:T(8,128)S(1)} %collective-permute-done.3.refs_1_, f32[16,256]{1,0:T(8,128)S(1)} %collective-permute-done.4.refs_2_, f32[16,256]{1,0:T(8,128)S(1)} %collective-permute-done.5.refs_3_, ...), custom_call_target="tpu_custom_call" | custom-call | tf_op jit(solution)/shard_map/pallas_call | solution.py:481
  18.0 9.6 %all_to_all.5.blocks_ref = bf16[8,16,768]{2,1,0:T(8,128)(2,1)S(1)} all-to-all(bf16[8,16,768]{2,1,0:T(8,128)(2,1)S(1)} %get-tuple-element.20), channel_id=1, replica_groups={{10,14,6,2,12,8,4,0},{11,15,7,3,13,9,5,1},{26,30,22,18,28,24,20,16},{27..., dimensions={0} | all-to-all | bytes 393216 | tf_op jit(solution)/shard_map/all_to_all | solution.py:495
  27.6 2.1 %shard_map.90 = (f32[2,4,208]{2,1,0:T(4,128)}, f32[1,1]{1,0:T(1,128)}) custom-call(bf16[8,16,768]{2,1,0:T(8,128)(2,1)S(1)} %all_to_all.5.blocks_ref, f32[128,256]{1,0:T(8,128)S(1)} %get-tuple-element.21.first_ref, bf16[128,256]{1,0:T(8,128)(2,1)S(1)} %get-tuple-element.19.refs_8_.picks_ref, bf16[128,128]{1,0:T(8,128)(2,1)S(1)} %get-tuple-element.22.fold_ref, ...), custom_call_target="tpu_custom_call" | custom-call | tf_op jit(solution)/shard_map/pallas_call | solution.py:498
Async XLA Ops:
  0.6 9.0 %copy-start.1 = (bf16[1,2,2,104,256]{4,3,2,1,0:T(8,128)(2,1)S(1)}, bf16[1,2,2,104,256]{4,3,2,1,0:T(8,128)(2,1)}, u32[]{:S(2)}) copy-start(bf16[1,2,2,104,256]{4,3,2,1,0:T(8,128)(2,1)} %param.10) | copy-start | bytes 638980
  0.6 9.0 %copy-start.2 = (f32[1,2,4,208]{3,2,1,0:T(4,128)S(1)}, f32[1,2,4,208]{3,2,1,0:T(4,128)}, u32[]{:S(2)}) copy-start(f32[1,2,4,208]{3,2,1,0:T(4,128)} %param.9) | copy-start | bytes 19972
  0.7 9.0 %copy-start.3 = (bf16[1,1,1,8,208]{4,3,2,1,0:T(8,128)(2,1)S(1)}, bf16[1,1,1,8,208]{4,3,2,1,0:T(8,128)(2,1)}, u32[]{:S(2)}) copy-start(bf16[1,1,1,8,208]{4,3,2,1,0:T(8,128)(2,1)} %param.7) | copy-start | bytes 9988
  0.7 16.4 %copy-start = (bf16[1,2,2,676,256]{4,2,3,1,0:T(2,128)(2,1)S(1)}, bf16[1,2,2,676,256]{4,2,3,1,0:T(2,128)(2,1)}, u32[]{:S(2)}) copy-start(bf16[1,2,2,676,256]{4,2,3,1,0:T(2,128)(2,1)} %param.11) | copy-start | bytes 4153348
  0.7 16.4 %copy-start.4 = (f32[1,1,4,256]{3,2,1,0:T(4,128)S(1)}, f32[1,1,4,256]{3,2,1,0:T(4,128)}, u32[]{:S(2)}) copy-start(f32[1,1,4,256]{3,2,1,0:T(4,128)} %param.8) | copy-start | bytes 12292
  0.7 7.7 %collective-permute-start.2 = (bf16[8,208]{1,0:T(8,128)(2,1)}, bf16[8,208]{1,0:T(8,128)(2,1)S(1)}, u32[]{:S(2)}, u32[]{:S(2)}) collective-permute-start(bf16[8,208]{1,0:T(8,128)(2,1)} %bitcast.15), channel_id=1, source_target_pairs={{12,0},{8,4},{4,12},{0,8},{13,1},{9,5},{5,13},{1,9},{14,2},{10,6},... | collective-permute-start | bytes 9992 | tf_op jit(solution)/shard_map/ppermute | solution.py:140
  4.8 4.7 %collective-permute-start.1 = (bf16[8,208]{1,0:T(8,128)(2,1)}, bf16[8,208]{1,0:T(8,128)(2,1)S(1)}, u32[]{:S(2)}, u32[]{:S(2)}) collective-permute-start(bf16[8,208]{1,0:T(8,128)(2,1)} %bitcast.16), channel_id=1, source_target_pairs={{12,4},{8,0},{0,12},{4,8},{13,5},{9,1},{1,13},{5,9},{14,6},{10,2},... | collective-permute-start | bytes 9992 | tf_op jit(solution)/shard_map/ppermute | solution.py:140
  5.8 3.8 %collective-permute-start = (bf16[8,208]{1,0:T(8,128)(2,1)}, bf16[8,208]{1,0:T(8,128)(2,1)S(1)}, u32[]{:S(2)}, u32[]{:S(2)}) collective-permute-start(bf16[8,208]{1,0:T(8,128)(2,1)} %bitcast.17), channel_id=1, source_target_pairs={{4,0},{12,8},{8,12},{0,4},{5,1},{13,9},{9,13},{1,5},{6,2},{14,10},... | collective-permute-start | bytes 9992 | tf_op jit(solution)/shard_map/ppermute | solution.py:140
  6.4 0.7 %copy-start.5 = (s32[2,8]{1,0:T(2,128)S(1)}, s32[2,8]{1,0:T(2,128)}, u32[]{:S(2)}) copy-start(s32[2,8]{1,0:T(2,128)} %map_ref.1) | copy-start | bytes 196
  7.0 0.7 %copy-start.6 = (s32[2]{0:T(128)S(1)}, s32[2]{0:T(128)}, u32[]{:S(2)}) copy-start(s32[2]{0:T(128)} %count_ref.1) | copy-start | bytes 28
  10.0 5.3 %collective-permute-start.5 = (f32[16,256]{1,0:T(8,128)S(1)}, f32[16,256]{1,0:T(8,128)S(1)}, u32[]{:S(2)}, u32[]{:S(2)}) collective-permute-start(f32[16,256]{1,0:T(8,128)S(1)} %get-tuple-element.15.refs_0_), channel_id=1, source_target_pairs={{0,4},{4,12},{8,0},{12,8},{1,5},{5,13},{9,1},{13,9},{2,6},{6,14},{... | collective-permute-start | bytes 49160 | tf_op jit(solution)/shard_map/ppermute | solution.py:140
  11.4 5.5 %collective-permute-start.4 = (f32[16,256]{1,0:T(8,128)S(1)}, f32[16,256]{1,0:T(8,128)S(1)}, u32[]{:S(2)}, u32[]{:S(2)}) collective-permute-start(f32[16,256]{1,0:T(8,128)S(1)} %get-tuple-element.15.refs_0_), channel_id=1, source_target_pairs={{0,12},{12,0},{4,8},{8,4},{1,13},{13,1},{5,9},{9,5},{2,14},{14,2},... | collective-permute-start | bytes 49160 | tf_op jit(solution)/shard_map/ppermute | solution.py:140
  13.3 3.8 %collective-permute-start.3 = (f32[16,256]{1,0:T(8,128)S(1)}, f32[16,256]{1,0:T(8,128)S(1)}, u32[]{:S(2)}, u32[]{:S(2)}) collective-permute-start(f32[16,256]{1,0:T(8,128)S(1)} %get-tuple-element.15.refs_0_), channel_id=1, source_target_pairs={{0,8},{4,0},{8,12},{12,4},{1,9},{5,1},{9,13},{13,5},{2,10},{6,2},{... | collective-permute-start | bytes 49160 | tf_op jit(solution)/shard_map/ppermute | solution.py:140

commit v16 on v10

--- a/solution.py
+++ b/solution.py
@@ -299,7 +299,8 @@
 
 
 def taylor_kernel(pb_count, normalizer, blocks_ref, *refs):
-    *windows, picks_ref, orbitals_ref, out_ref, energy_ref, turned, picked, term = refs
+    *windows, picks_ref, orbitals_ref = refs[:-8]
+    out_ref, energy_ref, turned, picked, term, result, total, sems = refs[-8:]
     pairs = M * M
     pair = NOCC * M
     k_local, walkers, _ = out_ref.shape
@@ -322,7 +323,9 @@
     lane = lax.broadcasted_iota(jnp.int32, shares.shape, 1)
     shares = jnp.where(lax.rem(lane, 2 * span) == ka_pos, shares, 0.0)
     shares = jnp.sum(jnp.sum(shares, axis=0, keepdims=True), axis=1, keepdims=True)
-    energy_ref[...] = shares / normalizer
+    total[...] = shares / normalizer
+    energy_copy = pltpu.make_async_copy(total, energy_ref, sems.at[0])
+    energy_copy.start()
     lane = lax.broadcasted_iota(jnp.int32, (M, LANES), 1)
     imaginary = lax.rem(lane, 2 * span) >= span
     sums = [jnp.zeros((M, LANES), F32) for _ in range(NOCC)]
@@ -342,7 +345,7 @@
             )
             applied = straight[i] + other
             applied = applied + pltpu.roll(applied, LANES // pb_count, 1)
-            current = applied / degree
+            current = applied * (1.0 / degree)
             sums[i] = sums[i] + current
             term[i * ROWS : i * ROWS + M] = current if degree < TAYLOR else sums[i]
         if degree < TAYLOR:
@@ -354,10 +357,14 @@
     both = jnp.concatenate([both[:, i * ROWS : i * ROWS + M] for i in range(NOCC)], axis=1)
     both = jnp.concatenate([both[:span], both[span:]], axis=1)
     for k in range(k_local):
-        out_ref[k] = orbitals_ref[k] + both[k * walkers : (k + 1) * walkers]
-
-
-def call(kernel, out, scratch=(), scalars=0, operands=0, flops=None):
+        result[k] = orbitals_ref[k] + both[k * walkers : (k + 1) * walkers]
+    result_copy = pltpu.make_async_copy(result, out_ref, sems.at[1])
+    result_copy.start()
+    energy_copy.wait()
+    result_copy.wait()
+
+
+def call(kernel, out, scratch=(), scalars=0, operands=0, flops=None, space=pltpu.VMEM):
     spaces = [pltpu.SMEM] * scalars + [pltpu.VMEM] * operands
     cost = None
     if flops is not None:
@@ -366,7 +373,7 @@
         kernel,
         out_shape=out,
         in_specs=[pl.BlockSpec(memory_space=space) for space in spaces],
-        out_specs=jax.tree.map(lambda _: pl.BlockSpec(memory_space=pltpu.VMEM), out),
+        out_specs=jax.tree.map(lambda _: pl.BlockSpec(memory_space=space), out),
         scratch_shapes=list(scratch),
         cost_estimate=cost,
         compiler_params=pltpu.CompilerParams(vmem_limit_bytes=24 * 2**20),
@@ -428,8 +435,12 @@
             pltpu.VMEM((width, LANES), F32),
             pltpu.VMEM((NOCC * ROWS, 2 * LANES), F32),
             pltpu.VMEM((LANES, LANES), F32),
+            pltpu.VMEM((k_local, walkers, 2 * pair_width), F32),
+            pltpu.VMEM((1, 1), F32),
+            pltpu.SemaphoreType.DMA((2,)),
         ],
         operands=len(parts) + 3,
+        space=pl.ANY,
     )(blocks, *parts, picks, own_orbitals)
     return (propagated[None], energy)
 

time: 29.8 us -> 29.9 us (level)
  no operation moved by 1% of the time
where the time goes in v16:
time: 29.9 us; the launch traced here: 29.7 us
  starting transfers between devices  10.6 us (35%)
  blocking collectives  9.62 us (32%)
  Pallas kernels  4.24 us (14%)
  waiting for transfers between devices  3.17 us (11%)
  local copies, waits for them, and re-layouts  1.35 us (5%)
  between operations  0.71 us (2%)
    ppermute x6, starting transfers between devices, exchange(): return [array] + [lax.ppermute(array, axis, pairs) for pairs in rounds]  10.6 us
    all_to_all x1, blocking collectives, direct(): lax.all_to_all(blocks, ('pb', 'ka'), 0, 0, axis_index_groups=[group], til...  9.62 us
    ppermute x6, waiting for transfers between devices, exchange(): return [array] + [lax.ppermute(array, axis, pairs) for pairs in rounds]  3.17 us
    pallas_call x1, Pallas kernels, direct(): call(functools.partial(taylor_kernel, pb_count, float(pb_count * chol_col...  2.18 us
    unnamed x14, local copies, waits for them, and re-layouts  1.35 us
    pallas_call x1, Pallas kernels, direct(): call(functools.partial(operator_kernel, k_local), shape((ka_count * pb_co...  0.76 us
    pallas_call x1, Pallas kernels, direct(): call(functools.partial(prepare_kernel, ka_count, pb_count, walkers), (sha...  0.66 us
  transfers between devices with their start and end apart: 6, of which 4 were waited for; matrix products, arithmetic and copies ran while one was open for 0% of the time, Pallas kernels for 3%

profile of v16, /device:TPU:0, one launch (start us, length us, event | category | flops | bytes accessed | tf_op | source)
XLA Modules:
  0.0 29.7 jit_solution(9362863155867175767)
XLA Ops:
  0.6 0.0 copy-start.1
  0.6 0.0 copy-start.2
  0.7 0.0 copy-start.3
  0.7 0.0 copy-start
  0.7 0.0 copy-start.4
  0.7 4.1 %collective-permute-start.2 = (bf16[8,208]{1,0:T(8,128)(2,1)}, bf16[8,208]{1,0:T(8,128)(2,1)S(1)}, u32[]{:S(2)}, u32[]{:S(2)}) collective-permute-start(bf16[8,208]{1,0:T(8,128)(2,1)} %bitcast.15), channel_id=1, source_target_pairs={{12,0},{8,4},{4,12},{0,8},{13,1},{9,5},{5,13},{1,9},{14,2},{10,6},... | collective-permute-start | bytes 9992 | tf_op jit(solution)/shard_map/ppermute | solution.py:140
  4.8 1.1 %collective-permute-start.1 = (bf16[8,208]{1,0:T(8,128)(2,1)}, bf16[8,208]{1,0:T(8,128)(2,1)S(1)}, u32[]{:S(2)}, u32[]{:S(2)}) collective-permute-start(bf16[8,208]{1,0:T(8,128)(2,1)} %bitcast.16), channel_id=1, source_target_pairs={{12,4},{8,0},{0,12},{4,8},{13,5},{9,1},{1,13},{5,9},{14,6},{10,2},... | collective-permute-start | bytes 9992 | tf_op jit(solution)/shard_map/ppermute | solution.py:140
  5.8 0.5 %collective-permute-start = (bf16[8,208]{1,0:T(8,128)(2,1)}, bf16[8,208]{1,0:T(8,128)(2,1)S(1)}, u32[]{:S(2)}, u32[]{:S(2)}) collective-permute-start(bf16[8,208]{1,0:T(8,128)(2,1)} %bitcast.17), channel_id=1, source_target_pairs={{4,0},{12,8},{8,12},{0,4},{5,1},{13,9},{9,13},{1,5},{6,2},{14,10},... | collective-permute-start | bytes 9992 | tf_op jit(solution)/shard_map/ppermute | solution.py:140
  6.4 0.0 copy-start.5
  6.4 0.7 %copy-done.5 = s32[2,8]{1,0:T(2,128)S(1)} copy-done((s32[2,8]{1,0:T(2,128)S(1)}, s32[2,8]{1,0:T(2,128)}, u32[]{:S(2)}) %copy-start.5) | copy-done | bytes 88
  7.0 0.0 copy-start.6
  7.0 0.7 %copy-done.6 = s32[2]{0:T(128)S(1)} copy-done((s32[2]{0:T(128)S(1)}, s32[2]{0:T(128)}, u32[]{:S(2)}) %copy-start.6) | copy-done | bytes 32
  7.7 0.7 %shard_map.86 = (f32[8,256]{1,0:T(8,128)S(1)}, bf16[128,256]{1,0:T(8,128)(2,1)S(1)}) custom-call(s32[2,8]{1,0:T(2,128)S(1)} %copy-done.5, s32[2]{0:T(128)S(1)} %copy-done.6), custom_call_target="tpu_custom_call" | custom-call | flops 1000000000 | tf_op jit(solution)/shard_map/pallas_call | solution.py:399
  8.4 0.0 collective-permute-done.2.refs_3_
  8.4 1.1 %collective-permute-done.1.refs_2_ = bf16[8,208]{1,0:T(8,128)(2,1)S(1)} collective-permute-done((bf16[8,208]{1,0:T(8,128)(2,1)}, bf16[8,208]{1,0:T(8,128)(2,1)S(1)}, u32[]{:S(2)}, u32[]{:S(2)}) %collective-permute-start.1) | collective-permute-done | bytes 3360 | tf_op jit(solution)/shard_map/ppermute | solution.py:140
  9.5 0.2 collective-permute-done.refs_1_
  9.7 0.0 copy-done.1
  9.7 0.0 copy-done.2
  9.7 0.0 copy-done.3
  9.7 0.3 shard_map.87
  10.0 1.4 %collective-permute-start.5 = (f32[16,256]{1,0:T(8,128)S(1)}, f32[16,256]{1,0:T(8,128)S(1)}, u32[]{:S(2)}, u32[]{:S(2)}) collective-permute-start(f32[16,256]{1,0:T(8,128)S(1)} %get-tuple-element.9.refs_0_), channel_id=1, source_target_pairs={{0,4},{4,12},{8,0},{12,8},{1,5},{5,13},{9,1},{13,9},{2,6},{6,14},{... | collective-permute-start | bytes 49160 | tf_op jit(solution)/shard_map/ppermute | solution.py:140
  11.4 1.9 %collective-permute-start.4 = (f32[16,256]{1,0:T(8,128)S(1)}, f32[16,256]{1,0:T(8,128)S(1)}, u32[]{:S(2)}, u32[]{:S(2)}) collective-permute-start(f32[16,256]{1,0:T(8,128)S(1)} %get-tuple-element.9.refs_0_), channel_id=1, source_target_pairs={{0,12},{12,0},{4,8},{8,4},{1,13},{13,1},{5,9},{9,5},{2,14},{14,2},... | collective-permute-start | bytes 49160 | tf_op jit(solution)/shard_map/ppermute | solution.py:140
  13.3 1.6 %collective-permute-start.3 = (f32[16,256]{1,0:T(8,128)S(1)}, f32[16,256]{1,0:T(8,128)S(1)}, u32[]{:S(2)}, u32[]{:S(2)}) collective-permute-start(f32[16,256]{1,0:T(8,128)S(1)} %get-tuple-element.9.refs_0_), channel_id=1, source_target_pairs={{0,8},{4,0},{8,12},{12,4},{1,9},{5,1},{9,13},{13,5},{2,10},{6,2},{... | collective-permute-start | bytes 49160 | tf_op jit(solution)/shard_map/ppermute | solution.py:140
  14.9 0.4 %shard_map.88.refs_6_ = f32[4,128]{1,0:T(4,128)S(1)} custom-call(f32[2,8,104]{2,1,0:T(8,128)S(1)} %get-tuple-element.10.own_ref, bf16[2,2,104,256]{3,2,1,0:T(8,128)(2,1)S(1)} %bitcast.12, f32[8,256]{1,0:T(8,128)S(1)} %get-tuple-element.8.refs_6_.mask_ref.refs_5_), custom_call_target="tpu_custom_call" | custom-call | tf_op jit(solution)/shard_map/pallas_call | solution.py:415
  15.2 0.0 collective-permute-done.5.refs_3_
  15.2 1.7 %collective-permute-done.4.refs_2_ = f32[16,256]{1,0:T(8,128)S(1)} collective-permute-done((f32[16,256]{1,0:T(8,128)S(1)}, f32[16,256]{1,0:T(8,128)S(1)}, u32[]{:S(2)}, u32[]{:S(2)}) %collective-permute-start.4) | collective-permute-done | bytes 16416 | tf_op jit(solution)/shard_map/ppermute | solution.py:140
  16.9 0.2 collective-permute-done.3.refs_1_
  17.1 0.0 copy-done
  17.1 0.0 copy-done.4
  17.1 0.8 %shard_map.89 = bf16[8,16,768]{2,1,0:T(8,128)(2,1)S(1)} custom-call(f32[16,256]{1,0:T(8,128)S(1)} %get-tuple-element.9.refs_0_, f32[16,256]{1,0:T(8,128)S(1)} %collective-permute-done.3.refs_1_, f32[16,256]{1,0:T(8,128)S(1)} %collective-permute-done.4.refs_2_, f32[16,256]{1,0:T(8,128)S(1)} %collective-permute-done.5.refs_3_, f32[4,256]{1,0:T(4,128)S(1)} %bitcast.19, ...), custom_call_target="tpu_custom_call" | custom-call | tf_op jit(solution)/shard_map/pallas_call | solution.py:421
  17.9 9.6 %all_to_all.5.blocks_ref = bf16[8,16,768]{2,1,0:T(8,128)(2,1)S(1)} all-to-all(bf16[8,16,768]{2,1,0:T(8,128)(2,1)S(1)} %shard_map.89), channel_id=1, replica_groups={{10,14,6,2,12,8,4,0},{11,15,7,3,13,9,5,1},{26,30,22,18,28,24,20,16},{27..., dimensions={0} | all-to-all | bytes 393216 | tf_op jit(solution)/shard_map/all_to_all | solution.py:428
  27.5 2.2 %shard_map.90 = (f32[2,4,208]{2,1,0:T(4,128)}, f32[1,1]{1,0:T(1,128)}) custom-call(bf16[8,16,768]{2,1,0:T(8,128)(2,1)S(1)} %all_to_all.5.blocks_ref, f32[16,256]{1,0:T(8,128)S(1)} %get-tuple-element.9.refs_0_, f32[16,256]{1,0:T(8,128)S(1)} %collective-permute-done.3.refs_1_, f32[16,256]{1,0:T(8,128)S(1)} %collective-permute-done.4.refs_2_, ...), custom_call_target="tpu_custom_call" | custom-call | tf_op jit(solution)/shard_map/pallas_call | solution.py:431
Async XLA Ops:
  0.6 9.0 %copy-start.1 = (bf16[1,2,2,104,256]{4,3,2,1,0:T(8,128)(2,1)S(1)}, bf16[1,2,2,104,256]{4,3,2,1,0:T(8,128)(2,1)}, u32[]{:S(2)}) copy-start(bf16[1,2,2,104,256]{4,3,2,1,0:T(8,128)(2,1)} %param.10) | copy-start | bytes 638980
  0.6 9.0 %copy-start.2 = (f32[1,2,4,208]{3,2,1,0:T(4,128)S(1)}, f32[1,2,4,208]{3,2,1,0:T(4,128)}, u32[]{:S(2)}) copy-start(f32[1,2,4,208]{3,2,1,0:T(4,128)} %param.9) | copy-start | bytes 19972
  0.7 9.0 %copy-start.3 = (bf16[1,1,1,8,208]{4,3,2,1,0:T(8,128)(2,1)S(1)}, bf16[1,1,1,8,208]{4,3,2,1,0:T(8,128)(2,1)}, u32[]{:S(2)}) copy-start(bf16[1,1,1,8,208]{4,3,2,1,0:T(8,128)(2,1)} %param.7) | copy-start | bytes 9988
  0.7 16.4 %copy-start = (bf16[1,2,2,676,256]{4,2,3,1,0:T(2,128)(2,1)S(1)}, bf16[1,2,2,676,256]{4,2,3,1,0:T(2,128)(2,1)}, u32[]{:S(2)}) copy-start(bf16[1,2,2,676,256]{4,2,3,1,0:T(2,128)(2,1)} %param.11) | copy-start | bytes 4153348
  0.7 16.4 %copy-start.4 = (f32[1,1,4,256]{3,2,1,0:T(4,128)S(1)}, f32[1,1,4,256]{3,2,1,0:T(4,128)}, u32[]{:S(2)}) copy-start(f32[1,1,4,256]{3,2,1,0:T(4,128)} %param.8) | copy-start | bytes 12292
  0.7 7.7 %collective-permute-start.2 = (bf16[8,208]{1,0:T(8,128)(2,1)}, bf16[8,208]{1,0:T(8,128)(2,1)S(1)}, u32[]{:S(2)}, u32[]{:S(2)}) collective-permute-start(bf16[8,208]{1,0:T(8,128)(2,1)} %bitcast.15), channel_id=1, source_target_pairs={{12,0},{8,4},{4,12},{0,8},{13,1},{9,5},{5,13},{1,9},{14,2},{10,6},... | collective-permute-start | bytes 9992 | tf_op jit(solution)/shard_map/ppermute | solution.py:140
  4.8 4.7 %collective-permute-start.1 = (bf16[8,208]{1,0:T(8,128)(2,1)}, bf16[8,208]{1,0:T(8,128)(2,1)S(1)}, u32[]{:S(2)}, u32[]{:S(2)}) collective-permute-start(bf16[8,208]{1,0:T(8,128)(2,1)} %bitcast.16), channel_id=1, source_target_pairs={{12,4},{8,0},{0,12},{4,8},{13,5},{9,1},{1,13},{5,9},{14,6},{10,2},... | collective-permute-start | bytes 9992 | tf_op jit(solution)/shard_map/ppermute | solution.py:140
  5.8 3.8 %collective-permute-start = (bf16[8,208]{1,0:T(8,128)(2,1)}, bf16[8,208]{1,0:T(8,128)(2,1)S(1)}, u32[]{:S(2)}, u32[]{:S(2)}) collective-permute-start(bf16[8,208]{1,0:T(8,128)(2,1)} %bitcast.17), channel_id=1, source_target_pairs={{4,0},{12,8},{8,12},{0,4},{5,1},{13,9},{9,13},{1,5},{6,2},{14,10},... | collective-permute-start | bytes 9992 | tf_op jit(solution)/shard_map/ppermute | solution.py:140
  6.4 0.7 %copy-start.5 = (s32[2,8]{1,0:T(2,128)S(1)}, s32[2,8]{1,0:T(2,128)}, u32[]{:S(2)}) copy-start(s32[2,8]{1,0:T(2,128)} %map_ref.1) | copy-start | bytes 196
  7.0 0.7 %copy-start.6 = (s32[2]{0:T(128)S(1)}, s32[2]{0:T(128)}, u32[]{:S(2)}) copy-start(s32[2]{0:T(128)} %count_ref.1) | copy-start | bytes 28
  10.0 5.3 %collective-permute-start.5 = (f32[16,256]{1,0:T(8,128)S(1)}, f32[16,256]{1,0:T(8,128)S(1)}, u32[]{:S(2)}, u32[]{:S(2)}) collective-permute-start(f32[16,256]{1,0:T(8,128)S(1)} %get-tuple-element.9.refs_0_), channel_id=1, source_target_pairs={{0,4},{4,12},{8,0},{12,8},{1,5},{5,13},{9,1},{13,9},{2,6},{6,14},{... | collective-permute-start | bytes 49160 | tf_op jit(solution)/shard_map/ppermute | solution.py:140
  11.4 5.5 %collective-permute-start.4 = (f32[16,256]{1,0:T(8,128)S(1)}, f32[16,256]{1,0:T(8,128)S(1)}, u32[]{:S(2)}, u32[]{:S(2)}) collective-permute-start(f32[16,256]{1,0:T(8,128)S(1)} %get-tuple-element.9.refs_0_), channel_id=1, source_target_pairs={{0,12},{12,0},{4,8},{8,4},{1,13},{13,1},{5,9},{9,5},{2,14},{14,2},... | collective-permute-start | bytes 49160 | tf_op jit(solution)/shard_map/ppermute | solution.py:140
  13.3 3.8 %collective-permute-start.3 = (f32[16,256]{1,0:T(8,128)S(1)}, f32[16,256]{1,0:T(8,128)S(1)}, u32[]{:S(2)}, u32[]{:S(2)}) collective-permute-start(f32[16,256]{1,0:T(8,128)S(1)} %get-tuple-element.9.refs_0_), channel_id=1, source_target_pairs={{0,8},{4,0},{8,12},{12,4},{1,9},{5,1},{9,13},{13,5},{2,10},{6,2},{... | collective-permute-start | bytes 49160 | tf_op jit(solution)/shard_map/ppermute | solution.py:140

commit v17 on v14

--- a/solution.py
+++ b/solution.py
@@ -153,8 +153,9 @@
 
 def operator_group(ka_count, pb_count):
     size = pb_count * ka_count
-    first = (pb_count - 1) * ka_count + ka_count // 2
-    return [(first - at) % size for at in range(size)]
+    cycle = [pb * ka_count + ka for ka in range(ka_count) for pb in range(pb_count)][::-1]
+    first = cycle.index((pb_count - 1) * ka_count + ka_count // 2)
+    return [cycle[(first + at) % size] for at in range(size)]
 
 
 def prepare_kernel(ka_count, pb_count, walkers, map_ref, count_ref, mask_ref, picks_ref):

time: 29.8 us -> 29.8 us (level)
  no operation moved by 1% of the time
where the time goes in v17:
time: 29.8 us; the launch traced here: 29.6 us
  starting transfers between devices  10.6 us (36%)
  blocking collectives  9.6 us (32%)
  Pallas kernels  4.2 us (14%)
  waiting for transfers between devices  3.17 us (11%)
  local copies, waits for them, and re-layouts  1.35 us (5%)
  between operations  0.71 us (2%)
    ppermute x6, starting transfers between devices, exchange(): return [array] + [lax.ppermute(array, axis, pairs) for pairs in rounds]  10.6 us
    all_to_all x1, blocking collectives, direct(): lax.all_to_all(blocks, ('pb', 'ka'), 0, 0, axis_index_groups=[group], til...  9.6 us
    ppermute x6, waiting for transfers between devices, exchange(): return [array] + [lax.ppermute(array, axis, pairs) for pairs in rounds]  3.17 us
    pallas_call x1, Pallas kernels, direct(): call(functools.partial(taylor_kernel, pb_count, float(pb_count * chol_col...  2.15 us
    unnamed x14, local copies, waits for them, and re-layouts  1.35 us
    pallas_call x1, Pallas kernels, direct(): call(functools.partial(operator_kernel, k_local), shape((ka_count * pb_co...  0.76 us
    pallas_call x1, Pallas kernels, direct(): call(functools.partial(prepare_kernel, ka_count, pb_count, walkers), (sha...  0.66 us
  transfers between devices with their start and end apart: 6, of which 4 were waited for; matrix products, arithmetic and copies ran while one was open for 0% of the time, Pallas kernels for 3%

profile of v17, /device:TPU:0, one launch (start us, length us, event | category | flops | bytes accessed | tf_op | source)
XLA Modules:
  0.0 29.6 jit_solution(2526512616306091899)
XLA Ops:
  0.6 0.0 copy-start.1
  0.6 0.0 copy-start.2
  0.7 0.0 copy-start.3
  0.7 0.0 copy-start
  0.7 0.0 copy-start.4
  0.7 4.1 %collective-permute-start.2 = (bf16[8,208]{1,0:T(8,128)(2,1)}, bf16[8,208]{1,0:T(8,128)(2,1)S(1)}, u32[]{:S(2)}, u32[]{:S(2)}) collective-permute-start(bf16[8,208]{1,0:T(8,128)(2,1)} %bitcast.15), channel_id=1, source_target_pairs={{12,0},{8,4},{4,12},{0,8},{13,1},{9,5},{5,13},{1,9},{14,2},{10,6},... | collective-permute-start | bytes 9992 | tf_op jit(solution)/shard_map/ppermute | solution.py:140
  4.8 1.1 %collective-permute-start.1 = (bf16[8,208]{1,0:T(8,128)(2,1)}, bf16[8,208]{1,0:T(8,128)(2,1)S(1)}, u32[]{:S(2)}, u32[]{:S(2)}) collective-permute-start(bf16[8,208]{1,0:T(8,128)(2,1)} %bitcast.16), channel_id=1, source_target_pairs={{12,4},{8,0},{0,12},{4,8},{13,5},{9,1},{1,13},{5,9},{14,6},{10,2},... | collective-permute-start | bytes 9992 | tf_op jit(solution)/shard_map/ppermute | solution.py:140
  5.8 0.5 %collective-permute-start = (bf16[8,208]{1,0:T(8,128)(2,1)}, bf16[8,208]{1,0:T(8,128)(2,1)S(1)}, u32[]{:S(2)}, u32[]{:S(2)}) collective-permute-start(bf16[8,208]{1,0:T(8,128)(2,1)} %bitcast.17), channel_id=1, source_target_pairs={{4,0},{12,8},{8,12},{0,4},{5,1},{13,9},{9,13},{1,5},{6,2},{14,10},... | collective-permute-start | bytes 9992 | tf_op jit(solution)/shard_map/ppermute | solution.py:140
  6.4 0.0 copy-start.5
  6.4 0.7 %copy-done.5 = s32[2,8]{1,0:T(2,128)S(1)} copy-done((s32[2,8]{1,0:T(2,128)S(1)}, s32[2,8]{1,0:T(2,128)}, u32[]{:S(2)}) %copy-start.5) | copy-done | bytes 88
  7.0 0.0 copy-start.6
  7.0 0.7 %copy-done.6 = s32[2]{0:T(128)S(1)} copy-done((s32[2]{0:T(128)S(1)}, s32[2]{0:T(128)}, u32[]{:S(2)}) %copy-start.6) | copy-done | bytes 32
  7.7 0.7 %shard_map.86 = (f32[8,256]{1,0:T(8,128)S(1)}, bf16[128,256]{1,0:T(8,128)(2,1)S(1)}) custom-call(s32[2,8]{1,0:T(2,128)S(1)} %copy-done.5, s32[2]{0:T(128)S(1)} %copy-done.6), custom_call_target="tpu_custom_call" | custom-call | flops 1000000000 | tf_op jit(solution)/shard_map/pallas_call | solution.py:393
  8.4 0.0 collective-permute-done.2.refs_3_
  8.4 1.1 %collective-permute-done.1.refs_2_ = bf16[8,208]{1,0:T(8,128)(2,1)S(1)} collective-permute-done((bf16[8,208]{1,0:T(8,128)(2,1)}, bf16[8,208]{1,0:T(8,128)(2,1)S(1)}, u32[]{:S(2)}, u32[]{:S(2)}) %collective-permute-start.1) | collective-permute-done | bytes 3360 | tf_op jit(solution)/shard_map/ppermute | solution.py:140
  9.5 0.2 collective-permute-done.refs_1_
  9.7 0.0 copy-done.1
  9.7 0.0 copy-done.2
  9.7 0.0 copy-done.3
  9.7 0.3 shard_map.87
  10.0 1.4 %collective-permute-start.5 = (f32[16,256]{1,0:T(8,128)S(1)}, f32[16,256]{1,0:T(8,128)S(1)}, u32[]{:S(2)}, u32[]{:S(2)}) collective-permute-start(f32[16,256]{1,0:T(8,128)S(1)} %get-tuple-element.9.refs_0_), channel_id=1, source_target_pairs={{0,4},{4,12},{8,0},{12,8},{1,5},{5,13},{9,1},{13,9},{2,6},{6,14},{... | collective-permute-start | bytes 49160 | tf_op jit(solution)/shard_map/ppermute | solution.py:140
  11.4 1.9 %collective-permute-start.4 = (f32[16,256]{1,0:T(8,128)S(1)}, f32[16,256]{1,0:T(8,128)S(1)}, u32[]{:S(2)}, u32[]{:S(2)}) collective-permute-start(f32[16,256]{1,0:T(8,128)S(1)} %get-tuple-element.9.refs_0_), channel_id=1, source_target_pairs={{0,12},{12,0},{4,8},{8,4},{1,13},{13,1},{5,9},{9,5},{2,14},{14,2},... | collective-permute-start | bytes 49160 | tf_op jit(solution)/shard_map/ppermute | solution.py:140
  13.3 1.6 %collective-permute-start.3 = (f32[16,256]{1,0:T(8,128)S(1)}, f32[16,256]{1,0:T(8,128)S(1)}, u32[]{:S(2)}, u32[]{:S(2)}) collective-permute-start(f32[16,256]{1,0:T(8,128)S(1)} %get-tuple-element.9.refs_0_), channel_id=1, source_target_pairs={{0,8},{4,0},{8,12},{12,4},{1,9},{5,1},{9,13},{13,5},{2,10},{6,2},{... | collective-permute-start | bytes 49160 | tf_op jit(solution)/shard_map/ppermute | solution.py:140
  14.9 0.4 %shard_map.88.refs_6_ = f32[4,128]{1,0:T(4,128)S(1)} custom-call(f32[2,8,104]{2,1,0:T(8,128)S(1)} %get-tuple-element.10.own_ref, bf16[2,2,104,256]{3,2,1,0:T(8,128)(2,1)S(1)} %bitcast.12, f32[8,256]{1,0:T(8,128)S(1)} %get-tuple-element.8.refs_6_.mask_ref.refs_5_), custom_call_target="tpu_custom_call" | custom-call | tf_op jit(solution)/shard_map/pallas_call | solution.py:409
  15.2 0.0 collective-permute-done.5.refs_3_
  15.2 1.7 %collective-permute-done.4.refs_2_ = f32[16,256]{1,0:T(8,128)S(1)} collective-permute-done((f32[16,256]{1,0:T(8,128)S(1)}, f32[16,256]{1,0:T(8,128)S(1)}, u32[]{:S(2)}, u32[]{:S(2)}) %collective-permute-start.4) | collective-permute-done | bytes 16416 | tf_op jit(solution)/shard_map/ppermute | solution.py:140
  16.9 0.2 collective-permute-done.3.refs_1_
  17.1 0.0 copy-done
  17.1 0.0 copy-done.4
  17.1 0.8 %shard_map.89 = bf16[8,16,768]{2,1,0:T(8,128)(2,1)S(1)} custom-call(f32[16,256]{1,0:T(8,128)S(1)} %get-tuple-element.9.refs_0_, f32[16,256]{1,0:T(8,128)S(1)} %collective-permute-done.3.refs_1_, f32[16,256]{1,0:T(8,128)S(1)} %collective-permute-done.4.refs_2_, f32[16,256]{1,0:T(8,128)S(1)} %collective-permute-done.5.refs_3_, f32[4,256]{1,0:T(4,128)S(1)} %bitcast.19, ...), custom_call_target="tpu_custom_call" | custom-call | tf_op jit(solution)/shard_map/pallas_call | solution.py:415
  17.9 9.6 %all_to_all.5.blocks_ref = bf16[8,16,768]{2,1,0:T(8,128)(2,1)S(1)} all-to-all(bf16[8,16,768]{2,1,0:T(8,128)(2,1)S(1)} %shard_map.89), channel_id=1, replica_groups={{10,8,6,4,2,0,14,12},{11,9,7,5,3,1,15,13},{26,24,22,20,18,16,30,28},{27..., dimensions={0} | all-to-all | bytes 393216 | tf_op jit(solution)/shard_map/all_to_all | solution.py:422
  27.5 2.1 %shard_map.90 = (f32[2,4,208]{2,1,0:T(4,128)}, f32[1,1]{1,0:T(1,128)}) custom-call(bf16[8,16,768]{2,1,0:T(8,128)(2,1)S(1)} %all_to_all.5.blocks_ref, f32[16,256]{1,0:T(8,128)S(1)} %get-tuple-element.9.refs_0_, f32[16,256]{1,0:T(8,128)S(1)} %collective-permute-done.3.refs_1_, f32[16,256]{1,0:T(8,128)S(1)} %collective-permute-done.4.refs_2_, ...), custom_call_target="tpu_custom_call" | custom-call | tf_op jit(solution)/shard_map/pallas_call | solution.py:425
Async XLA Ops:
  0.6 9.0 %copy-start.1 = (bf16[1,2,2,104,256]{4,3,2,1,0:T(8,128)(2,1)S(1)}, bf16[1,2,2,104,256]{4,3,2,1,0:T(8,128)(2,1)}, u32[]{:S(2)}) copy-start(bf16[1,2,2,104,256]{4,3,2,1,0:T(8,128)(2,1)} %param.10) | copy-start | bytes 638980
  0.6 9.0 %copy-start.2 = (f32[1,2,4,208]{3,2,1,0:T(4,128)S(1)}, f32[1,2,4,208]{3,2,1,0:T(4,128)}, u32[]{:S(2)}) copy-start(f32[1,2,4,208]{3,2,1,0:T(4,128)} %param.9) | copy-start | bytes 19972
  0.7 9.0 %copy-start.3 = (bf16[1,1,1,8,208]{4,3,2,1,0:T(8,128)(2,1)S(1)}, bf16[1,1,1,8,208]{4,3,2,1,0:T(8,128)(2,1)}, u32[]{:S(2)}) copy-start(bf16[1,1,1,8,208]{4,3,2,1,0:T(8,128)(2,1)} %param.7) | copy-start | bytes 9988
  0.7 16.4 %copy-start = (bf16[1,2,2,676,256]{4,2,3,1,0:T(2,128)(2,1)S(1)}, bf16[1,2,2,676,256]{4,2,3,1,0:T(2,128)(2,1)}, u32[]{:S(2)}) copy-start(bf16[1,2,2,676,256]{4,2,3,1,0:T(2,128)(2,1)} %param.11) | copy-start | bytes 4153348
  0.7 16.4 %copy-start.4 = (f32[1,1,4,256]{3,2,1,0:T(4,128)S(1)}, f32[1,1,4,256]{3,2,1,0:T(4,128)}, u32[]{:S(2)}) copy-start(f32[1,1,4,256]{3,2,1,0:T(4,128)} %param.8) | copy-start | bytes 12292
  0.7 7.7 %collective-permute-start.2 = (bf16[8,208]{1,0:T(8,128)(2,1)}, bf16[8,208]{1,0:T(8,128)(2,1)S(1)}, u32[]{:S(2)}, u32[]{:S(2)}) collective-permute-start(bf16[8,208]{1,0:T(8,128)(2,1)} %bitcast.15), channel_id=1, source_target_pairs={{12,0},{8,4},{4,12},{0,8},{13,1},{9,5},{5,13},{1,9},{14,2},{10,6},... | collective-permute-start | bytes 9992 | tf_op jit(solution)/shard_map/ppermute | solution.py:140
  4.8 4.7 %collective-permute-start.1 = (bf16[8,208]{1,0:T(8,128)(2,1)}, bf16[8,208]{1,0:T(8,128)(2,1)S(1)}, u32[]{:S(2)}, u32[]{:S(2)}) collective-permute-start(bf16[8,208]{1,0:T(8,128)(2,1)} %bitcast.16), channel_id=1, source_target_pairs={{12,4},{8,0},{0,12},{4,8},{13,5},{9,1},{1,13},{5,9},{14,6},{10,2},... | collective-permute-start | bytes 9992 | tf_op jit(solution)/shard_map/ppermute | solution.py:140
  5.8 3.8 %collective-permute-start = (bf16[8,208]{1,0:T(8,128)(2,1)}, bf16[8,208]{1,0:T(8,128)(2,1)S(1)}, u32[]{:S(2)}, u32[]{:S(2)}) collective-permute-start(bf16[8,208]{1,0:T(8,128)(2,1)} %bitcast.17), channel_id=1, source_target_pairs={{4,0},{12,8},{8,12},{0,4},{5,1},{13,9},{9,13},{1,5},{6,2},{14,10},... | collective-permute-start | bytes 9992 | tf_op jit(solution)/shard_map/ppermute | solution.py:140
  6.4 0.7 %copy-start.5 = (s32[2,8]{1,0:T(2,128)S(1)}, s32[2,8]{1,0:T(2,128)}, u32[]{:S(2)}) copy-start(s32[2,8]{1,0:T(2,128)} %map_ref.1) | copy-start | bytes 196
  7.0 0.7 %copy-start.6 = (s32[2]{0:T(128)S(1)}, s32[2]{0:T(128)}, u32[]{:S(2)}) copy-start(s32[2]{0:T(128)} %count_ref.1) | copy-start | bytes 28
  10.0 5.3 %collective-permute-start.5 = (f32[16,256]{1,0:T(8,128)S(1)}, f32[16,256]{1,0:T(8,128)S(1)}, u32[]{:S(2)}, u32[]{:S(2)}) collective-permute-start(f32[16,256]{1,0:T(8,128)S(1)} %get-tuple-element.9.refs_0_), channel_id=1, source_target_pairs={{0,4},{4,12},{8,0},{12,8},{1,5},{5,13},{9,1},{13,9},{2,6},{6,14},{... | collective-permute-start | bytes 49160 | tf_op jit(solution)/shard_map/ppermute | solution.py:140
  11.4 5.5 %collective-permute-start.4 = (f32[16,256]{1,0:T(8,128)S(1)}, f32[16,256]{1,0:T(8,128)S(1)}, u32[]{:S(2)}, u32[]{:S(2)}) collective-permute-start(f32[16,256]{1,0:T(8,128)S(1)} %get-tuple-element.9.refs_0_), channel_id=1, source_target_pairs={{0,12},{12,0},{4,8},{8,4},{1,13},{13,1},{5,9},{9,5},{2,14},{14,2},... | collective-permute-start | bytes 49160 | tf_op jit(solution)/shard_map/ppermute | solution.py:140
  13.3 3.8 %collective-permute-start.3 = (f32[16,256]{1,0:T(8,128)S(1)}, f32[16,256]{1,0:T(8,128)S(1)}, u32[]{:S(2)}, u32[]{:S(2)}) collective-permute-start(f32[16,256]{1,0:T(8,128)S(1)} %get-tuple-element.9.refs_0_), channel_id=1, source_target_pairs={{0,8},{4,0},{8,12},{12,4},{1,9},{5,1},{9,13},{13,5},{2,10},{6,2},{... | collective-permute-start | bytes 49160 | tf_op jit(solution)/shard_map/ppermute | solution.py:140

commit v18 on v15

--- a/solution.py
+++ b/solution.py
@@ -267,8 +267,7 @@
 
 
 def operator_kernel(k_local, *refs):
-    *parts, fields_ref, mask_ref, exchange_ref, chol_ref, picks_ref = refs[:-5]
-    out_ref, first_ref, products, turned_ref, term = refs[-5:]
+    *parts, fields_ref, mask_ref, exchange_ref, chol_ref, out_ref, products, turned_ref = refs
     walkers, columns = fields_ref.shape
     bias = parts[0][: 2 * walkers]
     for part in parts[1:]:
@@ -284,16 +283,6 @@
     shift_re = (fields_ref[...] - BIAS_STEP * bias_re) * kept
     shift_im = -BIAS_STEP * bias_im * kept
     span = k_local * walkers
-    pair = NOCC * M
-    term[...] = jnp.zeros_like(term)
-    for source, part in zip(origins("ka", BIAS_ROUNDS), parts):
-        start = pl.multiple_of(source * (2 * span), 2 * span)
-        window = part[2 * walkers :]
-        term[pl.ds(start, span), :pair] = window[:, :pair]
-        term[pl.ds(start + span, span), :pair] = window[:, pair : 2 * pair]
-    first_ref[...] = jnp.dot(
-        term[...].T.astype(BF16), picks_ref[...], preferred_element_type=F32
-    )
     weights = []
     for k in range(k_local):
         before, after = k * walkers, span - (k + 1) * walkers
@@ -337,17 +326,27 @@
             out_ref[copy, :, at : at + LANES] = block.astype(BF16)
 
 
-def taylor_kernel(
-    pb_count, normalizer, blocks_ref, first_ref, picks_ref, fold_ref, own_picks_ref, orbitals_ref,
-    out_ref, energy_ref, turned, folded, picked, term, kept,
-):
+def taylor_kernel(pb_count, normalizer, blocks_ref, *refs):
+    *windows, picks_ref, fold_ref, own_picks_ref, orbitals_ref = refs[:-7]
+    out_ref, energy_ref, turned, folded, picked, term, kept = refs[-7:]
     pairs = M * M
+    pair = NOCC * M
     k_local, walkers, _ = out_ref.shape
     span = k_local * walkers
     ka_pos = lax.axis_index("ka")
+    picks = picks_ref[...]
+    term[...] = jnp.zeros_like(term)
+    for source, window_ref in zip(origins("ka", BIAS_ROUNDS), windows):
+        start = pl.multiple_of(source * (2 * span), 2 * span)
+        window = window_ref[window_ref.shape[0] - span :]
+        term[pl.ds(start, span), :pair] = window[:, :pair]
+        term[pl.ds(start + span, span), :pair] = window[:, pair : 2 * pair]
+    picked[...] = jnp.dot(term[...].T.astype(BF16), picks, preferred_element_type=F32)
     count, _, width = blocks_ref.shape
     group = operator_group(count // pb_count, pb_count)
     places = [group.index(n) for n in range(count)]
+    turned[width:] = jnp.zeros((turned.shape[0] - width, LANES), F32)
+    folded[width:] = jnp.zeros((folded.shape[0] - width, LANES), F32)
     for at in range(0, width, LANES):
         tile = jnp.concatenate([blocks_ref[n, :, at : at + LANES] for n in places], axis=0).T
         turned[at : at + LANES] = tile.astype(F32)
@@ -357,7 +356,7 @@
     shares = jnp.where(lax.rem(lane, 2 * span) == ka_pos, shares, 0.0)
     shares = jnp.sum(jnp.sum(shares, axis=0, keepdims=True), axis=1, keepdims=True)
     energy_ref[...] = shares / normalizer
-    lane = lax.broadcasted_iota(jnp.int32, (M, LANES), 1)
+    lane = lax.broadcasted_iota(jnp.int32, (ROWS, LANES), 1)
     imaginary = lax.rem(lane, 2 * span) >= span
 
     def joined(straight, crossed):
@@ -366,46 +365,36 @@
 
     sums = [None] * NOCC
     for degree in range(1, TAYLOR):
-        source, stride = (first_ref, M) if degree == 1 else (picked, ROWS)
-        straight = [jnp.zeros((M, LANES), F32) for _ in range(NOCC)]
-        crossed = [jnp.zeros((M, LANES), F32) for _ in range(NOCC)]
+        stride = M if degree == 1 else ROWS
+        straight = [jnp.zeros((ROWS, LANES), F32) for _ in range(NOCC)]
+        crossed = [jnp.zeros((ROWS, LANES), F32) for _ in range(NOCC)]
         for c in range(M):
-            column = turned[pl.ds(c, M, stride=M), :]
+            column = turned[pl.ds(c, ROWS, stride=M), :]
             for i in range(NOCC):
                 at = i * stride + c
-                straight[i] += column * source[at : at + 1, :LANES]
-                crossed[i] += column * source[at : at + 1, LANES:]
+                straight[i] += column * picked[at : at + 1, :LANES]
+                crossed[i] += column * picked[at : at + 1, LANES:]
+        currents = []
         for i in range(NOCC):
             applied = joined(straight[i], crossed[i])
             applied = applied + pltpu.roll(applied, LANES // pb_count, 1)
-            current = applied * (1.0 / degree)
-            sums[i] = current if degree == 1 else sums[i] + current
-            at = i * ROWS
-            term[at : at + M] = current
-            if degree == 1:
-                term[at + M : at + ROWS] = jnp.zeros((ROWS - M, LANES), F32)
+            currents.append(applied * (1.0 / degree))
+            sums[i] = currents[i] if degree == 1 else sums[i] + currents[i]
         if degree < TAYLOR - 1:
-            picked[...] = jnp.dot(
-                term[...].astype(BF16), picks_ref[...], preferred_element_type=F32
-            )
-    wide = jnp.concatenate([term[i * ROWS : (i + 1) * ROWS] for i in range(NOCC)], axis=1)
-    picked[:ROWS] = jnp.dot(wide.astype(BF16), own_picks_ref[...], preferred_element_type=F32)
-    for i in range(NOCC):
-        kept[i * ROWS : i * ROWS + M] = sums[i]
-        kept[i * ROWS + M : (i + 1) * ROWS] = jnp.zeros((ROWS - M, LANES), F32)
-    turned[:LANES] = kept[...].T
-    sums = turned[pl.ds(pl.multiple_of(ka_pos * (2 * span), 2 * span), 2 * span), :]
-    straight = [jnp.zeros((M, LANES), F32) for _ in range(2)]
-    crossed = [jnp.zeros((M, LANES), F32) for _ in range(2)]
+            rows = jnp.concatenate(currents, axis=0).astype(BF16)
+            picked[...] = jnp.dot(rows, picks, preferred_element_type=F32)
+    wide = jnp.concatenate(currents, axis=1).astype(BF16)
+    picked[:ROWS] = jnp.dot(wide, own_picks_ref[...], preferred_element_type=F32)
+    kept[...] = jnp.concatenate(sums, axis=0).T
+    sums = kept[pl.ds(pl.multiple_of(ka_pos * (2 * span), 2 * span), 2 * span), :]
+    straight = [jnp.zeros((ROWS, LANES), F32) for _ in range(2)]
+    crossed = [jnp.zeros((ROWS, LANES), F32) for _ in range(2)]
     for c in range(M):
-        column = folded[pl.ds(c, M, stride=M), :]
+        column = folded[pl.ds(c, ROWS, stride=M), :]
         straight[c % 2] += column * picked[c : c + 1, :LANES]
         crossed[c % 2] += column * picked[c : c + 1, LANES:]
     applied = joined(straight[0] + straight[1], crossed[0] + crossed[1])
-    applied = (applied + pltpu.roll(applied, LANES - 2 * span, 1)) * (1.0 / TAYLOR)
-    kept[:M] = applied
-    kept[M:ROWS] = jnp.zeros((ROWS - M, LANES), F32)
-    last = kept[:ROWS].T
+    last = ((applied + pltpu.roll(applied, LANES - 2 * span, 1)) * (1.0 / TAYLOR)).T
     last = jnp.concatenate(
         [last[i * ROWS : i * ROWS + 2 * span] for i in range(NOCC)], axis=1
     )
@@ -478,19 +467,12 @@
         operands=4,
     )(own, half, mask, own_lanes)
     width = -(-(M * M + 3) // LANES) * LANES
-    blocks, first = call(
+    blocks = call(
         functools.partial(operator_kernel, k_local),
-        (
-            shape((ka_count * pb_count, 2 * span, width), BF16),
-            shape((LANES, 2 * LANES), F32),
-        ),
-        [
-            pltpu.VMEM((2 * M * M * tiles, LANES), F32),
-            pltpu.VMEM((width, LANES), F32),
-            pltpu.VMEM((LANES, LANES), F32),
-        ],
-        operands=len(parts) + 5,
-    )(*parts, own_fields, mask, shares, full, picks)
+        shape((ka_count * pb_count, 2 * span, width), BF16),
+        [pltpu.VMEM((2 * M * M * tiles, LANES), F32), pltpu.VMEM((width, LANES), F32)],
+        operands=len(parts) + 4,
+    )(*parts, own_fields, mask, shares, full)
     group = operator_group(ka_count, pb_count)
     blocks = lax.all_to_all(
         blocks, ("pb", "ka"), 0, 0, axis_index_groups=[group], tiled=True
@@ -499,14 +481,14 @@
         functools.partial(taylor_kernel, pb_count, float(pb_count * chol_cols)),
         (shape((k_local, walkers, 2 * pair_width), F32), shape((1, 1), F32)),
         [
-            pltpu.VMEM((width, LANES), F32),
-            pltpu.VMEM((width, LANES), F32),
+            pltpu.VMEM((ROWS * M, LANES), F32),
+            pltpu.VMEM((ROWS * M, LANES), F32),
             pltpu.VMEM((NOCC * ROWS, 2 * LANES), F32),
-            pltpu.VMEM((NOCC * ROWS, LANES), F32),
-            pltpu.VMEM((NOCC * ROWS, LANES), F32),
+            pltpu.VMEM((LANES, LANES), F32),
+            pltpu.VMEM((LANES, LANES), F32),
         ],
-        operands=6,
-    )(blocks, first, picks, fold, own_picks, own_orbitals)
+        operands=len(parts) + 5,
+    )(blocks, *parts, picks, fold, own_picks, own_orbitals)
     return (propagated[None], energy)
 
 

time: 29.9 us -> 29.9 us (level)
  no operation moved by 1% of the time
where the time goes in v18:
time: 29.9 us; the launch traced here: 29.7 us
  starting transfers between devices  10.6 us (35%)
  blocking collectives  9.62 us (32%)
  Pallas kernels  4.31 us (14%)
  waiting for transfers between devices  3.16 us (11%)
  local copies, waits for them, and re-layouts  1.35 us (5%)
  between operations  0.71 us (2%)
    ppermute x6, starting transfers between devices, exchange(): return [array] + [lax.ppermute(array, axis, pairs) for pairs in rounds]  10.6 us
    all_to_all x1, blocking collectives, direct(): lax.all_to_all(blocks, ('pb', 'ka'), 0, 0, axis_index_groups=[group], til...  9.62 us
    ppermute x6, waiting for transfers between devices, exchange(): return [array] + [lax.ppermute(array, axis, pairs) for pairs in rounds]  3.16 us
    pallas_call x1, Pallas kernels, direct(): call(functools.partial(taylor_kernel, pb_count, float(pb_count * chol_col...  2.24 us
    unnamed x14, local copies, waits for them, and re-layouts  1.35 us
    pallas_call x1, Pallas kernels, direct(): call(functools.partial(operator_kernel, k_local), shape((ka_count * pb_co...  0.76 us
    pallas_call x1, Pallas kernels, direct(): call(functools.partial(prepare_kernel, ka_count, pb_count, walkers), (sha...  0.67 us
  transfers between devices with their start and end apart: 6, of which 4 were waited for; matrix products, arithmetic and copies ran while one was open for 0% of the time, Pallas kernels for 3%

profile of v18, /device:TPU:0, one launch (start us, length us, event | category | flops | bytes accessed | tf_op | source)
XLA Modules:
  0.0 29.7 jit_solution(12349783725138059348)
XLA Ops:
  0.6 0.0 copy-start.1
  0.6 0.0 copy-start.2
  0.7 0.0 copy-start.3
  0.7 0.0 copy-start
  0.7 0.0 copy-start.4
  0.7 4.1 %collective-permute-start.2 = (bf16[8,208]{1,0:T(8,128)(2,1)}, bf16[8,208]{1,0:T(8,128)(2,1)S(1)}, u32[]{:S(2)}, u32[]{:S(2)}) collective-permute-start(bf16[8,208]{1,0:T(8,128)(2,1)} %bitcast.15), channel_id=1, source_target_pairs={{12,0},{8,4},{4,12},{0,8},{13,1},{9,5},{5,13},{1,9},{14,2},{10,6},... | collective-permute-start | bytes 9992 | tf_op jit(solution)/shard_map/ppermute | solution.py:140
  4.8 1.1 %collective-permute-start.1 = (bf16[8,208]{1,0:T(8,128)(2,1)}, bf16[8,208]{1,0:T(8,128)(2,1)S(1)}, u32[]{:S(2)}, u32[]{:S(2)}) collective-permute-start(bf16[8,208]{1,0:T(8,128)(2,1)} %bitcast.16), channel_id=1, source_target_pairs={{12,4},{8,0},{0,12},{4,8},{13,5},{9,1},{1,13},{5,9},{14,6},{10,2},... | collective-permute-start | bytes 9992 | tf_op jit(solution)/shard_map/ppermute | solution.py:140
  5.8 0.5 %collective-permute-start = (bf16[8,208]{1,0:T(8,128)(2,1)}, bf16[8,208]{1,0:T(8,128)(2,1)S(1)}, u32[]{:S(2)}, u32[]{:S(2)}) collective-permute-start(bf16[8,208]{1,0:T(8,128)(2,1)} %bitcast.17), channel_id=1, source_target_pairs={{4,0},{12,8},{8,12},{0,4},{5,1},{13,9},{9,13},{1,5},{6,2},{14,10},... | collective-permute-start | bytes 9992 | tf_op jit(solution)/shard_map/ppermute | solution.py:140
  6.4 0.0 copy-start.5
  6.4 0.7 %copy-done.5 = s32[2,8]{1,0:T(2,128)S(1)} copy-done((s32[2,8]{1,0:T(2,128)S(1)}, s32[2,8]{1,0:T(2,128)}, u32[]{:S(2)}) %copy-start.5) | copy-done | bytes 88
  7.0 0.0 copy-start.6
  7.0 0.7 %copy-done.6 = s32[2]{0:T(128)S(1)} copy-done((s32[2]{0:T(128)S(1)}, s32[2]{0:T(128)}, u32[]{:S(2)}) %copy-start.6) | copy-done | bytes 32
  7.7 0.7 %shard_map.86 = (f32[8,256]{1,0:T(8,128)S(1)}, bf16[128,256]{1,0:T(8,128)(2,1)S(1)}, s32[8,128]{1,0:T(8,128)S(1)}) custom-call(s32[2,8]{1,0:T(2,128)S(1)} %copy-done.5, s32[2]{0:T(128)S(1)} %copy-done.6), custom_call_target="tpu_custom_call" | custom-call | flops 1000000000 | tf_op jit(solution)/shard_map/pallas_call | solution.py:440
  8.4 0.0 collective-permute-done.2.refs_3_
  8.4 1.1 %collective-permute-done.1.refs_2_ = bf16[8,208]{1,0:T(8,128)(2,1)S(1)} collective-permute-done((bf16[8,208]{1,0:T(8,128)(2,1)}, bf16[8,208]{1,0:T(8,128)(2,1)S(1)}, u32[]{:S(2)}, u32[]{:S(2)}) %collective-permute-start.1) | collective-permute-done | bytes 3360 | tf_op jit(solution)/shard_map/ppermute | solution.py:140
  9.5 0.2 collective-permute-done.refs_1_
  9.7 0.0 copy-done.1
  9.7 0.0 copy-done.2
  9.7 0.0 copy-done.3
  9.7 0.3 shard_map.87
  10.0 1.4 %collective-permute-start.5 = (f32[16,256]{1,0:T(8,128)S(1)}, f32[16,256]{1,0:T(8,128)S(1)}, u32[]{:S(2)}, u32[]{:S(2)}) collective-permute-start(f32[16,256]{1,0:T(8,128)S(1)} %get-tuple-element.13.refs_0_), channel_id=1, source_target_pairs={{0,4},{4,12},{8,0},{12,8},{1,5},{5,13},{9,1},{13,9},{2,6},{6,14},{... | collective-permute-start | bytes 49160 | tf_op jit(solution)/shard_map/ppermute | solution.py:140
  11.4 1.9 %collective-permute-start.4 = (f32[16,256]{1,0:T(8,128)S(1)}, f32[16,256]{1,0:T(8,128)S(1)}, u32[]{:S(2)}, u32[]{:S(2)}) collective-permute-start(f32[16,256]{1,0:T(8,128)S(1)} %get-tuple-element.13.refs_0_), channel_id=1, source_target_pairs={{0,12},{12,0},{4,8},{8,4},{1,13},{13,1},{5,9},{9,5},{2,14},{14,2},... | collective-permute-start | bytes 49160 | tf_op jit(solution)/shard_map/ppermute | solution.py:140
  13.3 1.6 %collective-permute-start.3 = (f32[16,256]{1,0:T(8,128)S(1)}, f32[16,256]{1,0:T(8,128)S(1)}, u32[]{:S(2)}, u32[]{:S(2)}) collective-permute-start(f32[16,256]{1,0:T(8,128)S(1)} %get-tuple-element.13.refs_0_), channel_id=1, source_target_pairs={{0,8},{4,0},{8,12},{12,4},{1,9},{5,1},{9,13},{13,5},{2,10},{6,2},{... | collective-permute-start | bytes 49160 | tf_op jit(solution)/shard_map/ppermute | solution.py:140
  14.9 0.4 %shard_map.88 = (f32[4,128]{1,0:T(4,128)S(1)}, bf16[128,128]{1,0:T(8,128)(2,1)S(1)}, bf16[512,256]{1,0:T(8,128)(2,1)S(1)}) custom-call(f32[2,8,104]{2,1,0:T(8,128)S(1)} %get-tuple-element.14.own_ref, bf16[2,2,104,256]{3,2,1,0:T(8,128)(2,1)S(1)} %bitcast.12, f32[8,256]{1,0:T(8,128)S(1)} %get-tuple-element.12.refs_6_.mask_ref.refs_5_, ...), custom_call_target="tpu_custom_call" | custom-call | tf_op jit(solution)/shard_map/pallas_call | solution.py:460
  15.2 0.0 collective-permute-done.5.refs_3_
  15.2 1.7 %collective-permute-done.4.refs_2_ = f32[16,256]{1,0:T(8,128)S(1)} collective-permute-done((f32[16,256]{1,0:T(8,128)S(1)}, f32[16,256]{1,0:T(8,128)S(1)}, u32[]{:S(2)}, u32[]{:S(2)}) %collective-permute-start.4) | collective-permute-done | bytes 16416 | tf_op jit(solution)/shard_map/ppermute | solution.py:140
  16.9 0.2 collective-permute-done.3.refs_1_
  17.1 0.0 copy-done
  17.1 0.0 copy-done.4
  17.1 0.8 %shard_map.89 = bf16[8,16,768]{2,1,0:T(8,128)(2,1)S(1)} custom-call(f32[16,256]{1,0:T(8,128)S(1)} %get-tuple-element.13.refs_0_, f32[16,256]{1,0:T(8,128)S(1)} %collective-permute-done.3.refs_1_, f32[16,256]{1,0:T(8,128)S(1)} %collective-permute-done.4.refs_2_, f32[16,256]{1,0:T(8,128)S(1)} %collective-permute-done.5.refs_3_, f32[4,256]{1,0:T(4,128)S(1)} %bitcast.19, ...), custom_call_target="tpu_custom_call" | custom-call | tf_op jit(solution)/shard_map/pallas_call | solution.py:470
  17.9 9.6 %all_to_all.5.blocks_ref = bf16[8,16,768]{2,1,0:T(8,128)(2,1)S(1)} all-to-all(bf16[8,16,768]{2,1,0:T(8,128)(2,1)S(1)} %shard_map.89), channel_id=1, replica_groups={{10,14,6,2,12,8,4,0},{11,15,7,3,13,9,5,1},{26,30,22,18,28,24,20,16},{27..., dimensions={0} | all-to-all | bytes 393216 | tf_op jit(solution)/shard_map/all_to_all | solution.py:477
  27.5 2.2 %shard_map.90 = (f32[2,4,208]{2,1,0:T(4,128)}, f32[1,1]{1,0:T(1,128)}) custom-call(bf16[8,16,768]{2,1,0:T(8,128)(2,1)S(1)} %all_to_all.5.blocks_ref, f32[16,256]{1,0:T(8,128)S(1)} %get-tuple-element.13.refs_0_, f32[16,256]{1,0:T(8,128)S(1)} %collective-permute-done.3.refs_1_, f32[16,256]{1,0:T(8,128)S(1)} %collective-permute-done.4.refs_2_, ...), custom_call_target="tpu_custom_call" | custom-call | tf_op jit(solution)/shard_map/pallas_call | solution.py:480
Async XLA Ops:
  0.6 9.0 %copy-start.1 = (bf16[1,2,2,104,256]{4,3,2,1,0:T(8,128)(2,1)S(1)}, bf16[1,2,2,104,256]{4,3,2,1,0:T(8,128)(2,1)}, u32[]{:S(2)}) copy-start(bf16[1,2,2,104,256]{4,3,2,1,0:T(8,128)(2,1)} %param.10) | copy-start | bytes 638980
  0.6 9.0 %copy-start.2 = (f32[1,2,4,208]{3,2,1,0:T(4,128)S(1)}, f32[1,2,4,208]{3,2,1,0:T(4,128)}, u32[]{:S(2)}) copy-start(f32[1,2,4,208]{3,2,1,0:T(4,128)} %param.9) | copy-start | bytes 19972
  0.7 9.0 %copy-start.3 = (bf16[1,1,1,8,208]{4,3,2,1,0:T(8,128)(2,1)S(1)}, bf16[1,1,1,8,208]{4,3,2,1,0:T(8,128)(2,1)}, u32[]{:S(2)}) copy-start(bf16[1,1,1,8,208]{4,3,2,1,0:T(8,128)(2,1)} %param.7) | copy-start | bytes 9988
  0.7 16.4 %copy-start = (bf16[1,2,2,676,256]{4,2,3,1,0:T(2,128)(2,1)S(1)}, bf16[1,2,2,676,256]{4,2,3,1,0:T(2,128)(2,1)}, u32[]{:S(2)}) copy-start(bf16[1,2,2,676,256]{4,2,3,1,0:T(2,128)(2,1)} %param.11) | copy-start | bytes 4153348
  0.7 16.4 %copy-start.4 = (f32[1,1,4,256]{3,2,1,0:T(4,128)S(1)}, f32[1,1,4,256]{3,2,1,0:T(4,128)}, u32[]{:S(2)}) copy-start(f32[1,1,4,256]{3,2,1,0:T(4,128)} %param.8) | copy-start | bytes 12292
  0.7 7.7 %collective-permute-start.2 = (bf16[8,208]{1,0:T(8,128)(2,1)}, bf16[8,208]{1,0:T(8,128)(2,1)S(1)}, u32[]{:S(2)}, u32[]{:S(2)}) collective-permute-start(bf16[8,208]{1,0:T(8,128)(2,1)} %bitcast.15), channel_id=1, source_target_pairs={{12,0},{8,4},{4,12},{0,8},{13,1},{9,5},{5,13},{1,9},{14,2},{10,6},... | collective-permute-start | bytes 9992 | tf_op jit(solution)/shard_map/ppermute | solution.py:140
  4.8 4.7 %collective-permute-start.1 = (bf16[8,208]{1,0:T(8,128)(2,1)}, bf16[8,208]{1,0:T(8,128)(2,1)S(1)}, u32[]{:S(2)}, u32[]{:S(2)}) collective-permute-start(bf16[8,208]{1,0:T(8,128)(2,1)} %bitcast.16), channel_id=1, source_target_pairs={{12,4},{8,0},{0,12},{4,8},{13,5},{9,1},{1,13},{5,9},{14,6},{10,2},... | collective-permute-start | bytes 9992 | tf_op jit(solution)/shard_map/ppermute | solution.py:140
  5.8 3.8 %collective-permute-start = (bf16[8,208]{1,0:T(8,128)(2,1)}, bf16[8,208]{1,0:T(8,128)(2,1)S(1)}, u32[]{:S(2)}, u32[]{:S(2)}) collective-permute-start(bf16[8,208]{1,0:T(8,128)(2,1)} %bitcast.17), channel_id=1, source_target_pairs={{4,0},{12,8},{8,12},{0,4},{5,1},{13,9},{9,13},{1,5},{6,2},{14,10},... | collective-permute-start | bytes 9992 | tf_op jit(solution)/shard_map/ppermute | solution.py:140
  6.4 0.7 %copy-start.5 = (s32[2,8]{1,0:T(2,128)S(1)}, s32[2,8]{1,0:T(2,128)}, u32[]{:S(2)}) copy-start(s32[2,8]{1,0:T(2,128)} %map_ref.1) | copy-start | bytes 196
  7.0 0.7 %copy-start.6 = (s32[2]{0:T(128)S(1)}, s32[2]{0:T(128)}, u32[]{:S(2)}) copy-start(s32[2]{0:T(128)} %count_ref.1) | copy-start | bytes 28
  10.0 5.3 %collective-permute-start.5 = (f32[16,256]{1,0:T(8,128)S(1)}, f32[16,256]{1,0:T(8,128)S(1)}, u32[]{:S(2)}, u32[]{:S(2)}) collective-permute-start(f32[16,256]{1,0:T(8,128)S(1)} %get-tuple-element.13.refs_0_), channel_id=1, source_target_pairs={{0,4},{4,12},{8,0},{12,8},{1,5},{5,13},{9,1},{13,9},{2,6},{6,14},{... | collective-permute-start | bytes 49160 | tf_op jit(solution)/shard_map/ppermute | solution.py:140
  11.4 5.5 %collective-permute-start.4 = (f32[16,256]{1,0:T(8,128)S(1)}, f32[16,256]{1,0:T(8,128)S(1)}, u32[]{:S(2)}, u32[]{:S(2)}) collective-permute-start(f32[16,256]{1,0:T(8,128)S(1)} %get-tuple-element.13.refs_0_), channel_id=1, source_target_pairs={{0,12},{12,0},{4,8},{8,4},{1,13},{13,1},{5,9},{9,5},{2,14},{14,2},... | collective-permute-start | bytes 49160 | tf_op jit(solution)/shard_map/ppermute | solution.py:140
  13.3 3.8 %collective-permute-start.3 = (f32[16,256]{1,0:T(8,128)S(1)}, f32[16,256]{1,0:T(8,128)S(1)}, u32[]{:S(2)}, u32[]{:S(2)}) collective-permute-start(f32[16,256]{1,0:T(8,128)S(1)} %get-tuple-element.13.refs_0_), channel_id=1, source_target_pairs={{0,8},{4,0},{8,12},{12,4},{1,9},{5,1},{9,13},{13,5},{2,10},{6,2},{... | collective-permute-start | bytes 49160 | tf_op jit(solution)/shard_map/ppermute | solution.py:140

commit v19 on v10

--- a/solution.py
+++ b/solution.py
@@ -413,14 +413,12 @@
     width = -(-(M * M + 3) // LANES) * LANES
     blocks = call(
         functools.partial(operator_kernel, k_local),
-        shape((ka_count * pb_count, 2 * span, width), BF16),
+        shape((1, 2 * span, width), BF16),
         [pltpu.VMEM((2 * M * M * tiles, LANES), F32), pltpu.VMEM((width, LANES), F32)],
         operands=len(parts) + 4,
     )(*parts, own_fields, mask, shares, full)
     group = operator_group(ka_count, pb_count)
-    blocks = lax.all_to_all(
-        blocks, ("pb", "ka"), 0, 0, axis_index_groups=[group], tiled=True
-    )
+    blocks = lax.all_gather(blocks, ("pb", "ka"), axis_index_groups=[group], tiled=True)
     propagated, energy = call(
         functools.partial(taylor_kernel, pb_count, float(pb_count * chol_cols)),
         (shape((k_local, walkers, 2 * pair_width), F32), shape((1, 1), F32)),

time: 29.8 us -> 49.6 us (1.66)
  the two profiles are of different devices: /device:TPU:0 before, /device:TPU:6 now
where the time goes in v19:
time: 49.6 us; the launch traced here: 49.5 us
  blocking collectives  30.9 us (62%)
  starting transfers between devices  8.97 us (18%)
  Pallas kernels  4.21 us (8%)
  waiting for transfers between devices  3.33 us (7%)
  local copies, waits for them, and re-layouts  1.35 us (3%)
  between operations  0.71 us (1%)
    all_gather x1, blocking collectives, direct(): lax.all_gather(blocks, ('pb', 'ka'), axis_index_groups=[group], tiled=True)  30.9 us
    ppermute x6, starting transfers between devices, exchange(): return [array] + [lax.ppermute(array, axis, pairs) for pairs in rounds]  8.97 us
    ppermute x6, waiting for transfers between devices, exchange(): return [array] + [lax.ppermute(array, axis, pairs) for pairs in rounds]  3.33 us
    pallas_call x1, Pallas kernels, direct(): call(functools.partial(taylor_kernel, pb_count, float(pb_count * chol_col...  2.16 us
    unnamed x14, local copies, waits for them, and re-layouts  1.35 us
  transfers between devices with their start and end apart: 6, of which 4 were waited for; matrix products, arithmetic and copies ran while one was open for 0% of the time, Pallas kernels for 2%

profile of v19, /device:TPU:6, one launch (start us, length us, event | category | flops | bytes accessed | tf_op | source)
XLA Modules:
  0.0 49.5 jit_solution(11143919050068020603)
XLA Ops:
  0.6 0.0 copy-start.1
  0.6 0.0 copy-start.2
  0.7 0.0 copy-start.3
  0.7 0.0 copy-start
  0.7 0.0 copy-start.4
  0.7 2.6 %collective-permute-start.2 = (bf16[8,208]{1,0:T(8,128)(2,1)}, bf16[8,208]{1,0:T(8,128)(2,1)S(1)}, u32[]{:S(2)}, u32[]{:S(2)}) collective-permute-start(bf16[8,208]{1,0:T(8,128)(2,1)} %bitcast.15), channel_id=1, source_target_pairs={{12,0},{8,4},{4,12},{0,8},{13,1},{9,5},{5,13},{1,9},{14,2},{10,6},... | collective-permute-start | bytes 9992 | tf_op jit(solution)/shard_map/ppermute | solution.py:140
  3.3 1.2 %collective-permute-start.1 = (bf16[8,208]{1,0:T(8,128)(2,1)}, bf16[8,208]{1,0:T(8,128)(2,1)S(1)}, u32[]{:S(2)}, u32[]{:S(2)}) collective-permute-start(bf16[8,208]{1,0:T(8,128)(2,1)} %bitcast.16), channel_id=1, source_target_pairs={{12,4},{8,0},{0,12},{4,8},{13,5},{9,1},{1,13},{5,9},{14,6},{10,2},... | collective-permute-start | bytes 9992 | tf_op jit(solution)/shard_map/ppermute | solution.py:140
  4.6 0.3 collective-permute-start
  4.9 0.0 copy-start.5
  4.9 0.7 %copy-done.5 = s32[2,8]{1,0:T(2,128)S(1)} copy-done((s32[2,8]{1,0:T(2,128)S(1)}, s32[2,8]{1,0:T(2,128)}, u32[]{:S(2)}) %copy-start.5) | copy-done | bytes 88
  5.6 0.0 copy-start.6
  5.6 0.7 %copy-done.6 = s32[2]{0:T(128)S(1)} copy-done((s32[2]{0:T(128)S(1)}, s32[2]{0:T(128)}, u32[]{:S(2)}) %copy-start.6) | copy-done | bytes 32
  6.2 0.7 %shard_map.86 = (f32[8,256]{1,0:T(8,128)S(1)}, bf16[128,256]{1,0:T(8,128)(2,1)S(1)}) custom-call(s32[2,8]{1,0:T(2,128)S(1)} %copy-done.5, s32[2]{0:T(128)S(1)} %copy-done.6), custom_call_target="tpu_custom_call" | custom-call | flops 1000000000 | tf_op jit(solution)/shard_map/pallas_call | solution.py:392
  6.9 0.0 collective-permute-done.2.refs_3_
  6.9 1.1 %collective-permute-done.1.refs_2_ = bf16[8,208]{1,0:T(8,128)(2,1)S(1)} collective-permute-done((bf16[8,208]{1,0:T(8,128)(2,1)}, bf16[8,208]{1,0:T(8,128)(2,1)S(1)}, u32[]{:S(2)}, u32[]{:S(2)}) %collective-permute-start.1) | collective-permute-done | bytes 3360 | tf_op jit(solution)/shard_map/ppermute | solution.py:140
  8.0 0.3 collective-permute-done.refs_1_
  8.4 0.0 copy-done.1
  8.4 0.0 copy-done.2
  8.4 0.0 copy-done.3
  8.4 0.3 shard_map.87
  8.7 1.3 %collective-permute-start.5 = (f32[16,256]{1,0:T(8,128)S(1)}, f32[16,256]{1,0:T(8,128)S(1)}, u32[]{:S(2)}, u32[]{:S(2)}) collective-permute-start(f32[16,256]{1,0:T(8,128)S(1)} %get-tuple-element.9.refs_0_), channel_id=1, source_target_pairs={{0,4},{4,12},{8,0},{12,8},{1,5},{5,13},{9,1},{13,9},{2,6},{6,14},{... | collective-permute-start | bytes 49160 | tf_op jit(solution)/shard_map/ppermute | solution.py:140
  9.9 1.9 %collective-permute-start.4 = (f32[16,256]{1,0:T(8,128)S(1)}, f32[16,256]{1,0:T(8,128)S(1)}, u32[]{:S(2)}, u32[]{:S(2)}) collective-permute-start(f32[16,256]{1,0:T(8,128)S(1)} %get-tuple-element.9.refs_0_), channel_id=1, source_target_pairs={{0,12},{12,0},{4,8},{8,4},{1,13},{13,1},{5,9},{9,5},{2,14},{14,2},... | collective-permute-start | bytes 49160 | tf_op jit(solution)/shard_map/ppermute | solution.py:140
  11.8 1.6 %collective-permute-start.3 = (f32[16,256]{1,0:T(8,128)S(1)}, f32[16,256]{1,0:T(8,128)S(1)}, u32[]{:S(2)}, u32[]{:S(2)}) collective-permute-start(f32[16,256]{1,0:T(8,128)S(1)} %get-tuple-element.9.refs_0_), channel_id=1, source_target_pairs={{0,8},{4,0},{8,12},{12,4},{1,9},{5,1},{9,13},{13,5},{2,10},{6,2},{... | collective-permute-start | bytes 49160 | tf_op jit(solution)/shard_map/ppermute | solution.py:140
  13.4 0.4 shard_map.88.refs_6_
  13.8 0.0 collective-permute-done.5.refs_3_
  13.8 1.7 %collective-permute-done.4.refs_2_ = f32[16,256]{1,0:T(8,128)S(1)} collective-permute-done((f32[16,256]{1,0:T(8,128)S(1)}, f32[16,256]{1,0:T(8,128)S(1)}, u32[]{:S(2)}, u32[]{:S(2)}) %collective-permute-start.4) | collective-permute-done | bytes 16416 | tf_op jit(solution)/shard_map/ppermute | solution.py:140
  15.5 0.2 collective-permute-done.3.refs_1_
  15.6 0.0 copy-done
  15.7 0.0 copy-done.4
  15.7 0.8 %shard_map.89 = bf16[1,16,768]{2,1,0:T(8,128)(2,1)S(1)} custom-call(f32[16,256]{1,0:T(8,128)S(1)} %get-tuple-element.9.refs_0_, f32[16,256]{1,0:T(8,128)S(1)} %collective-permute-done.3.refs_1_, f32[16,256]{1,0:T(8,128)S(1)} %collective-permute-done.4.refs_2_, f32[16,256]{1,0:T(8,128)S(1)} %collective-permute-done.5.refs_3_, f32[4,256]{1,0:T(4,128)S(1)} %bitcast.19, ...), custom_call_target="tpu_custom_call" | custom-call | tf_op jit(solution)/shard_map/pallas_call | solution.py:414
  16.4 30.9 %all_gather.3.blocks_ref = bf16[8,16,768]{2,1,0:T(8,128)(2,1)S(1)} all-gather(bf16[1,16,768]{2,1,0:T(8,128)(2,1)S(1)} %shard_map.89), channel_id=1, replica_groups={{10,14,6,2,12,8,4,0},{11,15,7,3,13,9,5,1},{26,30,22,18,28,24,20,16},{27..., dimensions={0}, use_global_device_ids=true | all-gather | bytes 221184 | tf_op jit(solution)/shard_map/all_gather | solution.py:421
  47.3 2.2 %shard_map.90 = (f32[2,4,208]{2,1,0:T(4,128)}, f32[1,1]{1,0:T(1,128)}) custom-call(bf16[8,16,768]{2,1,0:T(8,128)(2,1)S(1)} %all_gather.3.blocks_ref, f32[16,256]{1,0:T(8,128)S(1)} %get-tuple-element.9.refs_0_, f32[16,256]{1,0:T(8,128)S(1)} %collective-permute-done.3.refs_1_, f32[16,256]{1,0:T(8,128)S(1)} %collective-permute-done.4.refs_2_, ...), custom_call_target="tpu_custom_call" | custom-call | tf_op jit(solution)/shard_map/pallas_call | solution.py:422
Async XLA Ops:
  0.6 7.7 %copy-start.1 = (bf16[1,2,2,104,256]{4,3,2,1,0:T(8,128)(2,1)S(1)}, bf16[1,2,2,104,256]{4,3,2,1,0:T(8,128)(2,1)}, u32[]{:S(2)}) copy-start(bf16[1,2,2,104,256]{4,3,2,1,0:T(8,128)(2,1)} %param.10) | copy-start | bytes 638980
  0.6 7.7 %copy-start.2 = (f32[1,2,4,208]{3,2,1,0:T(4,128)S(1)}, f32[1,2,4,208]{3,2,1,0:T(4,128)}, u32[]{:S(2)}) copy-start(f32[1,2,4,208]{3,2,1,0:T(4,128)} %param.9) | copy-start | bytes 19972
  0.7 7.7 %copy-start.3 = (bf16[1,1,1,8,208]{4,3,2,1,0:T(8,128)(2,1)S(1)}, bf16[1,1,1,8,208]{4,3,2,1,0:T(8,128)(2,1)}, u32[]{:S(2)}) copy-start(bf16[1,1,1,8,208]{4,3,2,1,0:T(8,128)(2,1)} %param.7) | copy-start | bytes 9988
  0.7 15.0 %copy-start = (bf16[1,2,2,676,256]{4,2,3,1,0:T(2,128)(2,1)S(1)}, bf16[1,2,2,676,256]{4,2,3,1,0:T(2,128)(2,1)}, u32[]{:S(2)}) copy-start(bf16[1,2,2,676,256]{4,2,3,1,0:T(2,128)(2,1)} %param.11) | copy-start | bytes 4153348
  0.7 15.0 %copy-start.4 = (f32[1,1,4,256]{3,2,1,0:T(4,128)S(1)}, f32[1,1,4,256]{3,2,1,0:T(4,128)}, u32[]{:S(2)}) copy-start(f32[1,1,4,256]{3,2,1,0:T(4,128)} %param.8) | copy-start | bytes 12292
  0.7 6.2 %collective-permute-start.2 = (bf16[8,208]{1,0:T(8,128)(2,1)}, bf16[8,208]{1,0:T(8,128)(2,1)S(1)}, u32[]{:S(2)}, u32[]{:S(2)}) collective-permute-start(bf16[8,208]{1,0:T(8,128)(2,1)} %bitcast.15), channel_id=1, source_target_pairs={{12,0},{8,4},{4,12},{0,8},{13,1},{9,5},{5,13},{1,9},{14,2},{10,6},... | collective-permute-start | bytes 9992 | tf_op jit(solution)/shard_map/ppermute | solution.py:140
  3.3 4.7 %collective-permute-start.1 = (bf16[8,208]{1,0:T(8,128)(2,1)}, bf16[8,208]{1,0:T(8,128)(2,1)S(1)}, u32[]{:S(2)}, u32[]{:S(2)}) collective-permute-start(bf16[8,208]{1,0:T(8,128)(2,1)} %bitcast.16), channel_id=1, source_target_pairs={{12,4},{8,0},{0,12},{4,8},{13,5},{9,1},{1,13},{5,9},{14,6},{10,2},... | collective-permute-start | bytes 9992 | tf_op jit(solution)/shard_map/ppermute | solution.py:140
  4.6 3.8 %collective-permute-start = (bf16[8,208]{1,0:T(8,128)(2,1)}, bf16[8,208]{1,0:T(8,128)(2,1)S(1)}, u32[]{:S(2)}, u32[]{:S(2)}) collective-permute-start(bf16[8,208]{1,0:T(8,128)(2,1)} %bitcast.17), channel_id=1, source_target_pairs={{4,0},{12,8},{8,12},{0,4},{5,1},{13,9},{9,13},{1,5},{6,2},{14,10},... | collective-permute-start | bytes 9992 | tf_op jit(solution)/shard_map/ppermute | solution.py:140
  4.9 0.7 %copy-start.5 = (s32[2,8]{1,0:T(2,128)S(1)}, s32[2,8]{1,0:T(2,128)}, u32[]{:S(2)}) copy-start(s32[2,8]{1,0:T(2,128)} %map_ref.1) | copy-start | bytes 196
  5.6 0.7 %copy-start.6 = (s32[2]{0:T(128)S(1)}, s32[2]{0:T(128)}, u32[]{:S(2)}) copy-start(s32[2]{0:T(128)} %count_ref.1) | copy-start | bytes 28
  8.7 5.1 %collective-permute-start.5 = (f32[16,256]{1,0:T(8,128)S(1)}, f32[16,256]{1,0:T(8,128)S(1)}, u32[]{:S(2)}, u32[]{:S(2)}) collective-permute-start(f32[16,256]{1,0:T(8,128)S(1)} %get-tuple-element.9.refs_0_), channel_id=1, source_target_pairs={{0,4},{4,12},{8,0},{12,8},{1,5},{5,13},{9,1},{13,9},{2,6},{6,14},{... | collective-permute-start | bytes 49160 | tf_op jit(solution)/shard_map/ppermute | solution.py:140
  9.9 5.5 %collective-permute-start.4 = (f32[16,256]{1,0:T(8,128)S(1)}, f32[16,256]{1,0:T(8,128)S(1)}, u32[]{:S(2)}, u32[]{:S(2)}) collective-permute-start(f32[16,256]{1,0:T(8,128)S(1)} %get-tuple-element.9.refs_0_), channel_id=1, source_target_pairs={{0,12},{12,0},{4,8},{8,4},{1,13},{13,1},{5,9},{9,5},{2,14},{14,2},... | collective-permute-start | bytes 49160 | tf_op jit(solution)/shard_map/ppermute | solution.py:140
  11.8 3.8 %collective-permute-start.3 = (f32[16,256]{1,0:T(8,128)S(1)}, f32[16,256]{1,0:T(8,128)S(1)}, u32[]{:S(2)}, u32[]{:S(2)}) collective-permute-start(f32[16,256]{1,0:T(8,128)S(1)} %get-tuple-element.9.refs_0_), channel_id=1, source_target_pairs={{0,8},{4,0},{8,12},{12,4},{1,9},{5,1},{9,13},{13,5},{2,10},{6,2},{... | collective-permute-start | bytes 49160 | tf_op jit(solution)/shard_map/ppermute | solution.py:140

commit v20 on v10

--- a/solution.py
+++ b/solution.py
@@ -298,20 +298,30 @@
             out_ref[copy, :, at : at + LANES] = block.astype(BF16)
 
 
-def taylor_kernel(pb_count, normalizer, blocks_ref, *refs):
-    *windows, picks_ref, orbitals_ref, out_ref, energy_ref, turned, picked, term = refs
+def first_kernel(*refs):
+    *windows, picks_ref, first_ref, term = refs
+    pair = NOCC * M
+    term[...] = jnp.zeros_like(term)
+    for source, window_ref in zip(origins("ka", BIAS_ROUNDS), windows):
+        span = window_ref.shape[0] // 2
+        start = pl.multiple_of(source * (2 * span), 2 * span)
+        window = window_ref[span:]
+        term[pl.ds(start, span), :pair] = window[:, :pair]
+        term[pl.ds(start + span, span), :pair] = window[:, pair : 2 * pair]
+    first_ref[...] = jnp.dot(
+        term[...].T.astype(BF16), picks_ref[...], preferred_element_type=F32
+    )
+
+
+def taylor_kernel(
+    pb_count, normalizer, blocks_ref, first_ref, picks_ref, orbitals_ref, out_ref, energy_ref,
+    turned, picked, term,
+):
     pairs = M * M
-    pair = NOCC * M
     k_local, walkers, _ = out_ref.shape
     span = k_local * walkers
     ka_pos = lax.axis_index("ka")
     term[...] = jnp.zeros_like(term)
-    for source, window_ref in zip(origins("ka", BIAS_ROUNDS), windows):
-        start = pl.multiple_of(source * (2 * span), 2 * span)
-        window = window_ref[window_ref.shape[0] - span :]
-        term[pl.ds(start, span), :pair] = window[:, :pair]
-        term[pl.ds(start + span, span), :pair] = window[:, pair : 2 * pair]
-    picked[...] = jnp.dot(term[...].T.astype(BF16), picks_ref[...], preferred_element_type=F32)
     count, _, width = blocks_ref.shape
     group = operator_group(count // pb_count, pb_count)
     places = [group.index(n) for n in range(count)]
@@ -327,22 +337,22 @@
     imaginary = lax.rem(lane, 2 * span) >= span
     sums = [jnp.zeros((M, LANES), F32) for _ in range(NOCC)]
     for degree in range(1, TAYLOR + 1):
-        stride = M if degree == 1 else ROWS
+        source, stride = (first_ref, M) if degree == 1 else (picked, ROWS)
         straight = [jnp.zeros((M, LANES), F32) for _ in range(NOCC)]
         crossed = [jnp.zeros((M, LANES), F32) for _ in range(NOCC)]
         for c in range(M):
             column = turned[pl.ds(c, M, stride=M), :]
             for i in range(NOCC):
                 at = i * stride + c
-                straight[i] += column * picked[at : at + 1, :LANES]
-                crossed[i] += column * picked[at : at + 1, LANES:]
+                straight[i] += column * source[at : at + 1, :LANES]
+                crossed[i] += column * source[at : at + 1, LANES:]
         for i in range(NOCC):
             other = jnp.where(
                 imaginary, pltpu.roll(crossed[i], span, 1), pltpu.roll(crossed[i], LANES - span, 1)
             )
             applied = straight[i] + other
             applied = applied + pltpu.roll(applied, LANES // pb_count, 1)
-            current = applied / degree
+            current = applied * (1.0 / degree)
             sums[i] = sums[i] + current
             term[i * ROWS : i * ROWS + M] = current if degree < TAYLOR else sums[i]
         if degree < TAYLOR:
@@ -421,6 +431,12 @@
     blocks = lax.all_to_all(
         blocks, ("pb", "ka"), 0, 0, axis_index_groups=[group], tiled=True
     )
+    first = call(
+        first_kernel,
+        shape((LANES, 2 * LANES), F32),
+        [pltpu.VMEM((LANES, LANES), F32)],
+        operands=len(parts) + 1,
+    )(*parts, picks)
     propagated, energy = call(
         functools.partial(taylor_kernel, pb_count, float(pb_count * chol_cols)),
         (shape((k_local, walkers, 2 * pair_width), F32), shape((1, 1), F32)),
@@ -429,8 +445,8 @@
             pltpu.VMEM((NOCC * ROWS, 2 * LANES), F32),
             pltpu.VMEM((LANES, LANES), F32),
         ],
-        operands=len(parts) + 3,
-    )(blocks, *parts, picks, own_orbitals)
+        operands=4,
+    )(blocks, first, picks, own_orbitals)
     return (propagated[None], energy)
 
 

time: 29.8 us -> 31.2 us (1.047)
  blocking collectives: 9.62 us -> 0 us
  waiting for transfers between devices: 3.17 us -> 10.3 us
  starting transfers between devices: 10.6 us -> 13.6 us
  Pallas kernels: 4.2 us -> 5.01 us
    all_to_all x1 -> x0, blocking collectives: 9.62 us -> none  [direct(): lax.all_to_all(blocks, ('pb', 'ka'), 0, 0, axis_index_groups=[group], til...]
    all_to_all x0 -> x1, starting transfers between devices: none -> 5.57 us  [direct(): lax.all_to_all(blocks, ('pb', 'ka'), 0, 0, axis_index_groups=[group], til...]
    all_to_all x0 -> x1, waiting for transfers between devices: none -> 3.58 us  [direct(): lax.all_to_all(blocks, ('pb', 'ka'), 0, 0, axis_index_groups=[group], til...]
    ppermute x6, waiting for transfers between devices: 3.17 us -> 6.67 us  [exchange(): return [array] + [lax.ppermute(array, axis, pairs) for pairs in rounds]]
    ppermute x6, starting transfers between devices: 10.6 us -> 8.06 us  [exchange(): return [array] + [lax.ppermute(array, axis, pairs) for pairs in rounds]]
    pallas_call x1, Pallas kernels: 0.76 us -> 1.44 us  [direct(): call(functools.partial(operator_kernel, k_local), shape((ka_count * pb_co...]
  transfers between devices with their start and end apart: 6 -> 7, of which waited for: 4 -> 5; matrix products, arithmetic and copies ran while one was open for 0% -> 0% of each run, Pallas kernels for 3% -> 4%
where the time goes in v20:
time: 31.2 us; the launch traced here: 31 us
  starting transfers between devices  13.6 us (44%)
  waiting for transfers between devices  10.3 us (33%)
  Pallas kernels  5.01 us (16%)
  local copies, waits for them, and re-layouts  1.35 us (4%)
  between operations  0.71 us (2%)
    ppermute x6, starting transfers between devices, exchange(): return [array] + [lax.ppermute(array, axis, pairs) for pairs in rounds]  8.06 us
    ppermute x6, waiting for transfers between devices, exchange(): return [array] + [lax.ppermute(array, axis, pairs) for pairs in rounds]  6.67 us
    all_to_all x1, starting transfers between devices, direct(): lax.all_to_all(blocks, ('pb', 'ka'), 0, 0, axis_index_groups=[group], til...  5.57 us
    all_to_all x1, waiting for transfers between devices, direct(): lax.all_to_all(blocks, ('pb', 'ka'), 0, 0, axis_index_groups=[group], til...  3.58 us
    pallas_call x1, Pallas kernels, direct(): call(functools.partial(taylor_kernel, pb_count, float(pb_count * chol_col...  1.99 us
    pallas_call x1, Pallas kernels, direct(): call(functools.partial(operator_kernel, k_local), shape((ka_count * pb_co...  1.44 us
    unnamed x14, local copies, waits for them, and re-layouts  1.35 us
    pallas_call x1, Pallas kernels, direct(): call(functools.partial(prepare_kernel, ka_count, pb_count, walkers), (sha...  0.66 us
  transfers between devices with their start and end apart: 7, of which 5 were waited for; matrix products, arithmetic and copies ran while one was open for 0% of the time, Pallas kernels for 4%

profile of v20, /device:TPU:0, one launch (start us, length us, event | category | flops | bytes accessed | tf_op | source)
XLA Modules:
  0.0 31.0 jit_solution(776836695988797672)
XLA Ops:
  0.6 0.0 copy-start.1
  0.6 0.0 copy-start.2
  0.7 0.0 copy-start.3
  0.7 0.0 copy-start
  0.7 0.0 copy-start.4
  0.7 3.1 %collective-permute-start = (bf16[8,208]{1,0:T(8,128)(2,1)}, bf16[8,208]{1,0:T(8,128)(2,1)S(1)}, u32[]{:S(2)}, u32[]{:S(2)}) collective-permute-start(bf16[8,208]{1,0:T(8,128)(2,1)} %bitcast.15), channel_id=1, source_target_pairs={{4,0},{12,8},{8,12},{0,4},{5,1},{13,9},{9,13},{1,5},{6,2},{14,10},... | collective-permute-start | bytes 9992 | tf_op jit(solution)/shard_map/ppermute | solution.py:140
  3.8 2.5 %collective-permute-start.1 = (bf16[8,208]{1,0:T(8,128)(2,1)}, bf16[8,208]{1,0:T(8,128)(2,1)S(1)}, u32[]{:S(2)}, u32[]{:S(2)}) collective-permute-start(bf16[8,208]{1,0:T(8,128)(2,1)} %bitcast.16), channel_id=1, source_target_pairs={{12,4},{8,0},{0,12},{4,8},{13,5},{9,1},{1,13},{5,9},{14,6},{10,2},... | collective-permute-start | bytes 9992 | tf_op jit(solution)/shard_map/ppermute | solution.py:140
  6.2 0.5 %collective-permute-start.2 = (bf16[8,208]{1,0:T(8,128)(2,1)}, bf16[8,208]{1,0:T(8,128)(2,1)S(1)}, u32[]{:S(2)}, u32[]{:S(2)}) collective-permute-start(bf16[8,208]{1,0:T(8,128)(2,1)} %bitcast.17), channel_id=1, source_target_pairs={{12,0},{8,4},{4,12},{0,8},{13,1},{9,5},{5,13},{1,9},{14,2},{10,6},... | collective-permute-start | bytes 9992 | tf_op jit(solution)/shard_map/ppermute | solution.py:140
  6.7 0.7 %copy-done.5 = s32[2,8]{1,0:T(2,128)S(1)} copy-done((s32[2,8]{1,0:T(2,128)S(1)}, s32[2,8]{1,0:T(2,128)}, u32[]{:S(2)}) %copy-start.5) | copy-done | bytes 88
  7.4 0.7 %copy-done.6 = s32[2]{0:T(128)S(1)} copy-done((s32[2]{0:T(128)S(1)}, s32[2]{0:T(128)}, u32[]{:S(2)}) %copy-start.6) | copy-done | bytes 32
  8.0 0.7 %shard_map.86 = (f32[8,256]{1,0:T(8,128)S(1)}, bf16[128,256]{1,0:T(8,128)(2,1)S(1)}) custom-call(s32[2,8]{1,0:T(2,128)S(1)} %copy-done.5, s32[2]{0:T(128)S(1)} %copy-done.6), custom_call_target="tpu_custom_call" | custom-call | flops 1000000000 | tf_op jit(solution)/shard_map/pallas_call | solution.py:402
  8.7 0.0 collective-permute-done.refs_1_
  8.7 0.0 collective-permute-done.1.refs_2_
  8.7 3.1 %collective-permute-done.2.refs_3_ = bf16[8,208]{1,0:T(8,128)(2,1)S(1)} collective-permute-done((bf16[8,208]{1,0:T(8,128)(2,1)}, bf16[8,208]{1,0:T(8,128)(2,1)S(1)}, u32[]{:S(2)}, u32[]{:S(2)}) %collective-permute-start.2) | collective-permute-done | bytes 3360 | tf_op jit(solution)/shard_map/ppermute | solution.py:140
  11.9 0.0 copy-done.1
  11.9 0.0 copy-done.2
  11.9 0.0 copy-done.3
  11.9 0.3 shard_map.87
  12.1 0.0 collective-permute-start.3
  12.2 1.3 %collective-permute-start.4 = (f32[16,256]{1,0:T(8,128)S(1)}, f32[16,256]{1,0:T(8,128)S(1)}, u32[]{:S(2)}, u32[]{:S(2)}) collective-permute-start(f32[16,256]{1,0:T(8,128)S(1)} %get-tuple-element.9.refs_0_), channel_id=1, source_target_pairs={{0,12},{12,0},{4,8},{8,4},{1,13},{13,1},{5,9},{9,5},{2,14},{14,2},... | collective-permute-start | bytes 49160 | tf_op jit(solution)/shard_map/ppermute | solution.py:140
  13.4 0.8 %collective-permute-start.5 = (f32[16,256]{1,0:T(8,128)S(1)}, f32[16,256]{1,0:T(8,128)S(1)}, u32[]{:S(2)}, u32[]{:S(2)}) collective-permute-start(f32[16,256]{1,0:T(8,128)S(1)} %get-tuple-element.9.refs_0_), channel_id=1, source_target_pairs={{0,4},{4,12},{8,0},{12,8},{1,5},{5,13},{9,1},{13,9},{2,6},{6,14},{... | collective-permute-start | bytes 49160 | tf_op jit(solution)/shard_map/ppermute | solution.py:140
  14.2 0.4 %shard_map.88.refs_6_ = f32[4,128]{1,0:T(4,128)S(1)} custom-call(f32[2,8,104]{2,1,0:T(8,128)S(1)} %get-tuple-element.10.own_ref, bf16[2,2,104,256]{3,2,1,0:T(8,128)(2,1)S(1)} %bitcast.12, f32[8,256]{1,0:T(8,128)S(1)} %get-tuple-element.8.refs_6_.mask_ref.refs_5_), custom_call_target="tpu_custom_call" | custom-call | tf_op jit(solution)/shard_map/pallas_call | solution.py:418
  14.6 1.3 %collective-permute-done.3.refs_1_ = f32[16,256]{1,0:T(8,128)S(1)} collective-permute-done((f32[16,256]{1,0:T(8,128)S(1)}, f32[16,256]{1,0:T(8,128)S(1)}, u32[]{:S(2)}, u32[]{:S(2)}) %collective-permute-start.3) | collective-permute-done | bytes 16416 | tf_op jit(solution)/shard_map/ppermute | solution.py:140
  15.9 1.8 %collective-permute-done.4.refs_2_ = f32[16,256]{1,0:T(8,128)S(1)} collective-permute-done((f32[16,256]{1,0:T(8,128)S(1)}, f32[16,256]{1,0:T(8,128)S(1)}, u32[]{:S(2)}, u32[]{:S(2)}) %collective-permute-start.4) | collective-permute-done | bytes 16416 | tf_op jit(solution)/shard_map/ppermute | solution.py:140
  17.8 0.3 %collective-permute-done.5.refs_3_ = f32[16,256]{1,0:T(8,128)S(1)} collective-permute-done((f32[16,256]{1,0:T(8,128)S(1)}, f32[16,256]{1,0:T(8,128)S(1)}, u32[]{:S(2)}, u32[]{:S(2)}) %collective-permute-start.5) | collective-permute-done | bytes 16416 | tf_op jit(solution)/shard_map/ppermute | solution.py:140
  18.1 0.0 copy-done
  18.1 0.0 copy-done.4
  18.1 1.4 %shard_map.89 = bf16[8,16,768]{2,1,0:T(8,128)(2,1)} custom-call(f32[16,256]{1,0:T(8,128)S(1)} %get-tuple-element.9.refs_0_, f32[16,256]{1,0:T(8,128)S(1)} %collective-permute-done.3.refs_1_, f32[16,256]{1,0:T(8,128)S(1)} %collective-permute-done.4.refs_2_, f32[16,256]{1,0:T(8,128)S(1)} %collective-permute-done.5.refs_3_, f32[4,256]{1,0:T(4,128)S(1)} %bitcast.19, ...), custom_call_target="tpu_custom_call" | custom-call | tf_op jit(solution)/shard_map/pallas_call | solution.py:424
  19.5 5.6 %all-to-all-start = ((bf16[8,16,768]{2,1,0:T(8,128)(2,1)}), bf16[8,16,768]{2,1,0:T(8,128)(2,1)S(1)}, u32[]{:S(2)}, u32[]{:S(2)}) async-start(bf16[8,16,768]{2,1,0:T(8,128)(2,1)} %shard_map.89), calls=%async_computation | async-start | bytes 393216 | tf_op jit(solution)/shard_map/all_to_all | solution.py:431
  25.1 0.3 shard_map.90.first_ref
  25.4 3.6 %all-to-all-done.blocks_ref = bf16[8,16,768]{2,1,0:T(8,128)(2,1)S(1)} async-done(((bf16[8,16,768]{2,1,0:T(8,128)(2,1)}), bf16[8,16,768]{2,1,0:T(8,128)(2,1)S(1)}, u32[]{:S(2)}, u32[]{:S(2)}) %all-to-all-start) | async-done | bytes 196640 | tf_op jit(solution)/shard_map/all_to_all | solution.py:431
  29.0 2.0 %shard_map.91 = (f32[2,4,208]{2,1,0:T(4,128)}, f32[1,1]{1,0:T(1,128)}) custom-call(bf16[8,16,768]{2,1,0:T(8,128)(2,1)S(1)} %all-to-all-done.blocks_ref, f32[128,256]{1,0:T(8,128)S(1)} %shard_map.90.first_ref, bf16[128,256]{1,0:T(8,128)(2,1)S(1)} %get-tuple-element.11.refs_4_.picks_ref, f32[2,4,208]{2,1,0:T(4,128)S(1)} %bitcast.14), custom_call_target="tpu_custom_call" | custom-call | tf_op jit(solution)/shard_map/pallas_call | solution.py:440
  (2 shorter events, 0.0 us)
Async XLA Ops:
  0.6 11.2 %copy-start.1 = (bf16[1,2,2,104,256]{4,3,2,1,0:T(8,128)(2,1)S(1)}, bf16[1,2,2,104,256]{4,3,2,1,0:T(8,128)(2,1)}, u32[]{:S(2)}) copy-start(bf16[1,2,2,104,256]{4,3,2,1,0:T(8,128)(2,1)} %param.10) | copy-start | bytes 638980
  0.6 11.2 %copy-start.2 = (f32[1,2,4,208]{3,2,1,0:T(4,128)S(1)}, f32[1,2,4,208]{3,2,1,0:T(4,128)}, u32[]{:S(2)}) copy-start(f32[1,2,4,208]{3,2,1,0:T(4,128)} %param.9) | copy-start | bytes 19972
  0.7 11.2 %copy-start.3 = (bf16[1,1,1,8,208]{4,3,2,1,0:T(8,128)(2,1)S(1)}, bf16[1,1,1,8,208]{4,3,2,1,0:T(8,128)(2,1)}, u32[]{:S(2)}) copy-start(bf16[1,1,1,8,208]{4,3,2,1,0:T(8,128)(2,1)} %param.7) | copy-start | bytes 9988
  0.7 17.4 %copy-start = (bf16[1,2,2,676,256]{4,2,3,1,0:T(2,128)(2,1)S(1)}, bf16[1,2,2,676,256]{4,2,3,1,0:T(2,128)(2,1)}, u32[]{:S(2)}) copy-start(bf16[1,2,2,676,256]{4,2,3,1,0:T(2,128)(2,1)} %param.11) | copy-start | bytes 4153348
  0.7 17.4 %copy-start.4 = (f32[1,1,4,256]{3,2,1,0:T(4,128)S(1)}, f32[1,1,4,256]{3,2,1,0:T(4,128)}, u32[]{:S(2)}) copy-start(f32[1,1,4,256]{3,2,1,0:T(4,128)} %param.8) | copy-start | bytes 12292
  0.7 8.0 %collective-permute-start = (bf16[8,208]{1,0:T(8,128)(2,1)}, bf16[8,208]{1,0:T(8,128)(2,1)S(1)}, u32[]{:S(2)}, u32[]{:S(2)}) collective-permute-start(bf16[8,208]{1,0:T(8,128)(2,1)} %bitcast.15), channel_id=1, source_target_pairs={{4,0},{12,8},{8,12},{0,4},{5,1},{13,9},{9,13},{1,5},{6,2},{14,10},... | collective-permute-start | bytes 9992 | tf_op jit(solution)/shard_map/ppermute | solution.py:140
  3.8 4.9 %collective-permute-start.1 = (bf16[8,208]{1,0:T(8,128)(2,1)}, bf16[8,208]{1,0:T(8,128)(2,1)S(1)}, u32[]{:S(2)}, u32[]{:S(2)}) collective-permute-start(bf16[8,208]{1,0:T(8,128)(2,1)} %bitcast.16), channel_id=1, source_target_pairs={{12,4},{8,0},{0,12},{4,8},{13,5},{9,1},{1,13},{5,9},{14,6},{10,2},... | collective-permute-start | bytes 9992 | tf_op jit(solution)/shard_map/ppermute | solution.py:140
  6.2 5.6 %collective-permute-start.2 = (bf16[8,208]{1,0:T(8,128)(2,1)}, bf16[8,208]{1,0:T(8,128)(2,1)S(1)}, u32[]{:S(2)}, u32[]{:S(2)}) collective-permute-start(bf16[8,208]{1,0:T(8,128)(2,1)} %bitcast.17), channel_id=1, source_target_pairs={{12,0},{8,4},{4,12},{0,8},{13,1},{9,5},{5,13},{1,9},{14,2},{10,6},... | collective-permute-start | bytes 9992 | tf_op jit(solution)/shard_map/ppermute | solution.py:140
  6.7 0.7 %copy-start.5 = (s32[2,8]{1,0:T(2,128)S(1)}, s32[2,8]{1,0:T(2,128)}, u32[]{:S(2)}) copy-start(s32[2,8]{1,0:T(2,128)} %map_ref.1) | copy-start | bytes 196
  7.4 0.7 %copy-start.6 = (s32[2]{0:T(128)S(1)}, s32[2]{0:T(128)}, u32[]{:S(2)}) copy-start(s32[2]{0:T(128)} %count_ref.1) | copy-start | bytes 28
  12.1 3.8 %collective-permute-start.3 = (f32[16,256]{1,0:T(8,128)S(1)}, f32[16,256]{1,0:T(8,128)S(1)}, u32[]{:S(2)}, u32[]{:S(2)}) collective-permute-start(f32[16,256]{1,0:T(8,128)S(1)} %get-tuple-element.9.refs_0_), channel_id=1, source_target_pairs={{0,8},{4,0},{8,12},{12,4},{1,9},{5,1},{9,13},{13,5},{2,10},{6,2},{... | collective-permute-start | bytes 49160 | tf_op jit(solution)/shard_map/ppermute | solution.py:140
  12.2 5.6 %collective-permute-start.4 = (f32[16,256]{1,0:T(8,128)S(1)}, f32[16,256]{1,0:T(8,128)S(1)}, u32[]{:S(2)}, u32[]{:S(2)}) collective-permute-start(f32[16,256]{1,0:T(8,128)S(1)} %get-tuple-element.9.refs_0_), channel_id=1, source_target_pairs={{0,12},{12,0},{4,8},{8,4},{1,13},{13,1},{5,9},{9,5},{2,14},{14,2},... | collective-permute-start | bytes 49160 | tf_op jit(solution)/shard_map/ppermute | solution.py:140
  13.4 4.6 %collective-permute-start.5 = (f32[16,256]{1,0:T(8,128)S(1)}, f32[16,256]{1,0:T(8,128)S(1)}, u32[]{:S(2)}, u32[]{:S(2)}) collective-permute-start(f32[16,256]{1,0:T(8,128)S(1)} %get-tuple-element.9.refs_0_), channel_id=1, source_target_pairs={{0,4},{4,12},{8,0},{12,8},{1,5},{5,13},{9,1},{13,9},{2,6},{6,14},{... | collective-permute-start | bytes 49160 | tf_op jit(solution)/shard_map/ppermute | solution.py:140
  19.5 9.4 %all-to-all-start = ((bf16[8,16,768]{2,1,0:T(8,128)(2,1)}), bf16[8,16,768]{2,1,0:T(8,128)(2,1)S(1)}, u32[]{:S(2)}, u32[]{:S(2)}) async-start(bf16[8,16,768]{2,1,0:T(8,128)(2,1)} %shard_map.89), calls=%async_computation | async-start | bytes 393216 | tf_op jit(solution)/shard_map/all_to_all | solution.py:431

commit v21 on v10

--- a/solution.py
+++ b/solution.py
@@ -315,6 +315,7 @@
     count, _, width = blocks_ref.shape
     group = operator_group(count // pb_count, pb_count)
     places = [group.index(n) for n in range(count)]
+    turned[width:] = jnp.zeros((turned.shape[0] - width, LANES), F32)
     for at in range(0, width, LANES):
         tile = jnp.concatenate([blocks_ref[n, :, at : at + LANES] for n in places], axis=0)
         turned[at : at + LANES] = tile.T.astype(F32)
@@ -323,34 +324,33 @@
     shares = jnp.where(lax.rem(lane, 2 * span) == ka_pos, shares, 0.0)
     shares = jnp.sum(jnp.sum(shares, axis=0, keepdims=True), axis=1, keepdims=True)
     energy_ref[...] = shares / normalizer
-    lane = lax.broadcasted_iota(jnp.int32, (M, LANES), 1)
+    lane = lax.broadcasted_iota(jnp.int32, (ROWS, LANES), 1)
     imaginary = lax.rem(lane, 2 * span) >= span
-    sums = [jnp.zeros((M, LANES), F32) for _ in range(NOCC)]
+    sums = [None] * NOCC
     for degree in range(1, TAYLOR + 1):
         stride = M if degree == 1 else ROWS
-        straight = [jnp.zeros((M, LANES), F32) for _ in range(NOCC)]
-        crossed = [jnp.zeros((M, LANES), F32) for _ in range(NOCC)]
+        straight = [jnp.zeros((ROWS, LANES), F32) for _ in range(NOCC)]
+        crossed = [jnp.zeros((ROWS, LANES), F32) for _ in range(NOCC)]
         for c in range(M):
-            column = turned[pl.ds(c, M, stride=M), :]
+            column = turned[pl.ds(c, ROWS, stride=M), :]
             for i in range(NOCC):
                 at = i * stride + c
                 straight[i] += column * picked[at : at + 1, :LANES]
                 crossed[i] += column * picked[at : at + 1, LANES:]
+        currents = []
         for i in range(NOCC):
             other = jnp.where(
                 imaginary, pltpu.roll(crossed[i], span, 1), pltpu.roll(crossed[i], LANES - span, 1)
             )
             applied = straight[i] + other
             applied = applied + pltpu.roll(applied, LANES // pb_count, 1)
-            current = applied / degree
-            sums[i] = sums[i] + current
-            term[i * ROWS : i * ROWS + M] = current if degree < TAYLOR else sums[i]
+            currents.append(applied * (1.0 / degree))
+            sums[i] = currents[i] if degree == 1 else sums[i] + currents[i]
         if degree < TAYLOR:
-            picked[...] = jnp.dot(
-                term[...].astype(BF16), picks_ref[...], preferred_element_type=F32
-            )
-    turned[:LANES] = term[...].T
-    both = turned[pl.ds(pl.multiple_of(ka_pos * (2 * span), 2 * span), 2 * span), :]
+            rows = jnp.concatenate(currents, axis=0).astype(BF16)
+            picked[...] = jnp.dot(rows, picks_ref[...], preferred_element_type=F32)
+    term[...] = jnp.concatenate(sums, axis=0).T
+    both = term[pl.ds(pl.multiple_of(ka_pos * (2 * span), 2 * span), 2 * span), :]
     both = jnp.concatenate([both[:, i * ROWS : i * ROWS + M] for i in range(NOCC)], axis=1)
     both = jnp.concatenate([both[:span], both[span:]], axis=1)
     for k in range(k_local):
@@ -425,7 +425,7 @@
         functools.partial(taylor_kernel, pb_count, float(pb_count * chol_cols)),
         (shape((k_local, walkers, 2 * pair_width), F32), shape((1, 1), F32)),
         [
-            pltpu.VMEM((width, LANES), F32),
+            pltpu.VMEM((ROWS * M, LANES), F32),
             pltpu.VMEM((NOCC * ROWS, 2 * LANES), F32),
             pltpu.VMEM((LANES, LANES), F32),
         ],

time: 29.8 us -> 29.8 us (level)
  no operation moved by 1% of the time
where the time goes in v21:
time: 29.8 us; the launch traced here: 29.6 us
  starting transfers between devices  10.6 us (36%)
  blocking collectives  9.62 us (32%)
  Pallas kernels  4.18 us (14%)
  waiting for transfers between devices  3.17 us (11%)
  local copies, waits for them, and re-layouts  1.35 us (5%)
  between operations  0.71 us (2%)
    ppermute x6, starting transfers between devices, exchange(): return [array] + [lax.ppermute(array, axis, pairs) for pairs in rounds]  10.6 us
    all_to_all x1, blocking collectives, direct(): lax.all_to_all(blocks, ('pb', 'ka'), 0, 0, axis_index_groups=[group], til...  9.62 us
    ppermute x6, waiting for transfers between devices, exchange(): return [array] + [lax.ppermute(array, axis, pairs) for pairs in rounds]  3.17 us
    pallas_call x1, Pallas kernels, direct(): call(functools.partial(taylor_kernel, pb_count, float(pb_count * chol_col...  2.12 us
    unnamed x14, local copies, waits for them, and re-layouts  1.35 us
    pallas_call x1, Pallas kernels, direct(): call(functools.partial(operator_kernel, k_local), shape((ka_count * pb_co...  0.76 us
    pallas_call x1, Pallas kernels, direct(): call(functools.partial(prepare_kernel, ka_count, pb_count, walkers), (sha...  0.66 us
  transfers between devices with their start and end apart: 6, of which 4 were waited for; matrix products, arithmetic and copies ran while one was open for 0% of the time, Pallas kernels for 3%

profile of v21, /device:TPU:0, one launch (start us, length us, event | category | flops | bytes accessed | tf_op | source)
XLA Modules:
  0.0 29.6 jit_solution(18388611207109305385)
XLA Ops:
  0.6 0.0 copy-start.1
  0.6 0.0 copy-start.2
  0.7 0.0 copy-start.3
  0.7 0.0 copy-start
  0.7 0.0 copy-start.4
  0.7 4.1 %collective-permute-start.2 = (bf16[8,208]{1,0:T(8,128)(2,1)}, bf16[8,208]{1,0:T(8,128)(2,1)S(1)}, u32[]{:S(2)}, u32[]{:S(2)}) collective-permute-start(bf16[8,208]{1,0:T(8,128)(2,1)} %bitcast.15), channel_id=1, source_target_pairs={{12,0},{8,4},{4,12},{0,8},{13,1},{9,5},{5,13},{1,9},{14,2},{10,6},... | collective-permute-start | bytes 9992 | tf_op jit(solution)/shard_map/ppermute | solution.py:140
  4.8 1.1 %collective-permute-start.1 = (bf16[8,208]{1,0:T(8,128)(2,1)}, bf16[8,208]{1,0:T(8,128)(2,1)S(1)}, u32[]{:S(2)}, u32[]{:S(2)}) collective-permute-start(bf16[8,208]{1,0:T(8,128)(2,1)} %bitcast.16), channel_id=1, source_target_pairs={{12,4},{8,0},{0,12},{4,8},{13,5},{9,1},{1,13},{5,9},{14,6},{10,2},... | collective-permute-start | bytes 9992 | tf_op jit(solution)/shard_map/ppermute | solution.py:140
  5.8 0.5 %collective-permute-start = (bf16[8,208]{1,0:T(8,128)(2,1)}, bf16[8,208]{1,0:T(8,128)(2,1)S(1)}, u32[]{:S(2)}, u32[]{:S(2)}) collective-permute-start(bf16[8,208]{1,0:T(8,128)(2,1)} %bitcast.17), channel_id=1, source_target_pairs={{4,0},{12,8},{8,12},{0,4},{5,1},{13,9},{9,13},{1,5},{6,2},{14,10},... | collective-permute-start | bytes 9992 | tf_op jit(solution)/shard_map/ppermute | solution.py:140
  6.4 0.0 copy-start.5
  6.4 0.7 %copy-done.5 = s32[2,8]{1,0:T(2,128)S(1)} copy-done((s32[2,8]{1,0:T(2,128)S(1)}, s32[2,8]{1,0:T(2,128)}, u32[]{:S(2)}) %copy-start.5) | copy-done | bytes 88
  7.0 0.0 copy-start.6
  7.0 0.7 %copy-done.6 = s32[2]{0:T(128)S(1)} copy-done((s32[2]{0:T(128)S(1)}, s32[2]{0:T(128)}, u32[]{:S(2)}) %copy-start.6) | copy-done | bytes 32
  7.7 0.7 %shard_map.86 = (f32[8,256]{1,0:T(8,128)S(1)}, bf16[128,256]{1,0:T(8,128)(2,1)S(1)}) custom-call(s32[2,8]{1,0:T(2,128)S(1)} %copy-done.5, s32[2]{0:T(128)S(1)} %copy-done.6), custom_call_target="tpu_custom_call" | custom-call | flops 1000000000 | tf_op jit(solution)/shard_map/pallas_call | solution.py:392
  8.4 0.0 collective-permute-done.2.refs_3_
  8.4 1.1 %collective-permute-done.1.refs_2_ = bf16[8,208]{1,0:T(8,128)(2,1)S(1)} collective-permute-done((bf16[8,208]{1,0:T(8,128)(2,1)}, bf16[8,208]{1,0:T(8,128)(2,1)S(1)}, u32[]{:S(2)}, u32[]{:S(2)}) %collective-permute-start.1) | collective-permute-done | bytes 3360 | tf_op jit(solution)/shard_map/ppermute | solution.py:140
  9.5 0.2 collective-permute-done.refs_1_
  9.7 0.0 copy-done.1
  9.7 0.0 copy-done.2
  9.7 0.0 copy-done.3
  9.7 0.3 shard_map.87
  10.0 1.4 %collective-permute-start.5 = (f32[16,256]{1,0:T(8,128)S(1)}, f32[16,256]{1,0:T(8,128)S(1)}, u32[]{:S(2)}, u32[]{:S(2)}) collective-permute-start(f32[16,256]{1,0:T(8,128)S(1)} %get-tuple-element.9.refs_0_), channel_id=1, source_target_pairs={{0,4},{4,12},{8,0},{12,8},{1,5},{5,13},{9,1},{13,9},{2,6},{6,14},{... | collective-permute-start | bytes 49160 | tf_op jit(solution)/shard_map/ppermute | solution.py:140
  11.4 1.9 %collective-permute-start.4 = (f32[16,256]{1,0:T(8,128)S(1)}, f32[16,256]{1,0:T(8,128)S(1)}, u32[]{:S(2)}, u32[]{:S(2)}) collective-permute-start(f32[16,256]{1,0:T(8,128)S(1)} %get-tuple-element.9.refs_0_), channel_id=1, source_target_pairs={{0,12},{12,0},{4,8},{8,4},{1,13},{13,1},{5,9},{9,5},{2,14},{14,2},... | collective-permute-start | bytes 49160 | tf_op jit(solution)/shard_map/ppermute | solution.py:140
  13.3 1.6 %collective-permute-start.3 = (f32[16,256]{1,0:T(8,128)S(1)}, f32[16,256]{1,0:T(8,128)S(1)}, u32[]{:S(2)}, u32[]{:S(2)}) collective-permute-start(f32[16,256]{1,0:T(8,128)S(1)} %get-tuple-element.9.refs_0_), channel_id=1, source_target_pairs={{0,8},{4,0},{8,12},{12,4},{1,9},{5,1},{9,13},{13,5},{2,10},{6,2},{... | collective-permute-start | bytes 49160 | tf_op jit(solution)/shard_map/ppermute | solution.py:140
  14.9 0.4 %shard_map.88.refs_6_ = f32[4,128]{1,0:T(4,128)S(1)} custom-call(f32[2,8,104]{2,1,0:T(8,128)S(1)} %get-tuple-element.10.own_ref, bf16[2,2,104,256]{3,2,1,0:T(8,128)(2,1)S(1)} %bitcast.12, f32[8,256]{1,0:T(8,128)S(1)} %get-tuple-element.8.refs_6_.mask_ref.refs_5_), custom_call_target="tpu_custom_call" | custom-call | tf_op jit(solution)/shard_map/pallas_call | solution.py:408
  15.2 0.0 collective-permute-done.5.refs_3_
  15.2 1.7 %collective-permute-done.4.refs_2_ = f32[16,256]{1,0:T(8,128)S(1)} collective-permute-done((f32[16,256]{1,0:T(8,128)S(1)}, f32[16,256]{1,0:T(8,128)S(1)}, u32[]{:S(2)}, u32[]{:S(2)}) %collective-permute-start.4) | collective-permute-done | bytes 16416 | tf_op jit(solution)/shard_map/ppermute | solution.py:140
  16.9 0.2 collective-permute-done.3.refs_1_
  17.1 0.0 copy-done
  17.1 0.0 copy-done.4
  17.1 0.8 %shard_map.89 = bf16[8,16,768]{2,1,0:T(8,128)(2,1)S(1)} custom-call(f32[16,256]{1,0:T(8,128)S(1)} %get-tuple-element.9.refs_0_, f32[16,256]{1,0:T(8,128)S(1)} %collective-permute-done.3.refs_1_, f32[16,256]{1,0:T(8,128)S(1)} %collective-permute-done.4.refs_2_, f32[16,256]{1,0:T(8,128)S(1)} %collective-permute-done.5.refs_3_, f32[4,256]{1,0:T(4,128)S(1)} %bitcast.19, ...), custom_call_target="tpu_custom_call" | custom-call | tf_op jit(solution)/shard_map/pallas_call | solution.py:414
  17.9 9.6 %all_to_all.5.blocks_ref = bf16[8,16,768]{2,1,0:T(8,128)(2,1)S(1)} all-to-all(bf16[8,16,768]{2,1,0:T(8,128)(2,1)S(1)} %shard_map.89), channel_id=1, replica_groups={{10,14,6,2,12,8,4,0},{11,15,7,3,13,9,5,1},{26,30,22,18,28,24,20,16},{27..., dimensions={0} | all-to-all | bytes 393216 | tf_op jit(solution)/shard_map/all_to_all | solution.py:421
  27.5 2.1 %shard_map.90 = (f32[2,4,208]{2,1,0:T(4,128)}, f32[1,1]{1,0:T(1,128)}) custom-call(bf16[8,16,768]{2,1,0:T(8,128)(2,1)S(1)} %all_to_all.5.blocks_ref, f32[16,256]{1,0:T(8,128)S(1)} %get-tuple-element.9.refs_0_, f32[16,256]{1,0:T(8,128)S(1)} %collective-permute-done.3.refs_1_, f32[16,256]{1,0:T(8,128)S(1)} %collective-permute-done.4.refs_2_, ...), custom_call_target="tpu_custom_call" | custom-call | tf_op jit(solution)/shard_map/pallas_call | solution.py:424
Async XLA Ops:
  0.6 9.0 %copy-start.1 = (bf16[1,2,2,104,256]{4,3,2,1,0:T(8,128)(2,1)S(1)}, bf16[1,2,2,104,256]{4,3,2,1,0:T(8,128)(2,1)}, u32[]{:S(2)}) copy-start(bf16[1,2,2,104,256]{4,3,2,1,0:T(8,128)(2,1)} %param.10) | copy-start | bytes 638980
  0.6 9.0 %copy-start.2 = (f32[1,2,4,208]{3,2,1,0:T(4,128)S(1)}, f32[1,2,4,208]{3,2,1,0:T(4,128)}, u32[]{:S(2)}) copy-start(f32[1,2,4,208]{3,2,1,0:T(4,128)} %param.9) | copy-start | bytes 19972
  0.7 9.0 %copy-start.3 = (bf16[1,1,1,8,208]{4,3,2,1,0:T(8,128)(2,1)S(1)}, bf16[1,1,1,8,208]{4,3,2,1,0:T(8,128)(2,1)}, u32[]{:S(2)}) copy-start(bf16[1,1,1,8,208]{4,3,2,1,0:T(8,128)(2,1)} %param.7) | copy-start | bytes 9988
  0.7 16.4 %copy-start = (bf16[1,2,2,676,256]{4,2,3,1,0:T(2,128)(2,1)S(1)}, bf16[1,2,2,676,256]{4,2,3,1,0:T(2,128)(2,1)}, u32[]{:S(2)}) copy-start(bf16[1,2,2,676,256]{4,2,3,1,0:T(2,128)(2,1)} %param.11) | copy-start | bytes 4153348
  0.7 16.4 %copy-start.4 = (f32[1,1,4,256]{3,2,1,0:T(4,128)S(1)}, f32[1,1,4,256]{3,2,1,0:T(4,128)}, u32[]{:S(2)}) copy-start(f32[1,1,4,256]{3,2,1,0:T(4,128)} %param.8) | copy-start | bytes 12292
  0.7 7.7 %collective-permute-start.2 = (bf16[8,208]{1,0:T(8,128)(2,1)}, bf16[8,208]{1,0:T(8,128)(2,1)S(1)}, u32[]{:S(2)}, u32[]{:S(2)}) collective-permute-start(bf16[8,208]{1,0:T(8,128)(2,1)} %bitcast.15), channel_id=1, source_target_pairs={{12,0},{8,4},{4,12},{0,8},{13,1},{9,5},{5,13},{1,9},{14,2},{10,6},... | collective-permute-start | bytes 9992 | tf_op jit(solution)/shard_map/ppermute | solution.py:140
  4.8 4.7 %collective-permute-start.1 = (bf16[8,208]{1,0:T(8,128)(2,1)}, bf16[8,208]{1,0:T(8,128)(2,1)S(1)}, u32[]{:S(2)}, u32[]{:S(2)}) collective-permute-start(bf16[8,208]{1,0:T(8,128)(2,1)} %bitcast.16), channel_id=1, source_target_pairs={{12,4},{8,0},{0,12},{4,8},{13,5},{9,1},{1,13},{5,9},{14,6},{10,2},... | collective-permute-start | bytes 9992 | tf_op jit(solution)/shard_map/ppermute | solution.py:140
  5.8 3.8 %collective-permute-start = (bf16[8,208]{1,0:T(8,128)(2,1)}, bf16[8,208]{1,0:T(8,128)(2,1)S(1)}, u32[]{:S(2)}, u32[]{:S(2)}) collective-permute-start(bf16[8,208]{1,0:T(8,128)(2,1)} %bitcast.17), channel_id=1, source_target_pairs={{4,0},{12,8},{8,12},{0,4},{5,1},{13,9},{9,13},{1,5},{6,2},{14,10},... | collective-permute-start | bytes 9992 | tf_op jit(solution)/shard_map/ppermute | solution.py:140
  6.4 0.7 %copy-start.5 = (s32[2,8]{1,0:T(2,128)S(1)}, s32[2,8]{1,0:T(2,128)}, u32[]{:S(2)}) copy-start(s32[2,8]{1,0:T(2,128)} %map_ref.1) | copy-start | bytes 196
  7.0 0.7 %copy-start.6 = (s32[2]{0:T(128)S(1)}, s32[2]{0:T(128)}, u32[]{:S(2)}) copy-start(s32[2]{0:T(128)} %count_ref.1) | copy-start | bytes 28
  10.0 5.3 %collective-permute-start.5 = (f32[16,256]{1,0:T(8,128)S(1)}, f32[16,256]{1,0:T(8,128)S(1)}, u32[]{:S(2)}, u32[]{:S(2)}) collective-permute-start(f32[16,256]{1,0:T(8,128)S(1)} %get-tuple-element.9.refs_0_), channel_id=1, source_target_pairs={{0,4},{4,12},{8,0},{12,8},{1,5},{5,13},{9,1},{13,9},{2,6},{6,14},{... | collective-permute-start | bytes 49160 | tf_op jit(solution)/shard_map/ppermute | solution.py:140
  11.4 5.5 %collective-permute-start.4 = (f32[16,256]{1,0:T(8,128)S(1)}, f32[16,256]{1,0:T(8,128)S(1)}, u32[]{:S(2)}, u32[]{:S(2)}) collective-permute-start(f32[16,256]{1,0:T(8,128)S(1)} %get-tuple-element.9.refs_0_), channel_id=1, source_target_pairs={{0,12},{12,0},{4,8},{8,4},{1,13},{13,1},{5,9},{9,5},{2,14},{14,2},... | collective-permute-start | bytes 49160 | tf_op jit(solution)/shard_map/ppermute | solution.py:140
  13.3 3.8 %collective-permute-start.3 = (f32[16,256]{1,0:T(8,128)S(1)}, f32[16,256]{1,0:T(8,128)S(1)}, u32[]{:S(2)}, u32[]{:S(2)}) collective-permute-start(f32[16,256]{1,0:T(8,128)S(1)} %get-tuple-element.9.refs_0_), channel_id=1, source_target_pairs={{0,8},{4,0},{8,12},{12,4},{1,9},{5,1},{9,13},{13,5},{2,10},{6,2},{... | collective-permute-start | bytes 49160 | tf_op jit(solution)/shard_map/ppermute | solution.py:140

commit v22 on v10

--- a/solution.py
+++ b/solution.py
@@ -239,7 +239,7 @@
 
 
 def operator_kernel(k_local, *refs):
-    *parts, fields_ref, mask_ref, exchange_ref, chol_ref, out_ref, products, turned_ref = refs
+    *parts, fields_ref, mask_ref, exchange_ref, chol_ref, out_ref, products = refs
     walkers, columns = fields_ref.shape
     bias = parts[0][: 2 * walkers]
     for part in parts[1:]:
@@ -276,26 +276,29 @@
         (((1,), (1,)), ((), ())),
         preferred_element_type=F32,
     )
-    lane = lax.broadcasted_iota(jnp.int32, (pairs, LANES), 1)
-    merged = products[pl.ds(0, pairs, stride=2 * tiles), :]
-    for at in range(1, 2 * tiles):
-        row = products[pl.ds(at, pairs, stride=2 * tiles), :]
-        merged = jnp.where(lane >= at * group, row, merged)
-    turned_ref[:pairs] = merged
     copies, rows, width = out_ref.shape
-    lane = lax.broadcasted_iota(jnp.int32, (rows, LANES), 1)
+    lane = lax.broadcasted_iota(jnp.int32, (LANES, LANES), 1)
+    place = lax.broadcasted_iota(jnp.int32, (rows, LANES), 1)
+    step = 2 * tiles
     for at in range(0, width, LANES):
-        block = turned_ref[at : at + LANES].T
-        block = PROP_STEP * sum(block[n * group : n * group + rows] for n in range(2 * tiles))
-        if at + LANES > pairs:
+        held = min(LANES, pairs - at)
+        merged = products[pl.ds(step * at, held, stride=step), :]
+        for part in range(1, step):
+            row = products[pl.ds(step * at + part, held, stride=step), :]
+            merged = jnp.where(lane[:held] >= part * group, row, merged)
+        if held < LANES:
+            merged = jnp.concatenate([merged, jnp.zeros((LANES - held, LANES), F32)], axis=0)
+        block = merged.T
+        block = PROP_STEP * sum(block[n * group : n * group + rows] for n in range(step))
+        if held < LANES:
             share = jnp.concatenate([energy, jnp.zeros((rows - walkers, 1), F32)], axis=0)
-            block = jnp.where(lane + at < pairs, block, 0.0)
             for piece in range(3):
                 head = share.astype(BF16).astype(F32)
-                block = jnp.where(lane + at == pairs + piece, head, block)
+                block = jnp.where(place == held + piece, head, block)
                 share = share - head
+        block = block.astype(BF16)
         for copy in range(copies):
-            out_ref[copy, :, at : at + LANES] = block.astype(BF16)
+            out_ref[copy, :, at : at + LANES] = block
 
 
 def taylor_kernel(pb_count, normalizer, blocks_ref, *refs):
@@ -414,7 +417,7 @@
     blocks = call(
         functools.partial(operator_kernel, k_local),
         shape((ka_count * pb_count, 2 * span, width), BF16),
-        [pltpu.VMEM((2 * M * M * tiles, LANES), F32), pltpu.VMEM((width, LANES), F32)],
+        [pltpu.VMEM((2 * M * M * tiles, LANES), F32)],
         operands=len(parts) + 4,
     )(*parts, own_fields, mask, shares, full)
     group = operator_group(ka_count, pb_count)

time: 29.8 us -> 29.8 us (level)
  no operation moved by 1% of the time
where the time goes in v22:
time: 29.8 us; the launch traced here: 29.6 us
  starting transfers between devices  10.6 us (36%)
  blocking collectives  9.61 us (32%)
  Pallas kernels  4.18 us (14%)
  waiting for transfers between devices  3.17 us (11%)
  local copies, waits for them, and re-layouts  1.35 us (5%)
  between operations  0.7 us (2%)
    ppermute x6, starting transfers between devices, exchange(): return [array] + [lax.ppermute(array, axis, pairs) for pairs in rounds]  10.6 us
    all_to_all x1, blocking collectives, direct(): lax.all_to_all(blocks, ('pb', 'ka'), 0, 0, axis_index_groups=[group], til...  9.61 us
    ppermute x6, waiting for transfers between devices, exchange(): return [array] + [lax.ppermute(array, axis, pairs) for pairs in rounds]  3.17 us
    pallas_call x1, Pallas kernels, direct(): call(functools.partial(taylor_kernel, pb_count, float(pb_count * chol_col...  2.15 us
    unnamed x14, local copies, waits for them, and re-layouts  1.35 us
    pallas_call x1, Pallas kernels, direct(): call(functools.partial(operator_kernel, k_local), shape((ka_count * pb_co...  0.73 us
    pallas_call x1, Pallas kernels, direct(): call(functools.partial(prepare_kernel, ka_count, pb_count, walkers), (sha...  0.66 us
  transfers between devices with their start and end apart: 6, of which 4 were waited for; matrix products, arithmetic and copies ran while one was open for 0% of the time, Pallas kernels for 3%

profile of v22, /device:TPU:0, one launch (start us, length us, event | category | flops | bytes accessed | tf_op | source)
XLA Modules:
  0.0 29.6 jit_solution(9407304863673447875)
XLA Ops:
  0.6 0.0 copy-start.1
  0.6 0.0 copy-start.2
  0.7 0.0 copy-start.3
  0.7 0.0 copy-start
  0.7 0.0 copy-start.4
  0.7 4.1 %collective-permute-start.2 = (bf16[8,208]{1,0:T(8,128)(2,1)}, bf16[8,208]{1,0:T(8,128)(2,1)S(1)}, u32[]{:S(2)}, u32[]{:S(2)}) collective-permute-start(bf16[8,208]{1,0:T(8,128)(2,1)} %bitcast.15), channel_id=1, source_target_pairs={{12,0},{8,4},{4,12},{0,8},{13,1},{9,5},{5,13},{1,9},{14,2},{10,6},... | collective-permute-start | bytes 9992 | tf_op jit(solution)/shard_map/ppermute | solution.py:140
  4.8 1.1 %collective-permute-start.1 = (bf16[8,208]{1,0:T(8,128)(2,1)}, bf16[8,208]{1,0:T(8,128)(2,1)S(1)}, u32[]{:S(2)}, u32[]{:S(2)}) collective-permute-start(bf16[8,208]{1,0:T(8,128)(2,1)} %bitcast.16), channel_id=1, source_target_pairs={{12,4},{8,0},{0,12},{4,8},{13,5},{9,1},{1,13},{5,9},{14,6},{10,2},... | collective-permute-start | bytes 9992 | tf_op jit(solution)/shard_map/ppermute | solution.py:140
  5.8 0.5 %collective-permute-start = (bf16[8,208]{1,0:T(8,128)(2,1)}, bf16[8,208]{1,0:T(8,128)(2,1)S(1)}, u32[]{:S(2)}, u32[]{:S(2)}) collective-permute-start(bf16[8,208]{1,0:T(8,128)(2,1)} %bitcast.17), channel_id=1, source_target_pairs={{4,0},{12,8},{8,12},{0,4},{5,1},{13,9},{9,13},{1,5},{6,2},{14,10},... | collective-permute-start | bytes 9992 | tf_op jit(solution)/shard_map/ppermute | solution.py:140
  6.4 0.0 copy-start.5
  6.4 0.7 %copy-done.5 = s32[2,8]{1,0:T(2,128)S(1)} copy-done((s32[2,8]{1,0:T(2,128)S(1)}, s32[2,8]{1,0:T(2,128)}, u32[]{:S(2)}) %copy-start.5) | copy-done | bytes 88
  7.0 0.0 copy-start.6
  7.0 0.7 %copy-done.6 = s32[2]{0:T(128)S(1)} copy-done((s32[2]{0:T(128)S(1)}, s32[2]{0:T(128)}, u32[]{:S(2)}) %copy-start.6) | copy-done | bytes 32
  7.7 0.7 %shard_map.86 = (f32[8,256]{1,0:T(8,128)S(1)}, bf16[128,256]{1,0:T(8,128)(2,1)S(1)}) custom-call(s32[2,8]{1,0:T(2,128)S(1)} %copy-done.5, s32[2]{0:T(128)S(1)} %copy-done.6), custom_call_target="tpu_custom_call" | custom-call | flops 1000000000 | tf_op jit(solution)/shard_map/pallas_call | solution.py:395
  8.4 0.0 collective-permute-done.2.refs_3_
  8.4 1.1 %collective-permute-done.1.refs_2_ = bf16[8,208]{1,0:T(8,128)(2,1)S(1)} collective-permute-done((bf16[8,208]{1,0:T(8,128)(2,1)}, bf16[8,208]{1,0:T(8,128)(2,1)S(1)}, u32[]{:S(2)}, u32[]{:S(2)}) %collective-permute-start.1) | collective-permute-done | bytes 3360 | tf_op jit(solution)/shard_map/ppermute | solution.py:140
  9.5 0.2 collective-permute-done.refs_1_
  9.7 0.0 copy-done.1
  9.7 0.0 copy-done.2
  9.7 0.0 copy-done.3
  9.7 0.3 shard_map.87
  10.0 1.4 %collective-permute-start.5 = (f32[16,256]{1,0:T(8,128)S(1)}, f32[16,256]{1,0:T(8,128)S(1)}, u32[]{:S(2)}, u32[]{:S(2)}) collective-permute-start(f32[16,256]{1,0:T(8,128)S(1)} %get-tuple-element.9.refs_0_), channel_id=1, source_target_pairs={{0,4},{4,12},{8,0},{12,8},{1,5},{5,13},{9,1},{13,9},{2,6},{6,14},{... | collective-permute-start | bytes 49160 | tf_op jit(solution)/shard_map/ppermute | solution.py:140
  11.4 1.9 %collective-permute-start.4 = (f32[16,256]{1,0:T(8,128)S(1)}, f32[16,256]{1,0:T(8,128)S(1)}, u32[]{:S(2)}, u32[]{:S(2)}) collective-permute-start(f32[16,256]{1,0:T(8,128)S(1)} %get-tuple-element.9.refs_0_), channel_id=1, source_target_pairs={{0,12},{12,0},{4,8},{8,4},{1,13},{13,1},{5,9},{9,5},{2,14},{14,2},... | collective-permute-start | bytes 49160 | tf_op jit(solution)/shard_map/ppermute | solution.py:140
  13.3 1.6 %collective-permute-start.3 = (f32[16,256]{1,0:T(8,128)S(1)}, f32[16,256]{1,0:T(8,128)S(1)}, u32[]{:S(2)}, u32[]{:S(2)}) collective-permute-start(f32[16,256]{1,0:T(8,128)S(1)} %get-tuple-element.9.refs_0_), channel_id=1, source_target_pairs={{0,8},{4,0},{8,12},{12,4},{1,9},{5,1},{9,13},{13,5},{2,10},{6,2},{... | collective-permute-start | bytes 49160 | tf_op jit(solution)/shard_map/ppermute | solution.py:140
  14.9 0.4 %shard_map.88.refs_6_ = f32[4,128]{1,0:T(4,128)S(1)} custom-call(f32[2,8,104]{2,1,0:T(8,128)S(1)} %get-tuple-element.10.own_ref, bf16[2,2,104,256]{3,2,1,0:T(8,128)(2,1)S(1)} %bitcast.12, f32[8,256]{1,0:T(8,128)S(1)} %get-tuple-element.8.refs_6_.mask_ref.refs_5_), custom_call_target="tpu_custom_call" | custom-call | tf_op jit(solution)/shard_map/pallas_call | solution.py:411
  15.2 0.0 collective-permute-done.5.refs_3_
  15.2 1.7 %collective-permute-done.4.refs_2_ = f32[16,256]{1,0:T(8,128)S(1)} collective-permute-done((f32[16,256]{1,0:T(8,128)S(1)}, f32[16,256]{1,0:T(8,128)S(1)}, u32[]{:S(2)}, u32[]{:S(2)}) %collective-permute-start.4) | collective-permute-done | bytes 16416 | tf_op jit(solution)/shard_map/ppermute | solution.py:140
  16.9 0.2 collective-permute-done.3.refs_1_
  17.1 0.0 copy-done
  17.1 0.0 copy-done.4
  17.1 0.7 %shard_map.89 = bf16[8,16,768]{2,1,0:T(8,128)(2,1)S(1)} custom-call(f32[16,256]{1,0:T(8,128)S(1)} %get-tuple-element.9.refs_0_, f32[16,256]{1,0:T(8,128)S(1)} %collective-permute-done.3.refs_1_, f32[16,256]{1,0:T(8,128)S(1)} %collective-permute-done.4.refs_2_, f32[16,256]{1,0:T(8,128)S(1)} %collective-permute-done.5.refs_3_, f32[4,256]{1,0:T(4,128)S(1)} %bitcast.19, ...), custom_call_target="tpu_custom_call" | custom-call | tf_op jit(solution)/shard_map/pallas_call | solution.py:417
  17.8 9.6 %all_to_all.5.blocks_ref = bf16[8,16,768]{2,1,0:T(8,128)(2,1)S(1)} all-to-all(bf16[8,16,768]{2,1,0:T(8,128)(2,1)S(1)} %shard_map.89), channel_id=1, replica_groups={{10,14,6,2,12,8,4,0},{11,15,7,3,13,9,5,1},{26,30,22,18,28,24,20,16},{27..., dimensions={0} | all-to-all | bytes 393216 | tf_op jit(solution)/shard_map/all_to_all | solution.py:424
  27.4 2.2 %shard_map.90 = (f32[2,4,208]{2,1,0:T(4,128)}, f32[1,1]{1,0:T(1,128)}) custom-call(bf16[8,16,768]{2,1,0:T(8,128)(2,1)S(1)} %all_to_all.5.blocks_ref, f32[16,256]{1,0:T(8,128)S(1)} %get-tuple-element.9.refs_0_, f32[16,256]{1,0:T(8,128)S(1)} %collective-permute-done.3.refs_1_, f32[16,256]{1,0:T(8,128)S(1)} %collective-permute-done.4.refs_2_, ...), custom_call_target="tpu_custom_call" | custom-call | tf_op jit(solution)/shard_map/pallas_call | solution.py:427
Async XLA Ops:
  0.6 9.0 %copy-start.1 = (bf16[1,2,2,104,256]{4,3,2,1,0:T(8,128)(2,1)S(1)}, bf16[1,2,2,104,256]{4,3,2,1,0:T(8,128)(2,1)}, u32[]{:S(2)}) copy-start(bf16[1,2,2,104,256]{4,3,2,1,0:T(8,128)(2,1)} %param.10) | copy-start | bytes 638980
  0.6 9.0 %copy-start.2 = (f32[1,2,4,208]{3,2,1,0:T(4,128)S(1)}, f32[1,2,4,208]{3,2,1,0:T(4,128)}, u32[]{:S(2)}) copy-start(f32[1,2,4,208]{3,2,1,0:T(4,128)} %param.9) | copy-start | bytes 19972
  0.7 9.0 %copy-start.3 = (bf16[1,1,1,8,208]{4,3,2,1,0:T(8,128)(2,1)S(1)}, bf16[1,1,1,8,208]{4,3,2,1,0:T(8,128)(2,1)}, u32[]{:S(2)}) copy-start(bf16[1,1,1,8,208]{4,3,2,1,0:T(8,128)(2,1)} %param.7) | copy-start | bytes 9988
  0.7 16.4 %copy-start = (bf16[1,2,2,676,256]{4,2,3,1,0:T(2,128)(2,1)S(1)}, bf16[1,2,2,676,256]{4,2,3,1,0:T(2,128)(2,1)}, u32[]{:S(2)}) copy-start(bf16[1,2,2,676,256]{4,2,3,1,0:T(2,128)(2,1)} %param.11) | copy-start | bytes 4153348
  0.7 16.4 %copy-start.4 = (f32[1,1,4,256]{3,2,1,0:T(4,128)S(1)}, f32[1,1,4,256]{3,2,1,0:T(4,128)}, u32[]{:S(2)}) copy-start(f32[1,1,4,256]{3,2,1,0:T(4,128)} %param.8) | copy-start | bytes 12292
  0.7 7.7 %collective-permute-start.2 = (bf16[8,208]{1,0:T(8,128)(2,1)}, bf16[8,208]{1,0:T(8,128)(2,1)S(1)}, u32[]{:S(2)}, u32[]{:S(2)}) collective-permute-start(bf16[8,208]{1,0:T(8,128)(2,1)} %bitcast.15), channel_id=1, source_target_pairs={{12,0},{8,4},{4,12},{0,8},{13,1},{9,5},{5,13},{1,9},{14,2},{10,6},... | collective-permute-start | bytes 9992 | tf_op jit(solution)/shard_map/ppermute | solution.py:140
  4.8 4.7 %collective-permute-start.1 = (bf16[8,208]{1,0:T(8,128)(2,1)}, bf16[8,208]{1,0:T(8,128)(2,1)S(1)}, u32[]{:S(2)}, u32[]{:S(2)}) collective-permute-start(bf16[8,208]{1,0:T(8,128)(2,1)} %bitcast.16), channel_id=1, source_target_pairs={{12,4},{8,0},{0,12},{4,8},{13,5},{9,1},{1,13},{5,9},{14,6},{10,2},... | collective-permute-start | bytes 9992 | tf_op jit(solution)/shard_map/ppermute | solution.py:140
  5.8 3.8 %collective-permute-start = (bf16[8,208]{1,0:T(8,128)(2,1)}, bf16[8,208]{1,0:T(8,128)(2,1)S(1)}, u32[]{:S(2)}, u32[]{:S(2)}) collective-permute-start(bf16[8,208]{1,0:T(8,128)(2,1)} %bitcast.17), channel_id=1, source_target_pairs={{4,0},{12,8},{8,12},{0,4},{5,1},{13,9},{9,13},{1,5},{6,2},{14,10},... | collective-permute-start | bytes 9992 | tf_op jit(solution)/shard_map/ppermute | solution.py:140
  6.4 0.7 %copy-start.5 = (s32[2,8]{1,0:T(2,128)S(1)}, s32[2,8]{1,0:T(2,128)}, u32[]{:S(2)}) copy-start(s32[2,8]{1,0:T(2,128)} %map_ref.1) | copy-start | bytes 196
  7.0 0.7 %copy-start.6 = (s32[2]{0:T(128)S(1)}, s32[2]{0:T(128)}, u32[]{:S(2)}) copy-start(s32[2]{0:T(128)} %count_ref.1) | copy-start | bytes 28
  10.0 5.3 %collective-permute-start.5 = (f32[16,256]{1,0:T(8,128)S(1)}, f32[16,256]{1,0:T(8,128)S(1)}, u32[]{:S(2)}, u32[]{:S(2)}) collective-permute-start(f32[16,256]{1,0:T(8,128)S(1)} %get-tuple-element.9.refs_0_), channel_id=1, source_target_pairs={{0,4},{4,12},{8,0},{12,8},{1,5},{5,13},{9,1},{13,9},{2,6},{6,14},{... | collective-permute-start | bytes 49160 | tf_op jit(solution)/shard_map/ppermute | solution.py:140
  11.4 5.5 %collective-permute-start.4 = (f32[16,256]{1,0:T(8,128)S(1)}, f32[16,256]{1,0:T(8,128)S(1)}, u32[]{:S(2)}, u32[]{:S(2)}) collective-permute-start(f32[16,256]{1,0:T(8,128)S(1)} %get-tuple-element.9.refs_0_), channel_id=1, source_target_pairs={{0,12},{12,0},{4,8},{8,4},{1,13},{13,1},{5,9},{9,5},{2,14},{14,2},... | collective-permute-start | bytes 49160 | tf_op jit(solution)/shard_map/ppermute | solution.py:140
  13.3 3.8 %collective-permute-start.3 = (f32[16,256]{1,0:T(8,128)S(1)}, f32[16,256]{1,0:T(8,128)S(1)}, u32[]{:S(2)}, u32[]{:S(2)}) collective-permute-start(f32[16,256]{1,0:T(8,128)S(1)} %get-tuple-element.9.refs_0_), channel_id=1, source_target_pairs={{0,8},{4,0},{8,12},{12,4},{1,9},{5,1},{9,13},{13,5},{2,10},{6,2},{... | collective-permute-start | bytes 49160 | tf_op jit(solution)/shard_map/ppermute | solution.py:140

commit v23 on v22

--- a/solution.py
+++ b/solution.py
@@ -152,9 +152,7 @@
 
 
 def operator_group(ka_count, pb_count):
-    first = (pb_count - 1) * ka_count + ka_count // 2
-    rest = [at for at in range(pb_count * ka_count) if at != first]
-    return [first] + rest[::-1]
+    return list(range(pb_count * ka_count))[::-1]
 
 
 def prepare_kernel(ka_count, pb_count, walkers, map_ref, count_ref, mask_ref, picks_ref):

time: 29.8 us -> 29.9 us (level)
  no operation moved by 1% of the time
where the time goes in v23:
time: 29.9 us; the launch traced here: 29.7 us
  starting transfers between devices  10.6 us (35%)
  blocking collectives  9.75 us (33%)
  Pallas kernels  4.18 us (14%)
  waiting for transfers between devices  3.17 us (11%)
  local copies, waits for them, and re-layouts  1.35 us (5%)
  between operations  0.7 us (2%)
    ppermute x6, starting transfers between devices, exchange(): return [array] + [lax.ppermute(array, axis, pairs) for pairs in rounds]  10.6 us
    all_to_all x1, blocking collectives, direct(): lax.all_to_all(blocks, ('pb', 'ka'), 0, 0, axis_index_groups=[group], til...  9.75 us
    ppermute x6, waiting for transfers between devices, exchange(): return [array] + [lax.ppermute(array, axis, pairs) for pairs in rounds]  3.17 us
    pallas_call x1, Pallas kernels, direct(): call(functools.partial(taylor_kernel, pb_count, float(pb_count * chol_col...  2.15 us
    unnamed x14, local copies, waits for them, and re-layouts  1.35 us
    pallas_call x1, Pallas kernels, direct(): call(functools.partial(operator_kernel, k_local), shape((ka_count * pb_co...  0.73 us
    pallas_call x1, Pallas kernels, direct(): call(functools.partial(prepare_kernel, ka_count, pb_count, walkers), (sha...  0.66 us
  transfers between devices with their start and end apart: 6, of which 4 were waited for; matrix products, arithmetic and copies ran while one was open for 0% of the time, Pallas kernels for 3%

profile of v23, /device:TPU:0, one launch (start us, length us, event | category | flops | bytes accessed | tf_op | source)
XLA Modules:
  0.0 29.7 jit_solution(11337885487725553759)
XLA Ops:
  0.6 0.0 copy-start.1
  0.6 0.0 copy-start.2
  0.7 0.0 copy-start.3
  0.7 0.0 copy-start
  0.7 0.0 copy-start.4
  0.7 4.1 %collective-permute-start.2 = (bf16[8,208]{1,0:T(8,128)(2,1)}, bf16[8,208]{1,0:T(8,128)(2,1)S(1)}, u32[]{:S(2)}, u32[]{:S(2)}) collective-permute-start(bf16[8,208]{1,0:T(8,128)(2,1)} %bitcast.15), channel_id=1, source_target_pairs={{12,0},{8,4},{4,12},{0,8},{13,1},{9,5},{5,13},{1,9},{14,2},{10,6},... | collective-permute-start | bytes 9992 | tf_op jit(solution)/shard_map/ppermute | solution.py:140
  4.8 1.1 %collective-permute-start.1 = (bf16[8,208]{1,0:T(8,128)(2,1)}, bf16[8,208]{1,0:T(8,128)(2,1)S(1)}, u32[]{:S(2)}, u32[]{:S(2)}) collective-permute-start(bf16[8,208]{1,0:T(8,128)(2,1)} %bitcast.16), channel_id=1, source_target_pairs={{12,4},{8,0},{0,12},{4,8},{13,5},{9,1},{1,13},{5,9},{14,6},{10,2},... | collective-permute-start | bytes 9992 | tf_op jit(solution)/shard_map/ppermute | solution.py:140
  5.8 0.5 %collective-permute-start = (bf16[8,208]{1,0:T(8,128)(2,1)}, bf16[8,208]{1,0:T(8,128)(2,1)S(1)}, u32[]{:S(2)}, u32[]{:S(2)}) collective-permute-start(bf16[8,208]{1,0:T(8,128)(2,1)} %bitcast.17), channel_id=1, source_target_pairs={{4,0},{12,8},{8,12},{0,4},{5,1},{13,9},{9,13},{1,5},{6,2},{14,10},... | collective-permute-start | bytes 9992 | tf_op jit(solution)/shard_map/ppermute | solution.py:140
  6.4 0.0 copy-start.5
  6.4 0.7 %copy-done.5 = s32[2,8]{1,0:T(2,128)S(1)} copy-done((s32[2,8]{1,0:T(2,128)S(1)}, s32[2,8]{1,0:T(2,128)}, u32[]{:S(2)}) %copy-start.5) | copy-done | bytes 88
  7.0 0.0 copy-start.6
  7.0 0.7 %copy-done.6 = s32[2]{0:T(128)S(1)} copy-done((s32[2]{0:T(128)S(1)}, s32[2]{0:T(128)}, u32[]{:S(2)}) %copy-start.6) | copy-done | bytes 32
  7.7 0.7 %shard_map.86 = (f32[8,256]{1,0:T(8,128)S(1)}, bf16[128,256]{1,0:T(8,128)(2,1)S(1)}) custom-call(s32[2,8]{1,0:T(2,128)S(1)} %copy-done.5, s32[2]{0:T(128)S(1)} %copy-done.6), custom_call_target="tpu_custom_call" | custom-call | flops 1000000000 | tf_op jit(solution)/shard_map/pallas_call | solution.py:393
  8.4 0.0 collective-permute-done.2.refs_3_
  8.4 1.1 %collective-permute-done.1.refs_2_ = bf16[8,208]{1,0:T(8,128)(2,1)S(1)} collective-permute-done((bf16[8,208]{1,0:T(8,128)(2,1)}, bf16[8,208]{1,0:T(8,128)(2,1)S(1)}, u32[]{:S(2)}, u32[]{:S(2)}) %collective-permute-start.1) | collective-permute-done | bytes 3360 | tf_op jit(solution)/shard_map/ppermute | solution.py:140
  9.5 0.2 collective-permute-done.refs_1_
  9.7 0.0 copy-done.1
  9.7 0.0 copy-done.2
  9.7 0.0 copy-done.3
  9.7 0.3 shard_map.87
  10.0 1.4 %collective-permute-start.5 = (f32[16,256]{1,0:T(8,128)S(1)}, f32[16,256]{1,0:T(8,128)S(1)}, u32[]{:S(2)}, u32[]{:S(2)}) collective-permute-start(f32[16,256]{1,0:T(8,128)S(1)} %get-tuple-element.9.refs_0_), channel_id=1, source_target_pairs={{0,4},{4,12},{8,0},{12,8},{1,5},{5,13},{9,1},{13,9},{2,6},{6,14},{... | collective-permute-start | bytes 49160 | tf_op jit(solution)/shard_map/ppermute | solution.py:140
  11.4 1.9 %collective-permute-start.4 = (f32[16,256]{1,0:T(8,128)S(1)}, f32[16,256]{1,0:T(8,128)S(1)}, u32[]{:S(2)}, u32[]{:S(2)}) collective-permute-start(f32[16,256]{1,0:T(8,128)S(1)} %get-tuple-element.9.refs_0_), channel_id=1, source_target_pairs={{0,12},{12,0},{4,8},{8,4},{1,13},{13,1},{5,9},{9,5},{2,14},{14,2},... | collective-permute-start | bytes 49160 | tf_op jit(solution)/shard_map/ppermute | solution.py:140
  13.3 1.6 %collective-permute-start.3 = (f32[16,256]{1,0:T(8,128)S(1)}, f32[16,256]{1,0:T(8,128)S(1)}, u32[]{:S(2)}, u32[]{:S(2)}) collective-permute-start(f32[16,256]{1,0:T(8,128)S(1)} %get-tuple-element.9.refs_0_), channel_id=1, source_target_pairs={{0,8},{4,0},{8,12},{12,4},{1,9},{5,1},{9,13},{13,5},{2,10},{6,2},{... | collective-permute-start | bytes 49160 | tf_op jit(solution)/shard_map/ppermute | solution.py:140
  14.9 0.4 %shard_map.88.refs_6_ = f32[4,128]{1,0:T(4,128)S(1)} custom-call(f32[2,8,104]{2,1,0:T(8,128)S(1)} %get-tuple-element.10.own_ref, bf16[2,2,104,256]{3,2,1,0:T(8,128)(2,1)S(1)} %bitcast.12, f32[8,256]{1,0:T(8,128)S(1)} %get-tuple-element.8.refs_6_.mask_ref.refs_5_), custom_call_target="tpu_custom_call" | custom-call | tf_op jit(solution)/shard_map/pallas_call | solution.py:409
  15.2 0.0 collective-permute-done.5.refs_3_
  15.2 1.7 %collective-permute-done.4.refs_2_ = f32[16,256]{1,0:T(8,128)S(1)} collective-permute-done((f32[16,256]{1,0:T(8,128)S(1)}, f32[16,256]{1,0:T(8,128)S(1)}, u32[]{:S(2)}, u32[]{:S(2)}) %collective-permute-start.4) | collective-permute-done | bytes 16416 | tf_op jit(solution)/shard_map/ppermute | solution.py:140
  16.9 0.2 collective-permute-done.3.refs_1_
  17.1 0.0 copy-done
  17.1 0.0 copy-done.4
  17.1 0.7 %shard_map.89 = bf16[8,16,768]{2,1,0:T(8,128)(2,1)S(1)} custom-call(f32[16,256]{1,0:T(8,128)S(1)} %get-tuple-element.9.refs_0_, f32[16,256]{1,0:T(8,128)S(1)} %collective-permute-done.3.refs_1_, f32[16,256]{1,0:T(8,128)S(1)} %collective-permute-done.4.refs_2_, f32[16,256]{1,0:T(8,128)S(1)} %collective-permute-done.5.refs_3_, f32[4,256]{1,0:T(4,128)S(1)} %bitcast.19, ...), custom_call_target="tpu_custom_call" | custom-call | tf_op jit(solution)/shard_map/pallas_call | solution.py:415
  17.8 9.7 %all_to_all.5.blocks_ref = bf16[8,16,768]{2,1,0:T(8,128)(2,1)S(1)} all-to-all(bf16[8,16,768]{2,1,0:T(8,128)(2,1)S(1)} %shard_map.89), channel_id=1, replica_groups={{14,10,6,2,12,8,4,0},{15,11,7,3,13,9,5,1},{30,26,22,18,28,24,20,16},{31..., dimensions={0} | all-to-all | bytes 393216 | tf_op jit(solution)/shard_map/all_to_all | solution.py:422
  27.6 2.1 %shard_map.90 = (f32[2,4,208]{2,1,0:T(4,128)}, f32[1,1]{1,0:T(1,128)}) custom-call(bf16[8,16,768]{2,1,0:T(8,128)(2,1)S(1)} %all_to_all.5.blocks_ref, f32[16,256]{1,0:T(8,128)S(1)} %get-tuple-element.9.refs_0_, f32[16,256]{1,0:T(8,128)S(1)} %collective-permute-done.3.refs_1_, f32[16,256]{1,0:T(8,128)S(1)} %collective-permute-done.4.refs_2_, ...), custom_call_target="tpu_custom_call" | custom-call | tf_op jit(solution)/shard_map/pallas_call | solution.py:425
Async XLA Ops:
  0.6 9.0 %copy-start.1 = (bf16[1,2,2,104,256]{4,3,2,1,0:T(8,128)(2,1)S(1)}, bf16[1,2,2,104,256]{4,3,2,1,0:T(8,128)(2,1)}, u32[]{:S(2)}) copy-start(bf16[1,2,2,104,256]{4,3,2,1,0:T(8,128)(2,1)} %param.10) | copy-start | bytes 638980
  0.6 9.0 %copy-start.2 = (f32[1,2,4,208]{3,2,1,0:T(4,128)S(1)}, f32[1,2,4,208]{3,2,1,0:T(4,128)}, u32[]{:S(2)}) copy-start(f32[1,2,4,208]{3,2,1,0:T(4,128)} %param.9) | copy-start | bytes 19972
  0.7 9.0 %copy-start.3 = (bf16[1,1,1,8,208]{4,3,2,1,0:T(8,128)(2,1)S(1)}, bf16[1,1,1,8,208]{4,3,2,1,0:T(8,128)(2,1)}, u32[]{:S(2)}) copy-start(bf16[1,1,1,8,208]{4,3,2,1,0:T(8,128)(2,1)} %param.7) | copy-start | bytes 9988
  0.7 16.4 %copy-start = (bf16[1,2,2,676,256]{4,2,3,1,0:T(2,128)(2,1)S(1)}, bf16[1,2,2,676,256]{4,2,3,1,0:T(2,128)(2,1)}, u32[]{:S(2)}) copy-start(bf16[1,2,2,676,256]{4,2,3,1,0:T(2,128)(2,1)} %param.11) | copy-start | bytes 4153348
  0.7 16.4 %copy-start.4 = (f32[1,1,4,256]{3,2,1,0:T(4,128)S(1)}, f32[1,1,4,256]{3,2,1,0:T(4,128)}, u32[]{:S(2)}) copy-start(f32[1,1,4,256]{3,2,1,0:T(4,128)} %param.8) | copy-start | bytes 12292
  0.7 7.7 %collective-permute-start.2 = (bf16[8,208]{1,0:T(8,128)(2,1)}, bf16[8,208]{1,0:T(8,128)(2,1)S(1)}, u32[]{:S(2)}, u32[]{:S(2)}) collective-permute-start(bf16[8,208]{1,0:T(8,128)(2,1)} %bitcast.15), channel_id=1, source_target_pairs={{12,0},{8,4},{4,12},{0,8},{13,1},{9,5},{5,13},{1,9},{14,2},{10,6},... | collective-permute-start | bytes 9992 | tf_op jit(solution)/shard_map/ppermute | solution.py:140
  4.8 4.7 %collective-permute-start.1 = (bf16[8,208]{1,0:T(8,128)(2,1)}, bf16[8,208]{1,0:T(8,128)(2,1)S(1)}, u32[]{:S(2)}, u32[]{:S(2)}) collective-permute-start(bf16[8,208]{1,0:T(8,128)(2,1)} %bitcast.16), channel_id=1, source_target_pairs={{12,4},{8,0},{0,12},{4,8},{13,5},{9,1},{1,13},{5,9},{14,6},{10,2},... | collective-permute-start | bytes 9992 | tf_op jit(solution)/shard_map/ppermute | solution.py:140
  5.8 3.8 %collective-permute-start = (bf16[8,208]{1,0:T(8,128)(2,1)}, bf16[8,208]{1,0:T(8,128)(2,1)S(1)}, u32[]{:S(2)}, u32[]{:S(2)}) collective-permute-start(bf16[8,208]{1,0:T(8,128)(2,1)} %bitcast.17), channel_id=1, source_target_pairs={{4,0},{12,8},{8,12},{0,4},{5,1},{13,9},{9,13},{1,5},{6,2},{14,10},... | collective-permute-start | bytes 9992 | tf_op jit(solution)/shard_map/ppermute | solution.py:140
  6.4 0.7 %copy-start.5 = (s32[2,8]{1,0:T(2,128)S(1)}, s32[2,8]{1,0:T(2,128)}, u32[]{:S(2)}) copy-start(s32[2,8]{1,0:T(2,128)} %map_ref.1) | copy-start | bytes 196
  7.0 0.7 %copy-start.6 = (s32[2]{0:T(128)S(1)}, s32[2]{0:T(128)}, u32[]{:S(2)}) copy-start(s32[2]{0:T(128)} %count_ref.1) | copy-start | bytes 28
  10.0 5.3 %collective-permute-start.5 = (f32[16,256]{1,0:T(8,128)S(1)}, f32[16,256]{1,0:T(8,128)S(1)}, u32[]{:S(2)}, u32[]{:S(2)}) collective-permute-start(f32[16,256]{1,0:T(8,128)S(1)} %get-tuple-element.9.refs_0_), channel_id=1, source_target_pairs={{0,4},{4,12},{8,0},{12,8},{1,5},{5,13},{9,1},{13,9},{2,6},{6,14},{... | collective-permute-start | bytes 49160 | tf_op jit(solution)/shard_map/ppermute | solution.py:140
  11.4 5.5 %collective-permute-start.4 = (f32[16,256]{1,0:T(8,128)S(1)}, f32[16,256]{1,0:T(8,128)S(1)}, u32[]{:S(2)}, u32[]{:S(2)}) collective-permute-start(f32[16,256]{1,0:T(8,128)S(1)} %get-tuple-element.9.refs_0_), channel_id=1, source_target_pairs={{0,12},{12,0},{4,8},{8,4},{1,13},{13,1},{5,9},{9,5},{2,14},{14,2},... | collective-permute-start | bytes 49160 | tf_op jit(solution)/shard_map/ppermute | solution.py:140
  13.3 3.8 %collective-permute-start.3 = (f32[16,256]{1,0:T(8,128)S(1)}, f32[16,256]{1,0:T(8,128)S(1)}, u32[]{:S(2)}, u32[]{:S(2)}) collective-permute-start(f32[16,256]{1,0:T(8,128)S(1)} %get-tuple-element.9.refs_0_), channel_id=1, source_target_pairs={{0,8},{4,0},{8,12},{12,4},{1,9},{5,1},{9,13},{13,5},{2,10},{6,2},{... | collective-permute-start | bytes 49160 | tf_op jit(solution)/shard_map/ppermute | solution.py:140

commit v24 on v22

--- a/solution.py
+++ b/solution.py
@@ -318,6 +318,7 @@
     count, _, width = blocks_ref.shape
     group = operator_group(count // pb_count, pb_count)
     places = [group.index(n) for n in range(count)]
+    turned[width:] = jnp.zeros((turned.shape[0] - width, LANES), F32)
     for at in range(0, width, LANES):
         tile = jnp.concatenate([blocks_ref[n, :, at : at + LANES] for n in places], axis=0)
         turned[at : at + LANES] = tile.T.astype(F32)
@@ -326,34 +327,33 @@
     shares = jnp.where(lax.rem(lane, 2 * span) == ka_pos, shares, 0.0)
     shares = jnp.sum(jnp.sum(shares, axis=0, keepdims=True), axis=1, keepdims=True)
     energy_ref[...] = shares / normalizer
-    lane = lax.broadcasted_iota(jnp.int32, (M, LANES), 1)
+    lane = lax.broadcasted_iota(jnp.int32, (ROWS, LANES), 1)
     imaginary = lax.rem(lane, 2 * span) >= span
-    sums = [jnp.zeros((M, LANES), F32) for _ in range(NOCC)]
+    sums = [None] * NOCC
     for degree in range(1, TAYLOR + 1):
         stride = M if degree == 1 else ROWS
-        straight = [jnp.zeros((M, LANES), F32) for _ in range(NOCC)]
-        crossed = [jnp.zeros((M, LANES), F32) for _ in range(NOCC)]
+        straight = [jnp.zeros((ROWS, LANES), F32) for _ in range(NOCC)]
+        crossed = [jnp.zeros((ROWS, LANES), F32) for _ in range(NOCC)]
         for c in range(M):
-            column = turned[pl.ds(c, M, stride=M), :]
+            column = turned[pl.ds(c, ROWS, stride=M), :]
             for i in range(NOCC):
                 at = i * stride + c
                 straight[i] += column * picked[at : at + 1, :LANES]
                 crossed[i] += column * picked[at : at + 1, LANES:]
+        currents = []
         for i in range(NOCC):
             other = jnp.where(
                 imaginary, pltpu.roll(crossed[i], span, 1), pltpu.roll(crossed[i], LANES - span, 1)
             )
             applied = straight[i] + other
             applied = applied + pltpu.roll(applied, LANES // pb_count, 1)
-            current = applied / degree
-            sums[i] = sums[i] + current
-            term[i * ROWS : i * ROWS + M] = current if degree < TAYLOR else sums[i]
+            currents.append(applied * (1.0 / degree))
+            sums[i] = currents[i] if degree == 1 else sums[i] + currents[i]
         if degree < TAYLOR:
-            picked[...] = jnp.dot(
-                term[...].astype(BF16), picks_ref[...], preferred_element_type=F32
-            )
-    turned[:LANES] = term[...].T
-    both = turned[pl.ds(pl.multiple_of(ka_pos * (2 * span), 2 * span), 2 * span), :]
+            rows = jnp.concatenate(currents, axis=0).astype(BF16)
+            picked[...] = jnp.dot(rows, picks_ref[...], preferred_element_type=F32)
+    term[...] = jnp.concatenate(sums, axis=0).T
+    both = term[pl.ds(pl.multiple_of(ka_pos * (2 * span), 2 * span), 2 * span), :]
     both = jnp.concatenate([both[:, i * ROWS : i * ROWS + M] for i in range(NOCC)], axis=1)
     both = jnp.concatenate([both[:span], both[span:]], axis=1)
     for k in range(k_local):
@@ -428,7 +428,7 @@
         functools.partial(taylor_kernel, pb_count, float(pb_count * chol_cols)),
         (shape((k_local, walkers, 2 * pair_width), F32), shape((1, 1), F32)),
         [
-            pltpu.VMEM((width, LANES), F32),
+            pltpu.VMEM((ROWS * M, LANES), F32),
             pltpu.VMEM((NOCC * ROWS, 2 * LANES), F32),
             pltpu.VMEM((LANES, LANES), F32),
         ],

time: 29.8 us -> 29.8 us (level)
  no operation moved by 1% of the time
where the time goes in v24:
time: 29.8 us; the launch traced here: 29.6 us
  starting transfers between devices  10.6 us (36%)
  blocking collectives  9.61 us (32%)
  Pallas kernels  4.15 us (14%)
  waiting for transfers between devices  3.17 us (11%)
  local copies, waits for them, and re-layouts  1.35 us (5%)
  between operations  0.7 us (2%)
    ppermute x6, starting transfers between devices, exchange(): return [array] + [lax.ppermute(array, axis, pairs) for pairs in rounds]  10.6 us
    all_to_all x1, blocking collectives, direct(): lax.all_to_all(blocks, ('pb', 'ka'), 0, 0, axis_index_groups=[group], til...  9.61 us
    ppermute x6, waiting for transfers between devices, exchange(): return [array] + [lax.ppermute(array, axis, pairs) for pairs in rounds]  3.17 us
    pallas_call x1, Pallas kernels, direct(): call(functools.partial(taylor_kernel, pb_count, float(pb_count * chol_col...  2.12 us
    unnamed x14, local copies, waits for them, and re-layouts  1.35 us
    pallas_call x1, Pallas kernels, direct(): call(functools.partial(operator_kernel, k_local), shape((ka_count * pb_co...  0.73 us
    pallas_call x1, Pallas kernels, direct(): call(functools.partial(prepare_kernel, ka_count, pb_count, walkers), (sha...  0.66 us
  transfers between devices with their start and end apart: 6, of which 4 were waited for; matrix products, arithmetic and copies ran while one was open for 0% of the time, Pallas kernels for 3%

profile of v24, /device:TPU:0, one launch (start us, length us, event | category | flops | bytes accessed | tf_op | source)
XLA Modules:
  0.0 29.6 jit_solution(5900668396372263476)
XLA Ops:
  0.6 0.0 copy-start.1
  0.6 0.0 copy-start.2
  0.7 0.0 copy-start.3
  0.7 0.0 copy-start
  0.7 0.0 copy-start.4
  0.7 4.1 %collective-permute-start.2 = (bf16[8,208]{1,0:T(8,128)(2,1)}, bf16[8,208]{1,0:T(8,128)(2,1)S(1)}, u32[]{:S(2)}, u32[]{:S(2)}) collective-permute-start(bf16[8,208]{1,0:T(8,128)(2,1)} %bitcast.15), channel_id=1, source_target_pairs={{12,0},{8,4},{4,12},{0,8},{13,1},{9,5},{5,13},{1,9},{14,2},{10,6},... | collective-permute-start | bytes 9992 | tf_op jit(solution)/shard_map/ppermute | solution.py:140
  4.8 1.1 %collective-permute-start.1 = (bf16[8,208]{1,0:T(8,128)(2,1)}, bf16[8,208]{1,0:T(8,128)(2,1)S(1)}, u32[]{:S(2)}, u32[]{:S(2)}) collective-permute-start(bf16[8,208]{1,0:T(8,128)(2,1)} %bitcast.16), channel_id=1, source_target_pairs={{12,4},{8,0},{0,12},{4,8},{13,5},{9,1},{1,13},{5,9},{14,6},{10,2},... | collective-permute-start | bytes 9992 | tf_op jit(solution)/shard_map/ppermute | solution.py:140
  5.8 0.5 %collective-permute-start = (bf16[8,208]{1,0:T(8,128)(2,1)}, bf16[8,208]{1,0:T(8,128)(2,1)S(1)}, u32[]{:S(2)}, u32[]{:S(2)}) collective-permute-start(bf16[8,208]{1,0:T(8,128)(2,1)} %bitcast.17), channel_id=1, source_target_pairs={{4,0},{12,8},{8,12},{0,4},{5,1},{13,9},{9,13},{1,5},{6,2},{14,10},... | collective-permute-start | bytes 9992 | tf_op jit(solution)/shard_map/ppermute | solution.py:140
  6.4 0.0 copy-start.5
  6.4 0.7 %copy-done.5 = s32[2,8]{1,0:T(2,128)S(1)} copy-done((s32[2,8]{1,0:T(2,128)S(1)}, s32[2,8]{1,0:T(2,128)}, u32[]{:S(2)}) %copy-start.5) | copy-done | bytes 88
  7.0 0.0 copy-start.6
  7.0 0.7 %copy-done.6 = s32[2]{0:T(128)S(1)} copy-done((s32[2]{0:T(128)S(1)}, s32[2]{0:T(128)}, u32[]{:S(2)}) %copy-start.6) | copy-done | bytes 32
  7.7 0.7 %shard_map.86 = (f32[8,256]{1,0:T(8,128)S(1)}, bf16[128,256]{1,0:T(8,128)(2,1)S(1)}) custom-call(s32[2,8]{1,0:T(2,128)S(1)} %copy-done.5, s32[2]{0:T(128)S(1)} %copy-done.6), custom_call_target="tpu_custom_call" | custom-call | flops 1000000000 | tf_op jit(solution)/shard_map/pallas_call | solution.py:395
  8.4 0.0 collective-permute-done.2.refs_3_
  8.4 1.1 %collective-permute-done.1.refs_2_ = bf16[8,208]{1,0:T(8,128)(2,1)S(1)} collective-permute-done((bf16[8,208]{1,0:T(8,128)(2,1)}, bf16[8,208]{1,0:T(8,128)(2,1)S(1)}, u32[]{:S(2)}, u32[]{:S(2)}) %collective-permute-start.1) | collective-permute-done | bytes 3360 | tf_op jit(solution)/shard_map/ppermute | solution.py:140
  9.5 0.2 collective-permute-done.refs_1_
  9.7 0.0 copy-done.1
  9.7 0.0 copy-done.2
  9.7 0.0 copy-done.3
  9.7 0.3 shard_map.87
  10.0 1.4 %collective-permute-start.5 = (f32[16,256]{1,0:T(8,128)S(1)}, f32[16,256]{1,0:T(8,128)S(1)}, u32[]{:S(2)}, u32[]{:S(2)}) collective-permute-start(f32[16,256]{1,0:T(8,128)S(1)} %get-tuple-element.9.refs_0_), channel_id=1, source_target_pairs={{0,4},{4,12},{8,0},{12,8},{1,5},{5,13},{9,1},{13,9},{2,6},{6,14},{... | collective-permute-start | bytes 49160 | tf_op jit(solution)/shard_map/ppermute | solution.py:140
  11.4 1.9 %collective-permute-start.4 = (f32[16,256]{1,0:T(8,128)S(1)}, f32[16,256]{1,0:T(8,128)S(1)}, u32[]{:S(2)}, u32[]{:S(2)}) collective-permute-start(f32[16,256]{1,0:T(8,128)S(1)} %get-tuple-element.9.refs_0_), channel_id=1, source_target_pairs={{0,12},{12,0},{4,8},{8,4},{1,13},{13,1},{5,9},{9,5},{2,14},{14,2},... | collective-permute-start | bytes 49160 | tf_op jit(solution)/shard_map/ppermute | solution.py:140
  13.3 1.6 %collective-permute-start.3 = (f32[16,256]{1,0:T(8,128)S(1)}, f32[16,256]{1,0:T(8,128)S(1)}, u32[]{:S(2)}, u32[]{:S(2)}) collective-permute-start(f32[16,256]{1,0:T(8,128)S(1)} %get-tuple-element.9.refs_0_), channel_id=1, source_target_pairs={{0,8},{4,0},{8,12},{12,4},{1,9},{5,1},{9,13},{13,5},{2,10},{6,2},{... | collective-permute-start | bytes 49160 | tf_op jit(solution)/shard_map/ppermute | solution.py:140
  14.9 0.4 %shard_map.88.refs_6_ = f32[4,128]{1,0:T(4,128)S(1)} custom-call(f32[2,8,104]{2,1,0:T(8,128)S(1)} %get-tuple-element.10.own_ref, bf16[2,2,104,256]{3,2,1,0:T(8,128)(2,1)S(1)} %bitcast.12, f32[8,256]{1,0:T(8,128)S(1)} %get-tuple-element.8.refs_6_.mask_ref.refs_5_), custom_call_target="tpu_custom_call" | custom-call | tf_op jit(solution)/shard_map/pallas_call | solution.py:411
  15.2 0.0 collective-permute-done.5.refs_3_
  15.2 1.7 %collective-permute-done.4.refs_2_ = f32[16,256]{1,0:T(8,128)S(1)} collective-permute-done((f32[16,256]{1,0:T(8,128)S(1)}, f32[16,256]{1,0:T(8,128)S(1)}, u32[]{:S(2)}, u32[]{:S(2)}) %collective-permute-start.4) | collective-permute-done | bytes 16416 | tf_op jit(solution)/shard_map/ppermute | solution.py:140
  16.9 0.2 collective-permute-done.3.refs_1_
  17.1 0.0 copy-done
  17.1 0.0 copy-done.4
  17.1 0.7 %shard_map.89 = bf16[8,16,768]{2,1,0:T(8,128)(2,1)S(1)} custom-call(f32[16,256]{1,0:T(8,128)S(1)} %get-tuple-element.9.refs_0_, f32[16,256]{1,0:T(8,128)S(1)} %collective-permute-done.3.refs_1_, f32[16,256]{1,0:T(8,128)S(1)} %collective-permute-done.4.refs_2_, f32[16,256]{1,0:T(8,128)S(1)} %collective-permute-done.5.refs_3_, f32[4,256]{1,0:T(4,128)S(1)} %bitcast.19, ...), custom_call_target="tpu_custom_call" | custom-call | tf_op jit(solution)/shard_map/pallas_call | solution.py:417
  17.8 9.6 %all_to_all.5.blocks_ref = bf16[8,16,768]{2,1,0:T(8,128)(2,1)S(1)} all-to-all(bf16[8,16,768]{2,1,0:T(8,128)(2,1)S(1)} %shard_map.89), channel_id=1, replica_groups={{10,14,6,2,12,8,4,0},{11,15,7,3,13,9,5,1},{26,30,22,18,28,24,20,16},{27..., dimensions={0} | all-to-all | bytes 393216 | tf_op jit(solution)/shard_map/all_to_all | solution.py:424
  27.4 2.1 %shard_map.90 = (f32[2,4,208]{2,1,0:T(4,128)}, f32[1,1]{1,0:T(1,128)}) custom-call(bf16[8,16,768]{2,1,0:T(8,128)(2,1)S(1)} %all_to_all.5.blocks_ref, f32[16,256]{1,0:T(8,128)S(1)} %get-tuple-element.9.refs_0_, f32[16,256]{1,0:T(8,128)S(1)} %collective-permute-done.3.refs_1_, f32[16,256]{1,0:T(8,128)S(1)} %collective-permute-done.4.refs_2_, ...), custom_call_target="tpu_custom_call" | custom-call | tf_op jit(solution)/shard_map/pallas_call | solution.py:427
Async XLA Ops:
  0.6 9.0 %copy-start.1 = (bf16[1,2,2,104,256]{4,3,2,1,0:T(8,128)(2,1)S(1)}, bf16[1,2,2,104,256]{4,3,2,1,0:T(8,128)(2,1)}, u32[]{:S(2)}) copy-start(bf16[1,2,2,104,256]{4,3,2,1,0:T(8,128)(2,1)} %param.10) | copy-start | bytes 638980
  0.6 9.0 %copy-start.2 = (f32[1,2,4,208]{3,2,1,0:T(4,128)S(1)}, f32[1,2,4,208]{3,2,1,0:T(4,128)}, u32[]{:S(2)}) copy-start(f32[1,2,4,208]{3,2,1,0:T(4,128)} %param.9) | copy-start | bytes 19972
  0.7 9.0 %copy-start.3 = (bf16[1,1,1,8,208]{4,3,2,1,0:T(8,128)(2,1)S(1)}, bf16[1,1,1,8,208]{4,3,2,1,0:T(8,128)(2,1)}, u32[]{:S(2)}) copy-start(bf16[1,1,1,8,208]{4,3,2,1,0:T(8,128)(2,1)} %param.7) | copy-start | bytes 9988
  0.7 16.4 %copy-start = (bf16[1,2,2,676,256]{4,2,3,1,0:T(2,128)(2,1)S(1)}, bf16[1,2,2,676,256]{4,2,3,1,0:T(2,128)(2,1)}, u32[]{:S(2)}) copy-start(bf16[1,2,2,676,256]{4,2,3,1,0:T(2,128)(2,1)} %param.11) | copy-start | bytes 4153348
  0.7 16.4 %copy-start.4 = (f32[1,1,4,256]{3,2,1,0:T(4,128)S(1)}, f32[1,1,4,256]{3,2,1,0:T(4,128)}, u32[]{:S(2)}) copy-start(f32[1,1,4,256]{3,2,1,0:T(4,128)} %param.8) | copy-start | bytes 12292
  0.7 7.7 %collective-permute-start.2 = (bf16[8,208]{1,0:T(8,128)(2,1)}, bf16[8,208]{1,0:T(8,128)(2,1)S(1)}, u32[]{:S(2)}, u32[]{:S(2)}) collective-permute-start(bf16[8,208]{1,0:T(8,128)(2,1)} %bitcast.15), channel_id=1, source_target_pairs={{12,0},{8,4},{4,12},{0,8},{13,1},{9,5},{5,13},{1,9},{14,2},{10,6},... | collective-permute-start | bytes 9992 | tf_op jit(solution)/shard_map/ppermute | solution.py:140
  4.8 4.7 %collective-permute-start.1 = (bf16[8,208]{1,0:T(8,128)(2,1)}, bf16[8,208]{1,0:T(8,128)(2,1)S(1)}, u32[]{:S(2)}, u32[]{:S(2)}) collective-permute-start(bf16[8,208]{1,0:T(8,128)(2,1)} %bitcast.16), channel_id=1, source_target_pairs={{12,4},{8,0},{0,12},{4,8},{13,5},{9,1},{1,13},{5,9},{14,6},{10,2},... | collective-permute-start | bytes 9992 | tf_op jit(solution)/shard_map/ppermute | solution.py:140
  5.8 3.8 %collective-permute-start = (bf16[8,208]{1,0:T(8,128)(2,1)}, bf16[8,208]{1,0:T(8,128)(2,1)S(1)}, u32[]{:S(2)}, u32[]{:S(2)}) collective-permute-start(bf16[8,208]{1,0:T(8,128)(2,1)} %bitcast.17), channel_id=1, source_target_pairs={{4,0},{12,8},{8,12},{0,4},{5,1},{13,9},{9,13},{1,5},{6,2},{14,10},... | collective-permute-start | bytes 9992 | tf_op jit(solution)/shard_map/ppermute | solution.py:140
  6.4 0.7 %copy-start.5 = (s32[2,8]{1,0:T(2,128)S(1)}, s32[2,8]{1,0:T(2,128)}, u32[]{:S(2)}) copy-start(s32[2,8]{1,0:T(2,128)} %map_ref.1) | copy-start | bytes 196
  7.0 0.7 %copy-start.6 = (s32[2]{0:T(128)S(1)}, s32[2]{0:T(128)}, u32[]{:S(2)}) copy-start(s32[2]{0:T(128)} %count_ref.1) | copy-start | bytes 28
  10.0 5.3 %collective-permute-start.5 = (f32[16,256]{1,0:T(8,128)S(1)}, f32[16,256]{1,0:T(8,128)S(1)}, u32[]{:S(2)}, u32[]{:S(2)}) collective-permute-start(f32[16,256]{1,0:T(8,128)S(1)} %get-tuple-element.9.refs_0_), channel_id=1, source_target_pairs={{0,4},{4,12},{8,0},{12,8},{1,5},{5,13},{9,1},{13,9},{2,6},{6,14},{... | collective-permute-start | bytes 49160 | tf_op jit(solution)/shard_map/ppermute | solution.py:140
  11.4 5.5 %collective-permute-start.4 = (f32[16,256]{1,0:T(8,128)S(1)}, f32[16,256]{1,0:T(8,128)S(1)}, u32[]{:S(2)}, u32[]{:S(2)}) collective-permute-start(f32[16,256]{1,0:T(8,128)S(1)} %get-tuple-element.9.refs_0_), channel_id=1, source_target_pairs={{0,12},{12,0},{4,8},{8,4},{1,13},{13,1},{5,9},{9,5},{2,14},{14,2},... | collective-permute-start | bytes 49160 | tf_op jit(solution)/shard_map/ppermute | solution.py:140
  13.3 3.8 %collective-permute-start.3 = (f32[16,256]{1,0:T(8,128)S(1)}, f32[16,256]{1,0:T(8,128)S(1)}, u32[]{:S(2)}, u32[]{:S(2)}) collective-permute-start(f32[16,256]{1,0:T(8,128)S(1)} %get-tuple-element.9.refs_0_), channel_id=1, source_target_pairs={{0,8},{4,0},{8,12},{12,4},{1,9},{5,1},{9,13},{13,5},{2,10},{6,2},{... | collective-permute-start | bytes 49160 | tf_op jit(solution)/shard_map/ppermute | solution.py:140
